TPU v7x, 32 devices: a whole 2x2x4 slice. The times are simulated.
32 devices in a mesh: seq: 4 (over z), enc: 8 (over y, x, core).
Axes of the slice: x: 2, y: 2, z: 4, core: 2. Of those that a mesh axis runs over, the one named last changes fastest.
Arguments:
- queries: bfloat16 [4096, 4096], P(('seq', 'enc')), may hold values from -8 to 8
- keys: bfloat16 [8, 1601, 512], P('enc'), may hold values from -8 to 8
- values: bfloat16 [8, 1601, 512], P('enc'), may hold values from -24 to 24
- reads: int32 [32, 4], replicated, may hold values from 0 to 7, all different within a row; in each aligned block of 8 rows (0 to 7, 8 to 15, ...) at most 6 rows name the same one
- grad_out: bfloat16 [4096, 4096], P(('seq', 'enc')), may hold values from -24 to 24
Outputs:
- attended: bfloat16 [4096, 4096], P(('seq', 'enc'))
- grad_queries: bfloat16 [4096, 4096], P(('seq', 'enc'))
- grad_keys: bfloat16 [8, 1601, 512], P('enc', None, 'seq')
- grad_values: bfloat16 [8, 1601, 512], P('enc', None, 'seq')
Inputs may be any that keep to these rules, and one draw needn't show every extreme that they name: `reads`: each row names 4 different images; in each aligned block of 8 rows (the text blocks of one index of seq) no image is named by more than 6 rows, and in some such block one image is named by exactly 6.
All inputs are finite; a program needn't handle non-finite values.
Results may differ from a plain program's by a relative error of at most 0.04.
Values may be sent and summed in bfloat16 or wider, within the bound.
No kernel may reach another device: no remote copies, remote signals or barrier semaphores. Data moves between devices by JAX's collectives and lax.ppermute only.
A program may use at most 128 MiB of HBM per device.

v0:
```python
import functools

import jax
import jax.numpy as jnp
from jax import lax
from jax.experimental import pallas as pl
from jax.experimental.pallas import tpu as pltpu
from jax.sharding import PartitionSpec as P

HQ = 32
KVH = 4
HD = 128
GROUP = HQ // KVH
WIDTH = GROUP * HD
SCALE = HD ** (-0.5)
LOG2E = 1.4426950408889634
CHUNK = 256
LOWEST = -3.0e38
PER_CHUNK = 2
ANY = pl.BlockSpec(memory_space=pl.ANY)
SMEM = pl.BlockSpec(memory_space=pltpu.SMEM)
VMEM = pl.BlockSpec(memory_space=pltpu.VMEM)


def head_at(turn):
    if lax.axis_size("seq") == KVH:
        return lax.axis_index("seq") ^ (KVH - 1 - turn)
    return turn


def route_kernel(turns, n_seg, seg_rows, reads, q_hbm, g_hbm, out, stage, in_sems, out_sems):
    row = lax.axis_index("seq") * lax.axis_size("enc") + lax.axis_index("enc")
    arriving = []
    for i, turn in enumerate(turns):
        column = pl.multiple_of(head_at(turn) * WIDTH, WIDTH)
        for which, source in enumerate((q_hbm, g_hbm)):
            arriving.append(
                pltpu.make_async_copy(
                    source.at[:, pl.ds(column, WIDTH)], stage.at[i, which], in_sems.at[i, which]
                )
            )
    for copy in arriving:
        copy.start()
    for copy in arriving:
        copy.wait()
    leaving = [
        pltpu.make_async_copy(
            stage.at[:, :, r * seg_rows : (r + 1) * seg_rows, :],
            out.at[reads[row, r]],
            out_sems.at[r],
        )
        for r in range(n_seg)
    ]
    for copy in leaving:
        copy.start()
    for copy in leaving:
        copy.wait()


def collect_kernel(chunks, n_seg, seg_rows, reads, *refs):
    returned = refs[: len(chunks)]
    o_out, dq_out, sems = refs[len(chunks) :]
    row = lax.axis_index("seq") * lax.axis_size("enc") + lax.axis_index("enc")
    copies = []
    for c, turns in enumerate(chunks):
        for i, turn in enumerate(turns):
            column = pl.multiple_of(head_at(turn) * WIDTH, WIDTH)
            for r in range(n_seg):
                for which, target in enumerate((o_out, dq_out)):
                    copies.append(
                        pltpu.make_async_copy(
                            returned[c].at[reads[row, r], i, which],
                            target.at[r * seg_rows : (r + 1) * seg_rows, pl.ds(column, WIDTH)],
                            sems.at[turn, r, which],
                        )
                    )
    for copy in copies:
        copy.start()
    for copy in copies:
        copy.wait()


def is_read(reads, row, image):
    found = jnp.int32(0)
    for r in range(reads.shape[1]):
        found = found + (reads[row, r] == image).astype(jnp.int32)
    return found > 0


def attend_kernel(turn, place, peers, seg_rows, tokens, reads, k_hbm, v_hbm, received, *refs):
    (
        returned,
        grads,
        k_raw,
        v_raw,
        k_pad,
        v_pad,
        k_turned,
        v_turned,
        inbox,
        outbox,
        scores,
        weights,
        dscores,
        dk_sum,
        dv_sum,
        kv_sems,
        in_sems,
        out_sems,
    ) = refs[-18:]
    me = lax.axis_index("enc")
    base = lax.axis_index("seq") * peers
    column = pl.multiple_of(head_at(turn) * HD, HD)
    padded = k_pad.shape[0]
    whole = tokens // 16 * 16

    kv_copies = [
        pltpu.make_async_copy(source.at[0, :, pl.ds(column, HD)], target, kv_sems.at[i])
        for i, (source, target) in enumerate(((k_hbm, k_raw), (v_hbm, v_raw)))
    ]
    for copy in kv_copies:
        copy.start()

    count = jnp.int32(0)
    plan = []
    for k in range(peers):
        found = is_read(reads, base + k, me)
        plan.append((found, count))
        count = count + found.astype(jnp.int32)

    def arriving(k, slot):
        return pltpu.make_async_copy(received.at[k, place], inbox.at[slot], in_sems.at[k])

    def leaving(k, slot):
        return pltpu.make_async_copy(outbox.at[slot], returned.at[k, place], out_sems.at[k])

    for k, (found, slot) in enumerate(plan):

        @pl.when(found)
        def _():
            arriving(k, slot).start()

    for copy in kv_copies:
        copy.wait()
    for raw, pad, turned in ((k_raw, k_pad, k_turned), (v_raw, v_pad, v_turned)):
        pad[0:whole, :] = raw[0:whole, :]
        if whole < tokens:
            last = jnp.zeros((padded - tokens, HD), jnp.bfloat16)
            pad[whole:padded, :] = jnp.concatenate([raw[whole:tokens, :], last], axis=0)
        turned[...] = pad[...].astype(jnp.float32).T.astype(jnp.bfloat16)
    dk_sum[...] = jnp.zeros_like(dk_sum)
    dv_sum[...] = jnp.zeros_like(dv_sum)

    for k, (found, slot) in enumerate(plan):

        @pl.when(found)
        def _():
            arriving(k, slot).wait()

    pieces = [(a, min(a + CHUNK, padded)) for a in range(0, padded, CHUNK)]
    lanes = GROUP * seg_rows
    over_d = (((1,), (1,)), ((), ()))

    def stacked(slot, which):
        return jnp.concatenate(
            [inbox[slot, which, :, h * HD : (h + 1) * HD] for h in range(GROUP)], axis=0
        )

    def store(slot, which, turned_value):
        value = turned_value.T.astype(jnp.bfloat16)
        for h in range(GROUP):
            outbox[slot, which, :, h * HD : (h + 1) * HD] = value[
                h * seg_rows : (h + 1) * seg_rows, :
            ]

    def one_slot(slot, carry):
        q = stacked(slot, 0)
        g = stacked(slot, 1)
        top = jnp.full((1, lanes), LOWEST, jnp.float32)
        for a, b in pieces:
            part = lax.dot_general(k_pad[a:b, :], q, over_d, preferred_element_type=jnp.float32)
            if b > tokens:
                token = lax.broadcasted_iota(jnp.int32, part.shape, 0) + a
                part = jnp.where(token < tokens, part, LOWEST)
            scores[a:b, :] = part
            top = jnp.maximum(top, jnp.max(part, axis=0, keepdims=True))
        total = jnp.zeros((1, lanes), jnp.float32)
        for a, b in pieces:
            part = jnp.exp2((scores[a:b, :] - top) * (SCALE * LOG2E))
            total = total + jnp.sum(part, axis=0, keepdims=True)
            scores[a:b, :] = part
            weights[a:b, :] = part.astype(jnp.bfloat16)
        inverse = 1.0 / total
        out = jnp.dot(v_turned[...], weights[...], preferred_element_type=jnp.float32) * inverse
        store(slot, 0, out)
        g_turned = g.astype(jnp.float32).T * inverse
        g_scaled = g_turned.T.astype(jnp.bfloat16)
        delta = jnp.sum(
            g_turned * out.astype(jnp.bfloat16).astype(jnp.float32), axis=0, keepdims=True
        )
        for a, b in pieces:
            part = lax.dot_general(
                v_pad[a:b, :], g_scaled, over_d, preferred_element_type=jnp.float32
            )
            part = (scores[a:b, :] * (part - delta)).astype(jnp.bfloat16)
            dscores[a:b, :] = part
            dk_sum[a:b, :] += jnp.dot(part, q, preferred_element_type=jnp.float32)
            dv_sum[a:b, :] += jnp.dot(
                weights[a:b, :], g_scaled, preferred_element_type=jnp.float32
            )
        turned_dq = jnp.dot(k_turned[...], dscores[...], preferred_element_type=jnp.float32)
        store(slot, 1, turned_dq * SCALE)
        return carry

    lax.fori_loop(0, count, one_slot, 0)

    for k, (found, slot) in enumerate(plan):

        @pl.when(found)
        def _():
            leaving(k, slot).start()

    grads[0] = (dk_sum[...] * SCALE).astype(jnp.bfloat16)
    grads[1] = dv_sum[...].astype(jnp.bfloat16)

    for k, (found, slot) in enumerate(plan):

        @pl.when(found)
        def _():
            leaving(k, slot).wait()


def xor_permute(array, axis, k):
    if k == 0:
        return array
    size = lax.axis_size(axis)
    return lax.ppermute(array, axis, [(i, i ^ k) for i in range(size)])


def per_device(queries, keys, values, reads, grad_out):
    peers = lax.axis_size("enc")
    n_seq = lax.axis_size("seq")
    n_seg = reads.shape[1]
    seg_rows = queries.shape[0] // n_seg
    slots = min(peers, 3 * n_seg // 2)
    tokens = keys.shape[1]
    padded = (tokens + 15) // 16 * 16
    lanes = GROUP * seg_rows
    bf16, f32 = jnp.bfloat16, jnp.float32
    chunks = [tuple(range(i, i + PER_CHUNK)) for i in range(0, KVH, PER_CHUNK)]
    message = jax.ShapeDtypeStruct((peers, PER_CHUNK, 2, seg_rows, WIDTH), bf16)

    def route(turns):
        return pl.pallas_call(
            functools.partial(route_kernel, turns, n_seg, seg_rows),
            out_shape=message,
            in_specs=[SMEM, ANY, ANY],
            out_specs=ANY,
            scratch_shapes=[
                pltpu.VMEM((PER_CHUNK, 2, n_seg * seg_rows, WIDTH), bf16),
                pltpu.SemaphoreType.DMA((PER_CHUNK, 2)),
                pltpu.SemaphoreType.DMA((n_seg,)),
            ],
            cost_estimate=pl.CostEstimate(flops=0, bytes_accessed=2 << 20, transcendentals=0),
            name=f"route_{turns[0]}",
        )(reads, queries, grad_out)

    def attend(turn, received, returned):
        work = slots * lanes * tokens * HD
        first = returned is None
        return pl.pallas_call(
            functools.partial(
                attend_kernel, turn, turn % PER_CHUNK, peers, seg_rows, tokens
            ),
            out_shape=[message, jax.ShapeDtypeStruct((2, padded, HD), bf16)],
            in_specs=[SMEM] + [ANY] * (3 if first else 4),
            out_specs=[ANY, VMEM],
            input_output_aliases={} if first else {4: 0},
            scratch_shapes=[
                pltpu.VMEM((tokens, HD), bf16),
                pltpu.VMEM((tokens, HD), bf16),
                pltpu.VMEM((padded, HD), bf16),
                pltpu.VMEM((padded, HD), bf16),
                pltpu.VMEM((HD, padded), bf16),
                pltpu.VMEM((HD, padded), bf16),
                pltpu.VMEM((slots, 2, seg_rows, WIDTH), bf16),
                pltpu.VMEM((slots, 2, seg_rows, WIDTH), bf16),
                pltpu.VMEM((padded, lanes), f32),
                pltpu.VMEM((padded, lanes), bf16),
                pltpu.VMEM((padded, lanes), bf16),
                pltpu.VMEM((padded, HD), f32),
                pltpu.VMEM((padded, HD), f32),
                pltpu.SemaphoreType.DMA((2,)),
                pltpu.SemaphoreType.DMA((peers,)),
                pltpu.SemaphoreType.DMA((peers,)),
            ],
            compiler_params=pltpu.CompilerParams(vmem_limit_bytes=40 << 20),
            cost_estimate=pl.CostEstimate(
                flops=24 * work, bytes_accessed=4 << 20, transcendentals=slots * lanes * tokens
            ),
            name=f"attend_{turn}",
        )(reads, keys, values, received, *([] if first else [returned]))

    def collect(returned):
        whole = jax.ShapeDtypeStruct(queries.shape, bf16)
        return pl.pallas_call(
            functools.partial(collect_kernel, chunks, n_seg, seg_rows),
            out_shape=[whole, whole],
            in_specs=[SMEM] + [ANY] * len(chunks),
            out_specs=[VMEM, VMEM],
            scratch_shapes=[pltpu.SemaphoreType.DMA((KVH, n_seg, 2))],
            cost_estimate=pl.CostEstimate(flops=0, bytes_accessed=4 << 20, transcendentals=0),
            name="collect",
        )(reads, *returned)

    def exchange(array):
        return lax.all_to_all(array, "enc", split_axis=0, concat_axis=0, tiled=True)

    received = [exchange(route(turns)) for turns in chunks]
    answers, grads = [], []
    for c, turns in enumerate(chunks):
        returned = None
        arrived = received[c]
        if grads:
            arrived, grads[-1] = lax.optimization_barrier((arrived, grads[-1]))
        for turn in turns:
            returned, grad = attend(turn, arrived, returned)
            grads.append(grad)
        answers.append(exchange(returned))
    attended, grad_queries = collect(answers)

    if n_seq == KVH:
        passed = xor_permute(grads[0], "seq", 1)
        pair = (grads[1].astype(f32) + passed.astype(f32)).astype(bf16)
        pair = xor_permute(pair, "seq", 2)
        near = xor_permute(grads[2], "seq", 1)
        total = grads[3].astype(f32) + near.astype(f32) + pair.astype(f32)
        total = total.astype(bf16)[:, :tokens]
        return attended, grad_queries, total[0][None], total[1][None]
    joined = jnp.concatenate(grads, axis=2)[:, :tokens]
    summed = lax.psum_scatter(joined, "seq", scatter_dimension=2, tiled=True)
    return attended, grad_queries, summed[0][None], summed[1][None]


def solution(mesh):
    placed = (
        P(("seq", "enc"), None),
        P("enc", None, None),
        P("enc", None, None),
        P(),
        P(("seq", "enc"), None),
    )
    return jax.shard_map(
        per_device,
        mesh=mesh,
        in_specs=placed,
        out_specs=(
            P(("seq", "enc"), None),
            P(("seq", "enc"), None),
            P("enc", None, "seq"),
            P("enc", None, "seq"),
        ),
        check_vma=False,
    )
```

profile of v0, /device:TPU:0, one launch (start us, length us, event | category | flops | bytes accessed | tf_op | source)
XLA Modules:
  0.0 175.4 jit_solution(14780814715760043333)
XLA Ops:
  0.6 1.4 copy.17.reads
  2.0 3.2 %route_0.1 = bf16[8,2,2,32,1024]{4,3,2,1,0:T(8,128)(2,1)} custom-call(s32[32,4]{1,0:T(8,128)} %copy.17.reads, bf16[128,4096]{1,0:T(8,128)(2,1)} %q_hbm.3, bf16[128,4096]{1,0:T(8,128)(2,1)} %g_hbm.3), custom_call_target="tpu_custom_call" | custom-call | bytes 2097152 | tf_op jit(solution)/shard_map/route_0/pallas_call | solution.py:254
  5.2 5.2 %all-to-all-start = ((bf16[8,2,2,32,1024]{4,3,2,1,0:T(8,128)(2,1)}), bf16[8,2,2,32,1024]{4,3,2,1,0:T(8,128)(2,1)S(1)}, u32[]{:S(2)}, u32[]{:S(2)}) async-start(bf16[8,2,2,32,1024]{4,3,2,1,0:T(8,128)(2,1)} %route_0.1), calls=%async_computation | async-start | bytes 4194304 | tf_op jit(solution)/shard_map/all_to_all | solution.py:317
  10.3 3.2 %route_2.1 = bf16[8,2,2,32,1024]{4,3,2,1,0:T(8,128)(2,1)} custom-call(s32[32,4]{1,0:T(8,128)} %copy.17.reads, bf16[128,4096]{1,0:T(8,128)(2,1)} %q_hbm.3, bf16[128,4096]{1,0:T(8,128)(2,1)} %g_hbm.3), custom_call_target="tpu_custom_call" | custom-call | bytes 2097152 | tf_op jit(solution)/shard_map/route_2/pallas_call | solution.py:254
  13.5 23.4 %all-to-all-done.received = bf16[8,2,2,32,1024]{4,3,2,1,0:T(8,128)(2,1)S(1)} async-done(((bf16[8,2,2,32,1024]{4,3,2,1,0:T(8,128)(2,1)}), bf16[8,2,2,32,1024]{4,3,2,1,0:T(8,128)(2,1)S(1)}, u32[]{:S(2)}, u32[]{:S(2)}) %all-to-all-start) | async-done | bytes 2097184 | tf_op jit(solution)/shard_map/all_to_all | solution.py:317
  37.0 1.3 copy-done
  38.3 3.6 %all-to-all-start.2 = ((bf16[8,2,2,32,1024]{4,3,2,1,0:T(8,128)(2,1)}), bf16[8,2,2,32,1024]{4,3,2,1,0:T(8,128)(2,1)S(1)}, u32[]{:S(2)}, u32[]{:S(2)}) async-start(bf16[8,2,2,32,1024]{4,3,2,1,0:T(8,128)(2,1)} %route_2.1), calls=%async_computation.2 | async-start | bytes 4194304 | tf_op jit(solution)/shard_map/all_to_all | solution.py:317
  41.9 1.6 copy-done.1
  43.5 1.4 copy-done.5
  44.9 1.4 copy-done.7
  46.4 16.8 %attend_0.1 = (bf16[8,2,2,32,1024]{4,3,2,1,0:T(8,128)(2,1)S(1)}, bf16[2,1616,128]{2,1,0:T(8,128)(2,1)}) custom-call(s32[32,4]{1,0:T(8,128)S(1)} %copy-done.4, bf16[1,1601,512]{2,1,0:T(8,128)(2,1)S(1)} %copy-done.5, bf16[1,1601,512]{2,1,0:T(8,128)(2,1)S(1)} %copy-done.7, bf16[8,2,2,32,1024]{4,3,2,1,0:T(8,128)(2,1)S(1)} %copy-done.1), custom_call_target="tpu_custom_call" | custom-call | flops 7554465792 | bytes 4194304 | tf_op jit(solution)/shard_map/attend_0/pallas_call | solution.py:271
  63.2 0.1 collective-permute-start.1
  63.2 15.9 %attend_1.1 = (bf16[8,2,2,32,1024]{4,3,2,1,0:T(8,128)(2,1)S(1)}, bf16[2,1616,128]{2,1,0:T(8,128)(2,1)S(1)}) custom-call(s32[32,4]{1,0:T(8,128)S(1)} %copy-done.4, bf16[1,1601,512]{2,1,0:T(8,128)(2,1)S(1)} %copy-done.5, bf16[1,1601,512]{2,1,0:T(8,128)(2,1)S(1)} %copy-done.7, ...), custom_call_target="tpu_custom_call", output_to_operand_aliasing={{0}: (4, {})} | custom-call | flops 7554465792 | bytes 4194304 | tf_op jit(solution)/shard_map/attend_1/pallas_call | solution.py:271
  79.1 1.3 copy-done.3
  80.4 0.0 all-to-all-done.2.received
  80.4 10.4 %all-to-all-start.1 = ((bf16[8,2,2,32,1024]{4,3,2,1,0:T(8,128)(2,1)}), bf16[8,2,2,32,1024]{4,3,2,1,0:T(8,128)(2,1)}, u32[]{:S(2)}, u32[]{:S(2)}) async-start(bf16[8,2,2,32,1024]{4,3,2,1,0:T(8,128)(2,1)} %copy-done.3), calls=%async_computation.1 | async-start | bytes 4194304 | tf_op jit(solution)/shard_map/all_to_all | solution.py:317
  90.8 1.4 copy-done.6
  92.2 1.4 copy-done.8
  93.7 16.8 %attend_2.1 = (bf16[8,2,2,32,1024]{4,3,2,1,0:T(8,128)(2,1)S(1)}, bf16[2,1616,128]{2,1,0:T(8,128)(2,1)}) custom-call(s32[32,4]{1,0:T(8,128)S(1)} %copy-done.4, bf16[1,1601,512]{2,1,0:T(8,128)(2,1)S(1)} %copy-done.6, bf16[1,1601,512]{2,1,0:T(8,128)(2,1)S(1)} %copy-done.8, bf16[8,2,2,32,1024]{4,3,2,1,0:T(8,128)(2,1)S(1)} %all-to-all-done.2.received), custom_call_target="tpu_custom_call" | custom-call | flops 7554465792 | bytes 4194304 | tf_op jit(solution)/shard_map/attend_2/pallas_call | solution.py:271
  110.5 0.1 collective-permute-start
  110.6 2.3 %add_convert_fusion.1 = bf16[2,1616,128]{2,1,0:T(8,128)(2,1)} fusion(bf16[2,1616,128]{2,1,0:T(8,128)(2,1)} %collective-permute-done.1, bf16[2,1616,128]{2,1,0:T(8,128)(2,1)S(1)} %get-tuple-element.26), kind=kLoop, calls=%fused_computation.1 | loop fusion | flops 1654784 | bytes 2482176 | tf_op jit(solution)/shard_map/convert_element_type | solution.py:334
  112.8 0.6 collective-permute-start.2
  113.4 16.0 %attend_3.1 = (bf16[8,2,2,32,1024]{4,3,2,1,0:T(8,128)(2,1)S(1)}, bf16[2,1616,128]{2,1,0:T(8,128)(2,1)S(1)}) custom-call(s32[32,4]{1,0:T(8,128)S(1)} %copy-done.4, bf16[1,1601,512]{2,1,0:T(8,128)(2,1)S(1)} %copy-done.6, bf16[1,1601,512]{2,1,0:T(8,128)(2,1)S(1)} %copy-done.8, ...), custom_call_target="tpu_custom_call", output_to_operand_aliasing={{0}: (4, {})} | custom-call | flops 7554465792 | bytes 4194304 | tf_op jit(solution)/shard_map/attend_3/pallas_call | solution.py:271
  129.4 1.4 copy-done.2
  130.8 0.0 all-to-all-done.1.refs_0_
  130.8 12.4 %all-to-all-start.3 = ((bf16[8,2,2,32,1024]{4,3,2,1,0:T(8,128)(2,1)}), bf16[8,2,2,32,1024]{4,3,2,1,0:T(8,128)(2,1)S(1)}, u32[]{:S(2)}, u32[]{:S(2)}) async-start(bf16[8,2,2,32,1024]{4,3,2,1,0:T(8,128)(2,1)} %copy-done.2), calls=%async_computation.3 | async-start | bytes 4194304 | tf_op jit(solution)/shard_map/all_to_all | solution.py:317
  143.2 9.8 %collective-permute-done.2 = bf16[2,1616,128]{2,1,0:T(8,128)(2,1)} collective-permute-done((bf16[2,1616,128]{2,1,0:T(8,128)(2,1)}, bf16[2,1616,128]{2,1,0:T(8,128)(2,1)}, u32[]{:S(2)}, u32[]{:S(2)}) %collective-permute-start.2) | collective-permute-done | bytes 827424 | tf_op jit(solution)/shard_map/ppermute | solution.py:237
  153.1 1.7 add_convert_fusion
  154.8 0.9 fusion
  155.7 14.1 %all-to-all-done.3.refs_1_ = bf16[8,2,2,32,1024]{4,3,2,1,0:T(8,128)(2,1)S(1)} async-done(((bf16[8,2,2,32,1024]{4,3,2,1,0:T(8,128)(2,1)}), bf16[8,2,2,32,1024]{4,3,2,1,0:T(8,128)(2,1)S(1)}, u32[]{:S(2)}, u32[]{:S(2)}) %all-to-all-start.3) | async-done | bytes 2097184 | tf_op jit(solution)/shard_map/all_to_all | solution.py:317
  169.9 1.3 copy-done.9
  171.2 4.1 %collect.1 = (bf16[128,4096]{1,0:T(8,128)(2,1)}, bf16[128,4096]{1,0:T(8,128)(2,1)}) custom-call(s32[32,4]{1,0:T(8,128)} %copy.17.reads, bf16[8,2,2,32,1024]{4,3,2,1,0:T(8,128)(2,1)} %all-to-all-done.1.refs_0_, bf16[8,2,2,32,1024]{4,3,2,1,0:T(8,128)(2,1)} %copy-done.9), custom_call_target="tpu_custom_call" | custom-call | bytes 4194304 | tf_op jit(solution)/shard_map/collect/pallas_call | solution.py:306
  (13 shorter events, 0.0 us)
Async XLA Ops:
  5.2 31.8 %all-to-all-start = ((bf16[8,2,2,32,1024]{4,3,2,1,0:T(8,128)(2,1)}), bf16[8,2,2,32,1024]{4,3,2,1,0:T(8,128)(2,1)S(1)}, u32[]{:S(2)}, u32[]{:S(2)}) async-start(bf16[8,2,2,32,1024]{4,3,2,1,0:T(8,128)(2,1)} %route_0.1), calls=%async_computation | async-start | bytes 4194304 | tf_op jit(solution)/shard_map/all_to_all | solution.py:317
  13.5 28.4 %copy-start.4 = (s32[32,4]{1,0:T(8,128)S(1)}, s32[32,4]{1,0:T(8,128)}, u32[]{:S(2)}) copy-start(s32[32,4]{1,0:T(8,128)} %copy.17.reads) | copy-start | bytes 1540
  37.0 1.3 copy-start
  38.3 42.2 %all-to-all-start.2 = ((bf16[8,2,2,32,1024]{4,3,2,1,0:T(8,128)(2,1)}), bf16[8,2,2,32,1024]{4,3,2,1,0:T(8,128)(2,1)S(1)}, u32[]{:S(2)}, u32[]{:S(2)}) async-start(bf16[8,2,2,32,1024]{4,3,2,1,0:T(8,128)(2,1)} %route_2.1), calls=%async_computation.2 | async-start | bytes 4194304 | tf_op jit(solution)/shard_map/all_to_all | solution.py:317
  41.9 1.6 copy-start.1
  43.5 1.4 copy-start.5
  44.9 1.4 copy-start.7
  63.2 47.4 %collective-permute-start.1 = (bf16[2,1616,128]{2,1,0:T(8,128)(2,1)}, bf16[2,1616,128]{2,1,0:T(8,128)(2,1)}, u32[]{:S(2)}, u32[]{:S(2)}) collective-permute-start(bf16[2,1616,128]{2,1,0:T(8,128)(2,1)} %get-tuple-element.27), channel_id=1, source_target_pairs={{0,8},{8,0},{16,24},{24,16},{1,9},{9,1},{17,25},{25,17},{2,10},{10... | collective-permute-start | bytes 2482184 | tf_op jit(solution)/shard_map/ppermute | solution.py:237
  79.1 1.3 copy-start.3
  80.4 50.4 %all-to-all-start.1 = ((bf16[8,2,2,32,1024]{4,3,2,1,0:T(8,128)(2,1)}), bf16[8,2,2,32,1024]{4,3,2,1,0:T(8,128)(2,1)}, u32[]{:S(2)}, u32[]{:S(2)}) async-start(bf16[8,2,2,32,1024]{4,3,2,1,0:T(8,128)(2,1)} %copy-done.3), calls=%async_computation.1 | async-start | bytes 4194304 | tf_op jit(solution)/shard_map/all_to_all | solution.py:317
  90.8 1.4 copy-start.6
  92.2 1.4 copy-start.8
  110.5 32.7 %collective-permute-start = (bf16[2,1616,128]{2,1,0:T(8,128)(2,1)}, bf16[2,1616,128]{2,1,0:T(8,128)(2,1)}, u32[]{:S(2)}, u32[]{:S(2)}) collective-permute-start(bf16[2,1616,128]{2,1,0:T(8,128)(2,1)} %get-tuple-element.25), channel_id=1, source_target_pairs={{0,8},{8,0},{16,24},{24,16},{1,9},{9,1},{17,25},{25,17},{2,10},{10... | collective-permute-start | bytes 2482184 | tf_op jit(solution)/shard_map/ppermute | solution.py:237
  112.8 40.2 %collective-permute-start.2 = (bf16[2,1616,128]{2,1,0:T(8,128)(2,1)}, bf16[2,1616,128]{2,1,0:T(8,128)(2,1)}, u32[]{:S(2)}, u32[]{:S(2)}) collective-permute-start(bf16[2,1616,128]{2,1,0:T(8,128)(2,1)} %add_convert_fusion.1), channel_id=1, source_target_pairs={{0,16},{8,24},{16,0},{24,8},{1,17},{9,25},{17,1},{25,9},{2,18},{10... | collective-permute-start | bytes 2482184 | tf_op jit(solution)/shard_map/ppermute | solution.py:237
  129.4 1.4 copy-start.2
  130.8 39.1 %all-to-all-start.3 = ((bf16[8,2,2,32,1024]{4,3,2,1,0:T(8,128)(2,1)}), bf16[8,2,2,32,1024]{4,3,2,1,0:T(8,128)(2,1)S(1)}, u32[]{:S(2)}, u32[]{:S(2)}) async-start(bf16[8,2,2,32,1024]{4,3,2,1,0:T(8,128)(2,1)} %copy-done.2), calls=%async_computation.3 | async-start | bytes 4194304 | tf_op jit(solution)/shard_map/all_to_all | solution.py:317
  169.9 1.3 copy-start.9
where the time goes:
time: 176 us; the launch traced here: 175 us
  Pallas kernels  75.9 us (43%)
  waiting for transfers between devices  47.4 us (27%)
  starting transfers between devices  32.3 us (18%)
  local copies, waits for them, and re-layouts  14.9 us (8%)
  other arithmetic  3.98 us (2%)
    pallas_call x4, Pallas kernels, attend(): pl.pallas_call(functools.partial(attend_kernel, turn, turn % PER_CHUNK, p...  65.5 us
    all_to_all x4, waiting for transfers between devices, exchange(): return lax.all_to_all(array, 'enc', split_axis=0, concat_axis=0, tiled=True)  37.6 us
    all_to_all x4, starting transfers between devices, exchange(): return lax.all_to_all(array, 'enc', split_axis=0, concat_axis=0, tiled=True)  31.5 us
    unnamed x21, local copies, waits for them, and re-layouts  13.9 us
    ppermute x3, waiting for transfers between devices, xor_permute(): return lax.ppermute(array, axis, [(i, i ^ k) for i in range(size)])  9.84 us
    pallas_call x2, Pallas kernels, route(): pl.pallas_call(functools.partial(route_kernel, turns, n_seg, seg_rows), o...  6.36 us
    pallas_call x1, Pallas kernels, collect(): pl.pallas_call(functools.partial(collect_kernel, chunks, n_seg, seg_rows)...  4.09 us
  transfers between devices with their start and end apart: 7, of which 3 were waited for; matrix products, arithmetic and copies ran while one was open for 3% of the time, Pallas kernels for 39%

commit v1 on v0

--- a/solution.py
+++ b/solution.py
@@ -14,9 +14,10 @@
 WIDTH = GROUP * HD
 SCALE = HD ** (-0.5)
 LOG2E = 1.4426950408889634
-CHUNK = 256
+CHUNK = 512
 LOWEST = -3.0e38
 PER_CHUNK = 2
+VMEM_BYTES = 58 << 20
 ANY = pl.BlockSpec(memory_space=pl.ANY)
 SMEM = pl.BlockSpec(memory_space=pltpu.SMEM)
 VMEM = pl.BlockSpec(memory_space=pltpu.VMEM)
@@ -46,7 +47,7 @@
     leaving = [
         pltpu.make_async_copy(
             stage.at[:, :, r * seg_rows : (r + 1) * seg_rows, :],
-            out.at[reads[row, r]],
+            out.at[reads[r, row]],
             out_sems.at[r],
         )
         for r in range(n_seg)
@@ -69,7 +70,7 @@
                 for which, target in enumerate((o_out, dq_out)):
                     copies.append(
                         pltpu.make_async_copy(
-                            returned[c].at[reads[row, r], i, which],
+                            returned[c].at[reads[r, row], i, which],
                             target.at[r * seg_rows : (r + 1) * seg_rows, pl.ds(column, WIDTH)],
                             sems.at[turn, r, which],
                         )
@@ -82,21 +83,34 @@
 
 def is_read(reads, row, image):
     found = jnp.int32(0)
-    for r in range(reads.shape[1]):
-        found = found + (reads[row, r] == image).astype(jnp.int32)
+    for r in range(reads.shape[0]):
+        found = found + (reads[r, row] == image).astype(jnp.int32)
     return found > 0
 
 
-def attend_kernel(turn, place, peers, seg_rows, tokens, reads, k_hbm, v_hbm, received, *refs):
+def prepare_kernel(tokens, k_in, v_in, straight, turned):
+    padded = straight.shape[2]
+    whole = tokens // 16 * 16
+    for which, source in enumerate((k_in, v_in)):
+        for head in range(KVH):
+            columns = slice(head * HD, (head + 1) * HD)
+            straight[head, which, 0:whole, :] = source[0, 0:whole, columns]
+            if whole < tokens:
+                last = jnp.zeros((padded - tokens, HD), jnp.bfloat16)
+                straight[head, which, whole:padded, :] = jnp.concatenate(
+                    [source[0, whole:tokens, columns], last], axis=0
+                )
+            turned[head, which] = (
+                straight[head, which].astype(jnp.float32).T.astype(jnp.bfloat16)
+            )
+
+
+def attend_kernel(turn, place, peers, seg_rows, tokens, reads, caches, turned_caches, received, *refs):
     (
         returned,
         grads,
-        k_raw,
-        v_raw,
-        k_pad,
-        v_pad,
-        k_turned,
-        v_turned,
+        straight,
+        turned,
         inbox,
         outbox,
         scores,
@@ -107,16 +121,13 @@
         kv_sems,
         in_sems,
         out_sems,
-    ) = refs[-18:]
+    ) = refs[-14:]
     me = lax.axis_index("enc")
     base = lax.axis_index("seq") * peers
-    column = pl.multiple_of(head_at(turn) * HD, HD)
-    padded = k_pad.shape[0]
-    whole = tokens // 16 * 16
-
+    padded = straight.shape[1]
     kv_copies = [
-        pltpu.make_async_copy(source.at[0, :, pl.ds(column, HD)], target, kv_sems.at[i])
-        for i, (source, target) in enumerate(((k_hbm, k_raw), (v_hbm, v_raw)))
+        pltpu.make_async_copy(source.at[head_at(turn)], target, kv_sems.at[i])
+        for i, (source, target) in enumerate(((caches, straight), (turned_caches, turned)))
     ]
     for copy in kv_copies:
         copy.start()
@@ -140,14 +151,6 @@
         def _():
             arriving(k, slot).start()
 
-    for copy in kv_copies:
-        copy.wait()
-    for raw, pad, turned in ((k_raw, k_pad, k_turned), (v_raw, v_pad, v_turned)):
-        pad[0:whole, :] = raw[0:whole, :]
-        if whole < tokens:
-            last = jnp.zeros((padded - tokens, HD), jnp.bfloat16)
-            pad[whole:padded, :] = jnp.concatenate([raw[whole:tokens, :], last], axis=0)
-        turned[...] = pad[...].astype(jnp.float32).T.astype(jnp.bfloat16)
     dk_sum[...] = jnp.zeros_like(dk_sum)
     dv_sum[...] = jnp.zeros_like(dv_sum)
 
@@ -157,9 +160,12 @@
         def _():
             arriving(k, slot).wait()
 
+    for copy in kv_copies:
+        copy.wait()
     pieces = [(a, min(a + CHUNK, padded)) for a in range(0, padded, CHUNK)]
     lanes = GROUP * seg_rows
-    over_d = (((1,), (1,)), ((), ()))
+    f32, bf16 = jnp.float32, jnp.bfloat16
+    keys, values = straight.at[0], straight.at[1]
 
     def stacked(slot, which):
         return jnp.concatenate(
@@ -167,52 +173,79 @@
         )
 
     def store(slot, which, turned_value):
-        value = turned_value.T.astype(jnp.bfloat16)
+        value = turned_value.T.astype(bf16)
         for h in range(GROUP):
             outbox[slot, which, :, h * HD : (h + 1) * HD] = value[
                 h * seg_rows : (h + 1) * seg_rows, :
             ]
 
+    def masked(part, a, b, other):
+        if b <= tokens:
+            return part
+        token = lax.broadcasted_iota(jnp.int32, part.shape, 0) + a
+        return jnp.where(token < tokens, part, other)
+
+    def forward(slot):
+        q, g = (stacked(slot, i).astype(f32).T for i in range(2))
+        q_turned = q.astype(bf16)
+        state = {"top": jnp.full((1, lanes), LOWEST, f32), "total": jnp.zeros((1, lanes), f32)}
+
+        def score(a, b):
+            part = jnp.dot(keys[a:b, :], q_turned, preferred_element_type=f32)
+            part = masked(part, a, b, LOWEST)
+            scores[a:b, :] = part
+            state["top"] = jnp.maximum(state["top"], jnp.max(part, axis=0, keepdims=True))
+
+        def weigh(a, b):
+            part = jnp.exp2((scores[a:b, :] - state["top"]) * (SCALE * LOG2E))
+            state["total"] = state["total"] + jnp.sum(part, axis=0, keepdims=True)
+            weights[a:b, :] = part.astype(bf16)
+
+        def finish():
+            out = jnp.dot(turned[1], weights[...], preferred_element_type=f32)
+            out = out * (1.0 / state["total"])
+            store(slot, 0, out)
+            delta = jnp.sum(g * out.astype(bf16).astype(f32), axis=0, keepdims=True)
+            lse = state["top"] * (SCALE * LOG2E) + jnp.log2(state["total"])
+            return lse, delta, q_turned, g.astype(bf16)
+
+        steps = [functools.partial(score, a, b) for a, b in pieces]
+        return steps + [functools.partial(weigh, a, b) for a, b in pieces], finish
+
+    def backward(slot, lse, delta, q_turned, g_turned):
+        q, g = stacked(slot, 0), stacked(slot, 1)
+
+        def step(a, b):
+            part = jnp.dot(keys[a:b, :], q_turned, preferred_element_type=f32)
+            prob = masked(jnp.exp2(part * (SCALE * LOG2E) - lse), a, b, 0.0)
+            dprob = jnp.dot(values[a:b, :], g_turned, preferred_element_type=f32)
+            dscore = (prob * (dprob - delta)).astype(bf16)
+            dscores[a:b, :] = dscore
+            dk_sum[a:b, :] += jnp.dot(dscore, q, preferred_element_type=f32)
+            dv_sum[a:b, :] += jnp.dot(prob.astype(bf16), g, preferred_element_type=f32)
+
+        def finish():
+            turned_dq = jnp.dot(turned[0], dscores[...], preferred_element_type=f32)
+            store(slot, 1, turned_dq * SCALE)
+
+        return [functools.partial(step, a, b) for a, b in pieces], finish
+
     def one_slot(slot, carry):
-        q = stacked(slot, 0)
-        g = stacked(slot, 1)
-        top = jnp.full((1, lanes), LOWEST, jnp.float32)
-        for a, b in pieces:
-            part = lax.dot_general(k_pad[a:b, :], q, over_d, preferred_element_type=jnp.float32)
-            if b > tokens:
-                token = lax.broadcasted_iota(jnp.int32, part.shape, 0) + a
-                part = jnp.where(token < tokens, part, LOWEST)
-            scores[a:b, :] = part
-            top = jnp.maximum(top, jnp.max(part, axis=0, keepdims=True))
-        total = jnp.zeros((1, lanes), jnp.float32)
-        for a, b in pieces:
-            part = jnp.exp2((scores[a:b, :] - top) * (SCALE * LOG2E))
-            total = total + jnp.sum(part, axis=0, keepdims=True)
-            scores[a:b, :] = part
-            weights[a:b, :] = part.astype(jnp.bfloat16)
-        inverse = 1.0 / total
-        out = jnp.dot(v_turned[...], weights[...], preferred_element_type=jnp.float32) * inverse
-        store(slot, 0, out)
-        g_turned = g.astype(jnp.float32).T * inverse
-        g_scaled = g_turned.T.astype(jnp.bfloat16)
-        delta = jnp.sum(
-            g_turned * out.astype(jnp.bfloat16).astype(jnp.float32), axis=0, keepdims=True
-        )
-        for a, b in pieces:
-            part = lax.dot_general(
-                v_pad[a:b, :], g_scaled, over_d, preferred_element_type=jnp.float32
-            )
-            part = (scores[a:b, :] * (part - delta)).astype(jnp.bfloat16)
-            dscores[a:b, :] = part
-            dk_sum[a:b, :] += jnp.dot(part, q, preferred_element_type=jnp.float32)
-            dv_sum[a:b, :] += jnp.dot(
-                weights[a:b, :], g_scaled, preferred_element_type=jnp.float32
-            )
-        turned_dq = jnp.dot(k_turned[...], dscores[...], preferred_element_type=jnp.float32)
-        store(slot, 1, turned_dq * SCALE)
-        return carry
-
-    lax.fori_loop(0, count, one_slot, 0)
+        ahead, ahead_finish = forward(jnp.minimum(slot + 1, count - 1))
+        behind, behind_finish = backward(slot, *carry)
+        for i, step in enumerate(behind):
+            for other in ahead[2 * i : 2 * i + 2]:
+                other()
+            step()
+        behind_finish()
+        return ahead_finish()
+
+    @pl.when(count > 0)
+    def _():
+        first, first_finish = forward(0)
+        for step in first:
+            step()
+        lax.fori_loop(0, count, one_slot, first_finish())
 
     for k, (found, slot) in enumerate(plan):
 
@@ -241,6 +274,7 @@
     peers = lax.axis_size("enc")
     n_seq = lax.axis_size("seq")
     n_seg = reads.shape[1]
+    by_segment = reads.T
     seg_rows = queries.shape[0] // n_seg
     slots = min(peers, 3 * n_seg // 2)
     tokens = keys.shape[1]
@@ -261,9 +295,23 @@
                 pltpu.SemaphoreType.DMA((PER_CHUNK, 2)),
                 pltpu.SemaphoreType.DMA((n_seg,)),
             ],
+            compiler_params=pltpu.CompilerParams(vmem_limit_bytes=VMEM_BYTES),
             cost_estimate=pl.CostEstimate(flops=0, bytes_accessed=2 << 20, transcendentals=0),
             name=f"route_{turns[0]}",
-        )(reads, queries, grad_out)
+        )(by_segment, queries, grad_out)
+
+    prepared = pl.pallas_call(
+        functools.partial(prepare_kernel, tokens),
+        out_shape=[
+            jax.ShapeDtypeStruct((KVH, 2, padded, HD), bf16),
+            jax.ShapeDtypeStruct((KVH, 2, HD, padded), bf16),
+        ],
+        in_specs=[VMEM, VMEM],
+        out_specs=[VMEM, VMEM],
+        compiler_params=pltpu.CompilerParams(vmem_limit_bytes=VMEM_BYTES),
+        cost_estimate=pl.CostEstimate(flops=0, bytes_accessed=16 << 20, transcendentals=0),
+        name="prepare",
+    )(keys, values)
 
     def attend(turn, received, returned):
         work = slots * lanes * tokens * HD
@@ -277,12 +325,8 @@
             out_specs=[ANY, VMEM],
             input_output_aliases={} if first else {4: 0},
             scratch_shapes=[
-                pltpu.VMEM((tokens, HD), bf16),
-                pltpu.VMEM((tokens, HD), bf16),
-                pltpu.VMEM((padded, HD), bf16),
-                pltpu.VMEM((padded, HD), bf16),
-                pltpu.VMEM((HD, padded), bf16),
-                pltpu.VMEM((HD, padded), bf16),
+                pltpu.VMEM((2, padded, HD), bf16),
+                pltpu.VMEM((2, HD, padded), bf16),
                 pltpu.VMEM((slots, 2, seg_rows, WIDTH), bf16),
                 pltpu.VMEM((slots, 2, seg_rows, WIDTH), bf16),
                 pltpu.VMEM((padded, lanes), f32),
@@ -294,12 +338,12 @@
                 pltpu.SemaphoreType.DMA((peers,)),
                 pltpu.SemaphoreType.DMA((peers,)),
             ],
-            compiler_params=pltpu.CompilerParams(vmem_limit_bytes=40 << 20),
+            compiler_params=pltpu.CompilerParams(vmem_limit_bytes=VMEM_BYTES),
             cost_estimate=pl.CostEstimate(
                 flops=24 * work, bytes_accessed=4 << 20, transcendentals=slots * lanes * tokens
             ),
             name=f"attend_{turn}",
-        )(reads, keys, values, received, *([] if first else [returned]))
+        )(by_segment, *prepared, received, *([] if first else [returned]))
 
     def collect(returned):
         whole = jax.ShapeDtypeStruct(queries.shape, bf16)
@@ -309,9 +353,10 @@
             in_specs=[SMEM] + [ANY] * len(chunks),
             out_specs=[VMEM, VMEM],
             scratch_shapes=[pltpu.SemaphoreType.DMA((KVH, n_seg, 2))],
+            compiler_params=pltpu.CompilerParams(vmem_limit_bytes=VMEM_BYTES),
             cost_estimate=pl.CostEstimate(flops=0, bytes_accessed=4 << 20, transcendentals=0),
             name="collect",
-        )(reads, *returned)
+        )(by_segment, *returned)
 
     def exchange(array):
         return lax.all_to_all(array, "enc", split_axis=0, concat_axis=0, tiled=True)

time: 176 us -> 170 us (0.966)
  Pallas kernels: 75.9 us -> 89.3 us
  starting transfers between devices: 32.3 us -> 21.5 us
  local copies, waits for them, and re-layouts: 14.9 us -> 4.96 us
    all_to_all x4, starting transfers between devices: 31.5 us -> 16.7 us  [exchange(): return lax.all_to_all(array, 'enc', split_axis=0, concat_axis=0, tiled=True)]
    unnamed x21 -> x8, local copies, waits for them, and re-layouts: 13.9 us -> 4.02 us
    pallas_call x4, Pallas kernels: 65.5 us -> 74.1 us  [attend(): pl.pallas_call(functools.partial(attend_kernel, turn, turn % PER_CHUNK, p...]
    pallas_call x0 -> x1, Pallas kernels: none -> 5.47 us  [per_device(): pl.pallas_call(functools.partial(prepare_kernel, tokens), out_shape=[jax....]
    ppermute x3, starting transfers between devices: 0.73 us -> 4.8 us  [xor_permute(): return lax.ppermute(array, axis, [(i, i ^ k) for i in range(size)])]
    ppermute x3, waiting for transfers between devices: 9.84 us -> 12.4 us  [xor_permute(): return lax.ppermute(array, axis, [(i, i ^ k) for i in range(size)])]
    all_to_all x4, waiting for transfers between devices: 37.6 us -> 35.2 us  [exchange(): return lax.all_to_all(array, 'enc', split_axis=0, concat_axis=0, tiled=True)]
  transfers between devices with their start and end apart: 7 -> 7, of which waited for: 3 -> 4; matrix products, arithmetic and copies ran while one was open for 3% -> 3% of each run, Pallas kernels for 39% -> 49%
where the time goes in v1:
time: 170 us; the launch traced here: 168 us
  Pallas kernels  89.3 us (53%)
  waiting for transfers between devices  47.7 us (28%)
  starting transfers between devices  21.5 us (13%)
  local copies, waits for them, and re-layouts  4.96 us (3%)
  other arithmetic  3.98 us (2%)
    pallas_call x4, Pallas kernels, attend(): pl.pallas_call(functools.partial(attend_kernel, turn, turn % PER_CHUNK, p...  74.1 us
    all_to_all x4, waiting for transfers between devices, exchange(): return lax.all_to_all(array, 'enc', split_axis=0, concat_axis=0, tiled=True)  35.2 us
    all_to_all x4, starting transfers between devices, exchange(): return lax.all_to_all(array, 'enc', split_axis=0, concat_axis=0, tiled=True)  16.7 us
    ppermute x3, waiting for transfers between devices, xor_permute(): return lax.ppermute(array, axis, [(i, i ^ k) for i in range(size)])  12.4 us
    pallas_call x2, Pallas kernels, route(): pl.pallas_call(functools.partial(route_kernel, turns, n_seg, seg_rows), o...  5.89 us
    pallas_call x1, Pallas kernels, per_device(): pl.pallas_call(functools.partial(prepare_kernel, tokens), out_shape=[jax....  5.47 us
    ppermute x3, starting transfers between devices, xor_permute(): return lax.ppermute(array, axis, [(i, i ^ k) for i in range(size)])  4.8 us
    unnamed x8, local copies, waits for them, and re-layouts  4.02 us
  transfers between devices with their start and end apart: 7, of which 4 were waited for; matrix products, arithmetic and copies ran while one was open for 3% of the time, Pallas kernels for 49%

profile of v1, /device:TPU:0, one launch (start us, length us, event | category | flops | bytes accessed | tf_op | source)
XLA Modules:
  0.0 168.4 jit_solution(17693177935526254377)
XLA Ops:
  0.6 2.9 %route_0.1 = bf16[8,2,2,32,1024]{4,3,2,1,0:T(8,128)(2,1)} custom-call(s32[4,32]{1,0:T(4,128)} %bitcast.1, bf16[128,4096]{1,0:T(8,128)(2,1)} %q_hbm.3, bf16[128,4096]{1,0:T(8,128)(2,1)} %g_hbm.3), custom_call_target="tpu_custom_call" | custom-call | bytes 2097152 | tf_op jit(solution)/shard_map/route_0/pallas_call | solution.py:288
  3.6 5.2 %all-to-all-start = ((bf16[8,2,2,32,1024]{4,3,2,1,0:T(8,128)(2,1)}), bf16[8,2,2,32,1024]{4,3,2,1,0:T(8,128)(2,1)S(1)}, u32[]{:S(2)}, u32[]{:S(2)}) async-start(bf16[8,2,2,32,1024]{4,3,2,1,0:T(8,128)(2,1)} %route_0.1), calls=%async_computation | async-start | bytes 4194304 | tf_op jit(solution)/shard_map/all_to_all | solution.py:362
  8.8 2.9 %route_2.1 = bf16[8,2,2,32,1024]{4,3,2,1,0:T(8,128)(2,1)} custom-call(s32[4,32]{1,0:T(4,128)} %bitcast.2, bf16[128,4096]{1,0:T(8,128)(2,1)} %q_hbm.3, bf16[128,4096]{1,0:T(8,128)(2,1)} %g_hbm.3), custom_call_target="tpu_custom_call" | custom-call | bytes 2097152 | tf_op jit(solution)/shard_map/route_2/pallas_call | solution.py:288
  11.7 23.7 %all-to-all-done.received = bf16[8,2,2,32,1024]{4,3,2,1,0:T(8,128)(2,1)S(1)} async-done(((bf16[8,2,2,32,1024]{4,3,2,1,0:T(8,128)(2,1)}), bf16[8,2,2,32,1024]{4,3,2,1,0:T(8,128)(2,1)S(1)}, u32[]{:S(2)}, u32[]{:S(2)}) %all-to-all-start) | async-done | bytes 2097184 | tf_op jit(solution)/shard_map/all_to_all | solution.py:362
  35.4 1.3 copy-done.2
  36.7 3.6 %all-to-all-start.2 = ((bf16[8,2,2,32,1024]{4,3,2,1,0:T(8,128)(2,1)}), bf16[8,2,2,32,1024]{4,3,2,1,0:T(8,128)(2,1)S(1)}, u32[]{:S(2)}, u32[]{:S(2)}) async-start(bf16[8,2,2,32,1024]{4,3,2,1,0:T(8,128)(2,1)} %route_2.1), calls=%async_computation.2 | async-start | bytes 4194304 | tf_op jit(solution)/shard_map/all_to_all | solution.py:362
  40.3 5.5 %prepare.1 = (bf16[4,2,1616,128]{3,2,1,0:T(8,128)(2,1)}, bf16[4,2,128,1616]{3,2,1,0:T(8,128)(2,1)}) custom-call(bf16[1,1601,512]{2,1,0:T(8,128)(2,1)} %k_in.1, bf16[1,1601,512]{2,1,0:T(8,128)(2,1)} %v_in.1), custom_call_target="tpu_custom_call" | custom-call | bytes 16777216 | tf_op jit(solution)/shard_map/prepare/pallas_call | solution.py:303
  45.8 18.5 %attend_0.1 = (bf16[8,2,2,32,1024]{4,3,2,1,0:T(8,128)(2,1)}, bf16[2,1616,128]{2,1,0:T(8,128)(2,1)}) custom-call(s32[4,32]{1,0:T(4,128)} %bitcast.3, bf16[4,2,1616,128]{3,2,1,0:T(8,128)(2,1)} %get-tuple-element.18.caches, bf16[4,2,128,1616]{3,2,1,0:T(8,128)(2,1)} %get-tuple-element.19.turned_caches, bf16[8,2,2,32,1024]{4,3,2,1,0:T(8,128)(2,1)} %copy-done.2), custom_call_target="tpu_custom_call" | custom-call | flops 7554465792 | bytes 4194304 | tf_op jit(solution)/shard_map/attend_0/pallas_call | solution.py:319
  64.3 1.6 collective-permute-start.1
  65.9 18.4 %attend_1.1 = (bf16[8,2,2,32,1024]{4,3,2,1,0:T(8,128)(2,1)}, bf16[2,1616,128]{2,1,0:T(8,128)(2,1)}) custom-call(s32[4,32]{1,0:T(4,128)} %bitcast.4, bf16[4,2,1616,128]{3,2,1,0:T(8,128)(2,1)} %get-tuple-element.18.caches, bf16[4,2,128,1616]{3,2,1,0:T(8,128)(2,1)} %get-tuple-element.19.turned_caches, ...), custom_call_target="tpu_custom_call", output_to_operand_aliasing={{0}: (4, {})} | custom-call | flops 7554465792 | bytes 4194304 | tf_op jit(solution)/shard_map/attend_1/pallas_call | solution.py:319
  84.3 0.0 all-to-all-done.2.received
  84.3 0.0 copy-start.1
  84.3 1.4 copy-done.1
  85.7 3.6 %all-to-all-start.1 = ((bf16[8,2,2,32,1024]{4,3,2,1,0:T(8,128)(2,1)}), bf16[8,2,2,32,1024]{4,3,2,1,0:T(8,128)(2,1)S(1)}, u32[]{:S(2)}, u32[]{:S(2)}) async-start(bf16[8,2,2,32,1024]{4,3,2,1,0:T(8,128)(2,1)} %get-tuple-element.21), calls=%async_computation.1 | async-start | bytes 4194304 | tf_op jit(solution)/shard_map/all_to_all | solution.py:362
  89.3 0.0 copy-start.3
  89.3 18.6 %attend_2.1 = (bf16[8,2,2,32,1024]{4,3,2,1,0:T(8,128)(2,1)}, bf16[2,1616,128]{2,1,0:T(8,128)(2,1)}) custom-call(s32[4,32]{1,0:T(4,128)} %bitcast.5, bf16[4,2,1616,128]{3,2,1,0:T(8,128)(2,1)} %get-tuple-element.18.caches, bf16[4,2,128,1616]{3,2,1,0:T(8,128)(2,1)} %get-tuple-element.19.turned_caches, bf16[8,2,2,32,1024]{4,3,2,1,0:T(8,128)(2,1)} %copy-done.1), custom_call_target="tpu_custom_call" | custom-call | flops 7554465792 | bytes 4194304 | tf_op jit(solution)/shard_map/attend_2/pallas_call | solution.py:319
  107.9 0.6 collective-permute-start
  108.5 0.0 collective-permute-done.1
  108.5 0.0 copy-done.3
  108.5 2.3 %add_convert_fusion.1 = bf16[2,1616,128]{2,1,0:T(8,128)(2,1)} fusion(bf16[2,1616,128]{2,1,0:T(8,128)(2,1)} %collective-permute-done.1, bf16[2,1616,128]{2,1,0:T(8,128)(2,1)S(1)} %copy-done.3), kind=kLoop, calls=%fused_computation.1 | loop fusion | flops 1654784 | bytes 2482176 | tf_op jit(solution)/shard_map/convert_element_type | solution.py:379
  110.7 2.6 %collective-permute-start.2 = (bf16[2,1616,128]{2,1,0:T(8,128)(2,1)}, bf16[2,1616,128]{2,1,0:T(8,128)(2,1)}, u32[]{:S(2)}, u32[]{:S(2)}) collective-permute-start(bf16[2,1616,128]{2,1,0:T(8,128)(2,1)} %add_convert_fusion.1), channel_id=1, source_target_pairs={{0,16},{8,24},{16,0},{24,8},{1,17},{9,25},{17,1},{25,9},{2,18},{10... | collective-permute-start | bytes 2482184 | tf_op jit(solution)/shard_map/ppermute | solution.py:270
  113.4 18.6 %attend_3.1 = (bf16[8,2,2,32,1024]{4,3,2,1,0:T(8,128)(2,1)}, bf16[2,1616,128]{2,1,0:T(8,128)(2,1)}) custom-call(s32[4,32]{1,0:T(4,128)} %bitcast.6, bf16[4,2,1616,128]{3,2,1,0:T(8,128)(2,1)} %get-tuple-element.18.caches, bf16[4,2,128,1616]{3,2,1,0:T(8,128)(2,1)} %get-tuple-element.19.turned_caches, ...), custom_call_target="tpu_custom_call", output_to_operand_aliasing={{0}: (4, {})} | custom-call | flops 7554465792 | bytes 4194304 | tf_op jit(solution)/shard_map/attend_3/pallas_call | solution.py:319
  132.0 0.0 all-to-all-done.1.refs_0_
  132.0 0.0 copy-start
  132.0 1.3 copy-done
  133.3 4.3 %all-to-all-start.3 = ((bf16[8,2,2,32,1024]{4,3,2,1,0:T(8,128)(2,1)}), bf16[8,2,2,32,1024]{4,3,2,1,0:T(8,128)(2,1)}, u32[]{:S(2)}, u32[]{:S(2)}) async-start(bf16[8,2,2,32,1024]{4,3,2,1,0:T(8,128)(2,1)} %get-tuple-element.25), calls=%async_computation.3 | async-start | bytes 4194304 | tf_op jit(solution)/shard_map/all_to_all | solution.py:362
  137.7 6.6 %collective-permute-done = bf16[2,1616,128]{2,1,0:T(8,128)(2,1)S(1)} collective-permute-done((bf16[2,1616,128]{2,1,0:T(8,128)(2,1)}, bf16[2,1616,128]{2,1,0:T(8,128)(2,1)S(1)}, u32[]{:S(2)}, u32[]{:S(2)}) %collective-permute-start) | collective-permute-done | bytes 827424 | tf_op jit(solution)/shard_map/ppermute | solution.py:270
  144.2 5.9 %collective-permute-done.2 = bf16[2,1616,128]{2,1,0:T(8,128)(2,1)} collective-permute-done((bf16[2,1616,128]{2,1,0:T(8,128)(2,1)}, bf16[2,1616,128]{2,1,0:T(8,128)(2,1)}, u32[]{:S(2)}, u32[]{:S(2)}) %collective-permute-start.2) | collective-permute-done | bytes 827424 | tf_op jit(solution)/shard_map/ppermute | solution.py:270
  150.1 1.7 %add_convert_fusion = bf16[2,1616,128]{2,1,0:T(8,128)(2,1)S(1)} fusion(bf16[2,1616,128]{2,1,0:T(8,128)(2,1)} %collective-permute-done.2, bf16[2,1616,128]{2,1,0:T(8,128)(2,1)S(1)} %collective-permute-done, bf16[2,1616,128]{2,1,0:T(8,128)(2,1)} %get-tuple-element.28), kind=kLoop, calls=%fused_computation | loop fusion | flops 2482176 | bytes 3309568 | tf_op jit(solution)/shard_map/convert_element_type | solution.py:383
  151.9 0.9 fusion
  152.8 11.5 %all-to-all-done.3.refs_1_ = bf16[8,2,2,32,1024]{4,3,2,1,0:T(8,128)(2,1)} async-done(((bf16[8,2,2,32,1024]{4,3,2,1,0:T(8,128)(2,1)}), bf16[8,2,2,32,1024]{4,3,2,1,0:T(8,128)(2,1)}, u32[]{:S(2)}, u32[]{:S(2)}) %all-to-all-start.3) | async-done | bytes 2097184 | tf_op jit(solution)/shard_map/all_to_all | solution.py:362
  164.3 3.9 %collect.1 = (bf16[128,4096]{1,0:T(8,128)(2,1)}, bf16[128,4096]{1,0:T(8,128)(2,1)}) custom-call(s32[4,32]{1,0:T(4,128)} %bitcast.7, bf16[8,2,2,32,1024]{4,3,2,1,0:T(8,128)(2,1)} %copy-done, bf16[8,2,2,32,1024]{4,3,2,1,0:T(8,128)(2,1)} %all-to-all-done.3.refs_1_), custom_call_target="tpu_custom_call" | custom-call | bytes 4194304 | tf_op jit(solution)/shard_map/collect/pallas_call | solution.py:350
  (1 shorter events, 0.0 us)
Async XLA Ops:
  3.6 31.8 %all-to-all-start = ((bf16[8,2,2,32,1024]{4,3,2,1,0:T(8,128)(2,1)}), bf16[8,2,2,32,1024]{4,3,2,1,0:T(8,128)(2,1)S(1)}, u32[]{:S(2)}, u32[]{:S(2)}) async-start(bf16[8,2,2,32,1024]{4,3,2,1,0:T(8,128)(2,1)} %route_0.1), calls=%async_computation | async-start | bytes 4194304 | tf_op jit(solution)/shard_map/all_to_all | solution.py:362
  35.4 1.3 copy-start.2
  36.7 47.6 %all-to-all-start.2 = ((bf16[8,2,2,32,1024]{4,3,2,1,0:T(8,128)(2,1)}), bf16[8,2,2,32,1024]{4,3,2,1,0:T(8,128)(2,1)S(1)}, u32[]{:S(2)}, u32[]{:S(2)}) async-start(bf16[8,2,2,32,1024]{4,3,2,1,0:T(8,128)(2,1)} %route_2.1), calls=%async_computation.2 | async-start | bytes 4194304 | tf_op jit(solution)/shard_map/all_to_all | solution.py:362
  64.3 44.2 %collective-permute-start.1 = (bf16[2,1616,128]{2,1,0:T(8,128)(2,1)}, bf16[2,1616,128]{2,1,0:T(8,128)(2,1)}, u32[]{:S(2)}, u32[]{:S(2)}) collective-permute-start(bf16[2,1616,128]{2,1,0:T(8,128)(2,1)} %get-tuple-element.31), channel_id=1, source_target_pairs={{0,8},{8,0},{16,24},{24,16},{1,9},{9,1},{17,25},{25,17},{2,10},{10... | collective-permute-start | bytes 2482184 | tf_op jit(solution)/shard_map/ppermute | solution.py:270
  84.3 1.4 copy-start.1
  85.7 46.3 %all-to-all-start.1 = ((bf16[8,2,2,32,1024]{4,3,2,1,0:T(8,128)(2,1)}), bf16[8,2,2,32,1024]{4,3,2,1,0:T(8,128)(2,1)S(1)}, u32[]{:S(2)}, u32[]{:S(2)}) async-start(bf16[8,2,2,32,1024]{4,3,2,1,0:T(8,128)(2,1)} %get-tuple-element.21), calls=%async_computation.1 | async-start | bytes 4194304 | tf_op jit(solution)/shard_map/all_to_all | solution.py:362
  89.3 19.1 %copy-start.3 = (bf16[2,1616,128]{2,1,0:T(8,128)(2,1)S(1)}, bf16[2,1616,128]{2,1,0:T(8,128)(2,1)}, u32[]{:S(2)}) copy-start(bf16[2,1616,128]{2,1,0:T(8,128)(2,1)} %get-tuple-element.30) | copy-start | bytes 2482180
  107.9 36.3 %collective-permute-start = (bf16[2,1616,128]{2,1,0:T(8,128)(2,1)}, bf16[2,1616,128]{2,1,0:T(8,128)(2,1)S(1)}, u32[]{:S(2)}, u32[]{:S(2)}) collective-permute-start(bf16[2,1616,128]{2,1,0:T(8,128)(2,1)} %get-tuple-element.29), channel_id=1, source_target_pairs={{0,8},{8,0},{16,24},{24,16},{1,9},{9,1},{17,25},{25,17},{2,10},{10... | collective-permute-start | bytes 2482184 | tf_op jit(solution)/shard_map/ppermute | solution.py:270
  110.7 39.4 %collective-permute-start.2 = (bf16[2,1616,128]{2,1,0:T(8,128)(2,1)}, bf16[2,1616,128]{2,1,0:T(8,128)(2,1)}, u32[]{:S(2)}, u32[]{:S(2)}) collective-permute-start(bf16[2,1616,128]{2,1,0:T(8,128)(2,1)} %add_convert_fusion.1), channel_id=1, source_target_pairs={{0,16},{8,24},{16,0},{24,8},{1,17},{9,25},{17,1},{25,9},{2,18},{10... | collective-permute-start | bytes 2482184 | tf_op jit(solution)/shard_map/ppermute | solution.py:270
  132.0 1.3 copy-start
  133.3 31.0 %all-to-all-start.3 = ((bf16[8,2,2,32,1024]{4,3,2,1,0:T(8,128)(2,1)}), bf16[8,2,2,32,1024]{4,3,2,1,0:T(8,128)(2,1)}, u32[]{:S(2)}, u32[]{:S(2)}) async-start(bf16[8,2,2,32,1024]{4,3,2,1,0:T(8,128)(2,1)} %get-tuple-element.25), calls=%async_computation.3 | async-start | bytes 4194304 | tf_op jit(solution)/shard_map/all_to_all | solution.py:362

commit v2 on v1

v2 whole, which is shorter than its diff:
```python
import functools

import jax
import jax.numpy as jnp
from jax import lax
from jax.experimental import pallas as pl
from jax.experimental.pallas import tpu as pltpu
from jax.sharding import PartitionSpec as P

HQ = 32
KVH = 4
HD = 128
GROUP = HQ // KVH
WIDTH = GROUP * HD
SCALE = HD ** (-0.5)
LOG2E = 1.4426950408889634
CHUNK = 2048
LOWEST = -3.0e38
PER_CHUNK = 2
VMEM_BYTES = 58 << 20
ANY = pl.BlockSpec(memory_space=pl.ANY)
SMEM = pl.BlockSpec(memory_space=pltpu.SMEM)
VMEM = pl.BlockSpec(memory_space=pltpu.VMEM)
HBM = pl.BlockSpec(memory_space=pltpu.HBM)


def head_at(turn):
    if lax.axis_size("seq") == KVH:
        return lax.axis_index("seq") ^ (KVH - 1 - turn)
    return turn


def route_kernel(turns, n_seg, seg_rows, tokens, reads, q_hbm, g_hbm, *refs):
    caches, (out, *prepared, stage, in_sems, out_sems) = refs[:-6], refs[-6:]
    if not caches:
        out, stage, in_sems, out_sems = refs
        prepared = ()
    row = lax.axis_index("seq") * lax.axis_size("enc") + lax.axis_index("enc")
    arriving = [[] for _ in range(n_seg)]
    for r in range(n_seg):
        rows = slice(r * seg_rows, (r + 1) * seg_rows)
        for i, turn in enumerate(turns):
            columns = pl.ds(pl.multiple_of(head_at(turn) * WIDTH, WIDTH), WIDTH)
            for which, source in enumerate((q_hbm, g_hbm)):
                arriving[r].append(
                    pltpu.make_async_copy(
                        source.at[rows, columns],
                        stage.at[r, i, which],
                        in_sems.at[r, i, which],
                    )
                )
    leaving = [
        pltpu.make_async_copy(stage.at[r], out.at[reads[r, row]], out_sems.at[r])
        for r in range(n_seg)
    ]
    for copies in arriving:
        for copy in copies:
            copy.start()
    for r, copies in enumerate(arriving):
        for copy in copies:
            copy.wait()
        leaving[r].start()
    if caches:
        prepare(tokens, *caches, *prepared)
    for copy in leaving:
        copy.wait()


def collect_kernel(chunks, n_seg, seg_rows, reads, *refs):
    returned = refs[: len(chunks)]
    o_out, dq_out, sems = refs[len(chunks) :]
    row = lax.axis_index("seq") * lax.axis_size("enc") + lax.axis_index("enc")
    copies = []
    for c, turns in enumerate(chunks):
        for i, turn in enumerate(turns):
            column = pl.multiple_of(head_at(turn) * WIDTH, WIDTH)
            for r in range(n_seg):
                for which, target in enumerate((o_out, dq_out)):
                    copies.append(
                        pltpu.make_async_copy(
                            returned[c].at[reads[r, row], i, which],
                            target.at[r * seg_rows : (r + 1) * seg_rows, pl.ds(column, WIDTH)],
                            sems.at[turn, r, which],
                        )
                    )
    for copy in copies:
        copy.start()
    for copy in copies:
        copy.wait()


def is_read(reads, row, image):
    found = jnp.int32(0)
    for r in range(reads.shape[0]):
        found = found + (reads[r, row] == image).astype(jnp.int32)
    return found > 0


def prepare(tokens, k_in, v_in, straight, turned):
    padded = straight.shape[2]
    whole = tokens // 16 * 16
    for which, source in enumerate((k_in, v_in)):
        for head in range(KVH):
            columns = slice(head * HD, (head + 1) * HD)
            straight[head, which, 0:whole, :] = source[0, 0:whole, columns]
            if whole < tokens:
                last = jnp.zeros((padded - tokens, HD), jnp.bfloat16)
                straight[head, which, whole:padded, :] = jnp.concatenate(
                    [source[0, whole:tokens, columns], last], axis=0
                )
            turned[head, which] = (
                straight[head, which].astype(jnp.float32).T.astype(jnp.bfloat16)
            )


def attend_kernel(turns, peers, seg_rows, tokens, reads, caches, turned_caches, received, *refs):
    returned, grads = refs[0], refs[1 : 1 + len(turns)]
    (
        straight,
        turned,
        inbox,
        outbox,
        scores,
        weights,
        dscores,
        sums,
        staged,
        owners,
        kv_sems,
        in_sems,
        out_sems,
        grad_sems,
    ) = refs[1 + len(turns) :]
    me = lax.axis_index("enc")
    base = lax.axis_index("seq") * peers
    slots = inbox.shape[1]
    padded = straight.shape[2]
    pieces = [(a, min(a + CHUNK, padded)) for a in range(0, padded, CHUNK)]
    lanes = GROUP * seg_rows
    f32, bf16 = jnp.float32, jnp.bfloat16

    kv_copies = [
        [
            pltpu.make_async_copy(source.at[head_at(turn)], target.at[i], kv_sems.at[i, j])
            for j, (source, target) in enumerate(((caches, straight), (turned_caches, turned)))
        ]
        for i, turn in enumerate(turns)
    ]

    def arriving(i, slot, owner):
        return pltpu.make_async_copy(
            received.at[owner, i], inbox.at[i, slot], in_sems.at[i, slot]
        )

    def leaving(i, slot, owner):
        return pltpu.make_async_copy(
            outbox.at[i, slot], returned.at[owner, i], out_sems.at[i, slot]
        )

    def handing(i):
        return pltpu.make_async_copy(staged.at[i], grads[i], grad_sems.at[i])

    for copy in kv_copies[0]:
        copy.start()
    count = jnp.int32(0)
    for k in range(peers):
        found = is_read(reads, base + k, me)

        @pl.when(found)
        def _():
            owners[count] = jnp.int32(k)
            arriving(0, count, k).start()

        count = count + found.astype(jnp.int32)
    for i in range(1, len(turns)):
        for copy in kv_copies[i]:
            copy.start()
        for slot in range(slots):

            @pl.when(slot < count)
            def _():
                arriving(i, slot, owners[slot]).start()

    sums[...] = jnp.zeros_like(sums)
    steps = count * len(turns)

    def place(step):
        return lax.div(step, count), lax.rem(step, count)

    def stacked(i, slot, which):
        return jnp.concatenate(
            [inbox[i, slot, which, :, h * HD : (h + 1) * HD] for h in range(GROUP)], axis=0
        )

    def store(i, slot, which, turned_value):
        value = turned_value.T.astype(bf16)
        for h in range(GROUP):
            outbox[i, slot, which, :, h * HD : (h + 1) * HD] = value[
                h * seg_rows : (h + 1) * seg_rows, :
            ]

    def masked(part, a, b, other):
        if b <= tokens:
            return part
        token = lax.broadcasted_iota(jnp.int32, part.shape, 0) + a
        return jnp.where(token < tokens, part, other)

    def await_step(step):
        i, slot = place(step)
        for head in range(len(turns)):

            @pl.when(step == head * count)
            def _():
                for copy in kv_copies[head]:
                    copy.wait()

        arriving(i, slot, 0).wait()

    def forward(i, slot):
        q, g = (stacked(i, slot, which).astype(f32).T for which in range(2))
        q_turned = q.astype(bf16)
        state = {"top": jnp.full((1, lanes), LOWEST, f32), "total": jnp.zeros((1, lanes), f32)}

        def score(a, b):
            part = jnp.dot(straight[i, 0, a:b, :], q_turned, preferred_element_type=f32)
            part = masked(part, a, b, LOWEST)
            scores[a:b, :] = part
            state["top"] = jnp.maximum(state["top"], jnp.max(part, axis=0, keepdims=True))

        def weigh(a, b):
            part = jnp.exp2((scores[a:b, :] - state["top"]) * (SCALE * LOG2E))
            state["total"] = state["total"] + jnp.sum(part, axis=0, keepdims=True)
            weights[a:b, :] = part.astype(bf16)

        def finish():
            out = jnp.dot(turned[i, 1], weights[...], preferred_element_type=f32)
            out = out * (1.0 / state["total"])
            store(i, slot, 0, out)
            delta = jnp.sum(g * out.astype(bf16).astype(f32), axis=0, keepdims=True)
            lse = state["top"] * (SCALE * LOG2E) + jnp.log2(state["total"])
            return lse, delta, q_turned, g.astype(bf16)

        parts = [functools.partial(score, a, b) for a, b in pieces]
        return parts + [functools.partial(weigh, a, b) for a, b in pieces], finish

    def backward(i, slot, lse, delta, q_turned, g_turned):
        q, g = stacked(i, slot, 0), stacked(i, slot, 1)

        def part(a, b):
            score = jnp.dot(straight[i, 0, a:b, :], q_turned, preferred_element_type=f32)
            prob = masked(jnp.exp2(score * (SCALE * LOG2E) - lse), a, b, 0.0)
            dprob = jnp.dot(straight[i, 1, a:b, :], g_turned, preferred_element_type=f32)
            dscore = (prob * (dprob - delta)).astype(bf16)
            dscores[a:b, :] = dscore
            sums[i, 0, a:b, :] += jnp.dot(dscore, q, preferred_element_type=f32)
            sums[i, 1, a:b, :] += jnp.dot(prob.astype(bf16), g, preferred_element_type=f32)

        def finish():
            turned_dq = jnp.dot(turned[i, 0], dscores[...], preferred_element_type=f32)
            store(i, slot, 1, turned_dq * SCALE)

        return [functools.partial(part, a, b) for a, b in pieces], finish

    def one_step(step, carry):
        i, slot = place(step)
        later = jnp.minimum(step + 1, steps - 1)

        @pl.when(step + 1 < steps)
        def _():
            await_step(step + 1)

        ahead, ahead_finish = forward(*place(later))
        behind, behind_finish = backward(i, slot, *carry)
        for j, part in enumerate(behind):
            for other in ahead[2 * j : 2 * j + 2]:
                other()
            part()
        behind_finish()
        carry = ahead_finish()
        leaving(i, slot, owners[slot]).start()

        @pl.when(slot == count - 1)
        def _():
            staged[i, 0] = (sums[i, 0] * SCALE).astype(bf16)
            staged[i, 1] = sums[i, 1].astype(bf16)
            for head in range(len(turns)):

                @pl.when(i == head)
                def _():
                    handing(head).start()

        return carry

    @pl.when(count > 0)
    def _():
        await_step(jnp.int32(0))
        first, first_finish = forward(0, 0)
        for part in first:
            part()
        lax.fori_loop(0, steps, one_step, first_finish())

    @pl.when(count == 0)
    def _():
        staged[...] = jnp.zeros_like(staged)
        for i in range(len(turns)):
            for copy in kv_copies[i]:
                copy.wait()
            handing(i).start()

    for i in range(len(turns)):
        for slot in range(slots):

            @pl.when(slot < count)
            def _():
                leaving(i, slot, 0).wait()

        handing(i).wait()


def xor_permute(array, axis, k):
    if k == 0:
        return array
    size = lax.axis_size(axis)
    return lax.ppermute(array, axis, [(i, i ^ k) for i in range(size)])


def per_device(queries, keys, values, reads, grad_out):
    peers = lax.axis_size("enc")
    n_seq = lax.axis_size("seq")
    n_seg = reads.shape[1]
    by_segment = reads.T
    seg_rows = queries.shape[0] // n_seg
    slots = min(peers, 3 * n_seg // 2)
    tokens = keys.shape[1]
    padded = (tokens + 15) // 16 * 16
    lanes = GROUP * seg_rows
    bf16, f32 = jnp.bfloat16, jnp.float32
    chunks = [tuple(range(i, i + PER_CHUNK)) for i in range(0, KVH, PER_CHUNK)]
    message = jax.ShapeDtypeStruct((peers, PER_CHUNK, 2, seg_rows, WIDTH), bf16)

    caches = [
        jax.ShapeDtypeStruct((KVH, 2, padded, HD), bf16),
        jax.ShapeDtypeStruct((KVH, 2, HD, padded), bf16),
    ]

    def route(turns, prepares):
        return pl.pallas_call(
            functools.partial(route_kernel, turns, n_seg, seg_rows, tokens),
            out_shape=[message] + caches * prepares,
            in_specs=[SMEM, HBM, HBM] + [VMEM] * 2 * prepares,
            out_specs=[ANY] + [VMEM] * 2 * prepares,
            scratch_shapes=[
                pltpu.VMEM((n_seg, PER_CHUNK, 2, seg_rows, WIDTH), bf16),
                pltpu.SemaphoreType.DMA((n_seg, PER_CHUNK, 2)),
                pltpu.SemaphoreType.DMA((n_seg,)),
            ],
            compiler_params=pltpu.CompilerParams(vmem_limit_bytes=VMEM_BYTES),
            cost_estimate=pl.CostEstimate(
                flops=0, bytes_accessed=(2 + 10 * prepares) << 20, transcendentals=0
            ),
            name=f"route_{turns[0]}",
        )(by_segment, queries, grad_out, *[keys, values] * prepares)

    def attend(turns, received):
        work = slots * lanes * tokens * HD * len(turns)
        results = pl.pallas_call(
            functools.partial(attend_kernel, turns, peers, seg_rows, tokens),
            out_shape=[message] + [jax.ShapeDtypeStruct((2, padded, HD), bf16)] * len(turns),
            in_specs=[SMEM] + [ANY] * 3,
            out_specs=[ANY] * (1 + len(turns)),
            scratch_shapes=[
                pltpu.VMEM((len(turns), 2, padded, HD), bf16),
                pltpu.VMEM((len(turns), 2, HD, padded), bf16),
                pltpu.VMEM((len(turns), slots, 2, seg_rows, WIDTH), bf16),
                pltpu.VMEM((len(turns), slots, 2, seg_rows, WIDTH), bf16),
                pltpu.VMEM((padded, lanes), f32),
                pltpu.VMEM((padded, lanes), bf16),
                pltpu.VMEM((padded, lanes), bf16),
                pltpu.VMEM((len(turns), 2, padded, HD), f32),
                pltpu.VMEM((len(turns), 2, padded, HD), bf16),
                pltpu.SMEM((slots,), jnp.int32),
                pltpu.SemaphoreType.DMA((len(turns), 2)),
                pltpu.SemaphoreType.DMA((len(turns), slots)),
                pltpu.SemaphoreType.DMA((len(turns), slots)),
                pltpu.SemaphoreType.DMA((len(turns),)),
            ],
            compiler_params=pltpu.CompilerParams(vmem_limit_bytes=VMEM_BYTES),
            cost_estimate=pl.CostEstimate(
                flops=24 * work, bytes_accessed=8 << 20, transcendentals=slots * lanes * tokens
            ),
            name=f"attend_{turns[0]}",
        )(by_segment, *prepared, received)
        return results[0], list(results[1:])

    def collect(returned):
        whole = jax.ShapeDtypeStruct(queries.shape, bf16)
        return pl.pallas_call(
            functools.partial(collect_kernel, chunks, n_seg, seg_rows),
            out_shape=[whole, whole],
            in_specs=[SMEM] + [ANY] * len(chunks),
            out_specs=[VMEM, VMEM],
            scratch_shapes=[pltpu.SemaphoreType.DMA((KVH, n_seg, 2))],
            compiler_params=pltpu.CompilerParams(vmem_limit_bytes=VMEM_BYTES),
            cost_estimate=pl.CostEstimate(flops=0, bytes_accessed=4 << 20, transcendentals=0),
            name="collect",
        )(by_segment, *returned)

    def exchange(array):
        return lax.all_to_all(array, "enc", split_axis=0, concat_axis=0, tiled=True)

    first, second = chunks
    routed, = route(first, 0)
    received = exchange(routed)
    routed, *prepared = route(second, 1)
    received, routed = lax.optimization_barrier((received, routed))
    received_later = exchange(routed)
    returned, grads = attend(first, received)
    answer = exchange(returned)
    passed = xor_permute(grads[0], "seq", 1)
    received_later, grads[1] = lax.optimization_barrier((received_later, grads[1]))
    returned, more = attend(second, received_later)
    grads += more
    if n_seq == KVH:
        pair = (grads[1].astype(f32) + passed.astype(f32)).astype(bf16)
        answer, returned, pair = lax.optimization_barrier((answer, returned, pair))
        pair = xor_permute(pair, "seq", 2)
        near = xor_permute(grads[2], "seq", 1)
    answers = [answer, exchange(returned)]
    attended, grad_queries = collect(answers)

    if n_seq == KVH:
        total = grads[3].astype(f32) + near.astype(f32) + pair.astype(f32)
        total = total.astype(bf16)[:, :tokens]
        return attended, grad_queries, total[0][None], total[1][None]
    joined = jnp.concatenate(grads, axis=2)[:, :tokens]
    summed = lax.psum_scatter(joined, "seq", scatter_dimension=2, tiled=True)
    return attended, grad_queries, summed[0][None], summed[1][None]


def solution(mesh):
    placed = (
        P(("seq", "enc"), None),
        P("enc", None, None),
        P("enc", None, None),
        P(),
        P(("seq", "enc"), None),
    )
    return jax.shard_map(
        per_device,
        mesh=mesh,
        in_specs=placed,
        out_specs=(
            P(("seq", "enc"), None),
            P(("seq", "enc"), None),
            P("enc", None, "seq"),
            P("enc", None, "seq"),
        ),
        check_vma=False,
    )
```

time: 170 us -> 156 us (0.918)
  Pallas kernels: 89.3 us -> 58.1 us
  starting transfers between devices: 21.5 us -> 38.5 us
  waiting for transfers between devices: 47.7 us -> 49.9 us
    pallas_call x7 -> x4, Pallas kernels: 85.4 us -> 54.3 us  [the longest x2 44.4 us: attend(): pl.pallas_call(functools.partial(attend_kernel, turns, peers, seg_rows, t...]
    ppermute x3, waiting for transfers between devices: 12.4 us -> 25.2 us  [xor_permute(): return lax.ppermute(array, axis, [(i, i ^ k) for i in range(size)])]
    all_to_all x4, waiting for transfers between devices: 35.2 us -> 24.7 us  [exchange(): return lax.all_to_all(array, 'enc', split_axis=0, concat_axis=0, tiled=True)]
    all_to_all x4, starting transfers between devices: 16.7 us -> 25.3 us  [exchange(): return lax.all_to_all(array, 'enc', split_axis=0, concat_axis=0, tiled=True)]
    ppermute x3, starting transfers between devices: 4.8 us -> 13.2 us  [xor_permute(): return lax.ppermute(array, axis, [(i, i ^ k) for i in range(size)])]
    unnamed x8 -> x10, local copies, waits for them, and re-layouts: 4.02 us -> 2.82 us
  transfers between devices with their start and end apart: 7 -> 7, of which waited for: 4 -> 5; matrix products, arithmetic and copies ran while one was open for 3% -> 3% of each run, Pallas kernels for 49% -> 33%
where the time goes in v2:
time: 156 us; the launch traced here: 155 us
  Pallas kernels  58.1 us (37%)
  waiting for transfers between devices  49.9 us (32%)
  starting transfers between devices  38.5 us (25%)
  other arithmetic  3.98 us (3%)
  local copies, waits for them, and re-layouts  3.76 us (2%)
    pallas_call x2, Pallas kernels, attend(): pl.pallas_call(functools.partial(attend_kernel, turns, peers, seg_rows, t...  44.4 us
    all_to_all x4, starting transfers between devices, exchange(): return lax.all_to_all(array, 'enc', split_axis=0, concat_axis=0, tiled=True)  25.3 us
    ppermute x3, waiting for transfers between devices, xor_permute(): return lax.ppermute(array, axis, [(i, i ^ k) for i in range(size)])  25.2 us
    all_to_all x4, waiting for transfers between devices, exchange(): return lax.all_to_all(array, 'enc', split_axis=0, concat_axis=0, tiled=True)  24.7 us
    ppermute x3, starting transfers between devices, xor_permute(): return lax.ppermute(array, axis, [(i, i ^ k) for i in range(size)])  13.2 us
    pallas_call x2, Pallas kernels, route(): pl.pallas_call(functools.partial(route_kernel, turns, n_seg, seg_rows, to...  9.91 us
    pallas_call x1, Pallas kernels, collect(): pl.pallas_call(functools.partial(collect_kernel, chunks, n_seg, seg_rows)...  3.85 us
  transfers between devices with their start and end apart: 7, of which 5 were waited for; matrix products, arithmetic and copies ran while one was open for 3% of the time, Pallas kernels for 33%

profile of v2, /device:TPU:0, one launch (start us, length us, event | category | flops | bytes accessed | tf_op | source)
XLA Modules:
  0.0 155.0 jit_solution(16251731405264991945)
XLA Ops:
  0.6 2.9 %route_0.1 = bf16[8,2,2,32,1024]{4,3,2,1,0:T(8,128)(2,1)} custom-call(s32[4,32]{1,0:T(4,128)} %bitcast.1, bf16[128,4096]{1,0:T(8,128)(2,1)} %q_hbm.3, bf16[128,4096]{1,0:T(8,128)(2,1)} %g_hbm.3), custom_call_target="tpu_custom_call" | custom-call | bytes 2097152 | tf_op jit(solution)/shard_map/route_0/pallas_call | solution.py:347
  3.5 5.2 %all-to-all-start = ((bf16[8,2,2,32,1024]{4,3,2,1,0:T(8,128)(2,1)}), bf16[8,2,2,32,1024]{4,3,2,1,0:T(8,128)(2,1)S(1)}, u32[]{:S(2)}, u32[]{:S(2)}) async-start(bf16[8,2,2,32,1024]{4,3,2,1,0:T(8,128)(2,1)} %route_0.1), calls=%async_computation | async-start | bytes 4194304 | tf_op jit(solution)/shard_map/all_to_all | solution.py:409
  8.7 7.1 %route_2.1 = (bf16[8,2,2,32,1024]{4,3,2,1,0:T(8,128)(2,1)}, bf16[4,2,1616,128]{3,2,1,0:T(8,128)(2,1)}, bf16[4,2,128,1616]{3,2,1,0:T(8,128)(2,1)}) custom-call(s32[4,32]{1,0:T(4,128)} %bitcast.2, bf16[128,4096]{1,0:T(8,128)(2,1)} %q_hbm.3, bf16[128,4096]{1,0:T(8,128)(2,1)} %g_hbm.3, bf16[1,1601,512]{2,1,0:T(8,128)(2,1)} %refs_0_.1, bf16[1,1601,512]{2,1,0:T(8,128)(2,1)} %refs_1_.1), custom_call_target="tpu_custom_call" | custom-call | bytes 12582912 | tf_op jit(solution)/shard_map/route_2/pallas_call | solution.py:347
  15.7 19.6 %all-to-all-done.received = bf16[8,2,2,32,1024]{4,3,2,1,0:T(8,128)(2,1)S(1)} async-done(((bf16[8,2,2,32,1024]{4,3,2,1,0:T(8,128)(2,1)}), bf16[8,2,2,32,1024]{4,3,2,1,0:T(8,128)(2,1)S(1)}, u32[]{:S(2)}, u32[]{:S(2)}) %all-to-all-start) | async-done | bytes 2097184 | tf_op jit(solution)/shard_map/all_to_all | solution.py:409
  35.3 0.0 copy-start.2
  35.3 1.4 copy-done.2
  36.7 3.6 %all-to-all-start.2 = ((bf16[8,2,2,32,1024]{4,3,2,1,0:T(8,128)(2,1)}), bf16[8,2,2,32,1024]{4,3,2,1,0:T(8,128)(2,1)S(1)}, u32[]{:S(2)}, u32[]{:S(2)}) async-start(bf16[8,2,2,32,1024]{4,3,2,1,0:T(8,128)(2,1)} %get-tuple-element.27), calls=%async_computation.2 | async-start | bytes 4194304 | tf_op jit(solution)/shard_map/all_to_all | solution.py:409
  40.3 22.2 %attend_0.1 = (bf16[8,2,2,32,1024]{4,3,2,1,0:T(8,128)(2,1)}, bf16[2,1616,128]{2,1,0:T(8,128)(2,1)}, bf16[2,1616,128]{2,1,0:T(8,128)(2,1)}) custom-call(s32[4,32]{1,0:T(4,128)} %bitcast.3, bf16[4,2,1616,128]{3,2,1,0:T(8,128)(2,1)} %get-tuple-element.22.caches, bf16[4,2,128,1616]{3,2,1,0:T(8,128)(2,1)} %get-tuple-element.23.turned_caches, ...), custom_call_target="tpu_custom_call" | custom-call | flops 15108931584 | bytes 8388608 | tf_op jit(solution)/shard_map/attend_0/pallas_call | solution.py:366
  62.5 5.9 %collective-permute-start = (bf16[2,1616,128]{2,1,0:T(8,128)(2,1)}, bf16[2,1616,128]{2,1,0:T(8,128)(2,1)}, u32[]{:S(2)}, u32[]{:S(2)}) collective-permute-start(bf16[2,1616,128]{2,1,0:T(8,128)(2,1)} %get-tuple-element.32), channel_id=1, source_target_pairs={{0,8},{8,0},{16,24},{24,16},{1,9},{9,1},{17,25},{25,17},{2,10},{10... | collective-permute-start | bytes 2482184 | tf_op jit(solution)/shard_map/ppermute | solution.py:324
  68.5 0.0 all-to-all-done.2.received
  68.5 0.0 copy-start.1
  68.5 0.0 copy-start.4
  68.5 1.4 copy-done.1
  69.9 7.5 %all-to-all-start.1 = ((bf16[8,2,2,32,1024]{4,3,2,1,0:T(8,128)(2,1)}), bf16[8,2,2,32,1024]{4,3,2,1,0:T(8,128)(2,1)S(1)}, u32[]{:S(2)}, u32[]{:S(2)}) async-start(bf16[8,2,2,32,1024]{4,3,2,1,0:T(8,128)(2,1)} %get-tuple-element.26), calls=%async_computation.1 | async-start | bytes 4194304 | tf_op jit(solution)/shard_map/all_to_all | solution.py:409
  77.4 6.3 %collective-permute-done = bf16[2,1616,128]{2,1,0:T(8,128)(2,1)} collective-permute-done((bf16[2,1616,128]{2,1,0:T(8,128)(2,1)}, bf16[2,1616,128]{2,1,0:T(8,128)(2,1)}, u32[]{:S(2)}, u32[]{:S(2)}) %collective-permute-start) | collective-permute-done | bytes 827424 | tf_op jit(solution)/shard_map/ppermute | solution.py:324
  83.6 0.0 copy-done.4
  83.6 2.3 %add_convert_fusion.1 = bf16[2,1616,128]{2,1,0:T(8,128)(2,1)} fusion(bf16[2,1616,128]{2,1,0:T(8,128)(2,1)} %collective-permute-done, bf16[2,1616,128]{2,1,0:T(8,128)(2,1)S(1)} %copy-done.4), kind=kLoop, calls=%fused_computation.1 | loop fusion | flops 1654784 | bytes 2482176 | tf_op jit(solution)/shard_map/convert_element_type | solution.py:424
  85.9 22.2 %attend_2.1 = (bf16[8,2,2,32,1024]{4,3,2,1,0:T(8,128)(2,1)}, bf16[2,1616,128]{2,1,0:T(8,128)(2,1)}, bf16[2,1616,128]{2,1,0:T(8,128)(2,1)}) custom-call(s32[4,32]{1,0:T(4,128)} %bitcast.4, bf16[4,2,1616,128]{3,2,1,0:T(8,128)(2,1)} %get-tuple-element.22.caches, bf16[4,2,128,1616]{3,2,1,0:T(8,128)(2,1)} %get-tuple-element.23.turned_caches, ...), custom_call_target="tpu_custom_call" | custom-call | flops 15108931584 | bytes 8388608 | tf_op jit(solution)/shard_map/attend_2/pallas_call | solution.py:366
  108.1 0.0 all-to-all-done.1.refs_0_
  108.1 0.0 copy-start
  108.1 7.0 %collective-permute-start.2 = (bf16[2,1616,128]{2,1,0:T(8,128)(2,1)}, bf16[2,1616,128]{2,1,0:T(8,128)(2,1)}, u32[]{:S(2)}, u32[]{:S(2)}) collective-permute-start(bf16[2,1616,128]{2,1,0:T(8,128)(2,1)} %add_convert_fusion.1), channel_id=1, source_target_pairs={{0,16},{8,24},{16,0},{24,8},{1,17},{9,25},{17,1},{25,9},{2,18},{10... | collective-permute-start | bytes 2482184 | tf_op jit(solution)/shard_map/ppermute | solution.py:324
  115.1 0.0 copy-start.3
  115.1 0.3 collective-permute-start.1
  115.3 0.0 copy-done
  115.3 9.1 %all-to-all-start.3 = ((bf16[8,2,2,32,1024]{4,3,2,1,0:T(8,128)(2,1)}), bf16[8,2,2,32,1024]{4,3,2,1,0:T(8,128)(2,1)}, u32[]{:S(2)}, u32[]{:S(2)}) async-start(bf16[8,2,2,32,1024]{4,3,2,1,0:T(8,128)(2,1)} %get-tuple-element.34), calls=%async_computation.3 | async-start | bytes 4194304 | tf_op jit(solution)/shard_map/all_to_all | solution.py:409
  124.4 18.7 %collective-permute-done.2 = bf16[2,1616,128]{2,1,0:T(8,128)(2,1)} collective-permute-done((bf16[2,1616,128]{2,1,0:T(8,128)(2,1)}, bf16[2,1616,128]{2,1,0:T(8,128)(2,1)}, u32[]{:S(2)}, u32[]{:S(2)}) %collective-permute-start.2) | collective-permute-done | bytes 827424 | tf_op jit(solution)/shard_map/ppermute | solution.py:324
  143.2 0.2 collective-permute-done.1
  143.4 0.0 copy-done.3
  143.4 1.7 %add_convert_fusion = bf16[2,1616,128]{2,1,0:T(8,128)(2,1)S(1)} fusion(bf16[2,1616,128]{2,1,0:T(8,128)(2,1)} %collective-permute-done.2, bf16[2,1616,128]{2,1,0:T(8,128)(2,1)} %collective-permute-done.1, bf16[2,1616,128]{2,1,0:T(8,128)(2,1)S(1)} %copy-done.3), kind=kLoop, calls=%fused_computation | loop fusion | flops 2482176 | bytes 3309568 | tf_op jit(solution)/shard_map/convert_element_type | solution.py:433
  145.1 0.9 fusion
  146.1 5.1 %all-to-all-done.3.refs_1_ = bf16[8,2,2,32,1024]{4,3,2,1,0:T(8,128)(2,1)} async-done(((bf16[8,2,2,32,1024]{4,3,2,1,0:T(8,128)(2,1)}), bf16[8,2,2,32,1024]{4,3,2,1,0:T(8,128)(2,1)}, u32[]{:S(2)}, u32[]{:S(2)}) %all-to-all-start.3) | async-done | bytes 2097184 | tf_op jit(solution)/shard_map/all_to_all | solution.py:409
  151.2 3.9 %collect.1 = (bf16[128,4096]{1,0:T(8,128)(2,1)}, bf16[128,4096]{1,0:T(8,128)(2,1)}) custom-call(s32[4,32]{1,0:T(4,128)} %bitcast.5, bf16[8,2,2,32,1024]{4,3,2,1,0:T(8,128)(2,1)} %copy-done, bf16[8,2,2,32,1024]{4,3,2,1,0:T(8,128)(2,1)} %all-to-all-done.3.refs_1_), custom_call_target="tpu_custom_call" | custom-call | bytes 4194304 | tf_op jit(solution)/shard_map/collect/pallas_call | solution.py:397
Async XLA Ops:
  3.5 31.8 %all-to-all-start = ((bf16[8,2,2,32,1024]{4,3,2,1,0:T(8,128)(2,1)}), bf16[8,2,2,32,1024]{4,3,2,1,0:T(8,128)(2,1)S(1)}, u32[]{:S(2)}, u32[]{:S(2)}) async-start(bf16[8,2,2,32,1024]{4,3,2,1,0:T(8,128)(2,1)} %route_0.1), calls=%async_computation | async-start | bytes 4194304 | tf_op jit(solution)/shard_map/all_to_all | solution.py:409
  35.3 1.4 copy-start.2
  36.7 31.7 %all-to-all-start.2 = ((bf16[8,2,2,32,1024]{4,3,2,1,0:T(8,128)(2,1)}), bf16[8,2,2,32,1024]{4,3,2,1,0:T(8,128)(2,1)S(1)}, u32[]{:S(2)}, u32[]{:S(2)}) async-start(bf16[8,2,2,32,1024]{4,3,2,1,0:T(8,128)(2,1)} %get-tuple-element.27), calls=%async_computation.2 | async-start | bytes 4194304 | tf_op jit(solution)/shard_map/all_to_all | solution.py:409
  62.5 21.1 %collective-permute-start = (bf16[2,1616,128]{2,1,0:T(8,128)(2,1)}, bf16[2,1616,128]{2,1,0:T(8,128)(2,1)}, u32[]{:S(2)}, u32[]{:S(2)}) collective-permute-start(bf16[2,1616,128]{2,1,0:T(8,128)(2,1)} %get-tuple-element.32), channel_id=1, source_target_pairs={{0,8},{8,0},{16,24},{24,16},{1,9},{9,1},{17,25},{25,17},{2,10},{10... | collective-permute-start | bytes 2482184 | tf_op jit(solution)/shard_map/ppermute | solution.py:324
  68.5 1.4 copy-start.1
  68.5 15.1 %copy-start.4 = (bf16[2,1616,128]{2,1,0:T(8,128)(2,1)S(1)}, bf16[2,1616,128]{2,1,0:T(8,128)(2,1)}, u32[]{:S(2)}) copy-start(bf16[2,1616,128]{2,1,0:T(8,128)(2,1)} %get-tuple-element.31) | copy-start | bytes 2482180
  69.9 38.2 %all-to-all-start.1 = ((bf16[8,2,2,32,1024]{4,3,2,1,0:T(8,128)(2,1)}), bf16[8,2,2,32,1024]{4,3,2,1,0:T(8,128)(2,1)S(1)}, u32[]{:S(2)}, u32[]{:S(2)}) async-start(bf16[8,2,2,32,1024]{4,3,2,1,0:T(8,128)(2,1)} %get-tuple-element.26), calls=%async_computation.1 | async-start | bytes 4194304 | tf_op jit(solution)/shard_map/all_to_all | solution.py:409
  108.1 7.3 %copy-start = (bf16[8,2,2,32,1024]{4,3,2,1,0:T(8,128)(2,1)}, bf16[8,2,2,32,1024]{4,3,2,1,0:T(8,128)(2,1)S(1)}, u32[]{:S(2)}) copy-start(bf16[8,2,2,32,1024]{4,3,2,1,0:T(8,128)(2,1)S(1)} %all-to-all-done.1.refs_0_) | copy-start | bytes 6291460
  108.1 35.1 %collective-permute-start.2 = (bf16[2,1616,128]{2,1,0:T(8,128)(2,1)}, bf16[2,1616,128]{2,1,0:T(8,128)(2,1)}, u32[]{:S(2)}, u32[]{:S(2)}) collective-permute-start(bf16[2,1616,128]{2,1,0:T(8,128)(2,1)} %add_convert_fusion.1), channel_id=1, source_target_pairs={{0,16},{8,24},{16,0},{24,8},{1,17},{9,25},{17,1},{25,9},{2,18},{10... | collective-permute-start | bytes 2482184 | tf_op jit(solution)/shard_map/ppermute | solution.py:324
  115.1 28.3 %copy-start.3 = (bf16[2,1616,128]{2,1,0:T(8,128)(2,1)S(1)}, bf16[2,1616,128]{2,1,0:T(8,128)(2,1)}, u32[]{:S(2)}) copy-start(bf16[2,1616,128]{2,1,0:T(8,128)(2,1)} %get-tuple-element.37) | copy-start | bytes 2482180
  115.1 28.3 %collective-permute-start.1 = (bf16[2,1616,128]{2,1,0:T(8,128)(2,1)}, bf16[2,1616,128]{2,1,0:T(8,128)(2,1)}, u32[]{:S(2)}, u32[]{:S(2)}) collective-permute-start(bf16[2,1616,128]{2,1,0:T(8,128)(2,1)} %get-tuple-element.38), channel_id=1, source_target_pairs={{0,8},{8,0},{16,24},{24,16},{1,9},{9,1},{17,25},{25,17},{2,10},{10... | collective-permute-start | bytes 2482184 | tf_op jit(solution)/shard_map/ppermute | solution.py:324
  115.3 35.8 %all-to-all-start.3 = ((bf16[8,2,2,32,1024]{4,3,2,1,0:T(8,128)(2,1)}), bf16[8,2,2,32,1024]{4,3,2,1,0:T(8,128)(2,1)}, u32[]{:S(2)}, u32[]{:S(2)}) async-start(bf16[8,2,2,32,1024]{4,3,2,1,0:T(8,128)(2,1)} %get-tuple-element.34), calls=%async_computation.3 | async-start | bytes 4194304 | tf_op jit(solution)/shard_map/all_to_all | solution.py:409

commit v3 on v2

--- a/solution.py
+++ b/solution.py
@@ -14,7 +14,8 @@
 WIDTH = GROUP * HD
 SCALE = HD ** (-0.5)
 LOG2E = 1.4426950408889634
-CHUNK = 2048
+CHUNK = 512
+SLICE = 128
 LOWEST = -3.0e38
 PER_CHUNK = 2
 VMEM_BYTES = 58 << 20
@@ -66,27 +67,37 @@
         copy.wait()
 
 
-def collect_kernel(chunks, n_seg, seg_rows, reads, *refs):
-    returned = refs[: len(chunks)]
-    o_out, dq_out, sems = refs[len(chunks) :]
+def collect_kernel(turns, n_seg, seg_rows, reads, returned, *refs):
+    o_hbm, dq_hbm, stage, in_sems, out_sems = refs[-5:]
     row = lax.axis_index("seq") * lax.axis_size("enc") + lax.axis_index("enc")
-    copies = []
-    for c, turns in enumerate(chunks):
-        for i, turn in enumerate(turns):
-            column = pl.multiple_of(head_at(turn) * WIDTH, WIDTH)
-            for r in range(n_seg):
-                for which, target in enumerate((o_out, dq_out)):
-                    copies.append(
-                        pltpu.make_async_copy(
-                            returned[c].at[reads[r, row], i, which],
-                            target.at[r * seg_rows : (r + 1) * seg_rows, pl.ds(column, WIDTH)],
-                            sems.at[turn, r, which],
-                        )
+    arriving, leaving = [], []
+    for i, turn in enumerate(turns):
+        columns = pl.ds(pl.multiple_of(head_at(turn) * WIDTH, WIDTH), WIDTH)
+        for which, target in enumerate((o_hbm, dq_hbm)):
+            arriving.append(
+                [
+                    pltpu.make_async_copy(
+                        returned.at[reads[r, row], i, which],
+                        stage.at[i, which, r * seg_rows : (r + 1) * seg_rows, :],
+                        in_sems.at[i, which, r],
                     )
-    for copy in copies:
-        copy.start()
-    for copy in copies:
-        copy.wait()
+                    for r in range(n_seg)
+                ]
+            )
+            leaving.append(
+                pltpu.make_async_copy(
+                    stage.at[i, which], target.at[:, columns], out_sems.at[i, which]
+                )
+            )
+    for copies in arriving:
+        for copy in copies:
+            copy.start()
+    for copies, out in zip(arriving, leaving):
+        for copy in copies:
+            copy.wait()
+        out.start()
+    for out in leaving:
+        out.wait()
 
 
 def is_read(reads, row, image):
@@ -121,7 +132,8 @@
         inbox,
         outbox,
         scores,
-        weights,
+        even,
+        odd,
         dscores,
         sums,
         staged,
@@ -199,12 +211,6 @@
                 h * seg_rows : (h + 1) * seg_rows, :
             ]
 
-    def masked(part, a, b, other):
-        if b <= tokens:
-            return part
-        token = lax.broadcasted_iota(jnp.int32, part.shape, 0) + a
-        return jnp.where(token < tokens, part, other)
-
     def await_step(step):
         i, slot = place(step)
         for head in range(len(turns)):
@@ -216,44 +222,57 @@
 
         arriving(i, slot, 0).wait()
 
-    def forward(i, slot):
-        q, g = (stacked(i, slot, which).astype(f32).T for which in range(2))
-        q_turned = q.astype(bf16)
-        state = {"top": jnp.full((1, lanes), LOWEST, f32), "total": jnp.zeros((1, lanes), f32)}
+    def slices(a, b):
+        return [(c, min(c + SLICE, b)) for c in range(a, b, SLICE)]
+
+    def folded(value, reduce):
+        return reduce(value.reshape(-1, 8, lanes), axis=0)
+
+    def forward(i, slot, weights):
+        q_turned = stacked(i, slot, 0).astype(f32).T.astype(bf16)
+        tops, totals = [], []
 
         def score(a, b):
             part = jnp.dot(straight[i, 0, a:b, :], q_turned, preferred_element_type=f32)
-            part = masked(part, a, b, LOWEST)
-            scores[a:b, :] = part
-            state["top"] = jnp.maximum(state["top"], jnp.max(part, axis=0, keepdims=True))
+            for c, d in slices(a, b):
+                piece = part[c - a : d - a, :]
+                if d > tokens:
+                    token = lax.broadcasted_iota(jnp.int32, piece.shape, 0) + c
+                    piece = jnp.where(token < tokens, piece, LOWEST)
+                scores[c:d, :] = piece
+                tops.append(folded(piece, jnp.max))
 
         def weigh(a, b):
-            part = jnp.exp2((scores[a:b, :] - state["top"]) * (SCALE * LOG2E))
-            state["total"] = state["total"] + jnp.sum(part, axis=0, keepdims=True)
-            weights[a:b, :] = part.astype(bf16)
+            if a == 0:
+                tops[:] = [jnp.max(functools.reduce(jnp.maximum, tops), axis=0, keepdims=True)]
+            for c, d in slices(a, b):
+                piece = jnp.exp2((scores[c:d, :] - tops[0]) * (SCALE * LOG2E))
+                totals.append(folded(piece, jnp.sum))
+                weights[c:d, :] = piece.astype(bf16)
 
         def finish():
-            out = jnp.dot(turned[i, 1], weights[...], preferred_element_type=f32)
-            out = out * (1.0 / state["total"])
+            total = jnp.sum(functools.reduce(jnp.add, totals), axis=0, keepdims=True)
+            inverse = 1.0 / total
+            out = jnp.dot(turned[i, 1], weights[...], preferred_element_type=f32) * inverse
             store(i, slot, 0, out)
-            delta = jnp.sum(g * out.astype(bf16).astype(f32), axis=0, keepdims=True)
-            lse = state["top"] * (SCALE * LOG2E) + jnp.log2(state["total"])
-            return lse, delta, q_turned, g.astype(bf16)
+            g = (stacked(i, slot, 1).astype(f32).T * inverse).astype(bf16)
+            exact = g.astype(f32)
+            delta = jnp.sum(exact * out.astype(bf16).astype(f32), axis=0, keepdims=True)
+            return delta, g, exact.T.astype(bf16)
 
         parts = [functools.partial(score, a, b) for a, b in pieces]
         return parts + [functools.partial(weigh, a, b) for a, b in pieces], finish
 
-    def backward(i, slot, lse, delta, q_turned, g_turned):
-        q, g = stacked(i, slot, 0), stacked(i, slot, 1)
+    def backward(i, slot, weights, delta, g_turned, g):
+        q = stacked(i, slot, 0)
 
         def part(a, b):
-            score = jnp.dot(straight[i, 0, a:b, :], q_turned, preferred_element_type=f32)
-            prob = masked(jnp.exp2(score * (SCALE * LOG2E) - lse), a, b, 0.0)
             dprob = jnp.dot(straight[i, 1, a:b, :], g_turned, preferred_element_type=f32)
-            dscore = (prob * (dprob - delta)).astype(bf16)
-            dscores[a:b, :] = dscore
-            sums[i, 0, a:b, :] += jnp.dot(dscore, q, preferred_element_type=f32)
-            sums[i, 1, a:b, :] += jnp.dot(prob.astype(bf16), g, preferred_element_type=f32)
+            for c, d in slices(a, b):
+                piece = weights[c:d, :].astype(f32) * (dprob[c - a : d - a, :] - delta)
+                dscores[c:d, :] = piece.astype(bf16)
+            sums[i, 0, a:b, :] += jnp.dot(dscores[a:b, :], q, preferred_element_type=f32)
+            sums[i, 1, a:b, :] += jnp.dot(weights[a:b, :], g, preferred_element_type=f32)
 
         def finish():
             turned_dq = jnp.dot(turned[i, 0], dscores[...], preferred_element_type=f32)
@@ -261,7 +280,7 @@
 
         return [functools.partial(part, a, b) for a, b in pieces], finish
 
-    def one_step(step, carry):
+    def one_step(step, carry, weights, next_weights):
         i, slot = place(step)
         later = jnp.minimum(step + 1, steps - 1)
 
@@ -269,8 +288,8 @@
         def _():
             await_step(step + 1)
 
-        ahead, ahead_finish = forward(*place(later))
-        behind, behind_finish = backward(i, slot, *carry)
+        ahead, ahead_finish = forward(*place(later), next_weights)
+        behind, behind_finish = backward(i, slot, weights, *carry)
         for j, part in enumerate(behind):
             for other in ahead[2 * j : 2 * j + 2]:
                 other()
@@ -291,13 +310,17 @@
 
         return carry
 
+    def two_steps(pair, carry):
+        carry = one_step(2 * pair, carry, even, odd)
+        return one_step(2 * pair + 1, carry, odd, even)
+
     @pl.when(count > 0)
     def _():
         await_step(jnp.int32(0))
-        first, first_finish = forward(0, 0)
+        first, first_finish = forward(0, 0, even)
         for part in first:
             part()
-        lax.fori_loop(0, steps, one_step, first_finish())
+        lax.fori_loop(0, steps // 2, two_steps, first_finish())
 
     @pl.when(count == 0)
     def _():
@@ -376,6 +399,7 @@
                 pltpu.VMEM((padded, lanes), f32),
                 pltpu.VMEM((padded, lanes), bf16),
                 pltpu.VMEM((padded, lanes), bf16),
+                pltpu.VMEM((padded, lanes), bf16),
                 pltpu.VMEM((len(turns), 2, padded, HD), f32),
                 pltpu.VMEM((len(turns), 2, padded, HD), bf16),
                 pltpu.SMEM((slots,), jnp.int32),
@@ -386,24 +410,29 @@
             ],
             compiler_params=pltpu.CompilerParams(vmem_limit_bytes=VMEM_BYTES),
             cost_estimate=pl.CostEstimate(
-                flops=24 * work, bytes_accessed=8 << 20, transcendentals=slots * lanes * tokens
+                flops=12 * work, bytes_accessed=8 << 20, transcendentals=slots * lanes * tokens
             ),
             name=f"attend_{turns[0]}",
         )(by_segment, *prepared, received)
         return results[0], list(results[1:])
 
-    def collect(returned):
+    def collect(turns, returned, before):
         whole = jax.ShapeDtypeStruct(queries.shape, bf16)
         return pl.pallas_call(
-            functools.partial(collect_kernel, chunks, n_seg, seg_rows),
+            functools.partial(collect_kernel, turns, n_seg, seg_rows),
             out_shape=[whole, whole],
-            in_specs=[SMEM] + [ANY] * len(chunks),
-            out_specs=[VMEM, VMEM],
-            scratch_shapes=[pltpu.SemaphoreType.DMA((KVH, n_seg, 2))],
+            in_specs=[SMEM, ANY] + [ANY] * len(before),
+            out_specs=[ANY, ANY],
+            input_output_aliases={2: 0, 3: 1} if before else {},
+            scratch_shapes=[
+                pltpu.VMEM((PER_CHUNK, 2, n_seg * seg_rows, WIDTH), bf16),
+                pltpu.SemaphoreType.DMA((PER_CHUNK, 2, n_seg)),
+                pltpu.SemaphoreType.DMA((PER_CHUNK, 2)),
+            ],
             compiler_params=pltpu.CompilerParams(vmem_limit_bytes=VMEM_BYTES),
             cost_estimate=pl.CostEstimate(flops=0, bytes_accessed=4 << 20, transcendentals=0),
-            name="collect",
-        )(by_segment, *returned)
+            name=f"collect_{turns[0]}",
+        )(by_segment, returned, *before)
 
     def exchange(array):
         return lax.all_to_all(array, "enc", split_axis=0, concat_axis=0, tiled=True)
@@ -420,13 +449,15 @@
     received_later, grads[1] = lax.optimization_barrier((received_later, grads[1]))
     returned, more = attend(second, received_later)
     grads += more
+    answer, returned = lax.optimization_barrier((answer, returned))
+    answer_later = exchange(returned)
     if n_seq == KVH:
+        passed, grads[1], grads[2] = lax.optimization_barrier((passed, grads[1], grads[2]))
         pair = (grads[1].astype(f32) + passed.astype(f32)).astype(bf16)
-        answer, returned, pair = lax.optimization_barrier((answer, returned, pair))
         pair = xor_permute(pair, "seq", 2)
         near = xor_permute(grads[2], "seq", 1)
-    answers = [answer, exchange(returned)]
-    attended, grad_queries = collect(answers)
+    half = collect(first, answer, [])
+    attended, grad_queries = collect(second, answer_later, half)
 
     if n_seq == KVH:
         total = grads[3].astype(f32) + near.astype(f32) + pair.astype(f32)

time: 156 us -> 151 us (0.968)
  Pallas kernels: 58.1 us -> 52.4 us
    all_to_all x4, waiting for transfers between devices: 24.7 us -> 33.9 us  [exchange(): return lax.all_to_all(array, 'enc', split_axis=0, concat_axis=0, tiled=True)]
    ppermute x3, waiting for transfers between devices: 25.2 us -> 16.6 us  [xor_permute(): return lax.ppermute(array, axis, [(i, i ^ k) for i in range(size)])]
    pallas_call x2, Pallas kernels: 44.4 us -> 36.7 us  [attend(): pl.pallas_call(functools.partial(attend_kernel, turns, peers, seg_rows, t...]
    ppermute x3, starting transfers between devices: 13.2 us -> 5.85 us  [xor_permute(): return lax.ppermute(array, axis, [(i, i ^ k) for i in range(size)])]
    all_to_all x4, starting transfers between devices: 25.3 us -> 31.6 us  [exchange(): return lax.all_to_all(array, 'enc', split_axis=0, concat_axis=0, tiled=True)]
    pallas_call x1 -> x2, Pallas kernels: 3.85 us -> 5.77 us  [collect(): pl.pallas_call(functools.partial(collect_kernel, turns, n_seg, seg_rows),...]
    unnamed x10 -> x12, local copies, waits for them, and re-layouts: 2.82 us -> 4.14 us
  transfers between devices with their start and end apart: 7 -> 7, of which waited for: 5 -> 7; matrix products, arithmetic and copies ran while one was open for 3% -> 2% of each run, Pallas kernels for 33% -> 31%
where the time goes in v3:
time: 151 us; the launch traced here: 149 us
  Pallas kernels  52.4 us (35%)
  waiting for transfers between devices  50.6 us (34%)
  starting transfers between devices  37.5 us (25%)
  local copies, waits for them, and re-layouts  5.08 us (3%)
  other arithmetic  2.59 us (2%)
    pallas_call x2, Pallas kernels, attend(): pl.pallas_call(functools.partial(attend_kernel, turns, peers, seg_rows, t...  36.7 us
    all_to_all x4, waiting for transfers between devices, exchange(): return lax.all_to_all(array, 'enc', split_axis=0, concat_axis=0, tiled=True)  33.9 us
    all_to_all x4, starting transfers between devices, exchange(): return lax.all_to_all(array, 'enc', split_axis=0, concat_axis=0, tiled=True)  31.6 us
    ppermute x3, waiting for transfers between devices, xor_permute(): return lax.ppermute(array, axis, [(i, i ^ k) for i in range(size)])  16.6 us
    pallas_call x2, Pallas kernels, route(): pl.pallas_call(functools.partial(route_kernel, turns, n_seg, seg_rows, to...  9.91 us
    ppermute x3, starting transfers between devices, xor_permute(): return lax.ppermute(array, axis, [(i, i ^ k) for i in range(size)])  5.85 us
    pallas_call x2, Pallas kernels, collect(): pl.pallas_call(functools.partial(collect_kernel, turns, n_seg, seg_rows),...  5.77 us
    unnamed x12, local copies, waits for them, and re-layouts  4.14 us
  transfers between devices with their start and end apart: 7, of which 7 were waited for; matrix products, arithmetic and copies ran while one was open for 2% of the time, Pallas kernels for 31%

profile of v3, /device:TPU:0, one launch (start us, length us, event | category | flops | bytes accessed | tf_op | source)
XLA Modules:
  0.0 149.0 jit_solution(9228062291307990159)
XLA Ops:
  0.6 2.8 %route_0.1 = bf16[8,2,2,32,1024]{4,3,2,1,0:T(8,128)(2,1)} custom-call(s32[4,32]{1,0:T(4,128)} %bitcast.1, bf16[128,4096]{1,0:T(8,128)(2,1)} %q_hbm.3, bf16[128,4096]{1,0:T(8,128)(2,1)} %g_hbm.3), custom_call_target="tpu_custom_call" | custom-call | bytes 2097152 | tf_op jit(solution)/shard_map/route_0/pallas_call | solution.py:370
  3.5 5.2 %all-to-all-start = ((bf16[8,2,2,32,1024]{4,3,2,1,0:T(8,128)(2,1)}), bf16[8,2,2,32,1024]{4,3,2,1,0:T(8,128)(2,1)S(1)}, u32[]{:S(2)}, u32[]{:S(2)}) async-start(bf16[8,2,2,32,1024]{4,3,2,1,0:T(8,128)(2,1)} %route_0.1), calls=%async_computation | async-start | bytes 4194304 | tf_op jit(solution)/shard_map/all_to_all | solution.py:438
  8.7 7.1 %route_2.1 = (bf16[8,2,2,32,1024]{4,3,2,1,0:T(8,128)(2,1)}, bf16[4,2,1616,128]{3,2,1,0:T(8,128)(2,1)}, bf16[4,2,128,1616]{3,2,1,0:T(8,128)(2,1)}) custom-call(s32[4,32]{1,0:T(4,128)} %bitcast.2, bf16[128,4096]{1,0:T(8,128)(2,1)} %q_hbm.3, bf16[128,4096]{1,0:T(8,128)(2,1)} %g_hbm.3, bf16[1,1601,512]{2,1,0:T(8,128)(2,1)} %refs_0_.1, bf16[1,1601,512]{2,1,0:T(8,128)(2,1)} %refs_1_.1), custom_call_target="tpu_custom_call" | custom-call | bytes 12582912 | tf_op jit(solution)/shard_map/route_2/pallas_call | solution.py:370
  15.7 19.6 %all-to-all-done.received = bf16[8,2,2,32,1024]{4,3,2,1,0:T(8,128)(2,1)S(1)} async-done(((bf16[8,2,2,32,1024]{4,3,2,1,0:T(8,128)(2,1)}), bf16[8,2,2,32,1024]{4,3,2,1,0:T(8,128)(2,1)S(1)}, u32[]{:S(2)}, u32[]{:S(2)}) %all-to-all-start) | async-done | bytes 2097184 | tf_op jit(solution)/shard_map/all_to_all | solution.py:438
  35.3 0.0 copy-start.2
  35.3 1.4 copy-done.2
  36.7 3.6 %all-to-all-start.2 = ((bf16[8,2,2,32,1024]{4,3,2,1,0:T(8,128)(2,1)}), bf16[8,2,2,32,1024]{4,3,2,1,0:T(8,128)(2,1)S(1)}, u32[]{:S(2)}, u32[]{:S(2)}) async-start(bf16[8,2,2,32,1024]{4,3,2,1,0:T(8,128)(2,1)} %get-tuple-element.31), calls=%async_computation.2 | async-start | bytes 4194304 | tf_op jit(solution)/shard_map/all_to_all | solution.py:438
  40.4 18.2 %attend_0.1 = (bf16[8,2,2,32,1024]{4,3,2,1,0:T(8,128)(2,1)}, bf16[2,1616,128]{2,1,0:T(8,128)(2,1)}, bf16[2,1616,128]{2,1,0:T(8,128)(2,1)}) custom-call(s32[4,32]{1,0:T(4,128)} %bitcast.3, bf16[4,2,1616,128]{3,2,1,0:T(8,128)(2,1)} %get-tuple-element.26.caches, bf16[4,2,128,1616]{3,2,1,0:T(8,128)(2,1)} %get-tuple-element.27.turned_caches, ...), custom_call_target="tpu_custom_call" | custom-call | flops 7554465792 | bytes 8388608 | tf_op jit(solution)/shard_map/attend_0/pallas_call | solution.py:389
  58.6 8.4 %all-to-all-done.2.received = bf16[8,2,2,32,1024]{4,3,2,1,0:T(8,128)(2,1)S(1)} async-done(((bf16[8,2,2,32,1024]{4,3,2,1,0:T(8,128)(2,1)}), bf16[8,2,2,32,1024]{4,3,2,1,0:T(8,128)(2,1)S(1)}, u32[]{:S(2)}, u32[]{:S(2)}) %all-to-all-start.2) | async-done | bytes 2097184 | tf_op jit(solution)/shard_map/all_to_all | solution.py:438
  66.9 0.0 copy-start.1
  66.9 0.0 copy-start.5
  66.9 1.4 copy-done.1
  68.3 8.7 %all-to-all-start.1 = ((bf16[8,2,2,32,1024]{4,3,2,1,0:T(8,128)(2,1)}), bf16[8,2,2,32,1024]{4,3,2,1,0:T(8,128)(2,1)S(1)}, u32[]{:S(2)}, u32[]{:S(2)}) async-start(bf16[8,2,2,32,1024]{4,3,2,1,0:T(8,128)(2,1)} %get-tuple-element.30), calls=%async_computation.1 | async-start | bytes 4194304 | tf_op jit(solution)/shard_map/all_to_all | solution.py:438
  77.0 0.0 copy-done.5
  77.0 1.7 %collective-permute-start = (bf16[2,1616,128]{2,1,0:T(8,128)(2,1)S(1)}, bf16[2,1616,128]{2,1,0:T(8,128)(2,1)S(1)}, u32[]{:S(2)}, u32[]{:S(2)}) collective-permute-start(bf16[2,1616,128]{2,1,0:T(8,128)(2,1)S(1)} %copy-done.5), channel_id=1, source_target_pairs={{0,8},{8,0},{16,24},{24,16},{1,9},{9,1},{17,25},{25,17},{2,10},{10... | collective-permute-start | bytes 2482184 | tf_op jit(solution)/shard_map/ppermute | solution.py:347
  78.8 18.5 %attend_2.1 = (bf16[8,2,2,32,1024]{4,3,2,1,0:T(8,128)(2,1)}, bf16[2,1616,128]{2,1,0:T(8,128)(2,1)}, bf16[2,1616,128]{2,1,0:T(8,128)(2,1)}) custom-call(s32[4,32]{1,0:T(4,128)} %bitcast.4, bf16[4,2,1616,128]{3,2,1,0:T(8,128)(2,1)} %get-tuple-element.26.caches, bf16[4,2,128,1616]{3,2,1,0:T(8,128)(2,1)} %get-tuple-element.27.turned_caches, ...), custom_call_target="tpu_custom_call" | custom-call | flops 7554465792 | bytes 8388608 | tf_op jit(solution)/shard_map/attend_2/pallas_call | solution.py:389
  97.3 0.6 collective-permute-done
  97.9 0.0 copy-done.4
  97.9 1.1 add_convert_fusion.1
  99.0 2.6 %collective-permute-start.2 = (bf16[2,1616,128]{2,1,0:T(8,128)(2,1)}, bf16[2,1616,128]{2,1,0:T(8,128)(2,1)S(1)}, u32[]{:S(2)}, u32[]{:S(2)}) collective-permute-start(bf16[2,1616,128]{2,1,0:T(8,128)(2,1)} %add_convert_fusion.1), channel_id=1, source_target_pairs={{0,16},{8,24},{16,0},{24,8},{1,17},{9,25},{17,1},{25,9},{2,18},{10... | collective-permute-start | bytes 2482184 | tf_op jit(solution)/shard_map/ppermute | solution.py:347
  101.6 1.6 %collective-permute-start.1 = (bf16[2,1616,128]{2,1,0:T(8,128)(2,1)}, bf16[2,1616,128]{2,1,0:T(8,128)(2,1)}, u32[]{:S(2)}, u32[]{:S(2)}) collective-permute-start(bf16[2,1616,128]{2,1,0:T(8,128)(2,1)} %get-tuple-element.45), channel_id=1, source_target_pairs={{0,8},{8,0},{16,24},{24,16},{1,9},{9,1},{17,25},{25,17},{2,10},{10... | collective-permute-start | bytes 2482184 | tf_op jit(solution)/shard_map/ppermute | solution.py:347
  103.1 0.5 all-to-all-done.1.returned
  103.7 1.3 copy-done
  105.0 14.1 %all-to-all-start.3 = ((bf16[8,2,2,32,1024]{4,3,2,1,0:T(8,128)(2,1)}), bf16[8,2,2,32,1024]{4,3,2,1,0:T(8,128)(2,1)}, u32[]{:S(2)}, u32[]{:S(2)}) async-start(bf16[8,2,2,32,1024]{4,3,2,1,0:T(8,128)(2,1)} %get-tuple-element.35), calls=%async_computation.3 | async-start | bytes 4194304 | tf_op jit(solution)/shard_map/all_to_all | solution.py:438
  119.1 3.0 %collect_0.1 = (bf16[128,4096]{1,0:T(8,128)(2,1)}, bf16[128,4096]{1,0:T(8,128)(2,1)}) custom-call(s32[4,32]{1,0:T(4,128)} %bitcast.5, bf16[8,2,2,32,1024]{4,3,2,1,0:T(8,128)(2,1)} %copy-done), custom_call_target="tpu_custom_call" | custom-call | bytes 4194304 | tf_op jit(solution)/shard_map/collect_0/pallas_call | solution.py:421
  122.1 15.8 %collective-permute-done.2 = bf16[2,1616,128]{2,1,0:T(8,128)(2,1)S(1)} collective-permute-done((bf16[2,1616,128]{2,1,0:T(8,128)(2,1)}, bf16[2,1616,128]{2,1,0:T(8,128)(2,1)S(1)}, u32[]{:S(2)}, u32[]{:S(2)}) %collective-permute-start.2) | collective-permute-done | bytes 827424 | tf_op jit(solution)/shard_map/ppermute | solution.py:347
  137.9 0.2 collective-permute-done.1
  138.1 0.0 copy-done.3
  138.1 1.5 add_convert_fusion
  139.6 0.9 fusion
  140.6 5.4 %all-to-all-done.3.returned = bf16[8,2,2,32,1024]{4,3,2,1,0:T(8,128)(2,1)} async-done(((bf16[8,2,2,32,1024]{4,3,2,1,0:T(8,128)(2,1)}), bf16[8,2,2,32,1024]{4,3,2,1,0:T(8,128)(2,1)}, u32[]{:S(2)}, u32[]{:S(2)}) %all-to-all-start.3) | async-done | bytes 2097184 | tf_op jit(solution)/shard_map/all_to_all | solution.py:438
  146.0 2.8 %collect_2.1 = (bf16[128,4096]{1,0:T(8,128)(2,1)}, bf16[128,4096]{1,0:T(8,128)(2,1)}) custom-call(s32[4,32]{1,0:T(4,128)} %bitcast.6, bf16[8,2,2,32,1024]{4,3,2,1,0:T(8,128)(2,1)} %all-to-all-done.3.returned, bf16[128,4096]{1,0:T(8,128)(2,1)} %get-tuple-element.37.refs_0_, ...), custom_call_target="tpu_custom_call", output_to_operand_aliasing={{0}: (2, {}), {1}: (3, {})} | custom-call | bytes 4194304 | tf_op jit(solution)/shard_map/collect_2/pallas_call | solution.py:421
  (3 shorter events, 0.0 us)
Async XLA Ops:
  3.5 31.8 %all-to-all-start = ((bf16[8,2,2,32,1024]{4,3,2,1,0:T(8,128)(2,1)}), bf16[8,2,2,32,1024]{4,3,2,1,0:T(8,128)(2,1)S(1)}, u32[]{:S(2)}, u32[]{:S(2)}) async-start(bf16[8,2,2,32,1024]{4,3,2,1,0:T(8,128)(2,1)} %route_0.1), calls=%async_computation | async-start | bytes 4194304 | tf_op jit(solution)/shard_map/all_to_all | solution.py:438
  35.3 1.4 copy-start.2
  36.7 30.2 %all-to-all-start.2 = ((bf16[8,2,2,32,1024]{4,3,2,1,0:T(8,128)(2,1)}), bf16[8,2,2,32,1024]{4,3,2,1,0:T(8,128)(2,1)S(1)}, u32[]{:S(2)}, u32[]{:S(2)}) async-start(bf16[8,2,2,32,1024]{4,3,2,1,0:T(8,128)(2,1)} %get-tuple-element.31), calls=%async_computation.2 | async-start | bytes 4194304 | tf_op jit(solution)/shard_map/all_to_all | solution.py:438
  66.9 1.4 copy-start.1
  66.9 10.1 %copy-start.5 = (bf16[2,1616,128]{2,1,0:T(8,128)(2,1)S(1)}, bf16[2,1616,128]{2,1,0:T(8,128)(2,1)}, u32[]{:S(2)}) copy-start(bf16[2,1616,128]{2,1,0:T(8,128)(2,1)} %get-tuple-element.42) | copy-start | bytes 2482180
  68.3 35.3 %all-to-all-start.1 = ((bf16[8,2,2,32,1024]{4,3,2,1,0:T(8,128)(2,1)}), bf16[8,2,2,32,1024]{4,3,2,1,0:T(8,128)(2,1)S(1)}, u32[]{:S(2)}, u32[]{:S(2)}) async-start(bf16[8,2,2,32,1024]{4,3,2,1,0:T(8,128)(2,1)} %get-tuple-element.30), calls=%async_computation.1 | async-start | bytes 4194304 | tf_op jit(solution)/shard_map/all_to_all | solution.py:438
  77.0 20.8 %collective-permute-start = (bf16[2,1616,128]{2,1,0:T(8,128)(2,1)S(1)}, bf16[2,1616,128]{2,1,0:T(8,128)(2,1)S(1)}, u32[]{:S(2)}, u32[]{:S(2)}) collective-permute-start(bf16[2,1616,128]{2,1,0:T(8,128)(2,1)S(1)} %copy-done.5), channel_id=1, source_target_pairs={{0,8},{8,0},{16,24},{24,16},{1,9},{9,1},{17,25},{25,17},{2,10},{10... | collective-permute-start | bytes 2482184 | tf_op jit(solution)/shard_map/ppermute | solution.py:347
  78.8 19.1 %copy-start.4 = (bf16[2,1616,128]{2,1,0:T(8,128)(2,1)S(1)}, bf16[2,1616,128]{2,1,0:T(8,128)(2,1)}, u32[]{:S(2)}) copy-start(bf16[2,1616,128]{2,1,0:T(8,128)(2,1)} %get-tuple-element.46) | copy-start | bytes 2482180
  99.0 38.9 %collective-permute-start.2 = (bf16[2,1616,128]{2,1,0:T(8,128)(2,1)}, bf16[2,1616,128]{2,1,0:T(8,128)(2,1)S(1)}, u32[]{:S(2)}, u32[]{:S(2)}) collective-permute-start(bf16[2,1616,128]{2,1,0:T(8,128)(2,1)} %add_convert_fusion.1), channel_id=1, source_target_pairs={{0,16},{8,24},{16,0},{24,8},{1,17},{9,25},{17,1},{25,9},{2,18},{10... | collective-permute-start | bytes 2482184 | tf_op jit(solution)/shard_map/ppermute | solution.py:347
  101.6 36.6 %collective-permute-start.1 = (bf16[2,1616,128]{2,1,0:T(8,128)(2,1)}, bf16[2,1616,128]{2,1,0:T(8,128)(2,1)}, u32[]{:S(2)}, u32[]{:S(2)}) collective-permute-start(bf16[2,1616,128]{2,1,0:T(8,128)(2,1)} %get-tuple-element.45), channel_id=1, source_target_pairs={{0,8},{8,0},{16,24},{24,16},{1,9},{9,1},{17,25},{25,17},{2,10},{10... | collective-permute-start | bytes 2482184 | tf_op jit(solution)/shard_map/ppermute | solution.py:347
  103.7 1.3 copy-start
  105.0 41.0 %all-to-all-start.3 = ((bf16[8,2,2,32,1024]{4,3,2,1,0:T(8,128)(2,1)}), bf16[8,2,2,32,1024]{4,3,2,1,0:T(8,128)(2,1)}, u32[]{:S(2)}, u32[]{:S(2)}) async-start(bf16[8,2,2,32,1024]{4,3,2,1,0:T(8,128)(2,1)} %get-tuple-element.35), calls=%async_computation.3 | async-start | bytes 4194304 | tf_op jit(solution)/shard_map/all_to_all | solution.py:438
  119.1 19.0 %copy-start.3 = (bf16[2,1616,128]{2,1,0:T(8,128)(2,1)S(1)}, bf16[2,1616,128]{2,1,0:T(8,128)(2,1)}, u32[]{:S(2)}) copy-start(bf16[2,1616,128]{2,1,0:T(8,128)(2,1)} %get-tuple-element.41) | copy-start | bytes 2482180

commit v4 on v3

--- a/solution.py
+++ b/solution.py
@@ -132,8 +132,7 @@
         inbox,
         outbox,
         scores,
-        even,
-        odd,
+        even_odd,
         dscores,
         sums,
         staged,
@@ -172,8 +171,9 @@
     def handing(i):
         return pltpu.make_async_copy(staged.at[i], grads[i], grad_sems.at[i])
 
-    for copy in kv_copies[0]:
-        copy.start()
+    for j in range(2):
+        for copies in kv_copies:
+            copies[j].start()
     count = jnp.int32(0)
     for k in range(peers):
         found = is_read(reads, base + k, me)
@@ -181,23 +181,12 @@
         @pl.when(found)
         def _():
             owners[count] = jnp.int32(k)
-            arriving(0, count, k).start()
+            for i in range(len(turns)):
+                arriving(i, count, k).start()
 
         count = count + found.astype(jnp.int32)
-    for i in range(1, len(turns)):
-        for copy in kv_copies[i]:
-            copy.start()
-        for slot in range(slots):
-
-            @pl.when(slot < count)
-            def _():
-                arriving(i, slot, owners[slot]).start()
 
     sums[...] = jnp.zeros_like(sums)
-    steps = count * len(turns)
-
-    def place(step):
-        return lax.div(step, count), lax.rem(step, count)
 
     def stacked(i, slot, which):
         return jnp.concatenate(
@@ -211,17 +200,6 @@
                 h * seg_rows : (h + 1) * seg_rows, :
             ]
 
-    def await_step(step):
-        i, slot = place(step)
-        for head in range(len(turns)):
-
-            @pl.when(step == head * count)
-            def _():
-                for copy in kv_copies[head]:
-                    copy.wait()
-
-        arriving(i, slot, 0).wait()
-
     def slices(a, b):
         return [(c, min(c + SLICE, b)) for c in range(a, b, SLICE)]
 
@@ -230,7 +208,7 @@
 
     def forward(i, slot, weights):
         q_turned = stacked(i, slot, 0).astype(f32).T.astype(bf16)
-        tops, totals = [], []
+        tops, totals, outs = [], [], []
 
         def score(a, b):
             part = jnp.dot(straight[i, 0, a:b, :], q_turned, preferred_element_type=f32)
@@ -239,88 +217,97 @@
                 if d > tokens:
                     token = lax.broadcasted_iota(jnp.int32, piece.shape, 0) + c
                     piece = jnp.where(token < tokens, piece, LOWEST)
-                scores[c:d, :] = piece
+                scores[i, c:d, :] = piece
                 tops.append(folded(piece, jnp.max))
 
         def weigh(a, b):
             if a == 0:
                 tops[:] = [jnp.max(functools.reduce(jnp.maximum, tops), axis=0, keepdims=True)]
             for c, d in slices(a, b):
-                piece = jnp.exp2((scores[c:d, :] - tops[0]) * (SCALE * LOG2E))
+                piece = jnp.exp2((scores[i, c:d, :] - tops[0]) * (SCALE * LOG2E))
                 totals.append(folded(piece, jnp.sum))
-                weights[c:d, :] = piece.astype(bf16)
+                weights[i, c:d, :] = piece.astype(bf16)
+            outs.append(
+                jnp.dot(turned[i, 1, :, a:b], weights[i, a:b, :], preferred_element_type=f32)
+            )
 
         def finish():
             total = jnp.sum(functools.reduce(jnp.add, totals), axis=0, keepdims=True)
             inverse = 1.0 / total
-            out = jnp.dot(turned[i, 1], weights[...], preferred_element_type=f32) * inverse
+            out = functools.reduce(jnp.add, outs) * inverse
             store(i, slot, 0, out)
             g = (stacked(i, slot, 1).astype(f32).T * inverse).astype(bf16)
             exact = g.astype(f32)
             delta = jnp.sum(exact * out.astype(bf16).astype(f32), axis=0, keepdims=True)
             return delta, g, exact.T.astype(bf16)
 
-        parts = [functools.partial(score, a, b) for a, b in pieces]
-        return parts + [functools.partial(weigh, a, b) for a, b in pieces], finish
+        return score, weigh, finish
 
     def backward(i, slot, weights, delta, g_turned, g):
         q = stacked(i, slot, 0)
-
-        def part(a, b):
+        turned_dq = []
+
+        def values_part(a, b):
             dprob = jnp.dot(straight[i, 1, a:b, :], g_turned, preferred_element_type=f32)
             for c, d in slices(a, b):
-                piece = weights[c:d, :].astype(f32) * (dprob[c - a : d - a, :] - delta)
-                dscores[c:d, :] = piece.astype(bf16)
-            sums[i, 0, a:b, :] += jnp.dot(dscores[a:b, :], q, preferred_element_type=f32)
-            sums[i, 1, a:b, :] += jnp.dot(weights[a:b, :], g, preferred_element_type=f32)
+                piece = weights[i, c:d, :].astype(f32) * (dprob[c - a : d - a, :] - delta)
+                dscores[i, c:d, :] = piece.astype(bf16)
+            sums[i, 1, a:b, :] += jnp.dot(weights[i, a:b, :], g, preferred_element_type=f32)
+
+        def keys_part(a, b):
+            sums[i, 0, a:b, :] += jnp.dot(dscores[i, a:b, :], q, preferred_element_type=f32)
+            turned_dq.append(
+                jnp.dot(turned[i, 0, :, a:b], dscores[i, a:b, :], preferred_element_type=f32)
+            )
 
         def finish():
-            turned_dq = jnp.dot(turned[i, 0], dscores[...], preferred_element_type=f32)
-            store(i, slot, 1, turned_dq * SCALE)
-
-        return [functools.partial(part, a, b) for a, b in pieces], finish
-
-    def one_step(step, carry, weights, next_weights):
-        i, slot = place(step)
-        later = jnp.minimum(step + 1, steps - 1)
-
-        @pl.when(step + 1 < steps)
+            store(i, slot, 1, functools.reduce(jnp.add, turned_dq) * SCALE)
+
+        return values_part, keys_part, finish
+
+    heads = range(len(turns))
+
+    def one_slot(slot, carry):
+        later = jnp.minimum(slot + 1, count - 1)
+
+        @pl.when(slot + 1 < count)
         def _():
-            await_step(step + 1)
-
-        ahead, ahead_finish = forward(*place(later), next_weights)
-        behind, behind_finish = backward(i, slot, weights, *carry)
-        for j, part in enumerate(behind):
-            for other in ahead[2 * j : 2 * j + 2]:
-                other()
-            part()
-        behind_finish()
-        carry = ahead_finish()
-        leaving(i, slot, owners[slot]).start()
-
-        @pl.when(slot == count - 1)
-        def _():
+            for i in heads:
+                arriving(i, later, 0).wait()
+
+        weights, next_weights = even_odd.at[slot & 1], even_odd.at[(slot + 1) & 1]
+        ahead = [forward(i, later, next_weights) for i in heads]
+        behind = [backward(i, slot, weights, *carry[i]) for i in heads]
+        for phase in range(2):
+            for a, b in pieces:
+                for i in heads:
+                    ahead[i][phase](a, b)
+                    behind[i][phase](a, b)
+        for i in heads:
+            behind[i][2]()
+        carry = [ahead[i][2]() for i in heads]
+        for i in heads:
+            leaving(i, slot, owners[slot]).start()
+        return carry
+
+    @pl.when(count > 0)
+    def _():
+        for i in heads:
+            arriving(i, 0, 0).wait()
+            kv_copies[i][0].wait()
+        first = [forward(i, 0, even_odd.at[0]) for i in heads]
+        for phase in range(2):
+            if phase == 1:
+                for i in heads:
+                    kv_copies[i][1].wait()
+            for a, b in pieces:
+                for i in heads:
+                    first[i][phase](a, b)
+        lax.fori_loop(0, count, one_slot, [first[i][2]() for i in heads])
+        for i in heads:
             staged[i, 0] = (sums[i, 0] * SCALE).astype(bf16)
             staged[i, 1] = sums[i, 1].astype(bf16)
-            for head in range(len(turns)):
-
-                @pl.when(i == head)
-                def _():
-                    handing(head).start()
-
-        return carry
-
-    def two_steps(pair, carry):
-        carry = one_step(2 * pair, carry, even, odd)
-        return one_step(2 * pair + 1, carry, odd, even)
-
-    @pl.when(count > 0)
-    def _():
-        await_step(jnp.int32(0))
-        first, first_finish = forward(0, 0, even)
-        for part in first:
-            part()
-        lax.fori_loop(0, steps // 2, two_steps, first_finish())
+            handing(i).start()
 
     @pl.when(count == 0)
     def _():
@@ -396,10 +383,9 @@
                 pltpu.VMEM((len(turns), 2, HD, padded), bf16),
                 pltpu.VMEM((len(turns), slots, 2, seg_rows, WIDTH), bf16),
                 pltpu.VMEM((len(turns), slots, 2, seg_rows, WIDTH), bf16),
-                pltpu.VMEM((padded, lanes), f32),
-                pltpu.VMEM((padded, lanes), bf16),
-                pltpu.VMEM((padded, lanes), bf16),
-                pltpu.VMEM((padded, lanes), bf16),
+                pltpu.VMEM((len(turns), padded, lanes), f32),
+                pltpu.VMEM((2, len(turns), padded, lanes), bf16),
+                pltpu.VMEM((len(turns), padded, lanes), bf16),
                 pltpu.VMEM((len(turns), 2, padded, HD), f32),
                 pltpu.VMEM((len(turns), 2, padded, HD), bf16),
                 pltpu.SMEM((slots,), jnp.int32),

time: 151 us -> 143 us (0.947)
  the two profiles are of different devices: /device:TPU:0 before, /device:TPU:6 now
where the time goes in v4:
time: 143 us; the launch traced here: 140 us
  Pallas kernels  55.8 us (39%)
  waiting for transfers between devices  44.4 us (31%)
  starting transfers between devices  31.3 us (22%)
  local copies, waits for them, and re-layouts  5.08 us (4%)
  other arithmetic  2.59 us (2%)
    pallas_call x2, Pallas kernels, attend(): pl.pallas_call(functools.partial(attend_kernel, turns, peers, seg_rows, t...  40.1 us
    all_to_all x4, starting transfers between devices, exchange(): return lax.all_to_all(array, 'enc', split_axis=0, concat_axis=0, tiled=True)  26.9 us
    ppermute x3, waiting for transfers between devices, xor_permute(): return lax.ppermute(array, axis, [(i, i ^ k) for i in range(size)])  22.7 us
    all_to_all x4, waiting for transfers between devices, exchange(): return lax.all_to_all(array, 'enc', split_axis=0, concat_axis=0, tiled=True)  21.7 us
    pallas_call x2, Pallas kernels, route(): pl.pallas_call(functools.partial(route_kernel, turns, n_seg, seg_rows, to...  9.91 us
    pallas_call x2, Pallas kernels, collect(): pl.pallas_call(functools.partial(collect_kernel, turns, n_seg, seg_rows),...  5.77 us
    ppermute x3, starting transfers between devices, xor_permute(): return lax.ppermute(array, axis, [(i, i ^ k) for i in range(size)])  4.4 us
    unnamed x12, local copies, waits for them, and re-layouts  4.14 us
  transfers between devices with their start and end apart: 7, of which 4 were waited for; matrix products, arithmetic and copies ran while one was open for 3% of the time, Pallas kernels for 36%

profile of v4, /device:TPU:6, one launch (start us, length us, event | category | flops | bytes accessed | tf_op | source)
XLA Modules:
  0.0 140.0 jit_solution(9323356012645973235)
XLA Ops:
  0.6 2.8 %route_0.1 = bf16[8,2,2,32,1024]{4,3,2,1,0:T(8,128)(2,1)} custom-call(s32[4,32]{1,0:T(4,128)} %bitcast.1, bf16[128,4096]{1,0:T(8,128)(2,1)} %q_hbm.3, bf16[128,4096]{1,0:T(8,128)(2,1)} %g_hbm.3), custom_call_target="tpu_custom_call" | custom-call | bytes 2097152 | tf_op jit(solution)/shard_map/route_0/pallas_call | solution.py:357
  3.5 4.2 %all-to-all-start = ((bf16[8,2,2,32,1024]{4,3,2,1,0:T(8,128)(2,1)}), bf16[8,2,2,32,1024]{4,3,2,1,0:T(8,128)(2,1)S(1)}, u32[]{:S(2)}, u32[]{:S(2)}) async-start(bf16[8,2,2,32,1024]{4,3,2,1,0:T(8,128)(2,1)} %route_0.1), calls=%async_computation | async-start | bytes 4194304 | tf_op jit(solution)/shard_map/all_to_all | solution.py:424
  7.7 7.1 %route_2.1 = (bf16[8,2,2,32,1024]{4,3,2,1,0:T(8,128)(2,1)}, bf16[4,2,1616,128]{3,2,1,0:T(8,128)(2,1)}, bf16[4,2,128,1616]{3,2,1,0:T(8,128)(2,1)}) custom-call(s32[4,32]{1,0:T(4,128)} %bitcast.2, bf16[128,4096]{1,0:T(8,128)(2,1)} %q_hbm.3, bf16[128,4096]{1,0:T(8,128)(2,1)} %g_hbm.3, bf16[1,1601,512]{2,1,0:T(8,128)(2,1)} %refs_0_.1, bf16[1,1601,512]{2,1,0:T(8,128)(2,1)} %refs_1_.1), custom_call_target="tpu_custom_call" | custom-call | bytes 12582912 | tf_op jit(solution)/shard_map/route_2/pallas_call | solution.py:357
  14.8 17.3 %all-to-all-done.received = bf16[8,2,2,32,1024]{4,3,2,1,0:T(8,128)(2,1)S(1)} async-done(((bf16[8,2,2,32,1024]{4,3,2,1,0:T(8,128)(2,1)}), bf16[8,2,2,32,1024]{4,3,2,1,0:T(8,128)(2,1)S(1)}, u32[]{:S(2)}, u32[]{:S(2)}) %all-to-all-start) | async-done | bytes 2097184 | tf_op jit(solution)/shard_map/all_to_all | solution.py:424
  32.0 0.0 copy-start.2
  32.0 1.4 %copy-done.2 = bf16[8,2,2,32,1024]{4,3,2,1,0:T(8,128)(2,1)} copy-done((bf16[8,2,2,32,1024]{4,3,2,1,0:T(8,128)(2,1)}, bf16[8,2,2,32,1024]{4,3,2,1,0:T(8,128)(2,1)S(1)}, u32[]{:S(2)}) %copy-start.2) | copy-done | bytes 2097176
  33.4 5.9 %all-to-all-start.2 = ((bf16[8,2,2,32,1024]{4,3,2,1,0:T(8,128)(2,1)}), bf16[8,2,2,32,1024]{4,3,2,1,0:T(8,128)(2,1)S(1)}, u32[]{:S(2)}, u32[]{:S(2)}) async-start(bf16[8,2,2,32,1024]{4,3,2,1,0:T(8,128)(2,1)} %get-tuple-element.31), calls=%async_computation.2 | async-start | bytes 4194304 | tf_op jit(solution)/shard_map/all_to_all | solution.py:424
  39.3 19.9 %attend_0.1 = (bf16[8,2,2,32,1024]{4,3,2,1,0:T(8,128)(2,1)}, bf16[2,1616,128]{2,1,0:T(8,128)(2,1)}, bf16[2,1616,128]{2,1,0:T(8,128)(2,1)}) custom-call(s32[4,32]{1,0:T(4,128)} %bitcast.3, bf16[4,2,1616,128]{3,2,1,0:T(8,128)(2,1)} %get-tuple-element.26.caches, bf16[4,2,128,1616]{3,2,1,0:T(8,128)(2,1)} %get-tuple-element.27.turned_caches, ...), custom_call_target="tpu_custom_call" | custom-call | flops 7554465792 | bytes 8388608 | tf_op jit(solution)/shard_map/attend_0/pallas_call | solution.py:376
  59.2 4.4 %all-to-all-done.2.received = bf16[8,2,2,32,1024]{4,3,2,1,0:T(8,128)(2,1)S(1)} async-done(((bf16[8,2,2,32,1024]{4,3,2,1,0:T(8,128)(2,1)}), bf16[8,2,2,32,1024]{4,3,2,1,0:T(8,128)(2,1)S(1)}, u32[]{:S(2)}, u32[]{:S(2)}) %all-to-all-start.2) | async-done | bytes 2097184 | tf_op jit(solution)/shard_map/all_to_all | solution.py:424
  63.6 0.0 copy-start.1
  63.6 0.0 copy-start.5
  63.6 1.4 %copy-done.1 = bf16[8,2,2,32,1024]{4,3,2,1,0:T(8,128)(2,1)} copy-done((bf16[8,2,2,32,1024]{4,3,2,1,0:T(8,128)(2,1)}, bf16[8,2,2,32,1024]{4,3,2,1,0:T(8,128)(2,1)S(1)}, u32[]{:S(2)}) %copy-start.1) | copy-done | bytes 2097176
  65.0 6.2 %all-to-all-start.1 = ((bf16[8,2,2,32,1024]{4,3,2,1,0:T(8,128)(2,1)}), bf16[8,2,2,32,1024]{4,3,2,1,0:T(8,128)(2,1)S(1)}, u32[]{:S(2)}, u32[]{:S(2)}) async-start(bf16[8,2,2,32,1024]{4,3,2,1,0:T(8,128)(2,1)} %get-tuple-element.30), calls=%async_computation.1 | async-start | bytes 4194304 | tf_op jit(solution)/shard_map/all_to_all | solution.py:424
  71.2 0.0 copy-done.5
  71.2 1.5 %collective-permute-start = (bf16[2,1616,128]{2,1,0:T(8,128)(2,1)S(1)}, bf16[2,1616,128]{2,1,0:T(8,128)(2,1)S(1)}, u32[]{:S(2)}, u32[]{:S(2)}) collective-permute-start(bf16[2,1616,128]{2,1,0:T(8,128)(2,1)S(1)} %copy-done.5), channel_id=1, source_target_pairs={{0,8},{8,0},{16,24},{24,16},{1,9},{9,1},{17,25},{25,17},{2,10},{10... | collective-permute-start | bytes 2482184 | tf_op jit(solution)/shard_map/ppermute | solution.py:334
  72.7 20.2 %attend_2.1 = (bf16[8,2,2,32,1024]{4,3,2,1,0:T(8,128)(2,1)}, bf16[2,1616,128]{2,1,0:T(8,128)(2,1)}, bf16[2,1616,128]{2,1,0:T(8,128)(2,1)}) custom-call(s32[4,32]{1,0:T(4,128)} %bitcast.4, bf16[4,2,1616,128]{3,2,1,0:T(8,128)(2,1)} %get-tuple-element.26.caches, bf16[4,2,128,1616]{3,2,1,0:T(8,128)(2,1)} %get-tuple-element.27.turned_caches, ...), custom_call_target="tpu_custom_call" | custom-call | flops 7554465792 | bytes 8388608 | tf_op jit(solution)/shard_map/attend_2/pallas_call | solution.py:376
  92.9 0.0 collective-permute-done
  92.9 0.0 copy-done.4
  92.9 1.1 add_convert_fusion.1
  94.0 2.6 %collective-permute-start.2 = (bf16[2,1616,128]{2,1,0:T(8,128)(2,1)}, bf16[2,1616,128]{2,1,0:T(8,128)(2,1)S(1)}, u32[]{:S(2)}, u32[]{:S(2)}) collective-permute-start(bf16[2,1616,128]{2,1,0:T(8,128)(2,1)} %add_convert_fusion.1), channel_id=1, source_target_pairs={{0,16},{8,24},{16,0},{24,8},{1,17},{9,25},{17,1},{25,9},{2,18},{10... | collective-permute-start | bytes 2482184 | tf_op jit(solution)/shard_map/ppermute | solution.py:334
  96.7 0.3 collective-permute-start.1
  96.9 0.0 all-to-all-done.1.returned
  96.9 1.3 copy-done
  98.2 10.6 %all-to-all-start.3 = ((bf16[8,2,2,32,1024]{4,3,2,1,0:T(8,128)(2,1)}), bf16[8,2,2,32,1024]{4,3,2,1,0:T(8,128)(2,1)}, u32[]{:S(2)}, u32[]{:S(2)}) async-start(bf16[8,2,2,32,1024]{4,3,2,1,0:T(8,128)(2,1)} %get-tuple-element.35), calls=%async_computation.3 | async-start | bytes 4194304 | tf_op jit(solution)/shard_map/all_to_all | solution.py:424
  108.9 3.0 %collect_0.1 = (bf16[128,4096]{1,0:T(8,128)(2,1)}, bf16[128,4096]{1,0:T(8,128)(2,1)}) custom-call(s32[4,32]{1,0:T(4,128)} %bitcast.5, bf16[8,2,2,32,1024]{4,3,2,1,0:T(8,128)(2,1)} %copy-done), custom_call_target="tpu_custom_call" | custom-call | bytes 4194304 | tf_op jit(solution)/shard_map/collect_0/pallas_call | solution.py:407
  111.8 20.5 %collective-permute-done.2 = bf16[2,1616,128]{2,1,0:T(8,128)(2,1)S(1)} collective-permute-done((bf16[2,1616,128]{2,1,0:T(8,128)(2,1)}, bf16[2,1616,128]{2,1,0:T(8,128)(2,1)S(1)}, u32[]{:S(2)}, u32[]{:S(2)}) %collective-permute-start.2) | collective-permute-done | bytes 827424 | tf_op jit(solution)/shard_map/ppermute | solution.py:334
  132.3 2.2 %collective-permute-done.1 = bf16[2,1616,128]{2,1,0:T(8,128)(2,1)} collective-permute-done((bf16[2,1616,128]{2,1,0:T(8,128)(2,1)}, bf16[2,1616,128]{2,1,0:T(8,128)(2,1)}, u32[]{:S(2)}, u32[]{:S(2)}) %collective-permute-start.1) | collective-permute-done | bytes 827424 | tf_op jit(solution)/shard_map/ppermute | solution.py:334
  134.6 0.0 copy-done.3
  134.6 1.5 %add_convert_fusion = bf16[2,1616,128]{2,1,0:T(8,128)(2,1)S(1)} fusion(bf16[2,1616,128]{2,1,0:T(8,128)(2,1)S(1)} %collective-permute-done.2, bf16[2,1616,128]{2,1,0:T(8,128)(2,1)} %collective-permute-done.1, bf16[2,1616,128]{2,1,0:T(8,128)(2,1)S(1)} %copy-done.3), kind=kLoop, calls=%fused_computation | loop fusion | flops 2482176 | bytes 3309568 | tf_op jit(solution)/shard_map/convert_element_type | solution.py:450
  136.0 0.9 fusion
  137.0 0.0 all-to-all-done.3.returned
  137.0 2.8 %collect_2.1 = (bf16[128,4096]{1,0:T(8,128)(2,1)}, bf16[128,4096]{1,0:T(8,128)(2,1)}) custom-call(s32[4,32]{1,0:T(4,128)} %bitcast.6, bf16[8,2,2,32,1024]{4,3,2,1,0:T(8,128)(2,1)} %all-to-all-done.3.returned, bf16[128,4096]{1,0:T(8,128)(2,1)} %get-tuple-element.37.refs_0_, ...), custom_call_target="tpu_custom_call", output_to_operand_aliasing={{0}: (2, {}), {1}: (3, {})} | custom-call | bytes 4194304 | tf_op jit(solution)/shard_map/collect_2/pallas_call | solution.py:407
  (3 shorter events, 0.0 us)
Async XLA Ops:
  3.5 28.5 %all-to-all-start = ((bf16[8,2,2,32,1024]{4,3,2,1,0:T(8,128)(2,1)}), bf16[8,2,2,32,1024]{4,3,2,1,0:T(8,128)(2,1)S(1)}, u32[]{:S(2)}, u32[]{:S(2)}) async-start(bf16[8,2,2,32,1024]{4,3,2,1,0:T(8,128)(2,1)} %route_0.1), calls=%async_computation | async-start | bytes 4194304 | tf_op jit(solution)/shard_map/all_to_all | solution.py:424
  32.0 1.4 %copy-start.2 = (bf16[8,2,2,32,1024]{4,3,2,1,0:T(8,128)(2,1)}, bf16[8,2,2,32,1024]{4,3,2,1,0:T(8,128)(2,1)S(1)}, u32[]{:S(2)}) copy-start(bf16[8,2,2,32,1024]{4,3,2,1,0:T(8,128)(2,1)S(1)} %all-to-all-done.received) | copy-start | bytes 6291460
  33.4 30.2 %all-to-all-start.2 = ((bf16[8,2,2,32,1024]{4,3,2,1,0:T(8,128)(2,1)}), bf16[8,2,2,32,1024]{4,3,2,1,0:T(8,128)(2,1)S(1)}, u32[]{:S(2)}, u32[]{:S(2)}) async-start(bf16[8,2,2,32,1024]{4,3,2,1,0:T(8,128)(2,1)} %get-tuple-element.31), calls=%async_computation.2 | async-start | bytes 4194304 | tf_op jit(solution)/shard_map/all_to_all | solution.py:424
  63.6 1.4 %copy-start.1 = (bf16[8,2,2,32,1024]{4,3,2,1,0:T(8,128)(2,1)}, bf16[8,2,2,32,1024]{4,3,2,1,0:T(8,128)(2,1)S(1)}, u32[]{:S(2)}) copy-start(bf16[8,2,2,32,1024]{4,3,2,1,0:T(8,128)(2,1)S(1)} %all-to-all-done.2.received) | copy-start | bytes 6291460
  63.6 7.6 %copy-start.5 = (bf16[2,1616,128]{2,1,0:T(8,128)(2,1)S(1)}, bf16[2,1616,128]{2,1,0:T(8,128)(2,1)}, u32[]{:S(2)}) copy-start(bf16[2,1616,128]{2,1,0:T(8,128)(2,1)} %get-tuple-element.42) | copy-start | bytes 2482180
  65.0 31.9 %all-to-all-start.1 = ((bf16[8,2,2,32,1024]{4,3,2,1,0:T(8,128)(2,1)}), bf16[8,2,2,32,1024]{4,3,2,1,0:T(8,128)(2,1)S(1)}, u32[]{:S(2)}, u32[]{:S(2)}) async-start(bf16[8,2,2,32,1024]{4,3,2,1,0:T(8,128)(2,1)} %get-tuple-element.30), calls=%async_computation.1 | async-start | bytes 4194304 | tf_op jit(solution)/shard_map/all_to_all | solution.py:424
  71.2 21.7 %collective-permute-start = (bf16[2,1616,128]{2,1,0:T(8,128)(2,1)S(1)}, bf16[2,1616,128]{2,1,0:T(8,128)(2,1)S(1)}, u32[]{:S(2)}, u32[]{:S(2)}) collective-permute-start(bf16[2,1616,128]{2,1,0:T(8,128)(2,1)S(1)} %copy-done.5), channel_id=1, source_target_pairs={{0,8},{8,0},{16,24},{24,16},{1,9},{9,1},{17,25},{25,17},{2,10},{10... | collective-permute-start | bytes 2482184 | tf_op jit(solution)/shard_map/ppermute | solution.py:334
  72.7 20.2 %copy-start.4 = (bf16[2,1616,128]{2,1,0:T(8,128)(2,1)S(1)}, bf16[2,1616,128]{2,1,0:T(8,128)(2,1)}, u32[]{:S(2)}) copy-start(bf16[2,1616,128]{2,1,0:T(8,128)(2,1)} %get-tuple-element.46) | copy-start | bytes 2482180
  94.0 38.3 %collective-permute-start.2 = (bf16[2,1616,128]{2,1,0:T(8,128)(2,1)}, bf16[2,1616,128]{2,1,0:T(8,128)(2,1)S(1)}, u32[]{:S(2)}, u32[]{:S(2)}) collective-permute-start(bf16[2,1616,128]{2,1,0:T(8,128)(2,1)} %add_convert_fusion.1), channel_id=1, source_target_pairs={{0,16},{8,24},{16,0},{24,8},{1,17},{9,25},{17,1},{25,9},{2,18},{10... | collective-permute-start | bytes 2482184 | tf_op jit(solution)/shard_map/ppermute | solution.py:334
  96.7 37.9 %collective-permute-start.1 = (bf16[2,1616,128]{2,1,0:T(8,128)(2,1)}, bf16[2,1616,128]{2,1,0:T(8,128)(2,1)}, u32[]{:S(2)}, u32[]{:S(2)}) collective-permute-start(bf16[2,1616,128]{2,1,0:T(8,128)(2,1)} %get-tuple-element.45), channel_id=1, source_target_pairs={{0,8},{8,0},{16,24},{24,16},{1,9},{9,1},{17,25},{25,17},{2,10},{10... | collective-permute-start | bytes 2482184 | tf_op jit(solution)/shard_map/ppermute | solution.py:334
  96.9 1.3 copy-start
  98.2 38.7 %all-to-all-start.3 = ((bf16[8,2,2,32,1024]{4,3,2,1,0:T(8,128)(2,1)}), bf16[8,2,2,32,1024]{4,3,2,1,0:T(8,128)(2,1)}, u32[]{:S(2)}, u32[]{:S(2)}) async-start(bf16[8,2,2,32,1024]{4,3,2,1,0:T(8,128)(2,1)} %get-tuple-element.35), calls=%async_computation.3 | async-start | bytes 4194304 | tf_op jit(solution)/shard_map/all_to_all | solution.py:424
  108.9 25.7 %copy-start.3 = (bf16[2,1616,128]{2,1,0:T(8,128)(2,1)S(1)}, bf16[2,1616,128]{2,1,0:T(8,128)(2,1)}, u32[]{:S(2)}) copy-start(bf16[2,1616,128]{2,1,0:T(8,128)(2,1)} %get-tuple-element.41) | copy-start | bytes 2482180

commit v5 on v4

--- a/solution.py
+++ b/solution.py
@@ -152,8 +152,17 @@
 
     kv_copies = [
         [
-            pltpu.make_async_copy(source.at[head_at(turn)], target.at[i], kv_sems.at[i, j])
-            for j, (source, target) in enumerate(((caches, straight), (turned_caches, turned)))
+            pltpu.make_async_copy(
+                source.at[head_at(turn), which], target.at[i, which], kv_sems.at[i, j]
+            )
+            for j, (source, target, which) in enumerate(
+                (
+                    (caches, straight, 0),
+                    (turned_caches, turned, 1),
+                    (caches, straight, 1),
+                    (turned_caches, turned, 0),
+                )
+            )
         ]
         for i, turn in enumerate(turns)
     ]
@@ -171,9 +180,8 @@
     def handing(i):
         return pltpu.make_async_copy(staged.at[i], grads[i], grad_sems.at[i])
 
-    for j in range(2):
-        for copies in kv_copies:
-            copies[j].start()
+    for copies in kv_copies:
+        copies[0].start()
     count = jnp.int32(0)
     for k in range(peers):
         found = is_read(reads, base + k, me)
@@ -185,6 +193,9 @@
                 arriving(i, count, k).start()
 
         count = count + found.astype(jnp.int32)
+    for j in range(1, 4):
+        for copies in kv_copies:
+            copies[j].start()
 
     sums[...] = jnp.zeros_like(sums)
 
@@ -210,10 +221,10 @@
         q_turned = stacked(i, slot, 0).astype(f32).T.astype(bf16)
         tops, totals, outs = [], [], []
 
-        def score(a, b):
-            part = jnp.dot(straight[i, 0, a:b, :], q_turned, preferred_element_type=f32)
-            for c, d in slices(a, b):
-                piece = part[c - a : d - a, :]
+        def score():
+            part = jnp.dot(straight[i, 0], q_turned, preferred_element_type=f32)
+            for c, d in slices(0, padded):
+                piece = part[c:d, :]
                 if d > tokens:
                     token = lax.broadcasted_iota(jnp.int32, piece.shape, 0) + c
                     piece = jnp.where(token < tokens, piece, LOWEST)
@@ -252,10 +263,14 @@
             for c, d in slices(a, b):
                 piece = weights[i, c:d, :].astype(f32) * (dprob[c - a : d - a, :] - delta)
                 dscores[i, c:d, :] = piece.astype(bf16)
-            sums[i, 1, a:b, :] += jnp.dot(weights[i, a:b, :], g, preferred_element_type=f32)
-
-        def keys_part(a, b):
-            sums[i, 0, a:b, :] += jnp.dot(dscores[i, a:b, :], q, preferred_element_type=f32)
+
+        def values_sum():
+            sums[i, 1] += jnp.dot(weights[i], g, preferred_element_type=f32)
+
+        def keys_sum():
+            sums[i, 0] += jnp.dot(dscores[i], q, preferred_element_type=f32)
+
+        def queries_part(a, b):
             turned_dq.append(
                 jnp.dot(turned[i, 0, :, a:b], dscores[i, a:b, :], preferred_element_type=f32)
             )
@@ -263,29 +278,35 @@
         def finish():
             store(i, slot, 1, functools.reduce(jnp.add, turned_dq) * SCALE)
 
-        return values_part, keys_part, finish
+        return values_part, values_sum, keys_sum, queries_part, finish
 
     heads = range(len(turns))
 
-    def one_slot(slot, carry):
-        later = jnp.minimum(slot + 1, count - 1)
-
-        @pl.when(slot + 1 < count)
-        def _():
+    def one_slot(slot, carry, last=False):
+        weights, next_weights = even_odd.at[slot & 1], even_odd.at[(slot + 1) & 1]
+        behind = [backward(i, slot, weights, *carry[i]) for i in heads]
+        ahead = []
+        if not last:
             for i in heads:
-                arriving(i, later, 0).wait()
-
-        weights, next_weights = even_odd.at[slot & 1], even_odd.at[(slot + 1) & 1]
-        ahead = [forward(i, later, next_weights) for i in heads]
-        behind = [backward(i, slot, weights, *carry[i]) for i in heads]
-        for phase in range(2):
-            for a, b in pieces:
-                for i in heads:
-                    ahead[i][phase](a, b)
-                    behind[i][phase](a, b)
-        for i in heads:
-            behind[i][2]()
-        carry = [ahead[i][2]() for i in heads]
+                arriving(i, slot + 1, 0).wait()
+            ahead = [forward(i, slot + 1, next_weights) for i in heads]
+
+        for score, _, _ in ahead:
+            score()
+        for a, b in pieces:
+            for values_part, *_ in behind:
+                values_part(a, b)
+        for _, values_sum, keys_sum, _, _ in behind:
+            values_sum()
+            keys_sum()
+        for a, b in pieces:
+            for _, weigh, _ in ahead:
+                weigh(a, b)
+            for _, _, _, queries_part, _ in behind:
+                queries_part(a, b)
+        for *_, finish in behind:
+            finish()
+        carry = [finish() for _, _, finish in ahead]
         for i in heads:
             leaving(i, slot, owners[slot]).start()
         return carry
@@ -296,14 +317,19 @@
             arriving(i, 0, 0).wait()
             kv_copies[i][0].wait()
         first = [forward(i, 0, even_odd.at[0]) for i in heads]
-        for phase in range(2):
-            if phase == 1:
-                for i in heads:
-                    kv_copies[i][1].wait()
-            for a, b in pieces:
-                for i in heads:
-                    first[i][phase](a, b)
-        lax.fori_loop(0, count, one_slot, [first[i][2]() for i in heads])
+        for score, _, _ in first:
+            score()
+        for i in heads:
+            kv_copies[i][1].wait()
+        for a, b in pieces:
+            for _, weigh, _ in first:
+                weigh(a, b)
+        carry = [finish() for _, _, finish in first]
+        for i in heads:
+            kv_copies[i][2].wait()
+            kv_copies[i][3].wait()
+        carry = lax.fori_loop(0, count - 1, one_slot, carry)
+        one_slot(count - 1, carry, last=True)
         for i in heads:
             staged[i, 0] = (sums[i, 0] * SCALE).astype(bf16)
             staged[i, 1] = sums[i, 1].astype(bf16)
@@ -389,7 +415,7 @@
                 pltpu.VMEM((len(turns), 2, padded, HD), f32),
                 pltpu.VMEM((len(turns), 2, padded, HD), bf16),
                 pltpu.SMEM((slots,), jnp.int32),
-                pltpu.SemaphoreType.DMA((len(turns), 2)),
+                pltpu.SemaphoreType.DMA((len(turns), 4)),
                 pltpu.SemaphoreType.DMA((len(turns), slots)),
                 pltpu.SemaphoreType.DMA((len(turns), slots)),
                 pltpu.SemaphoreType.DMA((len(turns),)),

time: 143 us -> 140 us (0.979)
  the two profiles are of different devices: /device:TPU:6 before, /device:TPU:0 now
where the time goes in v5:
time: 140 us; the launch traced here: 138 us
  waiting for transfers between devices  62.2 us (44%)
  Pallas kernels  42.8 us (31%)
  starting transfers between devices  24 us (17%)
  local copies, waits for them, and re-layouts  5.08 us (4%)
  other arithmetic  2.59 us (2%)
    all_to_all x4, waiting for transfers between devices, exchange(): return lax.all_to_all(array, 'enc', split_axis=0, concat_axis=0, tiled=True)  32.9 us
    ppermute x3, waiting for transfers between devices, xor_permute(): return lax.ppermute(array, axis, [(i, i ^ k) for i in range(size)])  29.4 us
    pallas_call x2, Pallas kernels, attend(): pl.pallas_call(functools.partial(attend_kernel, turns, peers, seg_rows, t...  27.1 us
    all_to_all x4, starting transfers between devices, exchange(): return lax.all_to_all(array, 'enc', split_axis=0, concat_axis=0, tiled=True)  17.8 us
    pallas_call x2, Pallas kernels, route(): pl.pallas_call(functools.partial(route_kernel, turns, n_seg, seg_rows, to...  9.91 us
    ppermute x3, starting transfers between devices, xor_permute(): return lax.ppermute(array, axis, [(i, i ^ k) for i in range(size)])  6.21 us
    pallas_call x2, Pallas kernels, collect(): pl.pallas_call(functools.partial(collect_kernel, turns, n_seg, seg_rows),...  5.77 us
    unnamed x12, local copies, waits for them, and re-layouts  4.14 us
  transfers between devices with their start and end apart: 7, of which 5 were waited for; matrix products, arithmetic and copies ran while one was open for 3% of the time, Pallas kernels for 27%

profile of v5, /device:TPU:0, one launch (start us, length us, event | category | flops | bytes accessed | tf_op | source)
XLA Modules:
  0.0 137.6 jit_solution(2234338048683792223)
XLA Ops:
  0.6 2.9 %route_0.1 = bf16[8,2,2,32,1024]{4,3,2,1,0:T(8,128)(2,1)} custom-call(s32[4,32]{1,0:T(4,128)} %bitcast.1, bf16[128,4096]{1,0:T(8,128)(2,1)} %q_hbm.3, bf16[128,4096]{1,0:T(8,128)(2,1)} %g_hbm.3), custom_call_target="tpu_custom_call" | custom-call | bytes 2097152 | tf_op jit(solution)/shard_map/route_0/pallas_call | solution.py:383
  3.5 5.2 %all-to-all-start = ((bf16[8,2,2,32,1024]{4,3,2,1,0:T(8,128)(2,1)}), bf16[8,2,2,32,1024]{4,3,2,1,0:T(8,128)(2,1)S(1)}, u32[]{:S(2)}, u32[]{:S(2)}) async-start(bf16[8,2,2,32,1024]{4,3,2,1,0:T(8,128)(2,1)} %route_0.1), calls=%async_computation | async-start | bytes 4194304 | tf_op jit(solution)/shard_map/all_to_all | solution.py:450
  8.7 7.1 %route_2.1 = (bf16[8,2,2,32,1024]{4,3,2,1,0:T(8,128)(2,1)}, bf16[4,2,1616,128]{3,2,1,0:T(8,128)(2,1)}, bf16[4,2,128,1616]{3,2,1,0:T(8,128)(2,1)}) custom-call(s32[4,32]{1,0:T(4,128)} %bitcast.2, bf16[128,4096]{1,0:T(8,128)(2,1)} %q_hbm.3, bf16[128,4096]{1,0:T(8,128)(2,1)} %g_hbm.3, bf16[1,1601,512]{2,1,0:T(8,128)(2,1)} %refs_0_.1, bf16[1,1601,512]{2,1,0:T(8,128)(2,1)} %refs_1_.1), custom_call_target="tpu_custom_call" | custom-call | bytes 12582912 | tf_op jit(solution)/shard_map/route_2/pallas_call | solution.py:383
  15.8 19.6 %all-to-all-done.received = bf16[8,2,2,32,1024]{4,3,2,1,0:T(8,128)(2,1)S(1)} async-done(((bf16[8,2,2,32,1024]{4,3,2,1,0:T(8,128)(2,1)}), bf16[8,2,2,32,1024]{4,3,2,1,0:T(8,128)(2,1)S(1)}, u32[]{:S(2)}, u32[]{:S(2)}) %all-to-all-start) | async-done | bytes 2097184 | tf_op jit(solution)/shard_map/all_to_all | solution.py:450
  35.4 0.0 copy-start.2
  35.4 1.4 %copy-done.2 = bf16[8,2,2,32,1024]{4,3,2,1,0:T(8,128)(2,1)} copy-done((bf16[8,2,2,32,1024]{4,3,2,1,0:T(8,128)(2,1)}, bf16[8,2,2,32,1024]{4,3,2,1,0:T(8,128)(2,1)S(1)}, u32[]{:S(2)}) %copy-start.2) | copy-done | bytes 2097176
  36.8 3.6 %all-to-all-start.2 = ((bf16[8,2,2,32,1024]{4,3,2,1,0:T(8,128)(2,1)}), bf16[8,2,2,32,1024]{4,3,2,1,0:T(8,128)(2,1)S(1)}, u32[]{:S(2)}, u32[]{:S(2)}) async-start(bf16[8,2,2,32,1024]{4,3,2,1,0:T(8,128)(2,1)} %get-tuple-element.31), calls=%async_computation.2 | async-start | bytes 4194304 | tf_op jit(solution)/shard_map/all_to_all | solution.py:450
  40.4 13.4 %attend_0.1 = (bf16[8,2,2,32,1024]{4,3,2,1,0:T(8,128)(2,1)}, bf16[2,1616,128]{2,1,0:T(8,128)(2,1)}, bf16[2,1616,128]{2,1,0:T(8,128)(2,1)}) custom-call(s32[4,32]{1,0:T(4,128)} %bitcast.3, bf16[4,2,1616,128]{3,2,1,0:T(8,128)(2,1)} %get-tuple-element.26.caches, bf16[4,2,128,1616]{3,2,1,0:T(8,128)(2,1)} %get-tuple-element.27.turned_caches, ...), custom_call_target="tpu_custom_call" | custom-call | flops 7554465792 | bytes 8388608 | tf_op jit(solution)/shard_map/attend_0/pallas_call | solution.py:402
  53.8 13.2 %all-to-all-done.2.received = bf16[8,2,2,32,1024]{4,3,2,1,0:T(8,128)(2,1)S(1)} async-done(((bf16[8,2,2,32,1024]{4,3,2,1,0:T(8,128)(2,1)}), bf16[8,2,2,32,1024]{4,3,2,1,0:T(8,128)(2,1)S(1)}, u32[]{:S(2)}, u32[]{:S(2)}) %all-to-all-start.2) | async-done | bytes 2097184 | tf_op jit(solution)/shard_map/all_to_all | solution.py:450
  67.0 0.0 copy-start.1
  67.0 0.0 copy-start.5
  67.0 1.4 %copy-done.1 = bf16[8,2,2,32,1024]{4,3,2,1,0:T(8,128)(2,1)} copy-done((bf16[8,2,2,32,1024]{4,3,2,1,0:T(8,128)(2,1)}, bf16[8,2,2,32,1024]{4,3,2,1,0:T(8,128)(2,1)S(1)}, u32[]{:S(2)}) %copy-start.1) | copy-done | bytes 2097176
  68.4 3.6 %all-to-all-start.1 = ((bf16[8,2,2,32,1024]{4,3,2,1,0:T(8,128)(2,1)}), bf16[8,2,2,32,1024]{4,3,2,1,0:T(8,128)(2,1)S(1)}, u32[]{:S(2)}, u32[]{:S(2)}) async-start(bf16[8,2,2,32,1024]{4,3,2,1,0:T(8,128)(2,1)} %get-tuple-element.30), calls=%async_computation.1 | async-start | bytes 4194304 | tf_op jit(solution)/shard_map/all_to_all | solution.py:450
  72.0 0.0 copy-done.5
  72.0 1.6 %collective-permute-start = (bf16[2,1616,128]{2,1,0:T(8,128)(2,1)S(1)}, bf16[2,1616,128]{2,1,0:T(8,128)(2,1)S(1)}, u32[]{:S(2)}, u32[]{:S(2)}) collective-permute-start(bf16[2,1616,128]{2,1,0:T(8,128)(2,1)S(1)} %copy-done.5), channel_id=1, source_target_pairs={{0,8},{8,0},{16,24},{24,16},{1,9},{9,1},{17,25},{25,17},{2,10},{10... | collective-permute-start | bytes 2482184 | tf_op jit(solution)/shard_map/ppermute | solution.py:360
  73.6 13.7 %attend_2.1 = (bf16[8,2,2,32,1024]{4,3,2,1,0:T(8,128)(2,1)}, bf16[2,1616,128]{2,1,0:T(8,128)(2,1)}, bf16[2,1616,128]{2,1,0:T(8,128)(2,1)}) custom-call(s32[4,32]{1,0:T(4,128)} %bitcast.4, bf16[4,2,1616,128]{3,2,1,0:T(8,128)(2,1)} %get-tuple-element.26.caches, bf16[4,2,128,1616]{3,2,1,0:T(8,128)(2,1)} %get-tuple-element.27.turned_caches, ...), custom_call_target="tpu_custom_call" | custom-call | flops 7554465792 | bytes 8388608 | tf_op jit(solution)/shard_map/attend_2/pallas_call | solution.py:402
  87.3 5.4 %collective-permute-done = bf16[2,1616,128]{2,1,0:T(8,128)(2,1)S(1)} collective-permute-done((bf16[2,1616,128]{2,1,0:T(8,128)(2,1)S(1)}, bf16[2,1616,128]{2,1,0:T(8,128)(2,1)S(1)}, u32[]{:S(2)}, u32[]{:S(2)}) %collective-permute-start) | collective-permute-done | bytes 827424 | tf_op jit(solution)/shard_map/ppermute | solution.py:360
  92.7 0.0 copy-done.4
  92.7 1.1 add_convert_fusion.1
  93.8 2.5 %collective-permute-start.2 = (bf16[2,1616,128]{2,1,0:T(8,128)(2,1)}, bf16[2,1616,128]{2,1,0:T(8,128)(2,1)S(1)}, u32[]{:S(2)}, u32[]{:S(2)}) collective-permute-start(bf16[2,1616,128]{2,1,0:T(8,128)(2,1)} %add_convert_fusion.1), channel_id=1, source_target_pairs={{0,16},{8,24},{16,0},{24,8},{1,17},{9,25},{17,1},{25,9},{2,18},{10... | collective-permute-start | bytes 2482184 | tf_op jit(solution)/shard_map/ppermute | solution.py:360
  96.4 2.1 %collective-permute-start.1 = (bf16[2,1616,128]{2,1,0:T(8,128)(2,1)}, bf16[2,1616,128]{2,1,0:T(8,128)(2,1)}, u32[]{:S(2)}, u32[]{:S(2)}) collective-permute-start(bf16[2,1616,128]{2,1,0:T(8,128)(2,1)} %get-tuple-element.45), channel_id=1, source_target_pairs={{0,8},{8,0},{16,24},{24,16},{1,9},{9,1},{17,25},{25,17},{2,10},{10... | collective-permute-start | bytes 2482184 | tf_op jit(solution)/shard_map/ppermute | solution.py:360
  98.5 0.1 all-to-all-done.1.returned
  98.6 1.3 copy-done
  99.9 5.4 %all-to-all-start.3 = ((bf16[8,2,2,32,1024]{4,3,2,1,0:T(8,128)(2,1)}), bf16[8,2,2,32,1024]{4,3,2,1,0:T(8,128)(2,1)}, u32[]{:S(2)}, u32[]{:S(2)}) async-start(bf16[8,2,2,32,1024]{4,3,2,1,0:T(8,128)(2,1)} %get-tuple-element.35), calls=%async_computation.3 | async-start | bytes 4194304 | tf_op jit(solution)/shard_map/all_to_all | solution.py:450
  105.3 3.0 %collect_0.1 = (bf16[128,4096]{1,0:T(8,128)(2,1)}, bf16[128,4096]{1,0:T(8,128)(2,1)}) custom-call(s32[4,32]{1,0:T(4,128)} %bitcast.5, bf16[8,2,2,32,1024]{4,3,2,1,0:T(8,128)(2,1)} %copy-done), custom_call_target="tpu_custom_call" | custom-call | bytes 4194304 | tf_op jit(solution)/shard_map/collect_0/pallas_call | solution.py:433
  108.2 24.0 %collective-permute-done.2 = bf16[2,1616,128]{2,1,0:T(8,128)(2,1)S(1)} collective-permute-done((bf16[2,1616,128]{2,1,0:T(8,128)(2,1)}, bf16[2,1616,128]{2,1,0:T(8,128)(2,1)S(1)}, u32[]{:S(2)}, u32[]{:S(2)}) %collective-permute-start.2) | collective-permute-done | bytes 827424 | tf_op jit(solution)/shard_map/ppermute | solution.py:360
  132.2 0.0 collective-permute-done.1
  132.2 0.0 copy-done.3
  132.2 1.5 %add_convert_fusion = bf16[2,1616,128]{2,1,0:T(8,128)(2,1)S(1)} fusion(bf16[2,1616,128]{2,1,0:T(8,128)(2,1)S(1)} %collective-permute-done.2, bf16[2,1616,128]{2,1,0:T(8,128)(2,1)} %collective-permute-done.1, bf16[2,1616,128]{2,1,0:T(8,128)(2,1)S(1)} %copy-done.3), kind=kLoop, calls=%fused_computation | loop fusion | flops 2482176 | bytes 3309568 | tf_op jit(solution)/shard_map/convert_element_type | solution.py:476
  133.7 0.9 fusion
  134.6 0.0 all-to-all-done.3.returned
  134.6 2.8 %collect_2.1 = (bf16[128,4096]{1,0:T(8,128)(2,1)}, bf16[128,4096]{1,0:T(8,128)(2,1)}) custom-call(s32[4,32]{1,0:T(4,128)} %bitcast.6, bf16[8,2,2,32,1024]{4,3,2,1,0:T(8,128)(2,1)} %all-to-all-done.3.returned, bf16[128,4096]{1,0:T(8,128)(2,1)} %get-tuple-element.37.refs_0_, ...), custom_call_target="tpu_custom_call", output_to_operand_aliasing={{0}: (2, {}), {1}: (3, {})} | custom-call | bytes 4194304 | tf_op jit(solution)/shard_map/collect_2/pallas_call | solution.py:433
  (3 shorter events, 0.0 us)
Async XLA Ops:
  3.5 31.9 %all-to-all-start = ((bf16[8,2,2,32,1024]{4,3,2,1,0:T(8,128)(2,1)}), bf16[8,2,2,32,1024]{4,3,2,1,0:T(8,128)(2,1)S(1)}, u32[]{:S(2)}, u32[]{:S(2)}) async-start(bf16[8,2,2,32,1024]{4,3,2,1,0:T(8,128)(2,1)} %route_0.1), calls=%async_computation | async-start | bytes 4194304 | tf_op jit(solution)/shard_map/all_to_all | solution.py:450
  35.4 1.4 %copy-start.2 = (bf16[8,2,2,32,1024]{4,3,2,1,0:T(8,128)(2,1)}, bf16[8,2,2,32,1024]{4,3,2,1,0:T(8,128)(2,1)S(1)}, u32[]{:S(2)}) copy-start(bf16[8,2,2,32,1024]{4,3,2,1,0:T(8,128)(2,1)S(1)} %all-to-all-done.received) | copy-start | bytes 6291460
  36.8 30.2 %all-to-all-start.2 = ((bf16[8,2,2,32,1024]{4,3,2,1,0:T(8,128)(2,1)}), bf16[8,2,2,32,1024]{4,3,2,1,0:T(8,128)(2,1)S(1)}, u32[]{:S(2)}, u32[]{:S(2)}) async-start(bf16[8,2,2,32,1024]{4,3,2,1,0:T(8,128)(2,1)} %get-tuple-element.31), calls=%async_computation.2 | async-start | bytes 4194304 | tf_op jit(solution)/shard_map/all_to_all | solution.py:450
  67.0 1.4 %copy-start.1 = (bf16[8,2,2,32,1024]{4,3,2,1,0:T(8,128)(2,1)}, bf16[8,2,2,32,1024]{4,3,2,1,0:T(8,128)(2,1)S(1)}, u32[]{:S(2)}) copy-start(bf16[8,2,2,32,1024]{4,3,2,1,0:T(8,128)(2,1)S(1)} %all-to-all-done.2.received) | copy-start | bytes 6291460
  67.0 5.0 %copy-start.5 = (bf16[2,1616,128]{2,1,0:T(8,128)(2,1)S(1)}, bf16[2,1616,128]{2,1,0:T(8,128)(2,1)}, u32[]{:S(2)}) copy-start(bf16[2,1616,128]{2,1,0:T(8,128)(2,1)} %get-tuple-element.42) | copy-start | bytes 2482180
  68.4 30.2 %all-to-all-start.1 = ((bf16[8,2,2,32,1024]{4,3,2,1,0:T(8,128)(2,1)}), bf16[8,2,2,32,1024]{4,3,2,1,0:T(8,128)(2,1)S(1)}, u32[]{:S(2)}, u32[]{:S(2)}) async-start(bf16[8,2,2,32,1024]{4,3,2,1,0:T(8,128)(2,1)} %get-tuple-element.30), calls=%async_computation.1 | async-start | bytes 4194304 | tf_op jit(solution)/shard_map/all_to_all | solution.py:450
  72.0 20.7 %collective-permute-start = (bf16[2,1616,128]{2,1,0:T(8,128)(2,1)S(1)}, bf16[2,1616,128]{2,1,0:T(8,128)(2,1)S(1)}, u32[]{:S(2)}, u32[]{:S(2)}) collective-permute-start(bf16[2,1616,128]{2,1,0:T(8,128)(2,1)S(1)} %copy-done.5), channel_id=1, source_target_pairs={{0,8},{8,0},{16,24},{24,16},{1,9},{9,1},{17,25},{25,17},{2,10},{10... | collective-permute-start | bytes 2482184 | tf_op jit(solution)/shard_map/ppermute | solution.py:360
  73.6 19.1 %copy-start.4 = (bf16[2,1616,128]{2,1,0:T(8,128)(2,1)S(1)}, bf16[2,1616,128]{2,1,0:T(8,128)(2,1)}, u32[]{:S(2)}) copy-start(bf16[2,1616,128]{2,1,0:T(8,128)(2,1)} %get-tuple-element.46) | copy-start | bytes 2482180
  93.8 38.3 %collective-permute-start.2 = (bf16[2,1616,128]{2,1,0:T(8,128)(2,1)}, bf16[2,1616,128]{2,1,0:T(8,128)(2,1)S(1)}, u32[]{:S(2)}, u32[]{:S(2)}) collective-permute-start(bf16[2,1616,128]{2,1,0:T(8,128)(2,1)} %add_convert_fusion.1), channel_id=1, source_target_pairs={{0,16},{8,24},{16,0},{24,8},{1,17},{9,25},{17,1},{25,9},{2,18},{10... | collective-permute-start | bytes 2482184 | tf_op jit(solution)/shard_map/ppermute | solution.py:360
  96.4 35.8 %collective-permute-start.1 = (bf16[2,1616,128]{2,1,0:T(8,128)(2,1)}, bf16[2,1616,128]{2,1,0:T(8,128)(2,1)}, u32[]{:S(2)}, u32[]{:S(2)}) collective-permute-start(bf16[2,1616,128]{2,1,0:T(8,128)(2,1)} %get-tuple-element.45), channel_id=1, source_target_pairs={{0,8},{8,0},{16,24},{24,16},{1,9},{9,1},{17,25},{25,17},{2,10},{10... | collective-permute-start | bytes 2482184 | tf_op jit(solution)/shard_map/ppermute | solution.py:360
  98.6 1.3 copy-start
  99.9 34.7 %all-to-all-start.3 = ((bf16[8,2,2,32,1024]{4,3,2,1,0:T(8,128)(2,1)}), bf16[8,2,2,32,1024]{4,3,2,1,0:T(8,128)(2,1)}, u32[]{:S(2)}, u32[]{:S(2)}) async-start(bf16[8,2,2,32,1024]{4,3,2,1,0:T(8,128)(2,1)} %get-tuple-element.35), calls=%async_computation.3 | async-start | bytes 4194304 | tf_op jit(solution)/shard_map/all_to_all | solution.py:450
  105.3 26.9 %copy-start.3 = (bf16[2,1616,128]{2,1,0:T(8,128)(2,1)S(1)}, bf16[2,1616,128]{2,1,0:T(8,128)(2,1)}, u32[]{:S(2)}) copy-start(bf16[2,1616,128]{2,1,0:T(8,128)(2,1)} %get-tuple-element.41) | copy-start | bytes 2482180

commit v6 on v5

--- a/solution.py
+++ b/solution.py
@@ -18,11 +18,10 @@
 SLICE = 128
 LOWEST = -3.0e38
 PER_CHUNK = 2
-VMEM_BYTES = 58 << 20
+VMEM_BYTES = 54 << 20
 ANY = pl.BlockSpec(memory_space=pl.ANY)
 SMEM = pl.BlockSpec(memory_space=pltpu.SMEM)
 VMEM = pl.BlockSpec(memory_space=pltpu.VMEM)
-HBM = pl.BlockSpec(memory_space=pltpu.HBM)
 
 
 def head_at(turn):
@@ -32,11 +31,10 @@
 
 
 def route_kernel(turns, n_seg, seg_rows, tokens, reads, q_hbm, g_hbm, *refs):
-    caches, (out, *prepared, stage, in_sems, out_sems) = refs[:-6], refs[-6:]
-    if not caches:
-        out, stage, in_sems, out_sems = refs
-        prepared = ()
-    row = lax.axis_index("seq") * lax.axis_size("enc") + lax.axis_index("enc")
+    stage, in_sems, out_sems = refs[-3:]
+    apart = len(refs) > 8
+    me = lax.axis_index("enc")
+    row = lax.axis_index("seq") * lax.axis_size("enc") + me
     arriving = [[] for _ in range(n_seg)]
     for r in range(n_seg):
         rows = slice(r * seg_rows, (r + 1) * seg_rows)
@@ -50,21 +48,30 @@
                         in_sems.at[r, i, which],
                     )
                 )
-    leaving = [
-        pltpu.make_async_copy(stage.at[r], out.at[reads[r, row]], out_sems.at[r])
-        for r in range(n_seg)
-    ]
+
+    def leaving(r, target):
+        return pltpu.make_async_copy(stage.at[r], target, out_sems.at[r])
+
     for copies in arriving:
         for copy in copies:
             copy.start()
     for r, copies in enumerate(arriving):
         for copy in copies:
             copy.wait()
-        leaving[r].start()
-    if caches:
-        prepare(tokens, *caches, *prepared)
-    for copy in leaving:
-        copy.wait()
+        if apart:
+            for k, out in enumerate(refs[:-3]):
+
+                @pl.when(reads[r, row] == me ^ k)
+                def _():
+                    leaving(r, out).start()
+
+        else:
+            leaving(r, refs[2].at[reads[r, row]]).start()
+    if not apart:
+        k_in, v_in, _, straight, turned = refs[:5]
+        prepare(tokens, k_in, v_in, straight, turned)
+    for r in range(n_seg):
+        leaving(r, refs[0] if apart else refs[2].at[0]).wait()
 
 
 def collect_kernel(turns, n_seg, seg_rows, reads, returned, *refs):
@@ -124,7 +131,8 @@
             )
 
 
-def attend_kernel(turns, peers, seg_rows, tokens, reads, caches, turned_caches, received, *refs):
+def attend_kernel(turns, peers, seg_rows, tokens, reads, caches, turned_caches, *refs):
+    received, refs = refs[: len(refs) - 15 - len(turns)], refs[len(refs) - 15 - len(turns) :]
     returned, grads = refs[0], refs[1 : 1 + len(turns)]
     (
         straight,
@@ -167,10 +175,9 @@
         for i, turn in enumerate(turns)
     ]
 
-    def arriving(i, slot, owner):
-        return pltpu.make_async_copy(
-            received.at[owner, i], inbox.at[i, slot], in_sems.at[i, slot]
-        )
+    def arriving(i, slot, k):
+        source = received[k] if len(received) > 1 else received[0].at[me ^ k]
+        return pltpu.make_async_copy(source.at[i], inbox.at[i, slot], in_sems.at[i, slot])
 
     def leaving(i, slot, owner):
         return pltpu.make_async_copy(
@@ -184,11 +191,11 @@
         copies[0].start()
     count = jnp.int32(0)
     for k in range(peers):
-        found = is_read(reads, base + k, me)
+        found = is_read(reads, base + (me ^ k), me)
 
         @pl.when(found)
         def _():
-            owners[count] = jnp.int32(k)
+            owners[count] = me ^ k
             for i in range(len(turns)):
                 arriving(i, count, k).start()
 
@@ -373,6 +380,7 @@
     bf16, f32 = jnp.bfloat16, jnp.float32
     chunks = [tuple(range(i, i + PER_CHUNK)) for i in range(0, KVH, PER_CHUNK)]
     message = jax.ShapeDtypeStruct((peers, PER_CHUNK, 2, seg_rows, WIDTH), bf16)
+    part = jax.ShapeDtypeStruct((PER_CHUNK, 2, seg_rows, WIDTH), bf16)
 
     caches = [
         jax.ShapeDtypeStruct((KVH, 2, padded, HD), bf16),
@@ -380,11 +388,12 @@
     ]
 
     def route(turns, prepares):
+        outputs = [message] + caches if prepares else [part] * peers
         return pl.pallas_call(
             functools.partial(route_kernel, turns, n_seg, seg_rows, tokens),
-            out_shape=[message] + caches * prepares,
-            in_specs=[SMEM, HBM, HBM] + [VMEM] * 2 * prepares,
-            out_specs=[ANY] + [VMEM] * 2 * prepares,
+            out_shape=outputs,
+            in_specs=[SMEM, ANY, ANY] + [VMEM] * 2 * prepares,
+            out_specs=[ANY, VMEM, VMEM] if prepares else [ANY] * peers,
             scratch_shapes=[
                 pltpu.VMEM((n_seg, PER_CHUNK, 2, seg_rows, WIDTH), bf16),
                 pltpu.SemaphoreType.DMA((n_seg, PER_CHUNK, 2)),
@@ -402,7 +411,7 @@
         results = pl.pallas_call(
             functools.partial(attend_kernel, turns, peers, seg_rows, tokens),
             out_shape=[message] + [jax.ShapeDtypeStruct((2, padded, HD), bf16)] * len(turns),
-            in_specs=[SMEM] + [ANY] * 3,
+            in_specs=[SMEM] + [ANY] * (2 + len(received)),
             out_specs=[ANY] * (1 + len(turns)),
             scratch_shapes=[
                 pltpu.VMEM((len(turns), 2, padded, HD), bf16),
@@ -425,7 +434,7 @@
                 flops=12 * work, bytes_accessed=8 << 20, transcendentals=slots * lanes * tokens
             ),
             name=f"attend_{turns[0]}",
-        )(by_segment, *prepared, received)
+        )(by_segment, *prepared, *received)
         return results[0], list(results[1:])
 
     def collect(turns, returned, before):
@@ -450,31 +459,28 @@
         return lax.all_to_all(array, "enc", split_axis=0, concat_axis=0, tiled=True)
 
     first, second = chunks
-    routed, = route(first, 0)
-    received = exchange(routed)
+    received = [xor_permute(array, "enc", k) for k, array in enumerate(route(first, 0))]
     routed, *prepared = route(second, 1)
-    received, routed = lax.optimization_barrier((received, routed))
+    *received, routed = lax.optimization_barrier((*received, routed))
     received_later = exchange(routed)
     returned, grads = attend(first, received)
     answer = exchange(returned)
-    passed = xor_permute(grads[0], "seq", 1)
+    if n_seq == KVH:
+        far = [xor_permute(grads[0], "seq", 3), xor_permute(grads[1], "seq", 2)]
     received_later, grads[1] = lax.optimization_barrier((received_later, grads[1]))
-    returned, more = attend(second, received_later)
-    grads += more
+    returned, more = attend(second, [received_later])
     answer, returned = lax.optimization_barrier((answer, returned))
     answer_later = exchange(returned)
     if n_seq == KVH:
-        passed, grads[1], grads[2] = lax.optimization_barrier((passed, grads[1], grads[2]))
-        pair = (grads[1].astype(f32) + passed.astype(f32)).astype(bf16)
-        pair = xor_permute(pair, "seq", 2)
-        near = xor_permute(grads[2], "seq", 1)
+        near = xor_permute(more[0], "seq", 1)
     half = collect(first, answer, [])
     attended, grad_queries = collect(second, answer_later, half)
 
     if n_seq == KVH:
-        total = grads[3].astype(f32) + near.astype(f32) + pair.astype(f32)
+        total = more[1].astype(f32) + near.astype(f32) + far[0].astype(f32) + far[1].astype(f32)
         total = total.astype(bf16)[:, :tokens]
         return attended, grad_queries, total[0][None], total[1][None]
+    grads += more
     joined = jnp.concatenate(grads, axis=2)[:, :tokens]
     summed = lax.psum_scatter(joined, "seq", scatter_dimension=2, tiled=True)
     return attended, grad_queries, summed[0][None], summed[1][None]

time: 140 us -> 151 us (1.079); the launches traced: 138 us -> 150 us
  waiting for transfers between devices: 62.2 us -> 79.5 us
  Pallas kernels: 42.8 us -> 35.8 us
  starting transfers between devices: 24 us -> 26.5 us
    ppermute x3 -> x10, waiting for transfers between devices: 29.4 us -> 51 us  [xor_permute(): return lax.ppermute(array, axis, [(i, i ^ k) for i in range(size)])]
    ppermute x3 -> x10, starting transfers between devices: 6.21 us -> 13.7 us  [xor_permute(): return lax.ppermute(array, axis, [(i, i ^ k) for i in range(size)])]
    pallas_call x2, Pallas kernels: 27.1 us -> 20.2 us  [attend(): pl.pallas_call(functools.partial(attend_kernel, turns, peers, seg_rows, t...]
    all_to_all x4 -> x3, starting transfers between devices: 17.8 us -> 12.8 us  [exchange(): return lax.all_to_all(array, 'enc', split_axis=0, concat_axis=0, tiled=True)]
    all_to_all x4 -> x3, waiting for transfers between devices: 32.9 us -> 28.6 us  [exchange(): return lax.all_to_all(array, 'enc', split_axis=0, concat_axis=0, tiled=True)]
    unnamed x12 -> x18, local copies, waits for them, and re-layouts: 4.14 us -> 4.8 us
  transfers between devices with their start and end apart: 7 -> 13, of which waited for: 5 -> 5; matrix products, arithmetic and copies ran while one was open for 3% -> 2% of each run, Pallas kernels for 27% -> 20%
where the time goes in v6:
time: 151 us; the launch traced here: 150 us
  waiting for transfers between devices  79.5 us (53%)
  Pallas kernels  35.8 us (24%)
  starting transfers between devices  26.5 us (18%)
  local copies, waits for them, and re-layouts  5.74 us (4%)
  other arithmetic  1.83 us (1%)
    ppermute x10, waiting for transfers between devices, xor_permute(): return lax.ppermute(array, axis, [(i, i ^ k) for i in range(size)])  51 us
    all_to_all x3, waiting for transfers between devices, exchange(): return lax.all_to_all(array, 'enc', split_axis=0, concat_axis=0, tiled=True)  28.6 us
    pallas_call x2, Pallas kernels, attend(): pl.pallas_call(functools.partial(attend_kernel, turns, peers, seg_rows, t...  20.2 us
    ppermute x10, starting transfers between devices, xor_permute(): return lax.ppermute(array, axis, [(i, i ^ k) for i in range(size)])  13.7 us
    all_to_all x3, starting transfers between devices, exchange(): return lax.all_to_all(array, 'enc', split_axis=0, concat_axis=0, tiled=True)  12.8 us
    pallas_call x2, Pallas kernels, route(): pl.pallas_call(functools.partial(route_kernel, turns, n_seg, seg_rows, to...  9.88 us
    pallas_call x2, Pallas kernels, collect(): pl.pallas_call(functools.partial(collect_kernel, turns, n_seg, seg_rows),...  5.77 us
    unnamed x18, local copies, waits for them, and re-layouts  4.8 us
  transfers between devices with their start and end apart: 13, of which 5 were waited for; matrix products, arithmetic and copies ran while one was open for 2% of the time, Pallas kernels for 20%

profile of v6, /device:TPU:0, one launch (start us, length us, event | category | flops | bytes accessed | tf_op | source)
XLA Modules:
  0.0 150.4 jit_solution(13122571310481806766)
XLA Ops:
  0.6 2.8 %route_0.1 = (bf16[2,2,32,1024]{3,2,1,0:T(8,128)(2,1)}, bf16[2,2,32,1024]{3,2,1,0:T(8,128)(2,1)}, bf16[2,2,32,1024]{3,2,1,0:T(8,128)(2,1)}, bf16[2,2,32,1024]{3,...) custom-call(s32[4,32]{1,0:T(4,128)} %bitcast.1, ...), custom_call_target="tpu_custom_call" | custom-call | bytes 2097152 | tf_op jit(solution)/shard_map/route_0/pallas_call | solution.py:392
  3.5 0.5 collective-permute-start
  4.0 2.6 %collective-permute-start.1 = (bf16[2,2,32,1024]{3,2,1,0:T(8,128)(2,1)}, bf16[2,2,32,1024]{3,2,1,0:T(8,128)(2,1)S(1)}, u32[]{:S(2)}, u32[]{:S(2)}) collective-permute-start(bf16[2,2,32,1024]{3,2,1,0:T(8,128)(2,1)} %get-tuple-element.41), channel_id=1, source_target_pairs={{0,2},{1,3},{2,0},{3,1},{4,6},{5,7},{6,4},{7,5},{8,10},{9,11},{10,... | collective-permute-start | bytes 786440 | tf_op jit(solution)/shard_map/ppermute | solution.py:367
  6.5 0.1 collective-permute-start.2
  6.6 1.8 %collective-permute-start.3 = (bf16[2,2,32,1024]{3,2,1,0:T(8,128)(2,1)}, bf16[2,2,32,1024]{3,2,1,0:T(8,128)(2,1)S(1)}, u32[]{:S(2)}, u32[]{:S(2)}) collective-permute-start(bf16[2,2,32,1024]{3,2,1,0:T(8,128)(2,1)} %get-tuple-element.43), channel_id=1, source_target_pairs={{0,4},{1,5},{2,6},{3,7},{4,0},{5,1},{6,2},{7,3},{8,12},{9,13},{10,... | collective-permute-start | bytes 786440 | tf_op jit(solution)/shard_map/ppermute | solution.py:367
  8.4 0.0 collective-permute-start.4
  8.4 0.0 collective-permute-done.refs_1_
  8.4 2.6 %collective-permute-start.5 = (bf16[2,2,32,1024]{3,2,1,0:T(8,128)(2,1)}, bf16[2,2,32,1024]{3,2,1,0:T(8,128)(2,1)}, u32[]{:S(2)}, u32[]{:S(2)}) collective-permute-start(bf16[2,2,32,1024]{3,2,1,0:T(8,128)(2,1)} %get-tuple-element.45), channel_id=1, source_target_pairs={{0,6},{1,7},{2,4},{3,5},{4,2},{5,3},{6,0},{7,1},{8,14},{9,15},{10,... | collective-permute-start | bytes 786440 | tf_op jit(solution)/shard_map/ppermute | solution.py:367
  11.0 2.9 %collective-permute-done.1.refs_2_ = bf16[2,2,32,1024]{3,2,1,0:T(8,128)(2,1)S(1)} collective-permute-done((bf16[2,2,32,1024]{3,2,1,0:T(8,128)(2,1)}, bf16[2,2,32,1024]{3,2,1,0:T(8,128)(2,1)S(1)}, u32[]{:S(2)}, u32[]{:S(2)}) %collective-permute-start.1) | collective-permute-done | bytes 262176 | tf_op jit(solution)/shard_map/ppermute | solution.py:367
  13.9 1.7 %collective-permute-start.6 = (bf16[2,2,32,1024]{3,2,1,0:T(8,128)(2,1)}, bf16[2,2,32,1024]{3,2,1,0:T(8,128)(2,1)}, u32[]{:S(2)}, u32[]{:S(2)}) collective-permute-start(bf16[2,2,32,1024]{3,2,1,0:T(8,128)(2,1)} %get-tuple-element.46), channel_id=1, source_target_pairs={{0,7},{1,6},{2,5},{3,4},{4,3},{5,2},{6,1},{7,0},{8,15},{9,14},{10,... | collective-permute-start | bytes 786440 | tf_op jit(solution)/shard_map/ppermute | solution.py:367
  15.6 7.1 %route_2.1 = (bf16[8,2,2,32,1024]{4,3,2,1,0:T(8,128)(2,1)}, bf16[4,2,1616,128]{3,2,1,0:T(8,128)(2,1)}, bf16[4,2,128,1616]{3,2,1,0:T(8,128)(2,1)}) custom-call(s32[4,32]{1,0:T(4,128)} %bitcast.2, bf16[128,4096]{1,0:T(8,128)(2,1)} %q_hbm.3, bf16[128,4096]{1,0:T(8,128)(2,1)} %g_hbm.3, bf16[1,1601,512]{2,1,0:T(8,128)(2,1)} %refs_0_.1, bf16[1,1601,512]{2,1,0:T(8,128)(2,1)} %refs_1_.1), custom_call_target="tpu_custom_call" | custom-call | bytes 12582912 | tf_op jit(solution)/shard_map/route_2/pallas_call | solution.py:392
  22.7 0.0 collective-permute-done.2.refs_3_
  22.7 0.0 copy-start.6
  22.8 8.8 %collective-permute-done.4.refs_5_ = bf16[2,2,32,1024]{3,2,1,0:T(8,128)(2,1)S(1)} collective-permute-done((bf16[2,2,32,1024]{3,2,1,0:T(8,128)(2,1)}, bf16[2,2,32,1024]{3,2,1,0:T(8,128)(2,1)S(1)}, u32[]{:S(2)}, u32[]{:S(2)}) %collective-permute-start.4) | collective-permute-done | bytes 262176 | tf_op jit(solution)/shard_map/ppermute | solution.py:367
  31.6 0.7 copy-done.8
  32.3 4.0 %all-to-all-start.1 = ((bf16[8,2,2,32,1024]{4,3,2,1,0:T(8,128)(2,1)}), bf16[8,2,2,32,1024]{4,3,2,1,0:T(8,128)(2,1)S(1)}, u32[]{:S(2)}, u32[]{:S(2)}) async-start(bf16[8,2,2,32,1024]{4,3,2,1,0:T(8,128)(2,1)} %get-tuple-element.57), calls=%async_computation.1 | async-start | bytes 4194304 | tf_op jit(solution)/shard_map/all_to_all | solution.py:459
  36.3 10.0 %attend_0.1 = (bf16[8,2,2,32,1024]{4,3,2,1,0:T(8,128)(2,1)}, bf16[2,1616,128]{2,1,0:T(8,128)(2,1)}, bf16[2,1616,128]{2,1,0:T(8,128)(2,1)}) custom-call(s32[4,32]{1,0:T(4,128)} %bitcast.3, bf16[4,2,1616,128]{3,2,1,0:T(8,128)(2,1)} %get-tuple-element.37.caches, bf16[4,2,128,1616]{3,2,1,0:T(8,128)(2,1)} %get-tuple-element.38.turned_caches, ...), custom_call_target="tpu_custom_call" | custom-call | flops 7554465792 | bytes 8388608 | tf_op jit(solution)/shard_map/attend_0/pallas_call | solution.py:411
  46.4 16.6 %all-to-all-done.1.refs_0_ = bf16[8,2,2,32,1024]{4,3,2,1,0:T(8,128)(2,1)S(1)} async-done(((bf16[8,2,2,32,1024]{4,3,2,1,0:T(8,128)(2,1)}), bf16[8,2,2,32,1024]{4,3,2,1,0:T(8,128)(2,1)S(1)}, u32[]{:S(2)}, u32[]{:S(2)}) %all-to-all-start.1) | async-done | bytes 2097184 | tf_op jit(solution)/shard_map/all_to_all | solution.py:459
  63.0 1.4 copy-done.2
  64.4 3.6 %all-to-all-start = ((bf16[8,2,2,32,1024]{4,3,2,1,0:T(8,128)(2,1)}), bf16[8,2,2,32,1024]{4,3,2,1,0:T(8,128)(2,1)S(1)}, u32[]{:S(2)}, u32[]{:S(2)}) async-start(bf16[8,2,2,32,1024]{4,3,2,1,0:T(8,128)(2,1)} %get-tuple-element.56), calls=%async_computation | async-start | bytes 4194304 | tf_op jit(solution)/shard_map/all_to_all | solution.py:459
  68.0 3.7 %collective-permute-start.8 = (bf16[2,1616,128]{2,1,0:T(8,128)(2,1)}, bf16[2,1616,128]{2,1,0:T(8,128)(2,1)S(1)}, u32[]{:S(2)}, u32[]{:S(2)}) collective-permute-start(bf16[2,1616,128]{2,1,0:T(8,128)(2,1)} %get-tuple-element.69), channel_id=1, source_target_pairs={{0,24},{8,16},{16,8},{24,0},{1,25},{9,17},{17,9},{25,1},{2,26},{10... | collective-permute-start | bytes 2482184 | tf_op jit(solution)/shard_map/ppermute | solution.py:367
  71.7 10.2 %attend_2.1 = (bf16[8,2,2,32,1024]{4,3,2,1,0:T(8,128)(2,1)}, bf16[2,1616,128]{2,1,0:T(8,128)(2,1)}, bf16[2,1616,128]{2,1,0:T(8,128)(2,1)}) custom-call(s32[4,32]{1,0:T(4,128)} %bitcast.4, bf16[4,2,1616,128]{3,2,1,0:T(8,128)(2,1)} %get-tuple-element.37.caches, bf16[4,2,128,1616]{3,2,1,0:T(8,128)(2,1)} %get-tuple-element.38.turned_caches, ...), custom_call_target="tpu_custom_call" | custom-call | flops 7554465792 | bytes 8388608 | tf_op jit(solution)/shard_map/attend_2/pallas_call | solution.py:411
  81.9 0.8 collective-permute-start.7
  82.7 11.9 %all-to-all-done.returned = bf16[8,2,2,32,1024]{4,3,2,1,0:T(8,128)(2,1)S(1)} async-done(((bf16[8,2,2,32,1024]{4,3,2,1,0:T(8,128)(2,1)}), bf16[8,2,2,32,1024]{4,3,2,1,0:T(8,128)(2,1)S(1)}, u32[]{:S(2)}, u32[]{:S(2)}) %all-to-all-start) | async-done | bytes 2097184 | tf_op jit(solution)/shard_map/all_to_all | solution.py:459
  94.6 1.3 copy-done.1
  95.9 5.1 %all-to-all-start.2 = ((bf16[8,2,2,32,1024]{4,3,2,1,0:T(8,128)(2,1)}), bf16[8,2,2,32,1024]{4,3,2,1,0:T(8,128)(2,1)S(1)}, u32[]{:S(2)}, u32[]{:S(2)}) async-start(bf16[8,2,2,32,1024]{4,3,2,1,0:T(8,128)(2,1)} %get-tuple-element.61), calls=%async_computation.2 | async-start | bytes 4194304 | tf_op jit(solution)/shard_map/all_to_all | solution.py:459
  101.1 3.0 %collect_0.1 = (bf16[128,4096]{1,0:T(8,128)(2,1)}, bf16[128,4096]{1,0:T(8,128)(2,1)}) custom-call(s32[4,32]{1,0:T(4,128)} %bitcast.5, bf16[8,2,2,32,1024]{4,3,2,1,0:T(8,128)(2,1)} %copy-done.1), custom_call_target="tpu_custom_call" | custom-call | bytes 4194304 | tf_op jit(solution)/shard_map/collect_0/pallas_call | solution.py:442
  104.1 39.2 %collective-permute-done.9 = bf16[2,1616,128]{2,1,0:T(8,128)(2,1)} collective-permute-done((bf16[2,1616,128]{2,1,0:T(8,128)(2,1)}, bf16[2,1616,128]{2,1,0:T(8,128)(2,1)}, u32[]{:S(2)}, u32[]{:S(2)}) %collective-permute-start.9) | collective-permute-done | bytes 827424 | tf_op jit(solution)/shard_map/ppermute | solution.py:367
  143.3 1.8 %add_convert_fusion = bf16[2,1616,128]{2,1,0:T(8,128)(2,1)S(1)} fusion(bf16[2,1616,128]{2,1,0:T(8,128)(2,1)} %collective-permute-done.9, bf16[2,1616,128]{2,1,0:T(8,128)(2,1)S(1)} %collective-permute-done.8, bf16[2,1616,128]{2,1,0:T(8,128)(2,1)} %collective-permute-done.7, bf16[2,1616,128]{2,1,0:T(8,128)(2,1)S(1)} %copy-done.3), kind=kLoop, calls=%fused_computation | loop fusion | flops 3309568 | bytes 4136960 | tf_op jit(solution)/shard_map/convert_element_type | solution.py:481
  145.1 0.9 fusion
  146.0 1.3 copy-done
  147.4 2.8 %collect_2.1 = (bf16[128,4096]{1,0:T(8,128)(2,1)}, bf16[128,4096]{1,0:T(8,128)(2,1)}) custom-call(s32[4,32]{1,0:T(4,128)} %bitcast.6, bf16[8,2,2,32,1024]{4,3,2,1,0:T(8,128)(2,1)} %copy-done, bf16[128,4096]{1,0:T(8,128)(2,1)} %get-tuple-element.63.refs_0_, bf16[128,4096]{1,0:T(8,128)(2,1)} %get-tuple-element.64.refs_1_), custom_call_target="tpu_custom_call", output_to_operand_aliasing={{0}: (2, {}), {1}: (3, {})} | custom-call | bytes 4194304 | tf_op jit(solution)/shard_map/collect_2/pallas_call | solution.py:442
  (20 shorter events, 0.0 us)
Async XLA Ops:
  3.5 4.9 %collective-permute-start = (bf16[2,2,32,1024]{3,2,1,0:T(8,128)(2,1)}, bf16[2,2,32,1024]{3,2,1,0:T(8,128)(2,1)S(1)}, u32[]{:S(2)}, u32[]{:S(2)}) collective-permute-start(bf16[2,2,32,1024]{3,2,1,0:T(8,128)(2,1)} %get-tuple-element.40), channel_id=1, source_target_pairs={{0,1},{1,0},{2,3},{3,2},{4,5},{5,4},{6,7},{7,6},{8,9},{9,8},{10,11... | collective-permute-start | bytes 786440 | tf_op jit(solution)/shard_map/ppermute | solution.py:367
  4.0 9.9 %collective-permute-start.1 = (bf16[2,2,32,1024]{3,2,1,0:T(8,128)(2,1)}, bf16[2,2,32,1024]{3,2,1,0:T(8,128)(2,1)S(1)}, u32[]{:S(2)}, u32[]{:S(2)}) collective-permute-start(bf16[2,2,32,1024]{3,2,1,0:T(8,128)(2,1)} %get-tuple-element.41), channel_id=1, source_target_pairs={{0,2},{1,3},{2,0},{3,1},{4,6},{5,7},{6,4},{7,5},{8,10},{9,11},{10,... | collective-permute-start | bytes 786440 | tf_op jit(solution)/shard_map/ppermute | solution.py:367
  6.5 16.2 %collective-permute-start.2 = (bf16[2,2,32,1024]{3,2,1,0:T(8,128)(2,1)}, bf16[2,2,32,1024]{3,2,1,0:T(8,128)(2,1)S(1)}, u32[]{:S(2)}, u32[]{:S(2)}) collective-permute-start(bf16[2,2,32,1024]{3,2,1,0:T(8,128)(2,1)} %get-tuple-element.42), channel_id=1, source_target_pairs={{0,3},{1,2},{2,1},{3,0},{4,7},{5,6},{6,5},{7,4},{8,11},{9,10},{10,... | collective-permute-start | bytes 786440 | tf_op jit(solution)/shard_map/ppermute | solution.py:367
  6.6 16.1 %collective-permute-start.3 = (bf16[2,2,32,1024]{3,2,1,0:T(8,128)(2,1)}, bf16[2,2,32,1024]{3,2,1,0:T(8,128)(2,1)S(1)}, u32[]{:S(2)}, u32[]{:S(2)}) collective-permute-start(bf16[2,2,32,1024]{3,2,1,0:T(8,128)(2,1)} %get-tuple-element.43), channel_id=1, source_target_pairs={{0,4},{1,5},{2,6},{3,7},{4,0},{5,1},{6,2},{7,3},{8,12},{9,13},{10,... | collective-permute-start | bytes 786440 | tf_op jit(solution)/shard_map/ppermute | solution.py:367
  8.4 23.2 %collective-permute-start.4 = (bf16[2,2,32,1024]{3,2,1,0:T(8,128)(2,1)}, bf16[2,2,32,1024]{3,2,1,0:T(8,128)(2,1)S(1)}, u32[]{:S(2)}, u32[]{:S(2)}) collective-permute-start(bf16[2,2,32,1024]{3,2,1,0:T(8,128)(2,1)} %get-tuple-element.44), channel_id=1, source_target_pairs={{0,5},{1,4},{2,7},{3,6},{4,1},{5,0},{6,3},{7,2},{8,13},{9,12},{10,... | collective-permute-start | bytes 786440 | tf_op jit(solution)/shard_map/ppermute | solution.py:367
  8.4 14.3 %copy-start.4 = (bf16[2,2,32,1024]{3,2,1,0:T(8,128)(2,1)}, bf16[2,2,32,1024]{3,2,1,0:T(8,128)(2,1)S(1)}, u32[]{:S(2)}) copy-start(bf16[2,2,32,1024]{3,2,1,0:T(8,128)(2,1)S(1)} %collective-permute-done.refs_1_) | copy-start | bytes 786436
  8.4 23.2 %collective-permute-start.5 = (bf16[2,2,32,1024]{3,2,1,0:T(8,128)(2,1)}, bf16[2,2,32,1024]{3,2,1,0:T(8,128)(2,1)}, u32[]{:S(2)}, u32[]{:S(2)}) collective-permute-start(bf16[2,2,32,1024]{3,2,1,0:T(8,128)(2,1)} %get-tuple-element.45), channel_id=1, source_target_pairs={{0,6},{1,7},{2,4},{3,5},{4,2},{5,3},{6,0},{7,1},{8,14},{9,15},{10,... | collective-permute-start | bytes 786440 | tf_op jit(solution)/shard_map/ppermute | solution.py:367
  13.9 8.8 %copy-start.5 = (bf16[2,2,32,1024]{3,2,1,0:T(8,128)(2,1)}, bf16[2,2,32,1024]{3,2,1,0:T(8,128)(2,1)S(1)}, u32[]{:S(2)}) copy-start(bf16[2,2,32,1024]{3,2,1,0:T(8,128)(2,1)S(1)} %collective-permute-done.1.refs_2_) | copy-start | bytes 786436
  13.9 17.7 %collective-permute-start.6 = (bf16[2,2,32,1024]{3,2,1,0:T(8,128)(2,1)}, bf16[2,2,32,1024]{3,2,1,0:T(8,128)(2,1)}, u32[]{:S(2)}, u32[]{:S(2)}) collective-permute-start(bf16[2,2,32,1024]{3,2,1,0:T(8,128)(2,1)} %get-tuple-element.46), channel_id=1, source_target_pairs={{0,7},{1,6},{2,5},{3,4},{4,3},{5,2},{6,1},{7,0},{8,15},{9,14},{10,... | collective-permute-start | bytes 786440 | tf_op jit(solution)/shard_map/ppermute | solution.py:367
  22.7 8.9 %copy-start.6 = (bf16[2,2,32,1024]{3,2,1,0:T(8,128)(2,1)}, bf16[2,2,32,1024]{3,2,1,0:T(8,128)(2,1)S(1)}, u32[]{:S(2)}) copy-start(bf16[2,2,32,1024]{3,2,1,0:T(8,128)(2,1)S(1)} %collective-permute-done.2.refs_3_) | copy-start | bytes 786436
  22.8 8.9 %copy-start.7 = (bf16[2,2,32,1024]{3,2,1,0:T(8,128)(2,1)}, bf16[2,2,32,1024]{3,2,1,0:T(8,128)(2,1)S(1)}, u32[]{:S(2)}) copy-start(bf16[2,2,32,1024]{3,2,1,0:T(8,128)(2,1)S(1)} %collective-permute-done.3.refs_4_) | copy-start | bytes 786436
  31.6 0.7 copy-start.8
  32.3 30.7 %all-to-all-start.1 = ((bf16[8,2,2,32,1024]{4,3,2,1,0:T(8,128)(2,1)}), bf16[8,2,2,32,1024]{4,3,2,1,0:T(8,128)(2,1)S(1)}, u32[]{:S(2)}, u32[]{:S(2)}) async-start(bf16[8,2,2,32,1024]{4,3,2,1,0:T(8,128)(2,1)} %get-tuple-element.57), calls=%async_computation.1 | async-start | bytes 4194304 | tf_op jit(solution)/shard_map/all_to_all | solution.py:459
  63.0 1.4 copy-start.2
  64.4 30.2 %all-to-all-start = ((bf16[8,2,2,32,1024]{4,3,2,1,0:T(8,128)(2,1)}), bf16[8,2,2,32,1024]{4,3,2,1,0:T(8,128)(2,1)S(1)}, u32[]{:S(2)}, u32[]{:S(2)}) async-start(bf16[8,2,2,32,1024]{4,3,2,1,0:T(8,128)(2,1)} %get-tuple-element.56), calls=%async_computation | async-start | bytes 4194304 | tf_op jit(solution)/shard_map/all_to_all | solution.py:459
  68.0 36.0 %collective-permute-start.8 = (bf16[2,1616,128]{2,1,0:T(8,128)(2,1)}, bf16[2,1616,128]{2,1,0:T(8,128)(2,1)S(1)}, u32[]{:S(2)}, u32[]{:S(2)}) collective-permute-start(bf16[2,1616,128]{2,1,0:T(8,128)(2,1)} %get-tuple-element.69), channel_id=1, source_target_pairs={{0,24},{8,16},{16,8},{24,0},{1,25},{9,17},{17,9},{25,1},{2,26},{10... | collective-permute-start | bytes 2482184 | tf_op jit(solution)/shard_map/ppermute | solution.py:367
  71.7 71.6 %collective-permute-start.9 = (bf16[2,1616,128]{2,1,0:T(8,128)(2,1)}, bf16[2,1616,128]{2,1,0:T(8,128)(2,1)}, u32[]{:S(2)}, u32[]{:S(2)}) collective-permute-start(bf16[2,1616,128]{2,1,0:T(8,128)(2,1)} %get-tuple-element.58), channel_id=1, source_target_pairs={{0,16},{8,24},{16,0},{24,8},{1,17},{9,25},{17,1},{25,9},{2,18},{10... | collective-permute-start | bytes 2482184 | tf_op jit(solution)/shard_map/ppermute | solution.py:367
  81.9 61.4 %collective-permute-start.7 = (bf16[2,1616,128]{2,1,0:T(8,128)(2,1)}, bf16[2,1616,128]{2,1,0:T(8,128)(2,1)}, u32[]{:S(2)}, u32[]{:S(2)}) collective-permute-start(bf16[2,1616,128]{2,1,0:T(8,128)(2,1)} %get-tuple-element.68), channel_id=1, source_target_pairs={{0,8},{8,0},{16,24},{24,16},{1,9},{9,1},{17,25},{25,17},{2,10},{10... | collective-permute-start | bytes 2482184 | tf_op jit(solution)/shard_map/ppermute | solution.py:367
  94.6 1.3 copy-start.1
  95.9 50.1 %all-to-all-start.2 = ((bf16[8,2,2,32,1024]{4,3,2,1,0:T(8,128)(2,1)}), bf16[8,2,2,32,1024]{4,3,2,1,0:T(8,128)(2,1)S(1)}, u32[]{:S(2)}, u32[]{:S(2)}) async-start(bf16[8,2,2,32,1024]{4,3,2,1,0:T(8,128)(2,1)} %get-tuple-element.61), calls=%async_computation.2 | async-start | bytes 4194304 | tf_op jit(solution)/shard_map/all_to_all | solution.py:459
  101.1 42.2 %copy-start.3 = (bf16[2,1616,128]{2,1,0:T(8,128)(2,1)S(1)}, bf16[2,1616,128]{2,1,0:T(8,128)(2,1)}, u32[]{:S(2)}) copy-start(bf16[2,1616,128]{2,1,0:T(8,128)(2,1)} %get-tuple-element.67) | copy-start | bytes 2482180
  146.0 1.3 copy-start

commit v7 on v6

--- a/solution.py
+++ b/solution.py
@@ -18,7 +18,7 @@
 SLICE = 128
 LOWEST = -3.0e38
 PER_CHUNK = 2
-VMEM_BYTES = 54 << 20
+VMEM_BYTES = 58 << 20
 ANY = pl.BlockSpec(memory_space=pl.ANY)
 SMEM = pl.BlockSpec(memory_space=pltpu.SMEM)
 VMEM = pl.BlockSpec(memory_space=pltpu.VMEM)
@@ -131,9 +131,10 @@
             )
 
 
-def attend_kernel(turns, peers, seg_rows, tokens, reads, caches, turned_caches, *refs):
-    received, refs = refs[: len(refs) - 15 - len(turns)], refs[len(refs) - 15 - len(turns) :]
-    returned, grads = refs[0], refs[1 : 1 + len(turns)]
+def attend_kernel(turns, hands, peers, seg_rows, tokens, reads, caches, turned_caches, *refs):
+    outs = 1 + hands * len(turns)
+    received, refs = refs[: len(refs) - 14 - outs], refs[len(refs) - 14 - outs :]
+    returned, grads = refs[0], refs[1:outs]
     (
         straight,
         turned,
@@ -149,7 +150,7 @@
         in_sems,
         out_sems,
         grad_sems,
-    ) = refs[1 + len(turns) :]
+    ) = refs[outs:]
     me = lax.axis_index("enc")
     base = lax.axis_index("seq") * peers
     slots = inbox.shape[1]
@@ -185,7 +186,13 @@
         )
 
     def handing(i):
-        return pltpu.make_async_copy(staged.at[i], grads[i], grad_sems.at[i])
+        pairs = [(staged.at[i], grads[i])]
+        if hands == 2:
+            pairs = [(staged.at[i, j], grads[2 * i + j]) for j in range(2)]
+        return [
+            pltpu.make_async_copy(source, target, grad_sems.at[i, j])
+            for j, (source, target) in enumerate(pairs)
+        ]
 
     for copies in kv_copies:
         copies[0].start()
@@ -340,7 +347,8 @@
         for i in heads:
             staged[i, 0] = (sums[i, 0] * SCALE).astype(bf16)
             staged[i, 1] = sums[i, 1].astype(bf16)
-            handing(i).start()
+            for copy in handing(i):
+                copy.start()
 
     @pl.when(count == 0)
     def _():
@@ -348,7 +356,8 @@
         for i in range(len(turns)):
             for copy in kv_copies[i]:
                 copy.wait()
-            handing(i).start()
+            for copy in handing(i):
+                copy.start()
 
     for i in range(len(turns)):
         for slot in range(slots):
@@ -357,7 +366,8 @@
             def _():
                 leaving(i, slot, 0).wait()
 
-        handing(i).wait()
+        for copy in handing(i):
+            copy.wait()
 
 
 def xor_permute(array, axis, k):
@@ -406,13 +416,14 @@
             name=f"route_{turns[0]}",
         )(by_segment, queries, grad_out, *[keys, values] * prepares)
 
-    def attend(turns, received):
+    def attend(turns, hands, received):
         work = slots * lanes * tokens * HD * len(turns)
+        grad = jax.ShapeDtypeStruct((2, padded, HD)[hands - 1 :], bf16)
         results = pl.pallas_call(
-            functools.partial(attend_kernel, turns, peers, seg_rows, tokens),
-            out_shape=[message] + [jax.ShapeDtypeStruct((2, padded, HD), bf16)] * len(turns),
+            functools.partial(attend_kernel, turns, hands, peers, seg_rows, tokens),
+            out_shape=[message] + [grad] * hands * len(turns),
             in_specs=[SMEM] + [ANY] * (2 + len(received)),
-            out_specs=[ANY] * (1 + len(turns)),
+            out_specs=[ANY] * (1 + hands * len(turns)),
             scratch_shapes=[
                 pltpu.VMEM((len(turns), 2, padded, HD), bf16),
                 pltpu.VMEM((len(turns), 2, HD, padded), bf16),
@@ -427,7 +438,7 @@
                 pltpu.SemaphoreType.DMA((len(turns), 4)),
                 pltpu.SemaphoreType.DMA((len(turns), slots)),
                 pltpu.SemaphoreType.DMA((len(turns), slots)),
-                pltpu.SemaphoreType.DMA((len(turns),)),
+                pltpu.SemaphoreType.DMA((len(turns), 2)),
             ],
             compiler_params=pltpu.CompilerParams(vmem_limit_bytes=VMEM_BYTES),
             cost_estimate=pl.CostEstimate(
@@ -435,7 +446,7 @@
             ),
             name=f"attend_{turns[0]}",
         )(by_segment, *prepared, *received)
-        return results[0], list(results[1:])
+        return results
 
     def collect(turns, returned, before):
         whole = jax.ShapeDtypeStruct(queries.shape, bf16)
@@ -461,27 +472,33 @@
     first, second = chunks
     received = [xor_permute(array, "enc", k) for k, array in enumerate(route(first, 0))]
     routed, *prepared = route(second, 1)
-    *received, routed = lax.optimization_barrier((*received, routed))
+    most = len(received) // 2 + 1
+    *received[:most], routed = lax.optimization_barrier((*received[:most], routed))
     received_later = exchange(routed)
-    returned, grads = attend(first, received)
+    butterfly = n_seq == KVH
+    returned, *grads = attend(first, 1 + butterfly, received)
     answer = exchange(returned)
-    if n_seq == KVH:
-        far = [xor_permute(grads[0], "seq", 3), xor_permute(grads[1], "seq", 2)]
-    received_later, grads[1] = lax.optimization_barrier((received_later, grads[1]))
-    returned, more = attend(second, [received_later])
+    if butterfly:
+        passed = xor_permute(grads[0], "seq", 1)
+        far = [xor_permute(grads[1], "seq", 3), xor_permute(grads[3], "seq", 2)]
+    received_later, grads[-1] = lax.optimization_barrier((received_later, grads[-1]))
+    returned, *more = attend(second, 1, [received_later])
+    if butterfly:
+        passed, grads[2], more[0] = lax.optimization_barrier((passed, grads[2], more[0]))
+        pair = (grads[2].astype(f32) + passed.astype(f32)).astype(bf16)
+        returned, pair = lax.optimization_barrier((returned, pair))
+        pair = xor_permute(pair, "seq", 2)
+        near = xor_permute(more[0], "seq", 1)
     answer, returned = lax.optimization_barrier((answer, returned))
     answer_later = exchange(returned)
-    if n_seq == KVH:
-        near = xor_permute(more[0], "seq", 1)
     half = collect(first, answer, [])
     attended, grad_queries = collect(second, answer_later, half)
 
-    if n_seq == KVH:
-        total = more[1].astype(f32) + near.astype(f32) + far[0].astype(f32) + far[1].astype(f32)
-        total = total.astype(bf16)[:, :tokens]
-        return attended, grad_queries, total[0][None], total[1][None]
-    grads += more
-    joined = jnp.concatenate(grads, axis=2)[:, :tokens]
+    if butterfly:
+        terms = [[more[1][0], near[0], pair], [more[1][1], near[1], *far]]
+        summed = [sum(term.astype(f32) for term in ones)[:tokens].astype(bf16) for ones in terms]
+        return attended, grad_queries, summed[0][None], summed[1][None]
+    joined = jnp.concatenate(grads + more, axis=2)[:, :tokens]
     summed = lax.psum_scatter(joined, "seq", scatter_dimension=2, tiled=True)
     return attended, grad_queries, summed[0][None], summed[1][None]
 

time: 151 us -> 191 us (1.26)
  Pallas kernels: 35.8 us -> 56.9 us
  waiting for transfers between devices: 79.5 us -> 93.6 us
  starting transfers between devices: 26.5 us -> 31 us
    ppermute x10 -> x12, waiting for transfers between devices: 51 us -> 90 us  [xor_permute(): return lax.ppermute(array, axis, [(i, i ^ k) for i in range(size)])]
    all_to_all x3, waiting for transfers between devices: 28.6 us -> 3.61 us  [exchange(): return lax.all_to_all(array, 'enc', split_axis=0, concat_axis=0, tiled=True)]
    pallas_call x2, Pallas kernels: 20.2 us -> 41.3 us  [attend(): pl.pallas_call(functools.partial(attend_kernel, turns, hands, peers, seg_...]
    ppermute x10 -> x12, starting transfers between devices: 13.7 us -> 17 us  [xor_permute(): return lax.ppermute(array, axis, [(i, i ^ k) for i in range(size)])]
    unnamed x18 -> x28, local copies, waits for them, and re-layouts: 4.8 us -> 5.84 us
  transfers between devices with their start and end apart: 13 -> 15, of which waited for: 5 -> 5; matrix products, arithmetic and copies ran while one was open for 2% -> 1% of each run, Pallas kernels for 20% -> 27%
where the time goes in v7:
time: 191 us; the launch traced here: 190 us
  waiting for transfers between devices  93.6 us (49%)
  Pallas kernels  56.9 us (30%)
  starting transfers between devices  31 us (16%)
  local copies, waits for them, and re-layouts  5.84 us (3%)
  other arithmetic  2.03 us (1%)
    ppermute x12, waiting for transfers between devices, xor_permute(): return lax.ppermute(array, axis, [(i, i ^ k) for i in range(size)])  90 us
    pallas_call x2, Pallas kernels, attend(): pl.pallas_call(functools.partial(attend_kernel, turns, hands, peers, seg_...  41.3 us
    ppermute x12, starting transfers between devices, xor_permute(): return lax.ppermute(array, axis, [(i, i ^ k) for i in range(size)])  17 us
    all_to_all x3, starting transfers between devices, exchange(): return lax.all_to_all(array, 'enc', split_axis=0, concat_axis=0, tiled=True)  14 us
    pallas_call x2, Pallas kernels, route(): pl.pallas_call(functools.partial(route_kernel, turns, n_seg, seg_rows, to...  9.91 us
    unnamed x28, local copies, waits for them, and re-layouts  5.84 us
    pallas_call x2, Pallas kernels, collect(): pl.pallas_call(functools.partial(collect_kernel, turns, n_seg, seg_rows),...  5.64 us
  transfers between devices with their start and end apart: 15, of which 5 were waited for; matrix products, arithmetic and copies ran while one was open for 1% of the time, Pallas kernels for 27%

profile of v7, /device:TPU:0, one launch (start us, length us, event | category | flops | bytes accessed | tf_op | source)
XLA Modules:
  0.0 190.3 jit_solution(14539503122947850)
XLA Ops:
  0.6 2.8 %route_0.1 = (bf16[2,2,32,1024]{3,2,1,0:T(8,128)(2,1)}, bf16[2,2,32,1024]{3,2,1,0:T(8,128)(2,1)}, bf16[2,2,32,1024]{3,2,1,0:T(8,128)(2,1)}, bf16[2,2,32,1024]{3,...) custom-call(s32[4,32]{1,0:T(4,128)} %bitcast.9, ...), custom_call_target="tpu_custom_call" | custom-call | bytes 2097152 | tf_op jit(solution)/shard_map/route_0/pallas_call | solution.py:402
  3.5 0.5 collective-permute-start
  4.0 2.6 %collective-permute-start.1 = (bf16[2,2,32,1024]{3,2,1,0:T(8,128)(2,1)}, bf16[2,2,32,1024]{3,2,1,0:T(8,128)(2,1)S(1)}, u32[]{:S(2)}, u32[]{:S(2)}) collective-permute-start(bf16[2,2,32,1024]{3,2,1,0:T(8,128)(2,1)} %get-tuple-element.45), channel_id=1, source_target_pairs={{0,2},{1,3},{2,0},{3,1},{4,6},{5,7},{6,4},{7,5},{8,10},{9,11},{10,... | collective-permute-start | bytes 786440 | tf_op jit(solution)/shard_map/ppermute | solution.py:377
  6.6 1.8 collective-permute-start.3
  8.4 7.1 %route_2.1 = (bf16[8,2,2,32,1024]{4,3,2,1,0:T(8,128)(2,1)}, bf16[4,2,1616,128]{3,2,1,0:T(8,128)(2,1)}, bf16[4,2,128,1616]{3,2,1,0:T(8,128)(2,1)}) custom-call(s32[4,32]{1,0:T(4,128)} %bitcast.10, bf16[128,4096]{1,0:T(8,128)(2,1)} %q_hbm.3, bf16[128,4096]{1,0:T(8,128)(2,1)} %g_hbm.3, bf16[1,1601,512]{2,1,0:T(8,128)(2,1)} %refs_0_.1, bf16[1,1601,512]{2,1,0:T(8,128)(2,1)} %refs_1_.1), custom_call_target="tpu_custom_call" | custom-call | bytes 12582912 | tf_op jit(solution)/shard_map/route_2/pallas_call | solution.py:402
  15.5 3.5 %collective-permute-done.2.refs_3_ = bf16[2,2,32,1024]{3,2,1,0:T(8,128)(2,1)S(1)} collective-permute-done((bf16[2,2,32,1024]{3,2,1,0:T(8,128)(2,1)}, bf16[2,2,32,1024]{3,2,1,0:T(8,128)(2,1)S(1)}, u32[]{:S(2)}, u32[]{:S(2)}) %collective-permute-start.2) | collective-permute-done | bytes 262176 | tf_op jit(solution)/shard_map/ppermute | solution.py:377
  19.0 0.7 copy-done.8
  19.8 3.8 %all-to-all-start.1 = ((bf16[8,2,2,32,1024]{4,3,2,1,0:T(8,128)(2,1)}), bf16[8,2,2,32,1024]{4,3,2,1,0:T(8,128)(2,1)S(1)}, u32[]{:S(2)}, u32[]{:S(2)}) async-start(bf16[8,2,2,32,1024]{4,3,2,1,0:T(8,128)(2,1)} %get-tuple-element.58), calls=%async_computation.1 | async-start | bytes 4194304 | tf_op jit(solution)/shard_map/all_to_all | solution.py:470
  23.6 1.8 collective-permute-start.4
  25.4 1.5 collective-permute-start.5
  26.9 1.1 collective-permute-start.6
  28.0 37.7 %collective-permute-done.4.refs_5_ = bf16[2,2,32,1024]{3,2,1,0:T(8,128)(2,1)S(1)} collective-permute-done((bf16[2,2,32,1024]{3,2,1,0:T(8,128)(2,1)}, bf16[2,2,32,1024]{3,2,1,0:T(8,128)(2,1)S(1)}, u32[]{:S(2)}, u32[]{:S(2)}) %collective-permute-start.4) | collective-permute-done | bytes 262176 | tf_op jit(solution)/shard_map/ppermute | solution.py:377
  65.7 0.7 copy-done.11
  66.6 20.5 %attend_0.1 = (bf16[8,2,2,32,1024]{4,3,2,1,0:T(8,128)(2,1)}, bf16[1616,128]{1,0:T(8,128)(2,1)}, bf16[1616,128]{1,0:T(8,128)(2,1)}, bf16[1616,128]{1,0:T(8,128)(2,1)}, bf16[1616,128]{1,0:T(8,128)(2,1)}) custom-call(s32[4,32]{1,0:T(4,128)} %bitcast.11, bf16[4,2,1616,128]{3,2,1,0:T(8,128)(2,1)} %get-tuple-element.41.caches, ...), custom_call_target="tpu_custom_call" | custom-call | flops 7554465792 | bytes 8388608 | tf_op jit(solution)/shard_map/attend_0/pallas_call | solution.py:422
  87.2 1.4 copy-done.2
  88.5 6.6 %all-to-all-start = ((bf16[8,2,2,32,1024]{4,3,2,1,0:T(8,128)(2,1)}), bf16[8,2,2,32,1024]{4,3,2,1,0:T(8,128)(2,1)S(1)}, u32[]{:S(2)}, u32[]{:S(2)}) async-start(bf16[8,2,2,32,1024]{4,3,2,1,0:T(8,128)(2,1)} %get-tuple-element.57), calls=%async_computation | async-start | bytes 4194304 | tf_op jit(solution)/shard_map/all_to_all | solution.py:470
  95.1 1.8 collective-permute-start.7
  96.9 20.8 %attend_2.1 = (bf16[8,2,2,32,1024]{4,3,2,1,0:T(8,128)(2,1)}, bf16[2,1616,128]{2,1,0:T(8,128)(2,1)}, bf16[2,1616,128]{2,1,0:T(8,128)(2,1)}) custom-call(s32[4,32]{1,0:T(4,128)} %bitcast.12, bf16[4,2,1616,128]{3,2,1,0:T(8,128)(2,1)} %get-tuple-element.41.caches, bf16[4,2,128,1616]{3,2,1,0:T(8,128)(2,1)} %get-tuple-element.42.turned_caches, ...), custom_call_target="tpu_custom_call" | custom-call | flops 7554465792 | bytes 8388608 | tf_op jit(solution)/shard_map/attend_2/pallas_call | solution.py:422
  117.7 0.3 collective-permute-start.8
  118.2 3.6 %all-to-all-done.returned = bf16[8,2,2,32,1024]{4,3,2,1,0:T(8,128)(2,1)S(1)} async-done(((bf16[8,2,2,32,1024]{4,3,2,1,0:T(8,128)(2,1)}), bf16[8,2,2,32,1024]{4,3,2,1,0:T(8,128)(2,1)S(1)}, u32[]{:S(2)}, u32[]{:S(2)}) %all-to-all-start) | async-done | bytes 2097184 | tf_op jit(solution)/shard_map/all_to_all | solution.py:470
  121.8 1.4 copy-done.1
  123.1 3.6 %all-to-all-start.2 = ((bf16[8,2,2,32,1024]{4,3,2,1,0:T(8,128)(2,1)}), bf16[8,2,2,32,1024]{4,3,2,1,0:T(8,128)(2,1)S(1)}, u32[]{:S(2)}, u32[]{:S(2)}) async-start(bf16[8,2,2,32,1024]{4,3,2,1,0:T(8,128)(2,1)} %get-tuple-element.68), calls=%async_computation.2 | async-start | bytes 4194304 | tf_op jit(solution)/shard_map/all_to_all | solution.py:470
  126.7 2.7 %collective-permute-start.11 = (bf16[1616,128]{1,0:T(8,128)(2,1)}, bf16[1616,128]{1,0:T(8,128)(2,1)S(1)}, u32[]{:S(2)}, u32[]{:S(2)}) collective-permute-start(bf16[1616,128]{1,0:T(8,128)(2,1)} %get-tuple-element.59), channel_id=1, source_target_pairs={{0,16},{8,24},{16,0},{24,8},{1,17},{9,25},{17,1},{25,9},{2,18},{10... | collective-permute-start | bytes 1241096 | tf_op jit(solution)/shard_map/ppermute | solution.py:377
  129.5 1.4 collective-permute-start.10
  130.9 1.6 collective-permute-start.9
  132.4 2.8 %collect_0.1 = (bf16[128,4096]{1,0:T(8,128)(2,1)}, bf16[128,4096]{1,0:T(8,128)(2,1)}) custom-call(s32[4,32]{1,0:T(4,128)} %bitcast.13, bf16[8,2,2,32,1024]{4,3,2,1,0:T(8,128)(2,1)} %copy-done.1), custom_call_target="tpu_custom_call" | custom-call | bytes 4194304 | tf_op jit(solution)/shard_map/collect_0/pallas_call | solution.py:453
  135.3 10.1 %collective-permute-done.8 = bf16[2,1616,128]{2,1,0:T(8,128)(2,1)S(1)} collective-permute-done((bf16[2,1616,128]{2,1,0:T(8,128)(2,1)}, bf16[2,1616,128]{2,1,0:T(8,128)(2,1)S(1)}, u32[]{:S(2)}, u32[]{:S(2)}) %collective-permute-start.8) | collective-permute-done | bytes 827424 | tf_op jit(solution)/shard_map/ppermute | solution.py:377
  145.5 38.7 %collective-permute-done.9 = bf16[1616,128]{1,0:T(8,128)(2,1)S(1)} collective-permute-done((bf16[1616,128]{1,0:T(8,128)(2,1)S(1)}, bf16[1616,128]{1,0:T(8,128)(2,1)S(1)}, u32[]{:S(2)}, u32[]{:S(2)}) %collective-permute-start.9) | collective-permute-done | bytes 413728 | tf_op jit(solution)/shard_map/ppermute | solution.py:377
  184.2 0.9 fusion.3
  185.0 0.9 fusion.4
  186.0 1.4 copy-done
  187.3 2.8 %collect_2.1 = (bf16[128,4096]{1,0:T(8,128)(2,1)}, bf16[128,4096]{1,0:T(8,128)(2,1)}) custom-call(s32[4,32]{1,0:T(4,128)} %bitcast.14, bf16[8,2,2,32,1024]{4,3,2,1,0:T(8,128)(2,1)} %copy-done, bf16[128,4096]{1,0:T(8,128)(2,1)} %get-tuple-element.70.refs_0_, bf16[128,4096]{1,0:T(8,128)(2,1)} %get-tuple-element.71.refs_1_), custom_call_target="tpu_custom_call", output_to_operand_aliasing={{0}: (2, {}), {1}: (3, {})} | custom-call | bytes 4194304 | tf_op jit(solution)/shard_map/collect_2/pallas_call | solution.py:453
  (36 shorter events, 0.7 us)
Async XLA Ops:
  3.5 12.0 %collective-permute-start = (bf16[2,2,32,1024]{3,2,1,0:T(8,128)(2,1)}, bf16[2,2,32,1024]{3,2,1,0:T(8,128)(2,1)S(1)}, u32[]{:S(2)}, u32[]{:S(2)}) collective-permute-start(bf16[2,2,32,1024]{3,2,1,0:T(8,128)(2,1)} %get-tuple-element.44), channel_id=1, source_target_pairs={{0,1},{1,0},{2,3},{3,2},{4,5},{5,4},{6,7},{7,6},{8,9},{9,8},{10,11... | collective-permute-start | bytes 786440 | tf_op jit(solution)/shard_map/ppermute | solution.py:377
  4.0 11.5 %collective-permute-start.1 = (bf16[2,2,32,1024]{3,2,1,0:T(8,128)(2,1)}, bf16[2,2,32,1024]{3,2,1,0:T(8,128)(2,1)S(1)}, u32[]{:S(2)}, u32[]{:S(2)}) collective-permute-start(bf16[2,2,32,1024]{3,2,1,0:T(8,128)(2,1)} %get-tuple-element.45), channel_id=1, source_target_pairs={{0,2},{1,3},{2,0},{3,1},{4,6},{5,7},{6,4},{7,5},{8,10},{9,11},{10,... | collective-permute-start | bytes 786440 | tf_op jit(solution)/shard_map/ppermute | solution.py:377
  6.5 12.5 %collective-permute-start.2 = (bf16[2,2,32,1024]{3,2,1,0:T(8,128)(2,1)}, bf16[2,2,32,1024]{3,2,1,0:T(8,128)(2,1)S(1)}, u32[]{:S(2)}, u32[]{:S(2)}) collective-permute-start(bf16[2,2,32,1024]{3,2,1,0:T(8,128)(2,1)} %get-tuple-element.46), channel_id=1, source_target_pairs={{0,3},{1,2},{2,1},{3,0},{4,7},{5,6},{6,5},{7,4},{8,11},{9,10},{10,... | collective-permute-start | bytes 786440 | tf_op jit(solution)/shard_map/ppermute | solution.py:377
  6.6 12.4 %collective-permute-start.3 = (bf16[2,2,32,1024]{3,2,1,0:T(8,128)(2,1)}, bf16[2,2,32,1024]{3,2,1,0:T(8,128)(2,1)S(1)}, u32[]{:S(2)}, u32[]{:S(2)}) collective-permute-start(bf16[2,2,32,1024]{3,2,1,0:T(8,128)(2,1)} %get-tuple-element.47), channel_id=1, source_target_pairs={{0,4},{1,5},{2,6},{3,7},{4,0},{5,1},{6,2},{7,3},{8,12},{9,13},{10,... | collective-permute-start | bytes 786440 | tf_op jit(solution)/shard_map/ppermute | solution.py:377
  15.5 3.6 %copy-start.6 = (bf16[2,2,32,1024]{3,2,1,0:T(8,128)(2,1)}, bf16[2,2,32,1024]{3,2,1,0:T(8,128)(2,1)S(1)}, u32[]{:S(2)}) copy-start(bf16[2,2,32,1024]{3,2,1,0:T(8,128)(2,1)S(1)} %collective-permute-done.refs_1_) | copy-start | bytes 786436
  15.5 3.5 %copy-start.7 = (bf16[2,2,32,1024]{3,2,1,0:T(8,128)(2,1)}, bf16[2,2,32,1024]{3,2,1,0:T(8,128)(2,1)S(1)}, u32[]{:S(2)}) copy-start(bf16[2,2,32,1024]{3,2,1,0:T(8,128)(2,1)S(1)} %collective-permute-done.1.refs_2_) | copy-start | bytes 786436
  19.0 0.7 copy-start.8
  19.0 0.8 copy-start.10
  19.0 7.9 %copy-start.9 = (bf16[2,2,32,1024]{3,2,1,0:T(8,128)(2,1)S(1)}, bf16[2,2,32,1024]{3,2,1,0:T(8,128)(2,1)}, u32[]{:S(2)}) copy-start(bf16[2,2,32,1024]{3,2,1,0:T(8,128)(2,1)} %get-tuple-element.56) | copy-start | bytes 786436
  19.8 67.3 %all-to-all-start.1 = ((bf16[8,2,2,32,1024]{4,3,2,1,0:T(8,128)(2,1)}), bf16[8,2,2,32,1024]{4,3,2,1,0:T(8,128)(2,1)S(1)}, u32[]{:S(2)}, u32[]{:S(2)}) async-start(bf16[8,2,2,32,1024]{4,3,2,1,0:T(8,128)(2,1)} %get-tuple-element.58), calls=%async_computation.1 | async-start | bytes 4194304 | tf_op jit(solution)/shard_map/all_to_all | solution.py:470
  23.6 42.1 %collective-permute-start.4 = (bf16[2,2,32,1024]{3,2,1,0:T(8,128)(2,1)}, bf16[2,2,32,1024]{3,2,1,0:T(8,128)(2,1)S(1)}, u32[]{:S(2)}, u32[]{:S(2)}) collective-permute-start(bf16[2,2,32,1024]{3,2,1,0:T(8,128)(2,1)} %get-tuple-element.54), channel_id=1, source_target_pairs={{0,5},{1,4},{2,7},{3,6},{4,1},{5,0},{6,3},{7,2},{8,13},{9,12},{10,... | collective-permute-start | bytes 786440 | tf_op jit(solution)/shard_map/ppermute | solution.py:377
  25.4 40.3 %collective-permute-start.5 = (bf16[2,2,32,1024]{3,2,1,0:T(8,128)(2,1)}, bf16[2,2,32,1024]{3,2,1,0:T(8,128)(2,1)S(1)}, u32[]{:S(2)}, u32[]{:S(2)}) collective-permute-start(bf16[2,2,32,1024]{3,2,1,0:T(8,128)(2,1)} %get-tuple-element.55), channel_id=1, source_target_pairs={{0,6},{1,7},{2,4},{3,5},{4,2},{5,3},{6,0},{7,1},{8,14},{9,15},{10,... | collective-permute-start | bytes 786440 | tf_op jit(solution)/shard_map/ppermute | solution.py:377
  26.9 38.8 %collective-permute-start.6 = (bf16[2,2,32,1024]{3,2,1,0:T(8,128)(2,1)S(1)}, bf16[2,2,32,1024]{3,2,1,0:T(8,128)(2,1)S(1)}, u32[]{:S(2)}, u32[]{:S(2)}) collective-permute-start(bf16[2,2,32,1024]{3,2,1,0:T(8,128)(2,1)S(1)} %copy-done.9), channel_id=1, source_target_pairs={{0,7},{1,6},{2,5},{3,4},{4,3},{5,2},{6,1},{7,0},{8,15},{9,14},{10,... | collective-permute-start | bytes 786440 | tf_op jit(solution)/shard_map/ppermute | solution.py:377
  65.7 0.7 copy-start.11
  65.7 0.8 copy-start.12
  65.7 0.9 copy-start.13
  87.1 1.4 copy-start.2
  87.1 8.0 %copy-start.5 = (bf16[1616,128]{1,0:T(8,128)(2,1)S(1)}, bf16[1616,128]{1,0:T(8,128)(2,1)}, u32[]{:S(2)}) copy-start(bf16[1616,128]{1,0:T(8,128)(2,1)} %get-tuple-element.62) | copy-start | bytes 1241092
  88.5 33.2 %all-to-all-start = ((bf16[8,2,2,32,1024]{4,3,2,1,0:T(8,128)(2,1)}), bf16[8,2,2,32,1024]{4,3,2,1,0:T(8,128)(2,1)S(1)}, u32[]{:S(2)}, u32[]{:S(2)}) async-start(bf16[8,2,2,32,1024]{4,3,2,1,0:T(8,128)(2,1)} %get-tuple-element.57), calls=%async_computation | async-start | bytes 4194304 | tf_op jit(solution)/shard_map/all_to_all | solution.py:470
  95.1 22.6 %collective-permute-start.7 = (bf16[1616,128]{1,0:T(8,128)(2,1)S(1)}, bf16[1616,128]{1,0:T(8,128)(2,1)S(1)}, u32[]{:S(2)}, u32[]{:S(2)}) collective-permute-start(bf16[1616,128]{1,0:T(8,128)(2,1)S(1)} %copy-done.5), channel_id=1, source_target_pairs={{0,8},{8,0},{16,24},{24,16},{1,9},{9,1},{17,25},{25,17},{2,10},{10... | collective-permute-start | bytes 1241096 | tf_op jit(solution)/shard_map/ppermute | solution.py:377
  96.9 21.2 %copy-start.4 = (bf16[1616,128]{1,0:T(8,128)(2,1)S(1)}, bf16[1616,128]{1,0:T(8,128)(2,1)}, u32[]{:S(2)}) copy-start(bf16[1616,128]{1,0:T(8,128)(2,1)} %get-tuple-element.65) | copy-start | bytes 1241092
  117.7 27.6 %collective-permute-start.8 = (bf16[2,1616,128]{2,1,0:T(8,128)(2,1)}, bf16[2,1616,128]{2,1,0:T(8,128)(2,1)S(1)}, u32[]{:S(2)}, u32[]{:S(2)}) collective-permute-start(bf16[2,1616,128]{2,1,0:T(8,128)(2,1)} %get-tuple-element.75), channel_id=1, source_target_pairs={{0,8},{8,0},{16,24},{24,16},{1,9},{9,1},{17,25},{25,17},{2,10},{10... | collective-permute-start | bytes 2482184 | tf_op jit(solution)/shard_map/ppermute | solution.py:377
  121.8 1.4 copy-start.1
  123.1 62.8 %all-to-all-start.2 = ((bf16[8,2,2,32,1024]{4,3,2,1,0:T(8,128)(2,1)}), bf16[8,2,2,32,1024]{4,3,2,1,0:T(8,128)(2,1)S(1)}, u32[]{:S(2)}, u32[]{:S(2)}) async-start(bf16[8,2,2,32,1024]{4,3,2,1,0:T(8,128)(2,1)} %get-tuple-element.68), calls=%async_computation.2 | async-start | bytes 4194304 | tf_op jit(solution)/shard_map/all_to_all | solution.py:470
  126.7 18.6 %copy-start.3 = (bf16[2,1616,128]{2,1,0:T(8,128)(2,1)S(1)}, bf16[2,1616,128]{2,1,0:T(8,128)(2,1)}, u32[]{:S(2)}) copy-start(bf16[2,1616,128]{2,1,0:T(8,128)(2,1)} %get-tuple-element.74) | copy-start | bytes 2482180
  126.7 58.3 %collective-permute-start.11 = (bf16[1616,128]{1,0:T(8,128)(2,1)}, bf16[1616,128]{1,0:T(8,128)(2,1)S(1)}, u32[]{:S(2)}, u32[]{:S(2)}) collective-permute-start(bf16[1616,128]{1,0:T(8,128)(2,1)} %get-tuple-element.59), channel_id=1, source_target_pairs={{0,16},{8,24},{16,0},{24,8},{1,17},{9,25},{17,1},{25,9},{2,18},{10... | collective-permute-start | bytes 1241096 | tf_op jit(solution)/shard_map/ppermute | solution.py:377
  129.5 55.6 %collective-permute-start.10 = (bf16[1616,128]{1,0:T(8,128)(2,1)}, bf16[1616,128]{1,0:T(8,128)(2,1)S(1)}, u32[]{:S(2)}, u32[]{:S(2)}) collective-permute-start(bf16[1616,128]{1,0:T(8,128)(2,1)} %get-tuple-element.77), channel_id=1, source_target_pairs={{0,24},{8,16},{16,8},{24,0},{1,25},{9,17},{17,9},{25,1},{2,26},{10... | collective-permute-start | bytes 1241096 | tf_op jit(solution)/shard_map/ppermute | solution.py:377
  130.9 53.3 %collective-permute-start.9 = (bf16[1616,128]{1,0:T(8,128)(2,1)S(1)}, bf16[1616,128]{1,0:T(8,128)(2,1)S(1)}, u32[]{:S(2)}, u32[]{:S(2)}) collective-permute-start(bf16[1616,128]{1,0:T(8,128)(2,1)S(1)} %add_convert_fusion), channel_id=1, source_target_pairs={{0,16},{8,24},{16,0},{24,8},{1,17},{9,25},{17,1},{25,9},{2,18},{10... | collective-permute-start | bytes 1241096 | tf_op jit(solution)/shard_map/ppermute | solution.py:377
  186.0 1.4 copy-start

commit v8 on v7

--- a/solution.py
+++ b/solution.py
@@ -472,8 +472,7 @@
     first, second = chunks
     received = [xor_permute(array, "enc", k) for k, array in enumerate(route(first, 0))]
     routed, *prepared = route(second, 1)
-    most = len(received) // 2 + 1
-    *received[:most], routed = lax.optimization_barrier((*received[:most], routed))
+    *received, routed = lax.optimization_barrier((*received, routed))
     received_later = exchange(routed)
     butterfly = n_seq == KVH
     returned, *grads = attend(first, 1 + butterfly, received)
@@ -491,6 +490,8 @@
         near = xor_permute(more[0], "seq", 1)
     answer, returned = lax.optimization_barrier((answer, returned))
     answer_later = exchange(returned)
+    if butterfly:
+        answer, *far = lax.optimization_barrier((answer, *far))
     half = collect(first, answer, [])
     attended, grad_queries = collect(second, answer_later, half)
 

time: 191 us -> 154 us (0.81)
  the two profiles are of different devices: /device:TPU:0 before, /device:TPU:2 now
where the time goes in v8:
time: 154 us; the launch traced here: 152 us
  Pallas kernels  63.6 us (41%)
  waiting for transfers between devices  54.3 us (35%)
  starting transfers between devices  26.9 us (17%)
  local copies, waits for them, and re-layouts  3.44 us (2%)
  other arithmetic  3.17 us (2%)
    ppermute x12, waiting for transfers between devices, xor_permute(): return lax.ppermute(array, axis, [(i, i ^ k) for i in range(size)])  53 us
    pallas_call x2, Pallas kernels, attend(): pl.pallas_call(functools.partial(attend_kernel, turns, hands, peers, seg_...  48.1 us
    all_to_all x3, starting transfers between devices, exchange(): return lax.all_to_all(array, 'enc', split_axis=0, concat_axis=0, tiled=True)  13.6 us
    ppermute x12, starting transfers between devices, xor_permute(): return lax.ppermute(array, axis, [(i, i ^ k) for i in range(size)])  13.3 us
    pallas_call x2, Pallas kernels, route(): pl.pallas_call(functools.partial(route_kernel, turns, n_seg, seg_rows, to...  9.88 us
    pallas_call x2, Pallas kernels, collect(): pl.pallas_call(functools.partial(collect_kernel, turns, n_seg, seg_rows),...  5.64 us
    unnamed x20, local copies, waits for them, and re-layouts  3.44 us
  transfers between devices with their start and end apart: 15, of which 5 were waited for; matrix products, arithmetic and copies ran while one was open for 2% of the time, Pallas kernels for 38%

profile of v8, /device:TPU:2, one launch (start us, length us, event | category | flops | bytes accessed | tf_op | source)
XLA Modules:
  0.0 152.4 jit_solution(15157677563618240850)
XLA Ops:
  0.6 2.8 %route_0.1 = (bf16[2,2,32,1024]{3,2,1,0:T(8,128)(2,1)}, bf16[2,2,32,1024]{3,2,1,0:T(8,128)(2,1)}, bf16[2,2,32,1024]{3,2,1,0:T(8,128)(2,1)}, bf16[2,2,32,1024]{3,...) custom-call(s32[4,32]{1,0:T(4,128)} %bitcast.9, ...), custom_call_target="tpu_custom_call" | custom-call | bytes 2097152 | tf_op jit(solution)/shard_map/route_0/pallas_call | solution.py:402
  3.5 0.1 collective-permute-start
  3.6 1.8 %collective-permute-start.2 = (bf16[2,2,32,1024]{3,2,1,0:T(8,128)(2,1)}, bf16[2,2,32,1024]{3,2,1,0:T(8,128)(2,1)S(1)}, u32[]{:S(2)}, u32[]{:S(2)}) collective-permute-start(bf16[2,2,32,1024]{3,2,1,0:T(8,128)(2,1)} %get-tuple-element.52), channel_id=1, source_target_pairs={{0,3},{1,2},{2,1},{3,0},{4,7},{5,6},{6,5},{7,4},{8,11},{9,10},{10,... | collective-permute-start | bytes 786440 | tf_op jit(solution)/shard_map/ppermute | solution.py:377
  5.4 1.5 %collective-permute-start.3 = (bf16[2,2,32,1024]{3,2,1,0:T(8,128)(2,1)}, bf16[2,2,32,1024]{3,2,1,0:T(8,128)(2,1)S(1)}, u32[]{:S(2)}, u32[]{:S(2)}) collective-permute-start(bf16[2,2,32,1024]{3,2,1,0:T(8,128)(2,1)} %get-tuple-element.53), channel_id=1, source_target_pairs={{0,4},{1,5},{2,6},{3,7},{4,0},{5,1},{6,2},{7,3},{8,12},{9,13},{10,... | collective-permute-start | bytes 786440 | tf_op jit(solution)/shard_map/ppermute | solution.py:377
  6.9 0.2 collective-permute-start.4
  7.1 1.5 collective-permute-start.5
  8.6 4.3 %collective-permute-done.1.refs_2_ = bf16[2,2,32,1024]{3,2,1,0:T(8,128)(2,1)S(1)} collective-permute-done((bf16[2,2,32,1024]{3,2,1,0:T(8,128)(2,1)}, bf16[2,2,32,1024]{3,2,1,0:T(8,128)(2,1)S(1)}, u32[]{:S(2)}, u32[]{:S(2)}) %collective-permute-start.1) | collective-permute-done | bytes 262176 | tf_op jit(solution)/shard_map/ppermute | solution.py:377
  12.9 0.3 collective-permute-start.6
  13.2 7.1 %route_2.1 = (bf16[8,2,2,32,1024]{4,3,2,1,0:T(8,128)(2,1)}, bf16[4,2,1616,128]{3,2,1,0:T(8,128)(2,1)}, bf16[4,2,128,1616]{3,2,1,0:T(8,128)(2,1)}) custom-call(s32[4,32]{1,0:T(4,128)} %bitcast.10, bf16[128,4096]{1,0:T(8,128)(2,1)} %q_hbm.3, bf16[128,4096]{1,0:T(8,128)(2,1)} %g_hbm.3, bf16[1,1601,512]{2,1,0:T(8,128)(2,1)} %refs_0_.1, bf16[1,1601,512]{2,1,0:T(8,128)(2,1)} %refs_1_.1), custom_call_target="tpu_custom_call" | custom-call | bytes 12582912 | tf_op jit(solution)/shard_map/route_2/pallas_call | solution.py:402
  20.4 10.1 %collective-permute-done.4.refs_5_ = bf16[2,2,32,1024]{3,2,1,0:T(8,128)(2,1)S(1)} collective-permute-done((bf16[2,2,32,1024]{3,2,1,0:T(8,128)(2,1)}, bf16[2,2,32,1024]{3,2,1,0:T(8,128)(2,1)S(1)}, u32[]{:S(2)}, u32[]{:S(2)}) %collective-permute-start.4) | collective-permute-done | bytes 262176 | tf_op jit(solution)/shard_map/ppermute | solution.py:377
  30.5 0.7 copy-done.9
  31.2 4.3 %all-to-all-start.1 = ((bf16[8,2,2,32,1024]{4,3,2,1,0:T(8,128)(2,1)}), bf16[8,2,2,32,1024]{4,3,2,1,0:T(8,128)(2,1)S(1)}, u32[]{:S(2)}, u32[]{:S(2)}) async-start(bf16[8,2,2,32,1024]{4,3,2,1,0:T(8,128)(2,1)} %get-tuple-element.67), calls=%async_computation.1 | async-start | bytes 4194304 | tf_op jit(solution)/shard_map/all_to_all | solution.py:470
  35.5 23.9 %attend_0.1 = (bf16[8,2,2,32,1024]{4,3,2,1,0:T(8,128)(2,1)}, bf16[1616,128]{1,0:T(8,128)(2,1)}, bf16[1616,128]{1,0:T(8,128)(2,1)}, bf16[1616,128]{1,0:T(8,128)(2,1)}, bf16[1616,128]{1,0:T(8,128)(2,1)}) custom-call(s32[4,32]{1,0:T(4,128)} %bitcast.11, bf16[4,2,1616,128]{3,2,1,0:T(8,128)(2,1)} %get-tuple-element.47.caches, ...), custom_call_target="tpu_custom_call" | custom-call | flops 7554465792 | bytes 8388608 | tf_op jit(solution)/shard_map/attend_0/pallas_call | solution.py:422
  59.3 1.3 all-to-all-done.1.refs_0_
  60.6 1.4 copy-done.1
  62.0 5.0 %all-to-all-start = ((bf16[8,2,2,32,1024]{4,3,2,1,0:T(8,128)(2,1)}), bf16[8,2,2,32,1024]{4,3,2,1,0:T(8,128)(2,1)S(1)}, u32[]{:S(2)}, u32[]{:S(2)}) async-start(bf16[8,2,2,32,1024]{4,3,2,1,0:T(8,128)(2,1)} %get-tuple-element.66), calls=%async_computation | async-start | bytes 4194304 | tf_op jit(solution)/shard_map/all_to_all | solution.py:470
  67.0 1.6 %collective-permute-start.7 = (bf16[1616,128]{1,0:T(8,128)(2,1)S(1)}, bf16[1616,128]{1,0:T(8,128)(2,1)S(1)}, u32[]{:S(2)}, u32[]{:S(2)}) collective-permute-start(bf16[1616,128]{1,0:T(8,128)(2,1)S(1)} %copy-done.4), channel_id=1, source_target_pairs={{0,8},{8,0},{16,24},{24,16},{1,9},{9,1},{17,25},{25,17},{2,10},{10... | collective-permute-start | bytes 1241096 | tf_op jit(solution)/shard_map/ppermute | solution.py:377
  68.6 24.2 %attend_2.1 = (bf16[8,2,2,32,1024]{4,3,2,1,0:T(8,128)(2,1)}, bf16[2,1616,128]{2,1,0:T(8,128)(2,1)}, bf16[2,1616,128]{2,1,0:T(8,128)(2,1)}) custom-call(s32[4,32]{1,0:T(4,128)} %bitcast.12, bf16[4,2,1616,128]{3,2,1,0:T(8,128)(2,1)} %get-tuple-element.47.caches, bf16[4,2,128,1616]{3,2,1,0:T(8,128)(2,1)} %get-tuple-element.48.turned_caches, ...), custom_call_target="tpu_custom_call" | custom-call | flops 7554465792 | bytes 8388608 | tf_op jit(solution)/shard_map/attend_2/pallas_call | solution.py:422
  92.8 0.6 collective-permute-start.10
  93.4 2.5 %collective-permute-start.9 = (bf16[1616,128]{1,0:T(8,128)(2,1)}, bf16[1616,128]{1,0:T(8,128)(2,1)}, u32[]{:S(2)}, u32[]{:S(2)}) collective-permute-start(bf16[1616,128]{1,0:T(8,128)(2,1)} %get-tuple-element.68), channel_id=1, source_target_pairs={{0,16},{8,24},{16,0},{24,8},{1,17},{9,25},{17,1},{25,9},{2,18},{10... | collective-permute-start | bytes 1241096 | tf_op jit(solution)/shard_map/ppermute | solution.py:377
  96.0 1.3 collective-permute-start.8
  97.3 0.1 add_convert_fusion
  97.4 1.3 copy-done
  98.7 4.3 %all-to-all-start.2 = ((bf16[8,2,2,32,1024]{4,3,2,1,0:T(8,128)(2,1)}), bf16[8,2,2,32,1024]{4,3,2,1,0:T(8,128)(2,1)}, u32[]{:S(2)}, u32[]{:S(2)}) async-start(bf16[8,2,2,32,1024]{4,3,2,1,0:T(8,128)(2,1)} %get-tuple-element.77), calls=%async_computation.2 | async-start | bytes 4194304 | tf_op jit(solution)/shard_map/all_to_all | solution.py:470
  103.1 1.8 %collective-permute-start.11 = (bf16[1616,128]{1,0:T(8,128)(2,1)S(1)}, bf16[1616,128]{1,0:T(8,128)(2,1)S(1)}, u32[]{:S(2)}, u32[]{:S(2)}) collective-permute-start(bf16[1616,128]{1,0:T(8,128)(2,1)S(1)} %add_convert_fusion), channel_id=1, source_target_pairs={{0,16},{8,24},{16,0},{24,8},{1,17},{9,25},{17,1},{25,9},{2,18},{10... | collective-permute-start | bytes 1241096 | tf_op jit(solution)/shard_map/ppermute | solution.py:377
  104.9 29.4 %collective-permute-done.8 = bf16[1616,128]{1,0:T(8,128)(2,1)} collective-permute-done((bf16[1616,128]{1,0:T(8,128)(2,1)}, bf16[1616,128]{1,0:T(8,128)(2,1)}, u32[]{:S(2)}, u32[]{:S(2)}) %collective-permute-start.8) | collective-permute-done | bytes 413728 | tf_op jit(solution)/shard_map/ppermute | solution.py:377
  134.3 2.8 %collect_0.1 = (bf16[128,4096]{1,0:T(8,128)(2,1)}, bf16[128,4096]{1,0:T(8,128)(2,1)}) custom-call(s32[4,32]{1,0:T(4,128)} %bitcast.13, bf16[8,2,2,32,1024]{4,3,2,1,0:T(8,128)(2,1)} %copy-done), custom_call_target="tpu_custom_call" | custom-call | bytes 4194304 | tf_op jit(solution)/shard_map/collect_0/pallas_call | solution.py:453
  137.1 0.2 add_bitcast_fusion
  137.3 9.2 %collective-permute-done.11 = bf16[1616,128]{1,0:T(8,128)(2,1)S(1)} collective-permute-done((bf16[1616,128]{1,0:T(8,128)(2,1)S(1)}, bf16[1616,128]{1,0:T(8,128)(2,1)S(1)}, u32[]{:S(2)}, u32[]{:S(2)}) %collective-permute-start.11) | collective-permute-done | bytes 413728 | tf_op jit(solution)/shard_map/ppermute | solution.py:377
  146.5 0.9 fusion.3
  147.4 2.0 %fusion.4 = bf16[1,1601,128]{2,1,0:T(8,128)(2,1)} fusion(f32[1616,128]{1,0:T(8,128)S(1)} %get-tuple-element.90, bf16[1616,128]{1,0:T(8,128)(2,1)} %collective-permute-done.9, bf16[1616,128]{1,0:T(8,128)(2,1)} %collective-permute-done.8), kind=kLoop, calls=%fused_computation.9 | loop fusion | flops 1024640 | bytes 2049280 | tf_op jit(solution)/shard_map/broadcast_in_dim | solution.py:501
  149.4 2.8 %collect_2.1 = (bf16[128,4096]{1,0:T(8,128)(2,1)}, bf16[128,4096]{1,0:T(8,128)(2,1)}) custom-call(s32[4,32]{1,0:T(4,128)} %bitcast.14, bf16[8,2,2,32,1024]{4,3,2,1,0:T(8,128)(2,1)} %all-to-all-done.2.returned, bf16[128,4096]{1,0:T(8,128)(2,1)} %get-tuple-element.81.refs_0_, ...), custom_call_target="tpu_custom_call", output_to_operand_aliasing={{0}: (2, {}), {1}: (3, {})} | custom-call | bytes 4194304 | tf_op jit(solution)/shard_map/collect_2/pallas_call | solution.py:453
  (28 shorter events, 0.1 us)
Async XLA Ops:
  3.5 3.6 %collective-permute-start = (bf16[2,2,32,1024]{3,2,1,0:T(8,128)(2,1)}, bf16[2,2,32,1024]{3,2,1,0:T(8,128)(2,1)S(1)}, u32[]{:S(2)}, u32[]{:S(2)}) collective-permute-start(bf16[2,2,32,1024]{3,2,1,0:T(8,128)(2,1)} %get-tuple-element.50), channel_id=1, source_target_pairs={{0,1},{1,0},{2,3},{3,2},{4,5},{5,4},{6,7},{7,6},{8,9},{9,8},{10,11... | collective-permute-start | bytes 786440 | tf_op jit(solution)/shard_map/ppermute | solution.py:377
  3.5 9.4 %collective-permute-start.1 = (bf16[2,2,32,1024]{3,2,1,0:T(8,128)(2,1)}, bf16[2,2,32,1024]{3,2,1,0:T(8,128)(2,1)S(1)}, u32[]{:S(2)}, u32[]{:S(2)}) collective-permute-start(bf16[2,2,32,1024]{3,2,1,0:T(8,128)(2,1)} %get-tuple-element.51), channel_id=1, source_target_pairs={{0,2},{1,3},{2,0},{3,1},{4,6},{5,7},{6,4},{7,5},{8,10},{9,11},{10,... | collective-permute-start | bytes 786440 | tf_op jit(solution)/shard_map/ppermute | solution.py:377
  3.6 16.7 %collective-permute-start.2 = (bf16[2,2,32,1024]{3,2,1,0:T(8,128)(2,1)}, bf16[2,2,32,1024]{3,2,1,0:T(8,128)(2,1)S(1)}, u32[]{:S(2)}, u32[]{:S(2)}) collective-permute-start(bf16[2,2,32,1024]{3,2,1,0:T(8,128)(2,1)} %get-tuple-element.52), channel_id=1, source_target_pairs={{0,3},{1,2},{2,1},{3,0},{4,7},{5,6},{6,5},{7,4},{8,11},{9,10},{10,... | collective-permute-start | bytes 786440 | tf_op jit(solution)/shard_map/ppermute | solution.py:377
  5.4 14.9 %collective-permute-start.3 = (bf16[2,2,32,1024]{3,2,1,0:T(8,128)(2,1)}, bf16[2,2,32,1024]{3,2,1,0:T(8,128)(2,1)S(1)}, u32[]{:S(2)}, u32[]{:S(2)}) collective-permute-start(bf16[2,2,32,1024]{3,2,1,0:T(8,128)(2,1)} %get-tuple-element.53), channel_id=1, source_target_pairs={{0,4},{1,5},{2,6},{3,7},{4,0},{5,1},{6,2},{7,3},{8,12},{9,13},{10,... | collective-permute-start | bytes 786440 | tf_op jit(solution)/shard_map/ppermute | solution.py:377
  6.9 23.5 %collective-permute-start.4 = (bf16[2,2,32,1024]{3,2,1,0:T(8,128)(2,1)}, bf16[2,2,32,1024]{3,2,1,0:T(8,128)(2,1)S(1)}, u32[]{:S(2)}, u32[]{:S(2)}) collective-permute-start(bf16[2,2,32,1024]{3,2,1,0:T(8,128)(2,1)} %get-tuple-element.54), channel_id=1, source_target_pairs={{0,5},{1,4},{2,7},{3,6},{4,1},{5,0},{6,3},{7,2},{8,13},{9,12},{10,... | collective-permute-start | bytes 786440 | tf_op jit(solution)/shard_map/ppermute | solution.py:377
  7.1 13.2 %copy-start.5 = (bf16[2,2,32,1024]{3,2,1,0:T(8,128)(2,1)}, bf16[2,2,32,1024]{3,2,1,0:T(8,128)(2,1)S(1)}, u32[]{:S(2)}) copy-start(bf16[2,2,32,1024]{3,2,1,0:T(8,128)(2,1)S(1)} %collective-permute-done.refs_1_) | copy-start | bytes 786436
  7.1 23.3 %collective-permute-start.5 = (bf16[2,2,32,1024]{3,2,1,0:T(8,128)(2,1)}, bf16[2,2,32,1024]{3,2,1,0:T(8,128)(2,1)}, u32[]{:S(2)}, u32[]{:S(2)}) collective-permute-start(bf16[2,2,32,1024]{3,2,1,0:T(8,128)(2,1)} %get-tuple-element.55), channel_id=1, source_target_pairs={{0,6},{1,7},{2,4},{3,5},{4,2},{5,3},{6,0},{7,1},{8,14},{9,15},{10,... | collective-permute-start | bytes 786440 | tf_op jit(solution)/shard_map/ppermute | solution.py:377
  12.9 7.4 %copy-start.6 = (bf16[2,2,32,1024]{3,2,1,0:T(8,128)(2,1)}, bf16[2,2,32,1024]{3,2,1,0:T(8,128)(2,1)S(1)}, u32[]{:S(2)}) copy-start(bf16[2,2,32,1024]{3,2,1,0:T(8,128)(2,1)S(1)} %collective-permute-done.1.refs_2_) | copy-start | bytes 786436
  12.9 17.5 %collective-permute-start.6 = (bf16[2,2,32,1024]{3,2,1,0:T(8,128)(2,1)}, bf16[2,2,32,1024]{3,2,1,0:T(8,128)(2,1)}, u32[]{:S(2)}, u32[]{:S(2)}) collective-permute-start(bf16[2,2,32,1024]{3,2,1,0:T(8,128)(2,1)} %get-tuple-element.56), channel_id=1, source_target_pairs={{0,7},{1,6},{2,5},{3,4},{4,3},{5,2},{6,1},{7,0},{8,15},{9,14},{10,... | collective-permute-start | bytes 786440 | tf_op jit(solution)/shard_map/ppermute | solution.py:377
  20.3 10.1 %copy-start.7 = (bf16[2,2,32,1024]{3,2,1,0:T(8,128)(2,1)}, bf16[2,2,32,1024]{3,2,1,0:T(8,128)(2,1)S(1)}, u32[]{:S(2)}) copy-start(bf16[2,2,32,1024]{3,2,1,0:T(8,128)(2,1)S(1)} %collective-permute-done.2.refs_3_) | copy-start | bytes 786436
  20.4 10.1 %copy-start.8 = (bf16[2,2,32,1024]{3,2,1,0:T(8,128)(2,1)}, bf16[2,2,32,1024]{3,2,1,0:T(8,128)(2,1)S(1)}, u32[]{:S(2)}) copy-start(bf16[2,2,32,1024]{3,2,1,0:T(8,128)(2,1)S(1)} %collective-permute-done.3.refs_4_) | copy-start | bytes 786436
  30.5 0.7 copy-start.9
  31.2 29.4 %all-to-all-start.1 = ((bf16[8,2,2,32,1024]{4,3,2,1,0:T(8,128)(2,1)}), bf16[8,2,2,32,1024]{4,3,2,1,0:T(8,128)(2,1)S(1)}, u32[]{:S(2)}, u32[]{:S(2)}) async-start(bf16[8,2,2,32,1024]{4,3,2,1,0:T(8,128)(2,1)} %get-tuple-element.67), calls=%async_computation.1 | async-start | bytes 4194304 | tf_op jit(solution)/shard_map/all_to_all | solution.py:470
  60.6 1.4 copy-start.1
  60.6 6.4 %copy-start.4 = (bf16[1616,128]{1,0:T(8,128)(2,1)S(1)}, bf16[1616,128]{1,0:T(8,128)(2,1)}, u32[]{:S(2)}) copy-start(bf16[1616,128]{1,0:T(8,128)(2,1)} %get-tuple-element.71) | copy-start | bytes 1241092
  62.0 35.4 %all-to-all-start = ((bf16[8,2,2,32,1024]{4,3,2,1,0:T(8,128)(2,1)}), bf16[8,2,2,32,1024]{4,3,2,1,0:T(8,128)(2,1)S(1)}, u32[]{:S(2)}, u32[]{:S(2)}) async-start(bf16[8,2,2,32,1024]{4,3,2,1,0:T(8,128)(2,1)} %get-tuple-element.66), calls=%async_computation | async-start | bytes 4194304 | tf_op jit(solution)/shard_map/all_to_all | solution.py:470
  67.0 25.8 %collective-permute-start.7 = (bf16[1616,128]{1,0:T(8,128)(2,1)S(1)}, bf16[1616,128]{1,0:T(8,128)(2,1)S(1)}, u32[]{:S(2)}, u32[]{:S(2)}) collective-permute-start(bf16[1616,128]{1,0:T(8,128)(2,1)S(1)} %copy-done.4), channel_id=1, source_target_pairs={{0,8},{8,0},{16,24},{24,16},{1,9},{9,1},{17,25},{25,17},{2,10},{10... | collective-permute-start | bytes 1241096 | tf_op jit(solution)/shard_map/ppermute | solution.py:377
  68.6 28.7 %copy-start.3 = (bf16[1616,128]{1,0:T(8,128)(2,1)S(1)}, bf16[1616,128]{1,0:T(8,128)(2,1)}, u32[]{:S(2)}) copy-start(bf16[1616,128]{1,0:T(8,128)(2,1)} %get-tuple-element.74) | copy-start | bytes 1241092
  92.8 44.3 %collective-permute-start.10 = (bf16[2,1616,128]{2,1,0:T(8,128)(2,1)}, bf16[2,1616,128]{2,1,0:T(8,128)(2,1)S(1)}, u32[]{:S(2)}, u32[]{:S(2)}) collective-permute-start(bf16[2,1616,128]{2,1,0:T(8,128)(2,1)} %get-tuple-element.86), channel_id=1, source_target_pairs={{0,8},{8,0},{16,24},{24,16},{1,9},{9,1},{17,25},{25,17},{2,10},{10... | collective-permute-start | bytes 2482184 | tf_op jit(solution)/shard_map/ppermute | solution.py:377
  93.4 40.8 %collective-permute-start.9 = (bf16[1616,128]{1,0:T(8,128)(2,1)}, bf16[1616,128]{1,0:T(8,128)(2,1)}, u32[]{:S(2)}, u32[]{:S(2)}) collective-permute-start(bf16[1616,128]{1,0:T(8,128)(2,1)} %get-tuple-element.68), channel_id=1, source_target_pairs={{0,16},{8,24},{16,0},{24,8},{1,17},{9,25},{17,1},{25,9},{2,18},{10... | collective-permute-start | bytes 1241096 | tf_op jit(solution)/shard_map/ppermute | solution.py:377
  96.0 38.3 %collective-permute-start.8 = (bf16[1616,128]{1,0:T(8,128)(2,1)}, bf16[1616,128]{1,0:T(8,128)(2,1)}, u32[]{:S(2)}, u32[]{:S(2)}) collective-permute-start(bf16[1616,128]{1,0:T(8,128)(2,1)} %get-tuple-element.79), channel_id=1, source_target_pairs={{0,24},{8,16},{16,8},{24,0},{1,25},{9,17},{17,9},{25,1},{2,26},{10... | collective-permute-start | bytes 1241096 | tf_op jit(solution)/shard_map/ppermute | solution.py:377
  97.4 1.3 copy-start
  98.7 50.7 %all-to-all-start.2 = ((bf16[8,2,2,32,1024]{4,3,2,1,0:T(8,128)(2,1)}), bf16[8,2,2,32,1024]{4,3,2,1,0:T(8,128)(2,1)}, u32[]{:S(2)}, u32[]{:S(2)}) async-start(bf16[8,2,2,32,1024]{4,3,2,1,0:T(8,128)(2,1)} %get-tuple-element.77), calls=%async_computation.2 | async-start | bytes 4194304 | tf_op jit(solution)/shard_map/all_to_all | solution.py:470
  103.1 34.0 %copy-start.2 = (bf16[2,1616,128]{2,1,0:T(8,128)(2,1)S(1)}, bf16[2,1616,128]{2,1,0:T(8,128)(2,1)}, u32[]{:S(2)}) copy-start(bf16[2,1616,128]{2,1,0:T(8,128)(2,1)} %get-tuple-element.85) | copy-start | bytes 2482180
  103.1 43.4 %collective-permute-start.11 = (bf16[1616,128]{1,0:T(8,128)(2,1)S(1)}, bf16[1616,128]{1,0:T(8,128)(2,1)S(1)}, u32[]{:S(2)}, u32[]{:S(2)}) collective-permute-start(bf16[1616,128]{1,0:T(8,128)(2,1)S(1)} %add_convert_fusion), channel_id=1, source_target_pairs={{0,16},{8,24},{16,0},{24,8},{1,17},{9,25},{17,1},{25,9},{2,18},{10... | collective-permute-start | bytes 1241096 | tf_op jit(solution)/shard_map/ppermute | solution.py:377

commit v9 on v8

--- a/solution.py
+++ b/solution.py
@@ -19,6 +19,8 @@
 LOWEST = -3.0e38
 PER_CHUNK = 2
 VMEM_BYTES = 58 << 20
+KERNEL_BYTES = 40 << 20
+SPARE = 8
 ANY = pl.BlockSpec(memory_space=pl.ANY)
 SMEM = pl.BlockSpec(memory_space=pltpu.SMEM)
 VMEM = pl.BlockSpec(memory_space=pltpu.VMEM)
@@ -30,9 +32,8 @@
     return turn
 
 
-def route_kernel(turns, n_seg, seg_rows, tokens, reads, q_hbm, g_hbm, *refs):
-    stage, in_sems, out_sems = refs[-3:]
-    apart = len(refs) > 8
+def route_kernel(turns, apart, n_seg, seg_rows, tokens, reads, q_hbm, g_hbm, *refs):
+    stage, in_sems, out_sems, *more = refs[-3:] if apart else refs[-6:]
     me = lax.axis_index("enc")
     row = lax.axis_index("seq") * lax.axis_size("enc") + me
     arriving = [[] for _ in range(n_seg)]
@@ -68,8 +69,17 @@
         else:
             leaving(r, refs[2].at[reads[r, row]]).start()
     if not apart:
-        k_in, v_in, _, straight, turned = refs[:5]
+        k_in, v_in, _, *targets = refs[:5]
+        straight, turned, cache_sems = more
         prepare(tokens, k_in, v_in, straight, turned)
+        copies = [
+            pltpu.make_async_copy(source, target.at[pl.ds(0, KVH)], cache_sems.at[i])
+            for i, (source, target) in enumerate(((straight, targets[0]), (turned, targets[1])))
+        ]
+        for copy in copies:
+            copy.start()
+        for copy in copies:
+            copy.wait()
     for r in range(n_seg):
         leaving(r, refs[0] if apart else refs[2].at[0]).wait()
 
@@ -393,22 +403,28 @@
     part = jax.ShapeDtypeStruct((PER_CHUNK, 2, seg_rows, WIDTH), bf16)
 
     caches = [
-        jax.ShapeDtypeStruct((KVH, 2, padded, HD), bf16),
-        jax.ShapeDtypeStruct((KVH, 2, HD, padded), bf16),
+        jax.ShapeDtypeStruct((KVH * SPARE, 2, padded, HD), bf16),
+        jax.ShapeDtypeStruct((KVH * SPARE, 2, HD, padded), bf16),
     ]
 
     def route(turns, prepares):
         outputs = [message] + caches if prepares else [part] * peers
         return pl.pallas_call(
-            functools.partial(route_kernel, turns, n_seg, seg_rows, tokens),
+            functools.partial(route_kernel, turns, not prepares, n_seg, seg_rows, tokens),
             out_shape=outputs,
             in_specs=[SMEM, ANY, ANY] + [VMEM] * 2 * prepares,
-            out_specs=[ANY, VMEM, VMEM] if prepares else [ANY] * peers,
+            out_specs=[ANY] * len(outputs),
             scratch_shapes=[
                 pltpu.VMEM((n_seg, PER_CHUNK, 2, seg_rows, WIDTH), bf16),
                 pltpu.SemaphoreType.DMA((n_seg, PER_CHUNK, 2)),
                 pltpu.SemaphoreType.DMA((n_seg,)),
-            ],
+            ]
+            + [
+                pltpu.VMEM((KVH, 2, padded, HD), bf16),
+                pltpu.VMEM((KVH, 2, HD, padded), bf16),
+                pltpu.SemaphoreType.DMA((2,)),
+            ]
+            * prepares,
             compiler_params=pltpu.CompilerParams(vmem_limit_bytes=VMEM_BYTES),
             cost_estimate=pl.CostEstimate(
                 flops=0, bytes_accessed=(2 + 10 * prepares) << 20, transcendentals=0
@@ -440,7 +456,7 @@
                 pltpu.SemaphoreType.DMA((len(turns), slots)),
                 pltpu.SemaphoreType.DMA((len(turns), 2)),
             ],
-            compiler_params=pltpu.CompilerParams(vmem_limit_bytes=VMEM_BYTES),
+            compiler_params=pltpu.CompilerParams(vmem_limit_bytes=KERNEL_BYTES),
             cost_estimate=pl.CostEstimate(
                 flops=12 * work, bytes_accessed=8 << 20, transcendentals=slots * lanes * tokens
             ),
@@ -461,7 +477,7 @@
                 pltpu.SemaphoreType.DMA((PER_CHUNK, 2, n_seg)),
                 pltpu.SemaphoreType.DMA((PER_CHUNK, 2)),
             ],
-            compiler_params=pltpu.CompilerParams(vmem_limit_bytes=VMEM_BYTES),
+            compiler_params=pltpu.CompilerParams(vmem_limit_bytes=KERNEL_BYTES),
             cost_estimate=pl.CostEstimate(flops=0, bytes_accessed=4 << 20, transcendentals=0),
             name=f"collect_{turns[0]}",
         )(by_segment, returned, *before)
@@ -475,29 +491,27 @@
     *received, routed = lax.optimization_barrier((*received, routed))
     received_later = exchange(routed)
     butterfly = n_seq == KVH
-    returned, *grads = attend(first, 1 + butterfly, received)
+    returned, *grads = attend(first, 1, received)
     answer = exchange(returned)
     if butterfly:
         passed = xor_permute(grads[0], "seq", 1)
-        far = [xor_permute(grads[1], "seq", 3), xor_permute(grads[3], "seq", 2)]
-    received_later, grads[-1] = lax.optimization_barrier((received_later, grads[-1]))
+    received_later, grads[1] = lax.optimization_barrier((received_later, grads[1]))
     returned, *more = attend(second, 1, [received_later])
-    if butterfly:
-        passed, grads[2], more[0] = lax.optimization_barrier((passed, grads[2], more[0]))
-        pair = (grads[2].astype(f32) + passed.astype(f32)).astype(bf16)
-        returned, pair = lax.optimization_barrier((returned, pair))
-        pair = xor_permute(pair, "seq", 2)
-        near = xor_permute(more[0], "seq", 1)
     answer, returned = lax.optimization_barrier((answer, returned))
     answer_later = exchange(returned)
     if butterfly:
-        answer, *far = lax.optimization_barrier((answer, *far))
+        passed, grads[1], more[0] = lax.optimization_barrier((passed, grads[1], more[0]))
+        pair = (grads[1].astype(f32) + passed.astype(f32)).astype(bf16)
+        pair = xor_permute(pair, "seq", 2)
+        near = xor_permute(more[0], "seq", 1)
     half = collect(first, answer, [])
     attended, grad_queries = collect(second, answer_later, half)
 
     if butterfly:
-        terms = [[more[1][0], near[0], pair], [more[1][1], near[1], *far]]
-        summed = [sum(term.astype(f32) for term in ones)[:tokens].astype(bf16) for ones in terms]
+        summed = [
+            sum(term[j, :tokens].astype(f32) for term in (more[1], near, pair)).astype(bf16)
+            for j in range(2)
+        ]
         return attended, grad_queries, summed[0][None], summed[1][None]
     joined = jnp.concatenate(grads + more, axis=2)[:, :tokens]
     summed = lax.psum_scatter(joined, "seq", scatter_dimension=2, tiled=True)

time: 154 us -> 160 us (1.039)
  the two profiles are of different devices: /device:TPU:2 before, /device:TPU:0 now
where the time goes in v9:
time: 160 us; the launch traced here: 159 us
  Pallas kernels  69.5 us (43%)
  waiting for transfers between devices  44.6 us (28%)
  starting transfers between devices  26.2 us (16%)
  local copies, waits for them, and re-layouts  15.3 us (10%)
  other arithmetic  2.7 us (2%)
    pallas_call x2, Pallas kernels, attend(): pl.pallas_call(functools.partial(attend_kernel, turns, hands, peers, seg_...  53.9 us
    ppermute x10, waiting for transfers between devices, xor_permute(): return lax.ppermute(array, axis, [(i, i ^ k) for i in range(size)])  44.6 us
    unnamed x42, local copies, waits for them, and re-layouts  15.3 us
    ppermute x10, starting transfers between devices, xor_permute(): return lax.ppermute(array, axis, [(i, i ^ k) for i in range(size)])  14 us
    all_to_all x3, starting transfers between devices, exchange(): return lax.all_to_all(array, 'enc', split_axis=0, concat_axis=0, tiled=True)  12.1 us
    pallas_call x2, Pallas kernels, route(): pl.pallas_call(functools.partial(route_kernel, turns, not prepares, n_seg...  9.84 us
    pallas_call x2, Pallas kernels, collect(): pl.pallas_call(functools.partial(collect_kernel, turns, n_seg, seg_rows),...  5.77 us
  transfers between devices with their start and end apart: 13, of which 4 were waited for; matrix products, arithmetic and copies ran while one was open for 2% of the time, Pallas kernels for 40%

profile of v9, /device:TPU:0, one launch (start us, length us, event | category | flops | bytes accessed | tf_op | source)
XLA Modules:
  0.0 159.2 jit_solution(15073009715328309983)
XLA Ops:
  0.6 2.8 %route_0.1 = (bf16[2,2,32,1024]{3,2,1,0:T(8,128)(2,1)}, bf16[2,2,32,1024]{3,2,1,0:T(8,128)(2,1)}, bf16[2,2,32,1024]{3,2,1,0:T(8,128)(2,1)}, bf16[2,2,32,1024]{3,...) custom-call(s32[4,32]{1,0:T(4,128)} %bitcast.1, ...), custom_call_target="tpu_custom_call" | custom-call | bytes 2097152 | tf_op jit(solution)/shard_map/route_0/pallas_call | solution.py:412
  4.0 2.6 %collective-permute-start.1 = (bf16[2,2,32,1024]{3,2,1,0:T(8,128)(2,1)}, bf16[2,2,32,1024]{3,2,1,0:T(8,128)(2,1)S(1)}, u32[]{:S(2)}, u32[]{:S(2)}) collective-permute-start(bf16[2,2,32,1024]{3,2,1,0:T(8,128)(2,1)} %get-tuple-element.45), channel_id=1, source_target_pairs={{0,2},{1,3},{2,0},{3,1},{4,6},{5,7},{6,4},{7,5},{8,10},{9,11},{10,... | collective-permute-start | bytes 786440 | tf_op jit(solution)/shard_map/ppermute | solution.py:387
  6.6 1.8 %collective-permute-start.3 = (bf16[2,2,32,1024]{3,2,1,0:T(8,128)(2,1)}, bf16[2,2,32,1024]{3,2,1,0:T(8,128)(2,1)S(1)}, u32[]{:S(2)}, u32[]{:S(2)}) collective-permute-start(bf16[2,2,32,1024]{3,2,1,0:T(8,128)(2,1)} %get-tuple-element.47), channel_id=1, source_target_pairs={{0,4},{1,5},{2,6},{3,7},{4,0},{5,1},{6,2},{7,3},{8,12},{9,13},{10,... | collective-permute-start | bytes 786440 | tf_op jit(solution)/shard_map/ppermute | solution.py:387
  8.4 2.6 %collective-permute-start.5 = (bf16[2,2,32,1024]{3,2,1,0:T(8,128)(2,1)}, bf16[2,2,32,1024]{3,2,1,0:T(8,128)(2,1)S(1)}, u32[]{:S(2)}, u32[]{:S(2)}) collective-permute-start(bf16[2,2,32,1024]{3,2,1,0:T(8,128)(2,1)} %get-tuple-element.49), channel_id=1, source_target_pairs={{0,6},{1,7},{2,4},{3,5},{4,2},{5,3},{6,0},{7,1},{8,14},{9,15},{10,... | collective-permute-start | bytes 786440 | tf_op jit(solution)/shard_map/ppermute | solution.py:387
  11.0 2.9 %collective-permute-done.1.refs_2_ = bf16[2,2,32,1024]{3,2,1,0:T(8,128)(2,1)S(1)} collective-permute-done((bf16[2,2,32,1024]{3,2,1,0:T(8,128)(2,1)}, bf16[2,2,32,1024]{3,2,1,0:T(8,128)(2,1)S(1)}, u32[]{:S(2)}, u32[]{:S(2)}) %collective-permute-start.1) | collective-permute-done | bytes 262176 | tf_op jit(solution)/shard_map/ppermute | solution.py:387
  14.6 1.7 %collective-permute-start.6 = (bf16[2,2,32,1024]{3,2,1,0:T(8,128)(2,1)}, bf16[2,2,32,1024]{3,2,1,0:T(8,128)(2,1)S(1)}, u32[]{:S(2)}, u32[]{:S(2)}) collective-permute-start(bf16[2,2,32,1024]{3,2,1,0:T(8,128)(2,1)} %get-tuple-element.50), channel_id=1, source_target_pairs={{0,7},{1,6},{2,5},{3,4},{4,3},{5,2},{6,1},{7,0},{8,15},{9,14},{10,... | collective-permute-start | bytes 786440 | tf_op jit(solution)/shard_map/ppermute | solution.py:387
  16.3 7.0 %route_2.1 = (bf16[8,2,2,32,1024]{4,3,2,1,0:T(8,128)(2,1)}, bf16[32,2,1616,128]{3,2,1,0:T(8,128)(2,1)}, bf16[32,2,128,1616]{3,2,1,0:T(8,128)(2,1)}) custom-call(s32[4,32]{1,0:T(4,128)} %bitcast.2, bf16[128,4096]{1,0:T(8,128)(2,1)} %q_hbm.3, bf16[128,4096]{1,0:T(8,128)(2,1)} %g_hbm.3, bf16[1,1601,512]{2,1,0:T(8,128)(2,1)} %refs_0_.1, ...), custom_call_target="tpu_custom_call" | custom-call | bytes 12582912 | tf_op jit(solution)/shard_map/route_2/pallas_call | solution.py:412
  24.8 6.8 %collective-permute-done.4.refs_5_ = bf16[2,2,32,1024]{3,2,1,0:T(8,128)(2,1)S(1)} collective-permute-done((bf16[2,2,32,1024]{3,2,1,0:T(8,128)(2,1)}, bf16[2,2,32,1024]{3,2,1,0:T(8,128)(2,1)S(1)}, u32[]{:S(2)}, u32[]{:S(2)}) %collective-permute-start.4) | collective-permute-done | bytes 262176 | tf_op jit(solution)/shard_map/ppermute | solution.py:387
  33.7 4.2 %all-to-all-start.1 = ((bf16[8,2,2,32,1024]{4,3,2,1,0:T(8,128)(2,1)}), bf16[8,2,2,32,1024]{4,3,2,1,0:T(8,128)(2,1)S(1)}, u32[]{:S(2)}, u32[]{:S(2)}) async-start(bf16[8,2,2,32,1024]{4,3,2,1,0:T(8,128)(2,1)} %get-tuple-element.61), calls=%async_computation.1 | async-start | bytes 4194304 | tf_op jit(solution)/shard_map/all_to_all | solution.py:486
  37.9 0.9 copy-done.6
  38.9 0.9 copy-done.8
  39.8 0.9 copy-done.10
  40.8 0.9 copy-done.12
  41.7 0.9 copy-done.14
  42.7 0.9 copy-done.16
  43.6 26.8 %attend_0.1 = (bf16[8,2,2,32,1024]{4,3,2,1,0:T(8,128)(2,1)S(1)}, bf16[2,1616,128]{2,1,0:T(8,128)(2,1)S(1)}, bf16[2,1616,128]{2,1,0:T(8,128)(2,1)S(1)}) custom-call(s32[4,32]{1,0:T(4,128)S(1)} %bitcast.3, bf16[32,2,1616,128]{3,2,1,0:T(8,128)(2,1)} %get-tuple-element.41.caches, bf16[32,2,128,1616]{3,2,1,0:T(8,128)(2,1)} %get-tuple-element.42.turned_caches, ...), custom_call_target="tpu_custom_call" | custom-call | flops 7554465792 | bytes 8388608 | tf_op jit(solution)/shard_map/attend_0/pallas_call | solution.py:438
  70.4 1.3 copy-done.1
  71.7 0.9 copy-done.18
  72.6 4.4 %all-to-all-start = ((bf16[8,2,2,32,1024]{4,3,2,1,0:T(8,128)(2,1)}), bf16[8,2,2,32,1024]{4,3,2,1,0:T(8,128)(2,1)}, u32[]{:S(2)}, u32[]{:S(2)}) async-start(bf16[8,2,2,32,1024]{4,3,2,1,0:T(8,128)(2,1)} %copy-done.1), calls=%async_computation | async-start | bytes 4194304 | tf_op jit(solution)/shard_map/all_to_all | solution.py:486
  77.0 1.7 %collective-permute-start.7 = (bf16[2,1616,128]{2,1,0:T(8,128)(2,1)}, bf16[2,1616,128]{2,1,0:T(8,128)(2,1)}, u32[]{:S(2)}, u32[]{:S(2)}) collective-permute-start(bf16[2,1616,128]{2,1,0:T(8,128)(2,1)} %copy-done.18), channel_id=1, source_target_pairs={{0,8},{8,0},{16,24},{24,16},{1,9},{9,1},{17,25},{25,17},{2,10},{10... | collective-permute-start | bytes 2482184 | tf_op jit(solution)/shard_map/ppermute | solution.py:387
  78.6 27.1 %attend_2.1 = (bf16[8,2,2,32,1024]{4,3,2,1,0:T(8,128)(2,1)S(1)}, bf16[2,1616,128]{2,1,0:T(8,128)(2,1)S(1)}, bf16[2,1616,128]{2,1,0:T(8,128)(2,1)S(1)}) custom-call(s32[4,32]{1,0:T(4,128)S(1)} %bitcast.4, bf16[32,2,1616,128]{3,2,1,0:T(8,128)(2,1)} %get-tuple-element.41.caches, bf16[32,2,128,1616]{3,2,1,0:T(8,128)(2,1)} %get-tuple-element.42.turned_caches, ...), custom_call_target="tpu_custom_call" | custom-call | flops 7554465792 | bytes 8388608 | tf_op jit(solution)/shard_map/attend_2/pallas_call | solution.py:438
  105.8 1.4 copy-done
  107.1 0.9 copy-done.2
  108.0 0.9 copy-done.19
  108.9 3.6 %all-to-all-start.2 = ((bf16[8,2,2,32,1024]{4,3,2,1,0:T(8,128)(2,1)}), bf16[8,2,2,32,1024]{4,3,2,1,0:T(8,128)(2,1)S(1)}, u32[]{:S(2)}, u32[]{:S(2)}) async-start(bf16[8,2,2,32,1024]{4,3,2,1,0:T(8,128)(2,1)} %copy-done), calls=%async_computation.2 | async-start | bytes 4194304 | tf_op jit(solution)/shard_map/all_to_all | solution.py:486
  112.5 1.5 add_convert_fusion
  114.0 2.7 %collective-permute-start.9 = (bf16[2,1616,128]{2,1,0:T(8,128)(2,1)S(1)}, bf16[2,1616,128]{2,1,0:T(8,128)(2,1)S(1)}, u32[]{:S(2)}, u32[]{:S(2)}) collective-permute-start(bf16[2,1616,128]{2,1,0:T(8,128)(2,1)S(1)} %add_convert_fusion), channel_id=1, source_target_pairs={{0,16},{8,24},{16,0},{24,8},{1,17},{9,25},{17,1},{25,9},{2,18},{10... | collective-permute-start | bytes 2482184 | tf_op jit(solution)/shard_map/ppermute | solution.py:387
  117.2 2.7 %collect_0.1 = (bf16[128,4096]{1,0:T(8,128)(2,1)}, bf16[128,4096]{1,0:T(8,128)(2,1)}) custom-call(s32[4,32]{1,0:T(4,128)S(1)} %bitcast.5, bf16[8,2,2,32,1024]{4,3,2,1,0:T(8,128)(2,1)} %all-to-all-done.returned), custom_call_target="tpu_custom_call" | custom-call | bytes 4194304 | tf_op jit(solution)/shard_map/collect_0/pallas_call | solution.py:469
  119.9 33.6 %collective-permute-done.9 = bf16[2,1616,128]{2,1,0:T(8,128)(2,1)S(1)} collective-permute-done((bf16[2,1616,128]{2,1,0:T(8,128)(2,1)S(1)}, bf16[2,1616,128]{2,1,0:T(8,128)(2,1)S(1)}, u32[]{:S(2)}, u32[]{:S(2)}) %collective-permute-start.9) | collective-permute-done | bytes 827424 | tf_op jit(solution)/shard_map/ppermute | solution.py:387
  153.4 1.3 collective-permute-done.8
  154.8 1.2 add_convert_fusion.1
  156.0 3.1 %collect_2.1 = (bf16[128,4096]{1,0:T(8,128)(2,1)}, bf16[128,4096]{1,0:T(8,128)(2,1)}) custom-call(s32[4,32]{1,0:T(4,128)S(1)} %bitcast.6, bf16[8,2,2,32,1024]{4,3,2,1,0:T(8,128)(2,1)S(1)} %all-to-all-done.2.returned, bf16[128,4096]{1,0:T(8,128)(2,1)} %get-tuple-element.67.refs_0_, ...), custom_call_target="tpu_custom_call", output_to_operand_aliasing={{0}: (2, {}), {1}: (3, {})} | custom-call | bytes 4194304 | tf_op jit(solution)/shard_map/collect_2/pallas_call | solution.py:469
  (44 shorter events, 5.3 us)
Async XLA Ops:
  3.5 4.9 %collective-permute-start = (bf16[2,2,32,1024]{3,2,1,0:T(8,128)(2,1)}, bf16[2,2,32,1024]{3,2,1,0:T(8,128)(2,1)S(1)}, u32[]{:S(2)}, u32[]{:S(2)}) collective-permute-start(bf16[2,2,32,1024]{3,2,1,0:T(8,128)(2,1)} %get-tuple-element.44), channel_id=1, source_target_pairs={{0,1},{1,0},{2,3},{3,2},{4,5},{5,4},{6,7},{7,6},{8,9},{9,8},{10,11... | collective-permute-start | bytes 786440 | tf_op jit(solution)/shard_map/ppermute | solution.py:387
  4.0 9.9 %collective-permute-start.1 = (bf16[2,2,32,1024]{3,2,1,0:T(8,128)(2,1)}, bf16[2,2,32,1024]{3,2,1,0:T(8,128)(2,1)S(1)}, u32[]{:S(2)}, u32[]{:S(2)}) collective-permute-start(bf16[2,2,32,1024]{3,2,1,0:T(8,128)(2,1)} %get-tuple-element.45), channel_id=1, source_target_pairs={{0,2},{1,3},{2,0},{3,1},{4,6},{5,7},{6,4},{7,5},{8,10},{9,11},{10,... | collective-permute-start | bytes 786440 | tf_op jit(solution)/shard_map/ppermute | solution.py:387
  6.5 16.8 %collective-permute-start.2 = (bf16[2,2,32,1024]{3,2,1,0:T(8,128)(2,1)}, bf16[2,2,32,1024]{3,2,1,0:T(8,128)(2,1)S(1)}, u32[]{:S(2)}, u32[]{:S(2)}) collective-permute-start(bf16[2,2,32,1024]{3,2,1,0:T(8,128)(2,1)} %get-tuple-element.46), channel_id=1, source_target_pairs={{0,3},{1,2},{2,1},{3,0},{4,7},{5,6},{6,5},{7,4},{8,11},{9,10},{10,... | collective-permute-start | bytes 786440 | tf_op jit(solution)/shard_map/ppermute | solution.py:387
  6.6 17.5 %collective-permute-start.3 = (bf16[2,2,32,1024]{3,2,1,0:T(8,128)(2,1)}, bf16[2,2,32,1024]{3,2,1,0:T(8,128)(2,1)S(1)}, u32[]{:S(2)}, u32[]{:S(2)}) collective-permute-start(bf16[2,2,32,1024]{3,2,1,0:T(8,128)(2,1)} %get-tuple-element.47), channel_id=1, source_target_pairs={{0,4},{1,5},{2,6},{3,7},{4,0},{5,1},{6,2},{7,3},{8,12},{9,13},{10,... | collective-permute-start | bytes 786440 | tf_op jit(solution)/shard_map/ppermute | solution.py:387
  8.4 23.2 %collective-permute-start.4 = (bf16[2,2,32,1024]{3,2,1,0:T(8,128)(2,1)}, bf16[2,2,32,1024]{3,2,1,0:T(8,128)(2,1)S(1)}, u32[]{:S(2)}, u32[]{:S(2)}) collective-permute-start(bf16[2,2,32,1024]{3,2,1,0:T(8,128)(2,1)} %get-tuple-element.48), channel_id=1, source_target_pairs={{0,5},{1,4},{2,7},{3,6},{4,1},{5,0},{6,3},{7,2},{8,13},{9,12},{10,... | collective-permute-start | bytes 786440 | tf_op jit(solution)/shard_map/ppermute | solution.py:387
  8.4 23.9 %collective-permute-start.5 = (bf16[2,2,32,1024]{3,2,1,0:T(8,128)(2,1)}, bf16[2,2,32,1024]{3,2,1,0:T(8,128)(2,1)S(1)}, u32[]{:S(2)}, u32[]{:S(2)}) collective-permute-start(bf16[2,2,32,1024]{3,2,1,0:T(8,128)(2,1)} %get-tuple-element.49), channel_id=1, source_target_pairs={{0,6},{1,7},{2,4},{3,5},{4,2},{5,3},{6,0},{7,1},{8,14},{9,15},{10,... | collective-permute-start | bytes 786440 | tf_op jit(solution)/shard_map/ppermute | solution.py:387
  13.9 0.7 copy-start.5
  14.6 18.4 %collective-permute-start.6 = (bf16[2,2,32,1024]{3,2,1,0:T(8,128)(2,1)}, bf16[2,2,32,1024]{3,2,1,0:T(8,128)(2,1)S(1)}, u32[]{:S(2)}, u32[]{:S(2)}) collective-permute-start(bf16[2,2,32,1024]{3,2,1,0:T(8,128)(2,1)} %get-tuple-element.50), channel_id=1, source_target_pairs={{0,7},{1,6},{2,5},{3,4},{4,3},{5,2},{6,1},{7,0},{8,15},{9,14},{10,... | collective-permute-start | bytes 786440 | tf_op jit(solution)/shard_map/ppermute | solution.py:387
  23.4 0.7 copy-start.7
  24.1 0.7 copy-start.9
  32.3 0.7 copy-start.13
  33.7 4.2 %copy-start.4 = (bf16[2,2,32,1024]{3,2,1,0:T(8,128)(2,1)S(1)}, bf16[2,2,32,1024]{3,2,1,0:T(8,128)(2,1)}, u32[]{:S(2)}) copy-start(bf16[2,2,32,1024]{3,2,1,0:T(8,128)(2,1)} %get-tuple-element.52.refs_0_) | copy-start | bytes 786436
  33.7 4.2 %copy-start.17 = (s32[32,4]{0,1:T(4,128)S(1)}, s32[32,4]{0,1:T(4,128)}, u32[]{:S(2)}) copy-start(s32[32,4]{0,1:T(4,128)} %param.8) | copy-start | bytes 1540
  33.7 38.9 %all-to-all-start.1 = ((bf16[8,2,2,32,1024]{4,3,2,1,0:T(8,128)(2,1)}), bf16[8,2,2,32,1024]{4,3,2,1,0:T(8,128)(2,1)S(1)}, u32[]{:S(2)}, u32[]{:S(2)}) async-start(bf16[8,2,2,32,1024]{4,3,2,1,0:T(8,128)(2,1)} %get-tuple-element.61), calls=%async_computation.1 | async-start | bytes 4194304 | tf_op jit(solution)/shard_map/all_to_all | solution.py:486
  37.9 1.0 copy-start.6
  38.9 0.9 copy-start.8
  39.8 0.9 copy-start.10
  40.8 0.9 copy-start.12
  41.7 0.9 copy-start.14
  42.7 0.9 copy-start.16
  70.4 1.3 copy-start.1
  71.7 0.9 copy-start.18
  72.6 36.3 %all-to-all-start = ((bf16[8,2,2,32,1024]{4,3,2,1,0:T(8,128)(2,1)}), bf16[8,2,2,32,1024]{4,3,2,1,0:T(8,128)(2,1)}, u32[]{:S(2)}, u32[]{:S(2)}) async-start(bf16[8,2,2,32,1024]{4,3,2,1,0:T(8,128)(2,1)} %copy-done.1), calls=%async_computation | async-start | bytes 4194304 | tf_op jit(solution)/shard_map/all_to_all | solution.py:486
  77.0 35.6 %collective-permute-start.7 = (bf16[2,1616,128]{2,1,0:T(8,128)(2,1)}, bf16[2,1616,128]{2,1,0:T(8,128)(2,1)}, u32[]{:S(2)}, u32[]{:S(2)}) collective-permute-start(bf16[2,1616,128]{2,1,0:T(8,128)(2,1)} %copy-done.18), channel_id=1, source_target_pairs={{0,8},{8,0},{16,24},{24,16},{1,9},{9,1},{17,25},{25,17},{2,10},{10... | collective-permute-start | bytes 2482184 | tf_op jit(solution)/shard_map/ppermute | solution.py:387
  105.7 1.4 copy-start
  107.1 0.9 copy-start.2
  108.0 0.9 copy-start.19
  108.9 47.1 %all-to-all-start.2 = ((bf16[8,2,2,32,1024]{4,3,2,1,0:T(8,128)(2,1)}), bf16[8,2,2,32,1024]{4,3,2,1,0:T(8,128)(2,1)S(1)}, u32[]{:S(2)}, u32[]{:S(2)}) async-start(bf16[8,2,2,32,1024]{4,3,2,1,0:T(8,128)(2,1)} %copy-done), calls=%async_computation.2 | async-start | bytes 4194304 | tf_op jit(solution)/shard_map/all_to_all | solution.py:486
  112.5 4.2 %copy-start.20 = (bf16[2,1616,128]{2,1,0:T(8,128)(2,1)S(1)}, bf16[2,1616,128]{2,1,0:T(8,128)(2,1)}, u32[]{:S(2)}) copy-start(bf16[2,1616,128]{2,1,0:T(8,128)(2,1)} %copy-done.19) | copy-start | bytes 2482180
  112.5 42.2 %copy-start.3 = (bf16[2,1616,128]{2,1,0:T(8,128)(2,1)S(1)}, bf16[2,1616,128]{2,1,0:T(8,128)(2,1)}, u32[]{:S(2)}) copy-start(bf16[2,1616,128]{2,1,0:T(8,128)(2,1)} %copy-done.2) | copy-start | bytes 2482180
  114.0 39.4 %collective-permute-start.9 = (bf16[2,1616,128]{2,1,0:T(8,128)(2,1)S(1)}, bf16[2,1616,128]{2,1,0:T(8,128)(2,1)S(1)}, u32[]{:S(2)}, u32[]{:S(2)}) collective-permute-start(bf16[2,1616,128]{2,1,0:T(8,128)(2,1)S(1)} %add_convert_fusion), channel_id=1, source_target_pairs={{0,16},{8,24},{16,0},{24,8},{1,17},{9,25},{17,1},{25,9},{2,18},{10... | collective-permute-start | bytes 2482184 | tf_op jit(solution)/shard_map/ppermute | solution.py:387
  116.7 38.0 %collective-permute-start.8 = (bf16[2,1616,128]{2,1,0:T(8,128)(2,1)S(1)}, bf16[2,1616,128]{2,1,0:T(8,128)(2,1)S(1)}, u32[]{:S(2)}, u32[]{:S(2)}) collective-permute-start(bf16[2,1616,128]{2,1,0:T(8,128)(2,1)S(1)} %copy-done.20), channel_id=1, source_target_pairs={{0,8},{8,0},{16,24},{24,16},{1,9},{9,1},{17,25},{25,17},{2,10},{10... | collective-permute-start | bytes 2482184 | tf_op jit(solution)/shard_map/ppermute | solution.py:387
  (2 other events, 1.4 us)

commit v10 on v9

--- a/solution.py
+++ b/solution.py
@@ -19,8 +19,8 @@
 LOWEST = -3.0e38
 PER_CHUNK = 2
 VMEM_BYTES = 58 << 20
-KERNEL_BYTES = 40 << 20
-SPARE = 8
+KERNEL_BYTES = 58 << 20
+SPARE = 1
 ANY = pl.BlockSpec(memory_space=pl.ANY)
 SMEM = pl.BlockSpec(memory_space=pltpu.SMEM)
 VMEM = pl.BlockSpec(memory_space=pltpu.VMEM)

time: 160 us -> 147 us (0.919)
  Pallas kernels: 69.5 us -> 49.3 us
  waiting for transfers between devices: 44.6 us -> 62.4 us
  local copies, waits for them, and re-layouts: 15.3 us -> 4.82 us
    pallas_call x2, Pallas kernels: 53.9 us -> 33.9 us  [attend(): pl.pallas_call(functools.partial(attend_kernel, turns, hands, peers, seg_...]
    all_to_all x3, waiting for transfers between devices: 0.01 us -> 17.7 us  [exchange(): return lax.all_to_all(array, 'enc', split_axis=0, concat_axis=0, tiled=True)]
    unnamed x42 -> x20, local copies, waits for them, and re-layouts: 15.3 us -> 4.82 us
  transfers between devices with their start and end apart: 13 -> 13, of which waited for: 4 -> 6; matrix products, arithmetic and copies ran while one was open for 2% -> 2% of each run, Pallas kernels for 40% -> 30%
where the time goes in v10:
time: 147 us
  waiting for transfers between devices  62.4 us (42%)
  Pallas kernels  49.3 us (34%)
  starting transfers between devices  26.4 us (18%)
  local copies, waits for them, and re-layouts  4.82 us (3%)
  other arithmetic  2.65 us (2%)
    ppermute x10, waiting for transfers between devices, xor_permute(): return lax.ppermute(array, axis, [(i, i ^ k) for i in range(size)])  44.7 us
    pallas_call x2, Pallas kernels, attend(): pl.pallas_call(functools.partial(attend_kernel, turns, hands, peers, seg_...  33.9 us
    all_to_all x3, waiting for transfers between devices, exchange(): return lax.all_to_all(array, 'enc', split_axis=0, concat_axis=0, tiled=True)  17.7 us
    ppermute x10, starting transfers between devices, xor_permute(): return lax.ppermute(array, axis, [(i, i ^ k) for i in range(size)])  15.2 us
    all_to_all x3, starting transfers between devices, exchange(): return lax.all_to_all(array, 'enc', split_axis=0, concat_axis=0, tiled=True)  11.2 us
    pallas_call x2, Pallas kernels, route(): pl.pallas_call(functools.partial(route_kernel, turns, not prepares, n_seg...  9.76 us
    pallas_call x2, Pallas kernels, collect(): pl.pallas_call(functools.partial(collect_kernel, turns, n_seg, seg_rows),...  5.64 us
    unnamed x20, local copies, waits for them, and re-layouts  4.82 us
  transfers between devices with their start and end apart: 13, of which 6 were waited for; matrix products, arithmetic and copies ran while one was open for 2% of the time, Pallas kernels for 30%

profile of v10, /device:TPU:0, one launch (start us, length us, event | category | flops | bytes accessed | tf_op | source)
XLA Modules:
  0.0 146.5 jit_solution(11549086532066123454)
XLA Ops:
  0.6 2.8 %route_0.1 = (bf16[2,2,32,1024]{3,2,1,0:T(8,128)(2,1)}, bf16[2,2,32,1024]{3,2,1,0:T(8,128)(2,1)}, bf16[2,2,32,1024]{3,2,1,0:T(8,128)(2,1)}, bf16[2,2,32,1024]{3,...) custom-call(s32[4,32]{1,0:T(4,128)} %bitcast.1, ...), custom_call_target="tpu_custom_call" | custom-call | bytes 2097152 | tf_op jit(solution)/shard_map/route_0/pallas_call | solution.py:412
  3.5 0.5 collective-permute-start
  4.0 2.6 %collective-permute-start.1 = (bf16[2,2,32,1024]{3,2,1,0:T(8,128)(2,1)}, bf16[2,2,32,1024]{3,2,1,0:T(8,128)(2,1)S(1)}, u32[]{:S(2)}, u32[]{:S(2)}) collective-permute-start(bf16[2,2,32,1024]{3,2,1,0:T(8,128)(2,1)} %get-tuple-element.45), channel_id=1, source_target_pairs={{0,2},{1,3},{2,0},{3,1},{4,6},{5,7},{6,4},{7,5},{8,10},{9,11},{10,... | collective-permute-start | bytes 786440 | tf_op jit(solution)/shard_map/ppermute | solution.py:387
  6.5 0.1 collective-permute-start.2
  6.6 1.8 %collective-permute-start.3 = (bf16[2,2,32,1024]{3,2,1,0:T(8,128)(2,1)}, bf16[2,2,32,1024]{3,2,1,0:T(8,128)(2,1)S(1)}, u32[]{:S(2)}, u32[]{:S(2)}) collective-permute-start(bf16[2,2,32,1024]{3,2,1,0:T(8,128)(2,1)} %get-tuple-element.47), channel_id=1, source_target_pairs={{0,4},{1,5},{2,6},{3,7},{4,0},{5,1},{6,2},{7,3},{8,12},{9,13},{10,... | collective-permute-start | bytes 786440 | tf_op jit(solution)/shard_map/ppermute | solution.py:387
  8.4 2.6 %collective-permute-start.5 = (bf16[2,2,32,1024]{3,2,1,0:T(8,128)(2,1)}, bf16[2,2,32,1024]{3,2,1,0:T(8,128)(2,1)}, u32[]{:S(2)}, u32[]{:S(2)}) collective-permute-start(bf16[2,2,32,1024]{3,2,1,0:T(8,128)(2,1)} %get-tuple-element.49), channel_id=1, source_target_pairs={{0,6},{1,7},{2,4},{3,5},{4,2},{5,3},{6,0},{7,1},{8,14},{9,15},{10,... | collective-permute-start | bytes 786440 | tf_op jit(solution)/shard_map/ppermute | solution.py:387
  11.0 2.9 %collective-permute-done.1.refs_2_ = bf16[2,2,32,1024]{3,2,1,0:T(8,128)(2,1)S(1)} collective-permute-done((bf16[2,2,32,1024]{3,2,1,0:T(8,128)(2,1)}, bf16[2,2,32,1024]{3,2,1,0:T(8,128)(2,1)S(1)}, u32[]{:S(2)}, u32[]{:S(2)}) %collective-permute-start.1) | collective-permute-done | bytes 262176 | tf_op jit(solution)/shard_map/ppermute | solution.py:387
  13.9 1.7 %collective-permute-start.6 = (bf16[2,2,32,1024]{3,2,1,0:T(8,128)(2,1)}, bf16[2,2,32,1024]{3,2,1,0:T(8,128)(2,1)}, u32[]{:S(2)}, u32[]{:S(2)}) collective-permute-start(bf16[2,2,32,1024]{3,2,1,0:T(8,128)(2,1)} %get-tuple-element.50), channel_id=1, source_target_pairs={{0,7},{1,6},{2,5},{3,4},{4,3},{5,2},{6,1},{7,0},{8,15},{9,14},{10,... | collective-permute-start | bytes 786440 | tf_op jit(solution)/shard_map/ppermute | solution.py:387
  15.6 6.9 %route_2.1 = (bf16[8,2,2,32,1024]{4,3,2,1,0:T(8,128)(2,1)}, bf16[4,2,1616,128]{3,2,1,0:T(8,128)(2,1)}, bf16[4,2,128,1616]{3,2,1,0:T(8,128)(2,1)}) custom-call(s32[4,32]{1,0:T(4,128)} %bitcast.2, bf16[128,4096]{1,0:T(8,128)(2,1)} %q_hbm.3, bf16[128,4096]{1,0:T(8,128)(2,1)} %g_hbm.3, bf16[1,1601,512]{2,1,0:T(8,128)(2,1)} %refs_0_.1, bf16[1,1601,512]{2,1,0:T(8,128)(2,1)} %refs_1_.1), custom_call_target="tpu_custom_call" | custom-call | bytes 12582912 | tf_op jit(solution)/shard_map/route_2/pallas_call | solution.py:412
  22.6 0.0 collective-permute-done.2.refs_3_
  22.6 0.0 collective-permute-done.3.refs_4_
  22.6 9.0 %collective-permute-done.4.refs_5_ = bf16[2,2,32,1024]{3,2,1,0:T(8,128)(2,1)S(1)} collective-permute-done((bf16[2,2,32,1024]{3,2,1,0:T(8,128)(2,1)}, bf16[2,2,32,1024]{3,2,1,0:T(8,128)(2,1)S(1)}, u32[]{:S(2)}, u32[]{:S(2)}) %collective-permute-start.4) | collective-permute-done | bytes 262176 | tf_op jit(solution)/shard_map/ppermute | solution.py:387
  31.6 0.7 copy-done.9
  32.3 4.0 %all-to-all-start.1 = ((bf16[8,2,2,32,1024]{4,3,2,1,0:T(8,128)(2,1)}), bf16[8,2,2,32,1024]{4,3,2,1,0:T(8,128)(2,1)S(1)}, u32[]{:S(2)}, u32[]{:S(2)}) async-start(bf16[8,2,2,32,1024]{4,3,2,1,0:T(8,128)(2,1)} %get-tuple-element.61), calls=%async_computation.1 | async-start | bytes 4194304 | tf_op jit(solution)/shard_map/all_to_all | solution.py:486
  36.4 16.9 %attend_0.1 = (bf16[8,2,2,32,1024]{4,3,2,1,0:T(8,128)(2,1)}, bf16[2,1616,128]{2,1,0:T(8,128)(2,1)}, bf16[2,1616,128]{2,1,0:T(8,128)(2,1)}) custom-call(s32[4,32]{1,0:T(4,128)} %bitcast.3, bf16[4,2,1616,128]{3,2,1,0:T(8,128)(2,1)} %get-tuple-element.41.caches, bf16[4,2,128,1616]{3,2,1,0:T(8,128)(2,1)} %get-tuple-element.42.turned_caches, ...), custom_call_target="tpu_custom_call" | custom-call | flops 7554465792 | bytes 8388608 | tf_op jit(solution)/shard_map/attend_0/pallas_call | solution.py:438
  53.2 9.8 %all-to-all-done.1.refs_0_ = bf16[8,2,2,32,1024]{4,3,2,1,0:T(8,128)(2,1)S(1)} async-done(((bf16[8,2,2,32,1024]{4,3,2,1,0:T(8,128)(2,1)}), bf16[8,2,2,32,1024]{4,3,2,1,0:T(8,128)(2,1)S(1)}, u32[]{:S(2)}, u32[]{:S(2)}) %all-to-all-start.1) | async-done | bytes 2097184 | tf_op jit(solution)/shard_map/all_to_all | solution.py:486
  63.0 1.4 copy-done.2
  64.4 3.6 %all-to-all-start = ((bf16[8,2,2,32,1024]{4,3,2,1,0:T(8,128)(2,1)}), bf16[8,2,2,32,1024]{4,3,2,1,0:T(8,128)(2,1)S(1)}, u32[]{:S(2)}, u32[]{:S(2)}) async-start(bf16[8,2,2,32,1024]{4,3,2,1,0:T(8,128)(2,1)} %get-tuple-element.60), calls=%async_computation | async-start | bytes 4194304 | tf_op jit(solution)/shard_map/all_to_all | solution.py:486
  68.0 1.6 %collective-permute-start.7 = (bf16[2,1616,128]{2,1,0:T(8,128)(2,1)}, bf16[2,1616,128]{2,1,0:T(8,128)(2,1)}, u32[]{:S(2)}, u32[]{:S(2)}) collective-permute-start(bf16[2,1616,128]{2,1,0:T(8,128)(2,1)} %get-tuple-element.72), channel_id=1, source_target_pairs={{0,8},{8,0},{16,24},{24,16},{1,9},{9,1},{17,25},{25,17},{2,10},{10... | collective-permute-start | bytes 2482184 | tf_op jit(solution)/shard_map/ppermute | solution.py:387
  69.7 17.0 %attend_2.1 = (bf16[8,2,2,32,1024]{4,3,2,1,0:T(8,128)(2,1)}, bf16[2,1616,128]{2,1,0:T(8,128)(2,1)}, bf16[2,1616,128]{2,1,0:T(8,128)(2,1)}) custom-call(s32[4,32]{1,0:T(4,128)} %bitcast.4, bf16[4,2,1616,128]{3,2,1,0:T(8,128)(2,1)} %get-tuple-element.41.caches, bf16[4,2,128,1616]{3,2,1,0:T(8,128)(2,1)} %get-tuple-element.42.turned_caches, ...), custom_call_target="tpu_custom_call" | custom-call | flops 7554465792 | bytes 8388608 | tf_op jit(solution)/shard_map/attend_2/pallas_call | solution.py:438
  86.7 7.9 %all-to-all-done.returned = bf16[8,2,2,32,1024]{4,3,2,1,0:T(8,128)(2,1)S(1)} async-done(((bf16[8,2,2,32,1024]{4,3,2,1,0:T(8,128)(2,1)}), bf16[8,2,2,32,1024]{4,3,2,1,0:T(8,128)(2,1)S(1)}, u32[]{:S(2)}, u32[]{:S(2)}) %all-to-all-start) | async-done | bytes 2097184 | tf_op jit(solution)/shard_map/all_to_all | solution.py:486
  94.6 1.4 copy-done.1
  96.0 3.6 %all-to-all-start.2 = ((bf16[8,2,2,32,1024]{4,3,2,1,0:T(8,128)(2,1)}), bf16[8,2,2,32,1024]{4,3,2,1,0:T(8,128)(2,1)S(1)}, u32[]{:S(2)}, u32[]{:S(2)}) async-start(bf16[8,2,2,32,1024]{4,3,2,1,0:T(8,128)(2,1)} %get-tuple-element.65), calls=%async_computation.2 | async-start | bytes 4194304 | tf_op jit(solution)/shard_map/all_to_all | solution.py:486
  99.6 1.4 add_convert_fusion
  101.0 2.7 %collective-permute-start.9 = (bf16[2,1616,128]{2,1,0:T(8,128)(2,1)S(1)}, bf16[2,1616,128]{2,1,0:T(8,128)(2,1)S(1)}, u32[]{:S(2)}, u32[]{:S(2)}) collective-permute-start(bf16[2,1616,128]{2,1,0:T(8,128)(2,1)S(1)} %add_convert_fusion), channel_id=1, source_target_pairs={{0,16},{8,24},{16,0},{24,8},{1,17},{9,25},{17,1},{25,9},{2,18},{10... | collective-permute-start | bytes 2482184 | tf_op jit(solution)/shard_map/ppermute | solution.py:387
  103.7 1.6 %collective-permute-start.8 = (bf16[2,1616,128]{2,1,0:T(8,128)(2,1)}, bf16[2,1616,128]{2,1,0:T(8,128)(2,1)S(1)}, u32[]{:S(2)}, u32[]{:S(2)}) collective-permute-start(bf16[2,1616,128]{2,1,0:T(8,128)(2,1)} %get-tuple-element.75), channel_id=1, source_target_pairs={{0,8},{8,0},{16,24},{24,16},{1,9},{9,1},{17,25},{25,17},{2,10},{10... | collective-permute-start | bytes 2482184 | tf_op jit(solution)/shard_map/ppermute | solution.py:387
  105.3 2.8 %collect_0.1 = (bf16[128,4096]{1,0:T(8,128)(2,1)}, bf16[128,4096]{1,0:T(8,128)(2,1)}) custom-call(s32[4,32]{1,0:T(4,128)} %bitcast.5, bf16[8,2,2,32,1024]{4,3,2,1,0:T(8,128)(2,1)} %copy-done.1), custom_call_target="tpu_custom_call" | custom-call | bytes 4194304 | tf_op jit(solution)/shard_map/collect_0/pallas_call | solution.py:469
  108.1 32.4 %collective-permute-done.9 = bf16[2,1616,128]{2,1,0:T(8,128)(2,1)S(1)} collective-permute-done((bf16[2,1616,128]{2,1,0:T(8,128)(2,1)S(1)}, bf16[2,1616,128]{2,1,0:T(8,128)(2,1)S(1)}, u32[]{:S(2)}, u32[]{:S(2)}) %collective-permute-start.9) | collective-permute-done | bytes 827424 | tf_op jit(solution)/shard_map/ppermute | solution.py:387
  140.6 0.4 collective-permute-done.8
  141.0 1.2 add_convert_fusion.1
  142.2 1.4 copy-done
  143.5 2.8 %collect_2.1 = (bf16[128,4096]{1,0:T(8,128)(2,1)}, bf16[128,4096]{1,0:T(8,128)(2,1)}) custom-call(s32[4,32]{1,0:T(4,128)} %bitcast.6, bf16[8,2,2,32,1024]{4,3,2,1,0:T(8,128)(2,1)} %copy-done, bf16[128,4096]{1,0:T(8,128)(2,1)} %get-tuple-element.67.refs_0_, bf16[128,4096]{1,0:T(8,128)(2,1)} %get-tuple-element.68.refs_1_), custom_call_target="tpu_custom_call", output_to_operand_aliasing={{0}: (2, {}), {1}: (3, {})} | custom-call | bytes 4194304 | tf_op jit(solution)/shard_map/collect_2/pallas_call | solution.py:469
  (22 shorter events, 0.0 us)
Async XLA Ops:
  3.5 4.9 %collective-permute-start = (bf16[2,2,32,1024]{3,2,1,0:T(8,128)(2,1)}, bf16[2,2,32,1024]{3,2,1,0:T(8,128)(2,1)S(1)}, u32[]{:S(2)}, u32[]{:S(2)}) collective-permute-start(bf16[2,2,32,1024]{3,2,1,0:T(8,128)(2,1)} %get-tuple-element.44), channel_id=1, source_target_pairs={{0,1},{1,0},{2,3},{3,2},{4,5},{5,4},{6,7},{7,6},{8,9},{9,8},{10,11... | collective-permute-start | bytes 786440 | tf_op jit(solution)/shard_map/ppermute | solution.py:387
  4.0 9.9 %collective-permute-start.1 = (bf16[2,2,32,1024]{3,2,1,0:T(8,128)(2,1)}, bf16[2,2,32,1024]{3,2,1,0:T(8,128)(2,1)S(1)}, u32[]{:S(2)}, u32[]{:S(2)}) collective-permute-start(bf16[2,2,32,1024]{3,2,1,0:T(8,128)(2,1)} %get-tuple-element.45), channel_id=1, source_target_pairs={{0,2},{1,3},{2,0},{3,1},{4,6},{5,7},{6,4},{7,5},{8,10},{9,11},{10,... | collective-permute-start | bytes 786440 | tf_op jit(solution)/shard_map/ppermute | solution.py:387
  6.5 16.1 %collective-permute-start.2 = (bf16[2,2,32,1024]{3,2,1,0:T(8,128)(2,1)}, bf16[2,2,32,1024]{3,2,1,0:T(8,128)(2,1)S(1)}, u32[]{:S(2)}, u32[]{:S(2)}) collective-permute-start(bf16[2,2,32,1024]{3,2,1,0:T(8,128)(2,1)} %get-tuple-element.46), channel_id=1, source_target_pairs={{0,3},{1,2},{2,1},{3,0},{4,7},{5,6},{6,5},{7,4},{8,11},{9,10},{10,... | collective-permute-start | bytes 786440 | tf_op jit(solution)/shard_map/ppermute | solution.py:387
  6.6 16.0 %collective-permute-start.3 = (bf16[2,2,32,1024]{3,2,1,0:T(8,128)(2,1)}, bf16[2,2,32,1024]{3,2,1,0:T(8,128)(2,1)S(1)}, u32[]{:S(2)}, u32[]{:S(2)}) collective-permute-start(bf16[2,2,32,1024]{3,2,1,0:T(8,128)(2,1)} %get-tuple-element.47), channel_id=1, source_target_pairs={{0,4},{1,5},{2,6},{3,7},{4,0},{5,1},{6,2},{7,3},{8,12},{9,13},{10,... | collective-permute-start | bytes 786440 | tf_op jit(solution)/shard_map/ppermute | solution.py:387
  8.4 23.2 %collective-permute-start.4 = (bf16[2,2,32,1024]{3,2,1,0:T(8,128)(2,1)}, bf16[2,2,32,1024]{3,2,1,0:T(8,128)(2,1)S(1)}, u32[]{:S(2)}, u32[]{:S(2)}) collective-permute-start(bf16[2,2,32,1024]{3,2,1,0:T(8,128)(2,1)} %get-tuple-element.48), channel_id=1, source_target_pairs={{0,5},{1,4},{2,7},{3,6},{4,1},{5,0},{6,3},{7,2},{8,13},{9,12},{10,... | collective-permute-start | bytes 786440 | tf_op jit(solution)/shard_map/ppermute | solution.py:387
  8.4 14.2 %copy-start.5 = (bf16[2,2,32,1024]{3,2,1,0:T(8,128)(2,1)}, bf16[2,2,32,1024]{3,2,1,0:T(8,128)(2,1)S(1)}, u32[]{:S(2)}) copy-start(bf16[2,2,32,1024]{3,2,1,0:T(8,128)(2,1)S(1)} %collective-permute-done.refs_1_) | copy-start | bytes 786436
  8.4 23.2 %collective-permute-start.5 = (bf16[2,2,32,1024]{3,2,1,0:T(8,128)(2,1)}, bf16[2,2,32,1024]{3,2,1,0:T(8,128)(2,1)}, u32[]{:S(2)}, u32[]{:S(2)}) collective-permute-start(bf16[2,2,32,1024]{3,2,1,0:T(8,128)(2,1)} %get-tuple-element.49), channel_id=1, source_target_pairs={{0,6},{1,7},{2,4},{3,5},{4,2},{5,3},{6,0},{7,1},{8,14},{9,15},{10,... | collective-permute-start | bytes 786440 | tf_op jit(solution)/shard_map/ppermute | solution.py:387
  13.9 8.7 %copy-start.6 = (bf16[2,2,32,1024]{3,2,1,0:T(8,128)(2,1)}, bf16[2,2,32,1024]{3,2,1,0:T(8,128)(2,1)S(1)}, u32[]{:S(2)}) copy-start(bf16[2,2,32,1024]{3,2,1,0:T(8,128)(2,1)S(1)} %collective-permute-done.1.refs_2_) | copy-start | bytes 786436
  13.9 17.7 %collective-permute-start.6 = (bf16[2,2,32,1024]{3,2,1,0:T(8,128)(2,1)}, bf16[2,2,32,1024]{3,2,1,0:T(8,128)(2,1)}, u32[]{:S(2)}, u32[]{:S(2)}) collective-permute-start(bf16[2,2,32,1024]{3,2,1,0:T(8,128)(2,1)} %get-tuple-element.50), channel_id=1, source_target_pairs={{0,7},{1,6},{2,5},{3,4},{4,3},{5,2},{6,1},{7,0},{8,15},{9,14},{10,... | collective-permute-start | bytes 786440 | tf_op jit(solution)/shard_map/ppermute | solution.py:387
  22.6 9.0 %copy-start.7 = (bf16[2,2,32,1024]{3,2,1,0:T(8,128)(2,1)}, bf16[2,2,32,1024]{3,2,1,0:T(8,128)(2,1)S(1)}, u32[]{:S(2)}) copy-start(bf16[2,2,32,1024]{3,2,1,0:T(8,128)(2,1)S(1)} %collective-permute-done.2.refs_3_) | copy-start | bytes 786436
  22.6 9.0 %copy-start.8 = (bf16[2,2,32,1024]{3,2,1,0:T(8,128)(2,1)}, bf16[2,2,32,1024]{3,2,1,0:T(8,128)(2,1)S(1)}, u32[]{:S(2)}) copy-start(bf16[2,2,32,1024]{3,2,1,0:T(8,128)(2,1)S(1)} %collective-permute-done.3.refs_4_) | copy-start | bytes 786436
  31.6 0.7 copy-start.9
  32.3 30.7 %all-to-all-start.1 = ((bf16[8,2,2,32,1024]{4,3,2,1,0:T(8,128)(2,1)}), bf16[8,2,2,32,1024]{4,3,2,1,0:T(8,128)(2,1)S(1)}, u32[]{:S(2)}, u32[]{:S(2)}) async-start(bf16[8,2,2,32,1024]{4,3,2,1,0:T(8,128)(2,1)} %get-tuple-element.61), calls=%async_computation.1 | async-start | bytes 4194304 | tf_op jit(solution)/shard_map/all_to_all | solution.py:486
  63.0 1.4 copy-start.2
  64.4 30.2 %all-to-all-start = ((bf16[8,2,2,32,1024]{4,3,2,1,0:T(8,128)(2,1)}), bf16[8,2,2,32,1024]{4,3,2,1,0:T(8,128)(2,1)S(1)}, u32[]{:S(2)}, u32[]{:S(2)}) async-start(bf16[8,2,2,32,1024]{4,3,2,1,0:T(8,128)(2,1)} %get-tuple-element.60), calls=%async_computation | async-start | bytes 4194304 | tf_op jit(solution)/shard_map/all_to_all | solution.py:486
  68.0 31.5 %collective-permute-start.7 = (bf16[2,1616,128]{2,1,0:T(8,128)(2,1)}, bf16[2,1616,128]{2,1,0:T(8,128)(2,1)}, u32[]{:S(2)}, u32[]{:S(2)}) collective-permute-start(bf16[2,1616,128]{2,1,0:T(8,128)(2,1)} %get-tuple-element.72), channel_id=1, source_target_pairs={{0,8},{8,0},{16,24},{24,16},{1,9},{9,1},{17,25},{25,17},{2,10},{10... | collective-permute-start | bytes 2482184 | tf_op jit(solution)/shard_map/ppermute | solution.py:387
  94.6 1.4 copy-start.1
  94.6 5.0 %copy-start.3 = (bf16[2,1616,128]{2,1,0:T(8,128)(2,1)S(1)}, bf16[2,1616,128]{2,1,0:T(8,128)(2,1)}, u32[]{:S(2)}) copy-start(bf16[2,1616,128]{2,1,0:T(8,128)(2,1)} %get-tuple-element.76) | copy-start | bytes 2482180
  96.0 46.2 %all-to-all-start.2 = ((bf16[8,2,2,32,1024]{4,3,2,1,0:T(8,128)(2,1)}), bf16[8,2,2,32,1024]{4,3,2,1,0:T(8,128)(2,1)S(1)}, u32[]{:S(2)}, u32[]{:S(2)}) async-start(bf16[8,2,2,32,1024]{4,3,2,1,0:T(8,128)(2,1)} %get-tuple-element.65), calls=%async_computation.2 | async-start | bytes 4194304 | tf_op jit(solution)/shard_map/all_to_all | solution.py:486
  99.6 41.4 %copy-start.4 = (bf16[2,1616,128]{2,1,0:T(8,128)(2,1)S(1)}, bf16[2,1616,128]{2,1,0:T(8,128)(2,1)}, u32[]{:S(2)}) copy-start(bf16[2,1616,128]{2,1,0:T(8,128)(2,1)} %get-tuple-element.71) | copy-start | bytes 2482180
  101.0 39.5 %collective-permute-start.9 = (bf16[2,1616,128]{2,1,0:T(8,128)(2,1)S(1)}, bf16[2,1616,128]{2,1,0:T(8,128)(2,1)S(1)}, u32[]{:S(2)}, u32[]{:S(2)}) collective-permute-start(bf16[2,1616,128]{2,1,0:T(8,128)(2,1)S(1)} %add_convert_fusion), channel_id=1, source_target_pairs={{0,16},{8,24},{16,0},{24,8},{1,17},{9,25},{17,1},{25,9},{2,18},{10... | collective-permute-start | bytes 2482184 | tf_op jit(solution)/shard_map/ppermute | solution.py:387
  103.7 37.2 %collective-permute-start.8 = (bf16[2,1616,128]{2,1,0:T(8,128)(2,1)}, bf16[2,1616,128]{2,1,0:T(8,128)(2,1)S(1)}, u32[]{:S(2)}, u32[]{:S(2)}) collective-permute-start(bf16[2,1616,128]{2,1,0:T(8,128)(2,1)} %get-tuple-element.75), channel_id=1, source_target_pairs={{0,8},{8,0},{16,24},{24,16},{1,9},{9,1},{17,25},{25,17},{2,10},{10... | collective-permute-start | bytes 2482184 | tf_op jit(solution)/shard_map/ppermute | solution.py:387
  142.2 1.4 copy-start

commit v11 on v10

--- a/solution.py
+++ b/solution.py
@@ -18,9 +18,7 @@
 SLICE = 128
 LOWEST = -3.0e38
 PER_CHUNK = 2
-VMEM_BYTES = 58 << 20
-KERNEL_BYTES = 58 << 20
-SPARE = 1
+VMEM_BYTES = 63 << 20
 ANY = pl.BlockSpec(memory_space=pl.ANY)
 SMEM = pl.BlockSpec(memory_space=pltpu.SMEM)
 VMEM = pl.BlockSpec(memory_space=pltpu.VMEM)
@@ -141,9 +139,10 @@
             )
 
 
-def attend_kernel(turns, hands, peers, seg_rows, tokens, reads, caches, turned_caches, *refs):
-    outs = 1 + hands * len(turns)
+def attend_kernel(turns, offset, before, peers, seg_rows, tokens, reads, caches, turned_caches, *refs):
+    outs = 1 + len(turns)
     received, refs = refs[: len(refs) - 14 - outs], refs[len(refs) - 14 - outs :]
+    received = received[: len(received) - before]
     returned, grads = refs[0], refs[1:outs]
     (
         straight,
@@ -188,21 +187,15 @@
 
     def arriving(i, slot, k):
         source = received[k] if len(received) > 1 else received[0].at[me ^ k]
-        return pltpu.make_async_copy(source.at[i], inbox.at[i, slot], in_sems.at[i, slot])
+        return pltpu.make_async_copy(source.at[offset + i], inbox.at[i, slot], in_sems.at[i, slot])
 
     def leaving(i, slot, owner):
         return pltpu.make_async_copy(
-            outbox.at[i, slot], returned.at[owner, i], out_sems.at[i, slot]
+            outbox.at[i, slot], returned.at[owner, offset + i], out_sems.at[i, slot]
         )
 
     def handing(i):
-        pairs = [(staged.at[i], grads[i])]
-        if hands == 2:
-            pairs = [(staged.at[i, j], grads[2 * i + j]) for j in range(2)]
-        return [
-            pltpu.make_async_copy(source, target, grad_sems.at[i, j])
-            for j, (source, target) in enumerate(pairs)
-        ]
+        return pltpu.make_async_copy(staged.at[i], grads[i], grad_sems.at[i])
 
     for copies in kv_copies:
         copies[0].start()
@@ -241,8 +234,9 @@
     def folded(value, reduce):
         return reduce(value.reshape(-1, 8, lanes), axis=0)
 
-    def forward(i, slot, weights):
-        q_turned = stacked(i, slot, 0).astype(f32).T.astype(bf16)
+    def forward(u, i, slot, weights):
+        source = jnp.minimum(slot, count - 1)
+        q_turned = stacked(i, source, 0).astype(f32).T.astype(bf16)
         tops, totals, outs = [], [], []
 
         def score():
@@ -252,51 +246,52 @@
                 if d > tokens:
                     token = lax.broadcasted_iota(jnp.int32, piece.shape, 0) + c
                     piece = jnp.where(token < tokens, piece, LOWEST)
-                scores[i, c:d, :] = piece
+                scores[u, c:d, :] = piece
                 tops.append(folded(piece, jnp.max))
 
         def weigh(a, b):
             if a == 0:
                 tops[:] = [jnp.max(functools.reduce(jnp.maximum, tops), axis=0, keepdims=True)]
             for c, d in slices(a, b):
-                piece = jnp.exp2((scores[i, c:d, :] - tops[0]) * (SCALE * LOG2E))
+                piece = jnp.exp2((scores[u, c:d, :] - tops[0]) * (SCALE * LOG2E))
                 totals.append(folded(piece, jnp.sum))
-                weights[i, c:d, :] = piece.astype(bf16)
+                weights[u, c:d, :] = piece.astype(bf16)
             outs.append(
-                jnp.dot(turned[i, 1, :, a:b], weights[i, a:b, :], preferred_element_type=f32)
+                jnp.dot(turned[i, 1, :, a:b], weights[u, a:b, :], preferred_element_type=f32)
             )
 
         def finish():
             total = jnp.sum(functools.reduce(jnp.add, totals), axis=0, keepdims=True)
             inverse = 1.0 / total
+            share = inverse * (slot < count).astype(f32)
             out = functools.reduce(jnp.add, outs) * inverse
             store(i, slot, 0, out)
-            g = (stacked(i, slot, 1).astype(f32).T * inverse).astype(bf16)
+            g = (stacked(i, source, 1).astype(f32).T * share).astype(bf16)
             exact = g.astype(f32)
             delta = jnp.sum(exact * out.astype(bf16).astype(f32), axis=0, keepdims=True)
             return delta, g, exact.T.astype(bf16)
 
         return score, weigh, finish
 
-    def backward(i, slot, weights, delta, g_turned, g):
-        q = stacked(i, slot, 0)
+    def backward(u, i, slot, weights, delta, g_turned, g):
+        q = stacked(i, jnp.minimum(slot, count - 1), 0)
         turned_dq = []
 
         def values_part(a, b):
             dprob = jnp.dot(straight[i, 1, a:b, :], g_turned, preferred_element_type=f32)
             for c, d in slices(a, b):
-                piece = weights[i, c:d, :].astype(f32) * (dprob[c - a : d - a, :] - delta)
-                dscores[i, c:d, :] = piece.astype(bf16)
+                piece = weights[u, c:d, :].astype(f32) * (dprob[c - a : d - a, :] - delta)
+                dscores[u, c:d, :] = piece.astype(bf16)
 
         def values_sum():
-            sums[i, 1] += jnp.dot(weights[i], g, preferred_element_type=f32)
+            sums[i, 1] += jnp.dot(weights[u], g, preferred_element_type=f32)
 
         def keys_sum():
-            sums[i, 0] += jnp.dot(dscores[i], q, preferred_element_type=f32)
+            sums[i, 0] += jnp.dot(dscores[u], q, preferred_element_type=f32)
 
         def queries_part(a, b):
             turned_dq.append(
-                jnp.dot(turned[i, 0, :, a:b], dscores[i, a:b, :], preferred_element_type=f32)
+                jnp.dot(turned[i, 0, :, a:b], dscores[u, a:b, :], preferred_element_type=f32)
             )
 
         def finish():
@@ -304,16 +299,27 @@
 
         return values_part, values_sum, keys_sum, queries_part, finish
 
-    heads = range(len(turns))
-
-    def one_slot(slot, carry, last=False):
-        weights, next_weights = even_odd.at[slot & 1], even_odd.at[(slot + 1) & 1]
-        behind = [backward(i, slot, weights, *carry[i]) for i in heads]
+    paired = len(turns) == 2
+    steps = count if paired else (count + 1) // 2
+
+    def unit(u, step):
+        return (u, step) if paired else (0, 2 * step + u)
+
+    def await_step(step):
+        for u in range(2):
+            i, slot = unit(u, step)
+
+            @pl.when(slot < count)
+            def _():
+                arriving(i, slot, 0).wait()
+
+    def one_step(step, carry, last=False):
+        weights, next_weights = even_odd.at[step & 1], even_odd.at[(step + 1) & 1]
+        behind = [backward(u, *unit(u, step), weights, *carry[u]) for u in range(2)]
         ahead = []
         if not last:
-            for i in heads:
-                arriving(i, slot + 1, 0).wait()
-            ahead = [forward(i, slot + 1, next_weights) for i in heads]
+            await_step(step + 1)
+            ahead = [forward(u, *unit(u, step + 1), next_weights) for u in range(2)]
 
         for score, _, _ in ahead:
             score()
@@ -331,16 +337,23 @@
         for *_, finish in behind:
             finish()
         carry = [finish() for _, _, finish in ahead]
-        for i in heads:
-            leaving(i, slot, owners[slot]).start()
+        for u in range(2):
+            i, slot = unit(u, step)
+
+            @pl.when(slot < count)
+            def _():
+                leaving(i, slot, owners[slot]).start()
+
         return carry
+
+    heads = range(len(turns))
 
     @pl.when(count > 0)
     def _():
+        await_step(0)
         for i in heads:
-            arriving(i, 0, 0).wait()
             kv_copies[i][0].wait()
-        first = [forward(i, 0, even_odd.at[0]) for i in heads]
+        first = [forward(u, *unit(u, 0), even_odd.at[0]) for u in range(2)]
         for score, _, _ in first:
             score()
         for i in heads:
@@ -352,13 +365,12 @@
         for i in heads:
             kv_copies[i][2].wait()
             kv_copies[i][3].wait()
-        carry = lax.fori_loop(0, count - 1, one_slot, carry)
-        one_slot(count - 1, carry, last=True)
+        carry = lax.fori_loop(0, steps - 1, one_step, carry)
+        one_step(steps - 1, carry, last=True)
         for i in heads:
             staged[i, 0] = (sums[i, 0] * SCALE).astype(bf16)
             staged[i, 1] = sums[i, 1].astype(bf16)
-            for copy in handing(i):
-                copy.start()
+            handing(i).start()
 
     @pl.when(count == 0)
     def _():
@@ -366,8 +378,7 @@
         for i in range(len(turns)):
             for copy in kv_copies[i]:
                 copy.wait()
-            for copy in handing(i):
-                copy.start()
+            handing(i).start()
 
     for i in range(len(turns)):
         for slot in range(slots):
@@ -376,8 +387,7 @@
             def _():
                 leaving(i, slot, 0).wait()
 
-        for copy in handing(i):
-            copy.wait()
+        handing(i).wait()
 
 
 def xor_permute(array, axis, k):
@@ -403,8 +413,8 @@
     part = jax.ShapeDtypeStruct((PER_CHUNK, 2, seg_rows, WIDTH), bf16)
 
     caches = [
-        jax.ShapeDtypeStruct((KVH * SPARE, 2, padded, HD), bf16),
-        jax.ShapeDtypeStruct((KVH * SPARE, 2, HD, padded), bf16),
+        jax.ShapeDtypeStruct((KVH, 2, padded, HD), bf16),
+        jax.ShapeDtypeStruct((KVH, 2, HD, padded), bf16),
     ]
 
     def route(turns, prepares):
@@ -432,37 +442,42 @@
             name=f"route_{turns[0]}",
         )(by_segment, queries, grad_out, *[keys, values] * prepares)
 
-    def attend(turns, hands, received):
+    def attend(turns, offset, received, before):
         work = slots * lanes * tokens * HD * len(turns)
-        grad = jax.ShapeDtypeStruct((2, padded, HD)[hands - 1 :], bf16)
-        results = pl.pallas_call(
-            functools.partial(attend_kernel, turns, hands, peers, seg_rows, tokens),
-            out_shape=[message] + [grad] * hands * len(turns),
-            in_specs=[SMEM] + [ANY] * (2 + len(received)),
-            out_specs=[ANY] * (1 + hands * len(turns)),
+        grad = jax.ShapeDtypeStruct((2, padded, HD), bf16)
+        room = slots + slots % 2
+        return pl.pallas_call(
+            functools.partial(
+                attend_kernel, turns, offset, len(before), peers, seg_rows, tokens
+            ),
+            out_shape=[message] + [grad] * len(turns),
+            in_specs=[SMEM] + [ANY] * (2 + len(received) + len(before)),
+            out_specs=[ANY] * (1 + len(turns)),
+            input_output_aliases={3 + len(received): 0} if before else {},
             scratch_shapes=[
                 pltpu.VMEM((len(turns), 2, padded, HD), bf16),
                 pltpu.VMEM((len(turns), 2, HD, padded), bf16),
                 pltpu.VMEM((len(turns), slots, 2, seg_rows, WIDTH), bf16),
-                pltpu.VMEM((len(turns), slots, 2, seg_rows, WIDTH), bf16),
-                pltpu.VMEM((len(turns), padded, lanes), f32),
-                pltpu.VMEM((2, len(turns), padded, lanes), bf16),
-                pltpu.VMEM((len(turns), padded, lanes), bf16),
+                pltpu.VMEM((len(turns), room, 2, seg_rows, WIDTH), bf16),
+                pltpu.VMEM((2, padded, lanes), f32),
+                pltpu.VMEM((2, 2, padded, lanes), bf16),
+                pltpu.VMEM((2, padded, lanes), bf16),
                 pltpu.VMEM((len(turns), 2, padded, HD), f32),
                 pltpu.VMEM((len(turns), 2, padded, HD), bf16),
                 pltpu.SMEM((slots,), jnp.int32),
                 pltpu.SemaphoreType.DMA((len(turns), 4)),
                 pltpu.SemaphoreType.DMA((len(turns), slots)),
                 pltpu.SemaphoreType.DMA((len(turns), slots)),
-                pltpu.SemaphoreType.DMA((len(turns), 2)),
+                pltpu.SemaphoreType.DMA((len(turns),)),
             ],
-            compiler_params=pltpu.CompilerParams(vmem_limit_bytes=KERNEL_BYTES),
+            compiler_params=pltpu.CompilerParams(vmem_limit_bytes=VMEM_BYTES),
             cost_estimate=pl.CostEstimate(
-                flops=12 * work, bytes_accessed=8 << 20, transcendentals=slots * lanes * tokens
+                flops=12 * work if len(turns) == 2 else work,
+                bytes_accessed=8 << 20 if len(turns) == 2 else 1 << 20,
+                transcendentals=slots * lanes * tokens if len(turns) == 2 else 0,
             ),
             name=f"attend_{turns[0]}",
-        )(by_segment, *prepared, *received)
-        return results
+        )(by_segment, *prepared, *received, *before)
 
     def collect(turns, returned, before):
         whole = jax.ShapeDtypeStruct(queries.shape, bf16)
@@ -477,7 +492,7 @@
                 pltpu.SemaphoreType.DMA((PER_CHUNK, 2, n_seg)),
                 pltpu.SemaphoreType.DMA((PER_CHUNK, 2)),
             ],
-            compiler_params=pltpu.CompilerParams(vmem_limit_bytes=KERNEL_BYTES),
+            compiler_params=pltpu.CompilerParams(vmem_limit_bytes=VMEM_BYTES),
             cost_estimate=pl.CostEstimate(flops=0, bytes_accessed=4 << 20, transcendentals=0),
             name=f"collect_{turns[0]}",
         )(by_segment, returned, *before)
@@ -491,25 +506,33 @@
     *received, routed = lax.optimization_barrier((*received, routed))
     received_later = exchange(routed)
     butterfly = n_seq == KVH
-    returned, *grads = attend(first, 1, received)
-    answer = exchange(returned)
+    returned, *grads = attend(first[:1], 0, received, [])
     if butterfly:
         passed = xor_permute(grads[0], "seq", 1)
-    received_later, grads[1] = lax.optimization_barrier((received_later, grads[1]))
-    returned, *more = attend(second, 1, [received_later])
+    returned, last = attend(first[1:], 1, received, [returned])
+    grads.append(last)
+    if butterfly:
+        passed, last = lax.optimization_barrier((passed, last))
+        pair = [(last[j].astype(f32) + passed[j].astype(f32)).astype(bf16) for j in range(2)]
+        returned, *pair = lax.optimization_barrier((returned, *pair))
+        pair = [xor_permute(one, "seq", 2) for one in pair]
+    answer = exchange(returned)
+    received_later, returned = lax.optimization_barrier((received_later, returned))
+    returned, *more = attend(second, 0, [received_later], [])
+    if butterfly:
+        pair[0], returned = lax.optimization_barrier((pair[0], returned))
     answer, returned = lax.optimization_barrier((answer, returned))
     answer_later = exchange(returned)
     if butterfly:
-        passed, grads[1], more[0] = lax.optimization_barrier((passed, grads[1], more[0]))
-        pair = (grads[1].astype(f32) + passed.astype(f32)).astype(bf16)
-        pair = xor_permute(pair, "seq", 2)
         near = xor_permute(more[0], "seq", 1)
     half = collect(first, answer, [])
     attended, grad_queries = collect(second, answer_later, half)
 
     if butterfly:
         summed = [
-            sum(term[j, :tokens].astype(f32) for term in (more[1], near, pair)).astype(bf16)
+            sum(
+                term[:tokens].astype(f32) for term in (more[1][j], near[j], pair[j])
+            ).astype(bf16)
             for j in range(2)
         ]
         return attended, grad_queries, summed[0][None], summed[1][None]

time: 147 us -> 144 us (0.980)
  waiting for transfers between devices: 62.4 us -> 56.1 us
  starting transfers between devices: 26.4 us -> 32.6 us
  local copies, waits for them, and re-layouts: 4.82 us -> 0.02 us
  other arithmetic: 2.65 us -> 4.81 us
    all_to_all x3, waiting for transfers between devices: 17.7 us -> 4.66 us  [exchange(): return lax.all_to_all(array, 'enc', split_axis=0, concat_axis=0, tiled=True)]
    ppermute x10 -> x11, waiting for transfers between devices: 44.7 us -> 51.4 us  [xor_permute(): return lax.ppermute(array, axis, [(i, i ^ k) for i in range(size)])]
    unnamed x20 -> x10, local copies, waits for them, and re-layouts: 4.82 us -> 0.02 us
    all_to_all x3, starting transfers between devices: 11.2 us -> 16 us  [exchange(): return lax.all_to_all(array, 'enc', split_axis=0, concat_axis=0, tiled=True)]
    broadcast_in_dim x0 -> x1, other arithmetic: none -> 2.58 us  [per_device(): return (attended, grad_queries, summed[0][None], summed[1][None])]
    ppermute x10 -> x11, starting transfers between devices: 15.2 us -> 16.6 us  [xor_permute(): return lax.ppermute(array, axis, [(i, i ^ k) for i in range(size)])]
    pallas_call x2 -> x3, Pallas kernels: 33.9 us -> 33.1 us  [attend(): pl.pallas_call(functools.partial(attend_kernel, turns, offset, len(before...]
  transfers between devices with their start and end apart: 13 -> 14, of which waited for: 6 -> 7; matrix products, arithmetic and copies ran while one was open for 2% -> 3% of each run, Pallas kernels for 30% -> 30%
where the time goes in v11:
time: 144 us; the launch traced here: 143 us
  waiting for transfers between devices  56.1 us (39%)
  Pallas kernels  48.5 us (34%)
  starting transfers between devices  32.6 us (23%)
  other arithmetic  4.81 us (3%)
    ppermute x11, waiting for transfers between devices, xor_permute(): return lax.ppermute(array, axis, [(i, i ^ k) for i in range(size)])  51.4 us
    pallas_call x3, Pallas kernels, attend(): pl.pallas_call(functools.partial(attend_kernel, turns, offset, len(before...  33.1 us
    ppermute x11, starting transfers between devices, xor_permute(): return lax.ppermute(array, axis, [(i, i ^ k) for i in range(size)])  16.6 us
    all_to_all x3, starting transfers between devices, exchange(): return lax.all_to_all(array, 'enc', split_axis=0, concat_axis=0, tiled=True)  16 us
    pallas_call x2, Pallas kernels, route(): pl.pallas_call(functools.partial(route_kernel, turns, not prepares, n_seg...  9.76 us
    pallas_call x2, Pallas kernels, collect(): pl.pallas_call(functools.partial(collect_kernel, turns, n_seg, seg_rows),...  5.64 us
    all_to_all x3, waiting for transfers between devices, exchange(): return lax.all_to_all(array, 'enc', split_axis=0, concat_axis=0, tiled=True)  4.66 us
  transfers between devices with their start and end apart: 14, of which 7 were waited for; matrix products, arithmetic and copies ran while one was open for 3% of the time, Pallas kernels for 30%

profile of v11, /device:TPU:0, one launch (start us, length us, event | category | flops | bytes accessed | tf_op | source)
XLA Modules:
  0.0 143.0 jit_solution(6215696143096806021)
XLA Ops:
  0.6 2.8 %route_0.1 = (bf16[2,2,32,1024]{3,2,1,0:T(8,128)(2,1)}, bf16[2,2,32,1024]{3,2,1,0:T(8,128)(2,1)}, bf16[2,2,32,1024]{3,2,1,0:T(8,128)(2,1)}, bf16[2,2,32,1024]{3,...) custom-call(s32[4,32]{1,0:T(4,128)} %bitcast.21, ...), custom_call_target="tpu_custom_call" | custom-call | bytes 2097152 | tf_op jit(solution)/shard_map/route_0/pallas_call | solution.py:422
  3.5 0.5 collective-permute-start
  4.0 2.6 %collective-permute-start.1 = (bf16[2,2,32,1024]{3,2,1,0:T(8,128)(2,1)}, bf16[2,2,32,1024]{3,2,1,0:T(8,128)(2,1)S(1)}, u32[]{:S(2)}, u32[]{:S(2)}) collective-permute-start(bf16[2,2,32,1024]{3,2,1,0:T(8,128)(2,1)} %get-tuple-element.49), channel_id=1, source_target_pairs={{0,2},{1,3},{2,0},{3,1},{4,6},{5,7},{6,4},{7,5},{8,10},{9,11},{10,... | collective-permute-start | bytes 786440 | tf_op jit(solution)/shard_map/ppermute | solution.py:397
  6.5 0.1 collective-permute-start.2
  6.6 1.8 %collective-permute-start.3 = (bf16[2,2,32,1024]{3,2,1,0:T(8,128)(2,1)}, bf16[2,2,32,1024]{3,2,1,0:T(8,128)(2,1)}, u32[]{:S(2)}, u32[]{:S(2)}) collective-permute-start(bf16[2,2,32,1024]{3,2,1,0:T(8,128)(2,1)} %get-tuple-element.51), channel_id=1, source_target_pairs={{0,4},{1,5},{2,6},{3,7},{4,0},{5,1},{6,2},{7,3},{8,12},{9,13},{10,... | collective-permute-start | bytes 786440 | tf_op jit(solution)/shard_map/ppermute | solution.py:397
  8.4 0.0 collective-permute-done.refs_1_
  8.4 2.6 %collective-permute-start.5 = (bf16[2,2,32,1024]{3,2,1,0:T(8,128)(2,1)}, bf16[2,2,32,1024]{3,2,1,0:T(8,128)(2,1)}, u32[]{:S(2)}, u32[]{:S(2)}) collective-permute-start(bf16[2,2,32,1024]{3,2,1,0:T(8,128)(2,1)} %get-tuple-element.53), channel_id=1, source_target_pairs={{0,6},{1,7},{2,4},{3,5},{4,2},{5,3},{6,0},{7,1},{8,14},{9,15},{10,... | collective-permute-start | bytes 786440 | tf_op jit(solution)/shard_map/ppermute | solution.py:397
  11.0 2.9 %collective-permute-done.1.refs_2_ = bf16[2,2,32,1024]{3,2,1,0:T(8,128)(2,1)S(1)} collective-permute-done((bf16[2,2,32,1024]{3,2,1,0:T(8,128)(2,1)}, bf16[2,2,32,1024]{3,2,1,0:T(8,128)(2,1)S(1)}, u32[]{:S(2)}, u32[]{:S(2)}) %collective-permute-start.1) | collective-permute-done | bytes 262176 | tf_op jit(solution)/shard_map/ppermute | solution.py:397
  13.9 1.8 %collective-permute-start.6 = (bf16[2,2,32,1024]{3,2,1,0:T(8,128)(2,1)}, bf16[2,2,32,1024]{3,2,1,0:T(8,128)(2,1)}, u32[]{:S(2)}, u32[]{:S(2)}) collective-permute-start(bf16[2,2,32,1024]{3,2,1,0:T(8,128)(2,1)} %get-tuple-element.54), channel_id=1, source_target_pairs={{0,7},{1,6},{2,5},{3,4},{4,3},{5,2},{6,1},{7,0},{8,15},{9,14},{10,... | collective-permute-start | bytes 786440 | tf_op jit(solution)/shard_map/ppermute | solution.py:397
  15.7 6.9 %route_2.1 = (bf16[8,2,2,32,1024]{4,3,2,1,0:T(8,128)(2,1)}, bf16[4,2,1616,128]{3,2,1,0:T(8,128)(2,1)}, bf16[4,2,128,1616]{3,2,1,0:T(8,128)(2,1)}) custom-call(s32[4,32]{1,0:T(4,128)} %bitcast.22, bf16[128,4096]{1,0:T(8,128)(2,1)} %q_hbm.3, bf16[128,4096]{1,0:T(8,128)(2,1)} %g_hbm.3, bf16[1,1601,512]{2,1,0:T(8,128)(2,1)} %refs_0_.1, bf16[1,1601,512]{2,1,0:T(8,128)(2,1)} %refs_1_.1), custom_call_target="tpu_custom_call" | custom-call | bytes 12582912 | tf_op jit(solution)/shard_map/route_2/pallas_call | solution.py:422
  22.7 0.0 collective-permute-done.2.refs_3_
  22.7 0.0 collective-permute-done.3.refs_4_
  22.7 8.9 %collective-permute-done.4.refs_5_ = bf16[2,2,32,1024]{3,2,1,0:T(8,128)(2,1)} collective-permute-done((bf16[2,2,32,1024]{3,2,1,0:T(8,128)(2,1)}, bf16[2,2,32,1024]{3,2,1,0:T(8,128)(2,1)}, u32[]{:S(2)}, u32[]{:S(2)}) %collective-permute-start.4) | collective-permute-done | bytes 262176 | tf_op jit(solution)/shard_map/ppermute | solution.py:397
  31.6 4.4 %all-to-all-start.1 = ((bf16[8,2,2,32,1024]{4,3,2,1,0:T(8,128)(2,1)}), bf16[8,2,2,32,1024]{4,3,2,1,0:T(8,128)(2,1)}, u32[]{:S(2)}, u32[]{:S(2)}) async-start(bf16[8,2,2,32,1024]{4,3,2,1,0:T(8,128)(2,1)} %get-tuple-element.72), calls=%async_computation.1 | async-start | bytes 4194304 | tf_op jit(solution)/shard_map/all_to_all | solution.py:501
  36.0 9.8 %attend_0.1 = (bf16[8,2,2,32,1024]{4,3,2,1,0:T(8,128)(2,1)}, bf16[2,1616,128]{2,1,0:T(8,128)(2,1)}) custom-call(s32[4,32]{1,0:T(4,128)} %bitcast.23, bf16[4,2,1616,128]{3,2,1,0:T(8,128)(2,1)} %get-tuple-element.45.caches, bf16[4,2,128,1616]{3,2,1,0:T(8,128)(2,1)} %get-tuple-element.46.turned_caches, bf16[2,2,32,1024]{3,2,1,0:T(8,128)(2,1)} %get-tuple-element.56.refs_0_, ...), custom_call_target="tpu_custom_call" | custom-call | flops 314769408 | bytes 1048576 | tf_op jit(solution)/shard_map/attend_0/pallas_call | solution.py:449
  45.8 0.1 collective-permute-start.7
  45.9 10.0 %attend_1.1 = (bf16[8,2,2,32,1024]{4,3,2,1,0:T(8,128)(2,1)}, bf16[2,1616,128]{2,1,0:T(8,128)(2,1)}) custom-call(s32[4,32]{1,0:T(4,128)} %bitcast.24, bf16[4,2,1616,128]{3,2,1,0:T(8,128)(2,1)} %get-tuple-element.45.caches, bf16[4,2,128,1616]{3,2,1,0:T(8,128)(2,1)} %get-tuple-element.46.turned_caches, ...), custom_call_target="tpu_custom_call", output_to_operand_aliasing={{0}: (11, {})} | custom-call | flops 314769408 | bytes 1048576 | tf_op jit(solution)/shard_map/attend_1/pallas_call | solution.py:449
  55.9 11.0 %collective-permute-done.7 = bf16[2,1616,128]{2,1,0:T(8,128)(2,1)S(1)} collective-permute-done((bf16[2,1616,128]{2,1,0:T(8,128)(2,1)}, bf16[2,1616,128]{2,1,0:T(8,128)(2,1)S(1)}, u32[]{:S(2)}, u32[]{:S(2)}) %collective-permute-start.7) | collective-permute-done | bytes 827424 | tf_op jit(solution)/shard_map/ppermute | solution.py:397
  66.9 2.2 %fusion.3 = (bf16[1616,128]{1,0:T(8,128)(2,1)}, bf16[1616,128]{1,0:T(8,128)(2,1)}) fusion(bf16[2,1616,128]{2,1,0:T(8,128)(2,1)S(1)} %collective-permute-done.7, bf16[2,1616,128]{2,1,0:T(8,128)(2,1)} %get-tuple-element.68), kind=kLoop, calls=%fused_computation.7 | loop fusion | flops 1654784 | bytes 2482176 | tf_op jit(solution)/shard_map/convert_element_type | solution.py:516
  69.1 7.3 %all-to-all-start = ((bf16[8,2,2,32,1024]{4,3,2,1,0:T(8,128)(2,1)}), bf16[8,2,2,32,1024]{4,3,2,1,0:T(8,128)(2,1)}, u32[]{:S(2)}, u32[]{:S(2)}) async-start(bf16[8,2,2,32,1024]{4,3,2,1,0:T(8,128)(2,1)} %get-tuple-element.70), calls=%async_computation | async-start | bytes 4194304 | tf_op jit(solution)/shard_map/all_to_all | solution.py:501
  76.4 2.8 %collective-permute-start.8 = (bf16[1616,128]{1,0:T(8,128)(2,1)}, bf16[1616,128]{1,0:T(8,128)(2,1)S(1)}, u32[]{:S(2)}, u32[]{:S(2)}) collective-permute-start(bf16[1616,128]{1,0:T(8,128)(2,1)} %get-tuple-element.71), channel_id=1, source_target_pairs={{0,16},{8,24},{16,0},{24,8},{1,17},{9,25},{17,1},{25,9},{2,18},{10... | collective-permute-start | bytes 1241096 | tf_op jit(solution)/shard_map/ppermute | solution.py:397
  79.2 13.3 %attend_2.1 = (bf16[8,2,2,32,1024]{4,3,2,1,0:T(8,128)(2,1)}, bf16[2,1616,128]{2,1,0:T(8,128)(2,1)}, bf16[2,1616,128]{2,1,0:T(8,128)(2,1)}) custom-call(s32[4,32]{1,0:T(4,128)} %bitcast.25, bf16[4,2,1616,128]{3,2,1,0:T(8,128)(2,1)} %get-tuple-element.45.caches, bf16[4,2,128,1616]{3,2,1,0:T(8,128)(2,1)} %get-tuple-element.46.turned_caches, ...), custom_call_target="tpu_custom_call" | custom-call | flops 7554465792 | bytes 8388608 | tf_op jit(solution)/shard_map/attend_2/pallas_call | solution.py:449
  92.5 6.0 %collective-permute-done.8 = bf16[1616,128]{1,0:T(8,128)(2,1)S(1)} collective-permute-done((bf16[1616,128]{1,0:T(8,128)(2,1)}, bf16[1616,128]{1,0:T(8,128)(2,1)S(1)}, u32[]{:S(2)}, u32[]{:S(2)}) %collective-permute-start.8) | collective-permute-done | bytes 413728 | tf_op jit(solution)/shard_map/ppermute | solution.py:397
  98.5 4.7 %all-to-all-done.returned = bf16[8,2,2,32,1024]{4,3,2,1,0:T(8,128)(2,1)} async-done(((bf16[8,2,2,32,1024]{4,3,2,1,0:T(8,128)(2,1)}), bf16[8,2,2,32,1024]{4,3,2,1,0:T(8,128)(2,1)}, u32[]{:S(2)}, u32[]{:S(2)}) %all-to-all-start) | async-done | bytes 2097184 | tf_op jit(solution)/shard_map/all_to_all | solution.py:501
  103.2 4.4 %all-to-all-start.2 = ((bf16[8,2,2,32,1024]{4,3,2,1,0:T(8,128)(2,1)}), bf16[8,2,2,32,1024]{4,3,2,1,0:T(8,128)(2,1)}, u32[]{:S(2)}, u32[]{:S(2)}) async-start(bf16[8,2,2,32,1024]{4,3,2,1,0:T(8,128)(2,1)} %get-tuple-element.76), calls=%async_computation.2 | async-start | bytes 4194304 | tf_op jit(solution)/shard_map/all_to_all | solution.py:501
  107.6 1.5 %collective-permute-start.9 = (bf16[2,1616,128]{2,1,0:T(8,128)(2,1)}, bf16[2,1616,128]{2,1,0:T(8,128)(2,1)}, u32[]{:S(2)}, u32[]{:S(2)}) collective-permute-start(bf16[2,1616,128]{2,1,0:T(8,128)(2,1)} %get-tuple-element.83), channel_id=1, source_target_pairs={{0,8},{8,0},{16,24},{24,16},{1,9},{9,1},{17,25},{25,17},{2,10},{10... | collective-permute-start | bytes 2482184 | tf_op jit(solution)/shard_map/ppermute | solution.py:397
  109.1 2.9 %collective-permute-start.10 = (bf16[1616,128]{1,0:T(8,128)(2,1)}, bf16[1616,128]{1,0:T(8,128)(2,1)}, u32[]{:S(2)}, u32[]{:S(2)}) collective-permute-start(bf16[1616,128]{1,0:T(8,128)(2,1)} %get-tuple-element.85), channel_id=1, source_target_pairs={{0,16},{8,24},{16,0},{24,8},{1,17},{9,25},{17,1},{25,9},{2,18},{10... | collective-permute-start | bytes 1241096 | tf_op jit(solution)/shard_map/ppermute | solution.py:397
  111.9 2.8 %collect_0.1 = (bf16[128,4096]{1,0:T(8,128)(2,1)}, bf16[128,4096]{1,0:T(8,128)(2,1)}) custom-call(s32[4,32]{1,0:T(4,128)} %bitcast.26, bf16[8,2,2,32,1024]{4,3,2,1,0:T(8,128)(2,1)} %all-to-all-done.returned), custom_call_target="tpu_custom_call" | custom-call | bytes 4194304 | tf_op jit(solution)/shard_map/collect_0/pallas_call | solution.py:484
  114.8 21.8 %collective-permute-done.10 = bf16[1616,128]{1,0:T(8,128)(2,1)} collective-permute-done((bf16[1616,128]{1,0:T(8,128)(2,1)}, bf16[1616,128]{1,0:T(8,128)(2,1)}, u32[]{:S(2)}, u32[]{:S(2)}) %collective-permute-start.10) | collective-permute-done | bytes 413728 | tf_op jit(solution)/shard_map/ppermute | solution.py:397
  136.5 0.9 collective-permute-done.9
  137.4 2.6 %fusion.5 = (bf16[1,1601,128]{2,1,0:T(8,128)(2,1)}, bf16[1,1601,128]{2,1,0:T(8,128)(2,1)}) fusion(bf16[1616,128]{1,0:T(8,128)(2,1)} %collective-permute-done.10, bf16[2,1616,128]{2,1,0:T(8,128)(2,1)} %collective-permute-done.9, bf16[2,1616,128]{2,1,0:T(8,128)(2,1)S(1)} %copy-done.3, bf16[1616,128]{1,0:T(8,128)(2,1)} %copy-done.4), kind=kLoop, calls=%fused_computation.9 | loop fusion | flops 2459136 | bytes 3278848 | tf_op jit(solution)/shard_map/broadcast_in_dim | solution.py:538
  140.0 2.8 %collect_2.1 = (bf16[128,4096]{1,0:T(8,128)(2,1)}, bf16[128,4096]{1,0:T(8,128)(2,1)}) custom-call(s32[4,32]{1,0:T(4,128)} %bitcast.27, bf16[8,2,2,32,1024]{4,3,2,1,0:T(8,128)(2,1)} %all-to-all-done.2.returned, bf16[128,4096]{1,0:T(8,128)(2,1)} %get-tuple-element.78.refs_0_, ...), custom_call_target="tpu_custom_call", output_to_operand_aliasing={{0}: (2, {}), {1}: (3, {})} | custom-call | bytes 4194304 | tf_op jit(solution)/shard_map/collect_2/pallas_call | solution.py:484
  (15 shorter events, 0.0 us)
Async XLA Ops:
  3.5 4.9 %collective-permute-start = (bf16[2,2,32,1024]{3,2,1,0:T(8,128)(2,1)}, bf16[2,2,32,1024]{3,2,1,0:T(8,128)(2,1)S(1)}, u32[]{:S(2)}, u32[]{:S(2)}) collective-permute-start(bf16[2,2,32,1024]{3,2,1,0:T(8,128)(2,1)} %get-tuple-element.48), channel_id=1, source_target_pairs={{0,1},{1,0},{2,3},{3,2},{4,5},{5,4},{6,7},{7,6},{8,9},{9,8},{10,11... | collective-permute-start | bytes 786440 | tf_op jit(solution)/shard_map/ppermute | solution.py:397
  4.0 9.9 %collective-permute-start.1 = (bf16[2,2,32,1024]{3,2,1,0:T(8,128)(2,1)}, bf16[2,2,32,1024]{3,2,1,0:T(8,128)(2,1)S(1)}, u32[]{:S(2)}, u32[]{:S(2)}) collective-permute-start(bf16[2,2,32,1024]{3,2,1,0:T(8,128)(2,1)} %get-tuple-element.49), channel_id=1, source_target_pairs={{0,2},{1,3},{2,0},{3,1},{4,6},{5,7},{6,4},{7,5},{8,10},{9,11},{10,... | collective-permute-start | bytes 786440 | tf_op jit(solution)/shard_map/ppermute | solution.py:397
  6.5 16.2 %collective-permute-start.2 = (bf16[2,2,32,1024]{3,2,1,0:T(8,128)(2,1)}, bf16[2,2,32,1024]{3,2,1,0:T(8,128)(2,1)S(1)}, u32[]{:S(2)}, u32[]{:S(2)}) collective-permute-start(bf16[2,2,32,1024]{3,2,1,0:T(8,128)(2,1)} %get-tuple-element.50), channel_id=1, source_target_pairs={{0,3},{1,2},{2,1},{3,0},{4,7},{5,6},{6,5},{7,4},{8,11},{9,10},{10,... | collective-permute-start | bytes 786440 | tf_op jit(solution)/shard_map/ppermute | solution.py:397
  6.6 16.1 %collective-permute-start.3 = (bf16[2,2,32,1024]{3,2,1,0:T(8,128)(2,1)}, bf16[2,2,32,1024]{3,2,1,0:T(8,128)(2,1)}, u32[]{:S(2)}, u32[]{:S(2)}) collective-permute-start(bf16[2,2,32,1024]{3,2,1,0:T(8,128)(2,1)} %get-tuple-element.51), channel_id=1, source_target_pairs={{0,4},{1,5},{2,6},{3,7},{4,0},{5,1},{6,2},{7,3},{8,12},{9,13},{10,... | collective-permute-start | bytes 786440 | tf_op jit(solution)/shard_map/ppermute | solution.py:397
  8.4 23.2 %collective-permute-start.4 = (bf16[2,2,32,1024]{3,2,1,0:T(8,128)(2,1)}, bf16[2,2,32,1024]{3,2,1,0:T(8,128)(2,1)}, u32[]{:S(2)}, u32[]{:S(2)}) collective-permute-start(bf16[2,2,32,1024]{3,2,1,0:T(8,128)(2,1)} %get-tuple-element.52), channel_id=1, source_target_pairs={{0,5},{1,4},{2,7},{3,6},{4,1},{5,0},{6,3},{7,2},{8,13},{9,12},{10,... | collective-permute-start | bytes 786440 | tf_op jit(solution)/shard_map/ppermute | solution.py:397
  8.4 14.3 %copy-start = (bf16[2,2,32,1024]{3,2,1,0:T(8,128)(2,1)}, bf16[2,2,32,1024]{3,2,1,0:T(8,128)(2,1)S(1)}, u32[]{:S(2)}) copy-start(bf16[2,2,32,1024]{3,2,1,0:T(8,128)(2,1)S(1)} %collective-permute-done.refs_1_) | copy-start | bytes 786436
  8.4 23.2 %collective-permute-start.5 = (bf16[2,2,32,1024]{3,2,1,0:T(8,128)(2,1)}, bf16[2,2,32,1024]{3,2,1,0:T(8,128)(2,1)}, u32[]{:S(2)}, u32[]{:S(2)}) collective-permute-start(bf16[2,2,32,1024]{3,2,1,0:T(8,128)(2,1)} %get-tuple-element.53), channel_id=1, source_target_pairs={{0,6},{1,7},{2,4},{3,5},{4,2},{5,3},{6,0},{7,1},{8,14},{9,15},{10,... | collective-permute-start | bytes 786440 | tf_op jit(solution)/shard_map/ppermute | solution.py:397
  13.9 8.8 %copy-start.1 = (bf16[2,2,32,1024]{3,2,1,0:T(8,128)(2,1)}, bf16[2,2,32,1024]{3,2,1,0:T(8,128)(2,1)S(1)}, u32[]{:S(2)}) copy-start(bf16[2,2,32,1024]{3,2,1,0:T(8,128)(2,1)S(1)} %collective-permute-done.1.refs_2_) | copy-start | bytes 786436
  13.9 17.7 %collective-permute-start.6 = (bf16[2,2,32,1024]{3,2,1,0:T(8,128)(2,1)}, bf16[2,2,32,1024]{3,2,1,0:T(8,128)(2,1)}, u32[]{:S(2)}, u32[]{:S(2)}) collective-permute-start(bf16[2,2,32,1024]{3,2,1,0:T(8,128)(2,1)} %get-tuple-element.54), channel_id=1, source_target_pairs={{0,7},{1,6},{2,5},{3,4},{4,3},{5,2},{6,1},{7,0},{8,15},{9,14},{10,... | collective-permute-start | bytes 786440 | tf_op jit(solution)/shard_map/ppermute | solution.py:397
  22.7 8.9 %copy-start.2 = (bf16[2,2,32,1024]{3,2,1,0:T(8,128)(2,1)}, bf16[2,2,32,1024]{3,2,1,0:T(8,128)(2,1)S(1)}, u32[]{:S(2)}) copy-start(bf16[2,2,32,1024]{3,2,1,0:T(8,128)(2,1)S(1)} %collective-permute-done.2.refs_3_) | copy-start | bytes 786436
  31.6 37.5 %all-to-all-start.1 = ((bf16[8,2,2,32,1024]{4,3,2,1,0:T(8,128)(2,1)}), bf16[8,2,2,32,1024]{4,3,2,1,0:T(8,128)(2,1)}, u32[]{:S(2)}, u32[]{:S(2)}) async-start(bf16[8,2,2,32,1024]{4,3,2,1,0:T(8,128)(2,1)} %get-tuple-element.72), calls=%async_computation.1 | async-start | bytes 4194304 | tf_op jit(solution)/shard_map/all_to_all | solution.py:501
  45.8 21.1 %collective-permute-start.7 = (bf16[2,1616,128]{2,1,0:T(8,128)(2,1)}, bf16[2,1616,128]{2,1,0:T(8,128)(2,1)S(1)}, u32[]{:S(2)}, u32[]{:S(2)}) collective-permute-start(bf16[2,1616,128]{2,1,0:T(8,128)(2,1)} %get-tuple-element.66), channel_id=1, source_target_pairs={{0,8},{8,0},{16,24},{24,16},{1,9},{9,1},{17,25},{25,17},{2,10},{10... | collective-permute-start | bytes 2482184 | tf_op jit(solution)/shard_map/ppermute | solution.py:397
  69.1 34.0 %all-to-all-start = ((bf16[8,2,2,32,1024]{4,3,2,1,0:T(8,128)(2,1)}), bf16[8,2,2,32,1024]{4,3,2,1,0:T(8,128)(2,1)}, u32[]{:S(2)}, u32[]{:S(2)}) async-start(bf16[8,2,2,32,1024]{4,3,2,1,0:T(8,128)(2,1)} %get-tuple-element.70), calls=%async_computation | async-start | bytes 4194304 | tf_op jit(solution)/shard_map/all_to_all | solution.py:501
  76.4 22.1 %collective-permute-start.8 = (bf16[1616,128]{1,0:T(8,128)(2,1)}, bf16[1616,128]{1,0:T(8,128)(2,1)S(1)}, u32[]{:S(2)}, u32[]{:S(2)}) collective-permute-start(bf16[1616,128]{1,0:T(8,128)(2,1)} %get-tuple-element.71), channel_id=1, source_target_pairs={{0,16},{8,24},{16,0},{24,8},{1,17},{9,25},{17,1},{25,9},{2,18},{10... | collective-permute-start | bytes 1241096 | tf_op jit(solution)/shard_map/ppermute | solution.py:397
  98.5 4.7 %copy-start.4 = (bf16[1616,128]{1,0:T(8,128)(2,1)}, bf16[1616,128]{1,0:T(8,128)(2,1)S(1)}, u32[]{:S(2)}) copy-start(bf16[1616,128]{1,0:T(8,128)(2,1)S(1)} %collective-permute-done.8) | copy-start | bytes 1241092
  103.2 36.8 %all-to-all-start.2 = ((bf16[8,2,2,32,1024]{4,3,2,1,0:T(8,128)(2,1)}), bf16[8,2,2,32,1024]{4,3,2,1,0:T(8,128)(2,1)}, u32[]{:S(2)}, u32[]{:S(2)}) async-start(bf16[8,2,2,32,1024]{4,3,2,1,0:T(8,128)(2,1)} %get-tuple-element.76), calls=%async_computation.2 | async-start | bytes 4194304 | tf_op jit(solution)/shard_map/all_to_all | solution.py:501
  107.6 29.9 %copy-start.3 = (bf16[2,1616,128]{2,1,0:T(8,128)(2,1)S(1)}, bf16[2,1616,128]{2,1,0:T(8,128)(2,1)}, u32[]{:S(2)}) copy-start(bf16[2,1616,128]{2,1,0:T(8,128)(2,1)} %get-tuple-element.82) | copy-start | bytes 2482180
  107.6 29.9 %collective-permute-start.9 = (bf16[2,1616,128]{2,1,0:T(8,128)(2,1)}, bf16[2,1616,128]{2,1,0:T(8,128)(2,1)}, u32[]{:S(2)}, u32[]{:S(2)}) collective-permute-start(bf16[2,1616,128]{2,1,0:T(8,128)(2,1)} %get-tuple-element.83), channel_id=1, source_target_pairs={{0,8},{8,0},{16,24},{24,16},{1,9},{9,1},{17,25},{25,17},{2,10},{10... | collective-permute-start | bytes 2482184 | tf_op jit(solution)/shard_map/ppermute | solution.py:397
  109.1 27.5 %collective-permute-start.10 = (bf16[1616,128]{1,0:T(8,128)(2,1)}, bf16[1616,128]{1,0:T(8,128)(2,1)}, u32[]{:S(2)}, u32[]{:S(2)}) collective-permute-start(bf16[1616,128]{1,0:T(8,128)(2,1)} %get-tuple-element.85), channel_id=1, source_target_pairs={{0,16},{8,24},{16,0},{24,8},{1,17},{9,25},{17,1},{25,9},{2,18},{10... | collective-permute-start | bytes 1241096 | tf_op jit(solution)/shard_map/ppermute | solution.py:397

commit v12 on v11

--- a/solution.py
+++ b/solution.py
@@ -500,8 +500,13 @@
     def exchange(array):
         return lax.all_to_all(array, "enc", split_axis=0, concat_axis=0, tiled=True)
 
+    def exchange_apart(arrays):
+        order = sorted(range(peers), key=lambda k: (-(k >> 1).bit_count(), k & 1, k))
+        arrived = {k: xor_permute(arrays[k], "enc", k) for k in order}
+        return [arrived[k] for k in range(peers)]
+
     first, second = chunks
-    received = [xor_permute(array, "enc", k) for k, array in enumerate(route(first, 0))]
+    received = exchange_apart(route(first, 0))
     routed, *prepared = route(second, 1)
     *received, routed = lax.optimization_barrier((*received, routed))
     received_later = exchange(routed)
@@ -514,7 +519,6 @@
     if butterfly:
         passed, last = lax.optimization_barrier((passed, last))
         pair = [(last[j].astype(f32) + passed[j].astype(f32)).astype(bf16) for j in range(2)]
-        returned, *pair = lax.optimization_barrier((returned, *pair))
         pair = [xor_permute(one, "seq", 2) for one in pair]
     answer = exchange(returned)
     received_later, returned = lax.optimization_barrier((received_later, returned))
@@ -524,7 +528,8 @@
     answer, returned = lax.optimization_barrier((answer, returned))
     answer_later = exchange(returned)
     if butterfly:
-        near = xor_permute(more[0], "seq", 1)
+        pair[1], turn_two = lax.optimization_barrier((pair[1], more[0]))
+        near = xor_permute(turn_two, "seq", 1)
     half = collect(first, answer, [])
     attended, grad_queries = collect(second, answer_later, half)
 

time: 144 us -> 151 us (1.049)
  Pallas kernels: 48.5 us -> 65.4 us
  starting transfers between devices: 32.6 us -> 27.7 us
  waiting for transfers between devices: 56.1 us -> 52 us
    pallas_call x3, Pallas kernels: 33.1 us -> 50 us  [attend(): pl.pallas_call(functools.partial(attend_kernel, turns, offset, len(before...]
    all_to_all x3, waiting for transfers between devices: 4.66 us -> 0.01 us  [exchange(): return lax.all_to_all(array, 'enc', split_axis=0, concat_axis=0, tiled=True)]
    all_to_all x3, starting transfers between devices: 16 us -> 13.2 us  [exchange(): return lax.all_to_all(array, 'enc', split_axis=0, concat_axis=0, tiled=True)]
    ppermute x11, starting transfers between devices: 16.6 us -> 14.5 us  [xor_permute(): return lax.ppermute(array, axis, [(i, i ^ k) for i in range(size)])]
  transfers between devices with their start and end apart: 14 -> 14, of which waited for: 7 -> 5; matrix products, arithmetic and copies ran while one was open for 3% -> 2% of each run, Pallas kernels for 30% -> 39%
where the time goes in v12:
time: 151 us
  Pallas kernels  65.4 us (43%)
  waiting for transfers between devices  52 us (34%)
  starting transfers between devices  27.7 us (18%)
  other arithmetic  3.69 us (2%)
    ppermute x11, waiting for transfers between devices, xor_permute(): return lax.ppermute(array, axis, [(i, i ^ k) for i in range(size)])  52 us
    pallas_call x3, Pallas kernels, attend(): pl.pallas_call(functools.partial(attend_kernel, turns, offset, len(before...  50 us
    ppermute x11, starting transfers between devices, xor_permute(): return lax.ppermute(array, axis, [(i, i ^ k) for i in range(size)])  14.5 us
    all_to_all x3, starting transfers between devices, exchange(): return lax.all_to_all(array, 'enc', split_axis=0, concat_axis=0, tiled=True)  13.2 us
    pallas_call x2, Pallas kernels, route(): pl.pallas_call(functools.partial(route_kernel, turns, not prepares, n_seg...  9.76 us
    pallas_call x2, Pallas kernels, collect(): pl.pallas_call(functools.partial(collect_kernel, turns, n_seg, seg_rows),...  5.64 us
  transfers between devices with their start and end apart: 14, of which 5 were waited for; matrix products, arithmetic and copies ran while one was open for 2% of the time, Pallas kernels for 39%

profile of v12, /device:TPU:0, one launch (start us, length us, event | category | flops | bytes accessed | tf_op | source)
XLA Modules:
  0.0 151.3 jit_solution(169873205656081304)
XLA Ops:
  0.6 2.8 %route_0.1 = (bf16[2,2,32,1024]{3,2,1,0:T(8,128)(2,1)}, bf16[2,2,32,1024]{3,2,1,0:T(8,128)(2,1)}, bf16[2,2,32,1024]{3,2,1,0:T(8,128)(2,1)}, bf16[2,2,32,1024]{3,...) custom-call(s32[4,32]{1,0:T(4,128)} %bitcast.21, ...), custom_call_target="tpu_custom_call" | custom-call | bytes 2097152 | tf_op jit(solution)/shard_map/route_0/pallas_call | solution.py:422
  3.5 0.5 collective-permute-start
  4.0 2.6 %collective-permute-start.1 = (bf16[2,2,32,1024]{3,2,1,0:T(8,128)(2,1)}, bf16[2,2,32,1024]{3,2,1,0:T(8,128)(2,1)S(1)}, u32[]{:S(2)}, u32[]{:S(2)}) collective-permute-start(bf16[2,2,32,1024]{3,2,1,0:T(8,128)(2,1)} %get-tuple-element.48), channel_id=1, source_target_pairs={{0,2},{1,3},{2,0},{3,1},{4,6},{5,7},{6,4},{7,5},{8,10},{9,11},{10,... | collective-permute-start | bytes 786440 | tf_op jit(solution)/shard_map/ppermute | solution.py:397
  6.5 0.1 collective-permute-start.2
  6.6 1.8 %collective-permute-start.3 = (bf16[2,2,32,1024]{3,2,1,0:T(8,128)(2,1)}, bf16[2,2,32,1024]{3,2,1,0:T(8,128)(2,1)}, u32[]{:S(2)}, u32[]{:S(2)}) collective-permute-start(bf16[2,2,32,1024]{3,2,1,0:T(8,128)(2,1)} %get-tuple-element.50), channel_id=1, source_target_pairs={{0,4},{1,5},{2,6},{3,7},{4,0},{5,1},{6,2},{7,3},{8,12},{9,13},{10,... | collective-permute-start | bytes 786440 | tf_op jit(solution)/shard_map/ppermute | solution.py:397
  8.4 0.0 collective-permute-start.4
  8.4 0.0 collective-permute-done.refs_1_
  8.4 2.6 %collective-permute-start.5 = (bf16[2,2,32,1024]{3,2,1,0:T(8,128)(2,1)}, bf16[2,2,32,1024]{3,2,1,0:T(8,128)(2,1)}, u32[]{:S(2)}, u32[]{:S(2)}) collective-permute-start(bf16[2,2,32,1024]{3,2,1,0:T(8,128)(2,1)} %get-tuple-element.52), channel_id=1, source_target_pairs={{0,6},{1,7},{2,4},{3,5},{4,2},{5,3},{6,0},{7,1},{8,14},{9,15},{10,... | collective-permute-start | bytes 786440 | tf_op jit(solution)/shard_map/ppermute | solution.py:397
  11.0 2.9 %collective-permute-done.1.refs_2_ = bf16[2,2,32,1024]{3,2,1,0:T(8,128)(2,1)S(1)} collective-permute-done((bf16[2,2,32,1024]{3,2,1,0:T(8,128)(2,1)}, bf16[2,2,32,1024]{3,2,1,0:T(8,128)(2,1)S(1)}, u32[]{:S(2)}, u32[]{:S(2)}) %collective-permute-start.1) | collective-permute-done | bytes 262176 | tf_op jit(solution)/shard_map/ppermute | solution.py:397
  13.9 1.8 %collective-permute-start.6 = (bf16[2,2,32,1024]{3,2,1,0:T(8,128)(2,1)}, bf16[2,2,32,1024]{3,2,1,0:T(8,128)(2,1)}, u32[]{:S(2)}, u32[]{:S(2)}) collective-permute-start(bf16[2,2,32,1024]{3,2,1,0:T(8,128)(2,1)} %get-tuple-element.53), channel_id=1, source_target_pairs={{0,7},{1,6},{2,5},{3,4},{4,3},{5,2},{6,1},{7,0},{8,15},{9,14},{10,... | collective-permute-start | bytes 786440 | tf_op jit(solution)/shard_map/ppermute | solution.py:397
  15.7 6.9 %route_2.1 = (bf16[8,2,2,32,1024]{4,3,2,1,0:T(8,128)(2,1)}, bf16[4,2,1616,128]{3,2,1,0:T(8,128)(2,1)}, bf16[4,2,128,1616]{3,2,1,0:T(8,128)(2,1)}) custom-call(s32[4,32]{1,0:T(4,128)} %bitcast.22, bf16[128,4096]{1,0:T(8,128)(2,1)} %q_hbm.3, bf16[128,4096]{1,0:T(8,128)(2,1)} %g_hbm.3, bf16[1,1601,512]{2,1,0:T(8,128)(2,1)} %refs_0_.1, bf16[1,1601,512]{2,1,0:T(8,128)(2,1)} %refs_1_.1), custom_call_target="tpu_custom_call" | custom-call | bytes 12582912 | tf_op jit(solution)/shard_map/route_2/pallas_call | solution.py:422
  22.7 8.9 %collective-permute-done.4.refs_5_ = bf16[2,2,32,1024]{3,2,1,0:T(8,128)(2,1)} collective-permute-done((bf16[2,2,32,1024]{3,2,1,0:T(8,128)(2,1)}, bf16[2,2,32,1024]{3,2,1,0:T(8,128)(2,1)}, u32[]{:S(2)}, u32[]{:S(2)}) %collective-permute-start.4) | collective-permute-done | bytes 262176 | tf_op jit(solution)/shard_map/ppermute | solution.py:397
  31.6 4.4 %all-to-all-start.1 = ((bf16[8,2,2,32,1024]{4,3,2,1,0:T(8,128)(2,1)}), bf16[8,2,2,32,1024]{4,3,2,1,0:T(8,128)(2,1)}, u32[]{:S(2)}, u32[]{:S(2)}) async-start(bf16[8,2,2,32,1024]{4,3,2,1,0:T(8,128)(2,1)} %get-tuple-element.69), calls=%async_computation.1 | async-start | bytes 4194304 | tf_op jit(solution)/shard_map/all_to_all | solution.py:501
  36.0 13.1 %attend_0.1 = (bf16[8,2,2,32,1024]{4,3,2,1,0:T(8,128)(2,1)}, bf16[2,1616,128]{2,1,0:T(8,128)(2,1)}) custom-call(s32[4,32]{1,0:T(4,128)} %bitcast.23, bf16[4,2,1616,128]{3,2,1,0:T(8,128)(2,1)} %get-tuple-element.44.caches, bf16[4,2,128,1616]{3,2,1,0:T(8,128)(2,1)} %get-tuple-element.45.turned_caches, bf16[2,2,32,1024]{3,2,1,0:T(8,128)(2,1)} %get-tuple-element.55.refs_0_, ...), custom_call_target="tpu_custom_call" | custom-call | flops 314769408 | bytes 1048576 | tf_op jit(solution)/shard_map/attend_0/pallas_call | solution.py:449
  49.1 2.1 %collective-permute-start.7 = (bf16[2,1616,128]{2,1,0:T(8,128)(2,1)}, bf16[2,1616,128]{2,1,0:T(8,128)(2,1)S(1)}, u32[]{:S(2)}, u32[]{:S(2)}) collective-permute-start(bf16[2,1616,128]{2,1,0:T(8,128)(2,1)} %get-tuple-element.65), channel_id=1, source_target_pairs={{0,8},{8,0},{16,24},{24,16},{1,9},{9,1},{17,25},{25,17},{2,10},{10... | collective-permute-start | bytes 2482184 | tf_op jit(solution)/shard_map/ppermute | solution.py:397
  51.2 13.2 %attend_1.1 = (bf16[8,2,2,32,1024]{4,3,2,1,0:T(8,128)(2,1)}, bf16[2,1616,128]{2,1,0:T(8,128)(2,1)}) custom-call(s32[4,32]{1,0:T(4,128)} %bitcast.24, bf16[4,2,1616,128]{3,2,1,0:T(8,128)(2,1)} %get-tuple-element.44.caches, bf16[4,2,128,1616]{3,2,1,0:T(8,128)(2,1)} %get-tuple-element.45.turned_caches, ...), custom_call_target="tpu_custom_call", output_to_operand_aliasing={{0}: (11, {})} | custom-call | flops 314769408 | bytes 1048576 | tf_op jit(solution)/shard_map/attend_1/pallas_call | solution.py:449
  64.4 0.0 copy-start.3
  64.4 4.5 %all-to-all-start = ((bf16[8,2,2,32,1024]{4,3,2,1,0:T(8,128)(2,1)}), bf16[8,2,2,32,1024]{4,3,2,1,0:T(8,128)(2,1)}, u32[]{:S(2)}, u32[]{:S(2)}) async-start(bf16[8,2,2,32,1024]{4,3,2,1,0:T(8,128)(2,1)} %get-tuple-element.64), calls=%async_computation | async-start | bytes 4194304 | tf_op jit(solution)/shard_map/all_to_all | solution.py:501
  68.9 1.3 collective-permute-done.7
  70.3 1.1 fusion.3
  71.4 2.8 %collective-permute-start.8 = (bf16[1616,128]{1,0:T(8,128)(2,1)}, bf16[1616,128]{1,0:T(8,128)(2,1)S(1)}, u32[]{:S(2)}, u32[]{:S(2)}) collective-permute-start(bf16[1616,128]{1,0:T(8,128)(2,1)} %get-tuple-element.87), channel_id=1, source_target_pairs={{0,16},{8,24},{16,0},{24,8},{1,17},{9,25},{17,1},{25,9},{2,18},{10... | collective-permute-start | bytes 1241096 | tf_op jit(solution)/shard_map/ppermute | solution.py:397
  74.2 23.7 %attend_2.1 = (bf16[8,2,2,32,1024]{4,3,2,1,0:T(8,128)(2,1)}, bf16[2,1616,128]{2,1,0:T(8,128)(2,1)}, bf16[2,1616,128]{2,1,0:T(8,128)(2,1)}) custom-call(s32[4,32]{1,0:T(4,128)} %bitcast.25, bf16[4,2,1616,128]{3,2,1,0:T(8,128)(2,1)} %get-tuple-element.44.caches, bf16[4,2,128,1616]{3,2,1,0:T(8,128)(2,1)} %get-tuple-element.45.turned_caches, ...), custom_call_target="tpu_custom_call" | custom-call | flops 7554465792 | bytes 8388608 | tf_op jit(solution)/shard_map/attend_2/pallas_call | solution.py:449
  98.0 0.0 copy-start.5
  98.0 0.7 copy-done.6
  98.7 4.4 %all-to-all-start.2 = ((bf16[8,2,2,32,1024]{4,3,2,1,0:T(8,128)(2,1)}), bf16[8,2,2,32,1024]{4,3,2,1,0:T(8,128)(2,1)}, u32[]{:S(2)}, u32[]{:S(2)}) async-start(bf16[8,2,2,32,1024]{4,3,2,1,0:T(8,128)(2,1)} %get-tuple-element.73), calls=%async_computation.2 | async-start | bytes 4194304 | tf_op jit(solution)/shard_map/all_to_all | solution.py:501
  103.1 0.2 collective-permute-start.9
  103.3 21.4 %collective-permute-done.9 = bf16[1616,128]{1,0:T(8,128)(2,1)S(1)} collective-permute-done((bf16[1616,128]{1,0:T(8,128)(2,1)S(1)}, bf16[1616,128]{1,0:T(8,128)(2,1)S(1)}, u32[]{:S(2)}, u32[]{:S(2)}) %collective-permute-start.9) | collective-permute-done | bytes 413728 | tf_op jit(solution)/shard_map/ppermute | solution.py:397
  124.7 0.7 copy-done.7
  125.5 2.8 %collect_0.1 = (bf16[128,4096]{1,0:T(8,128)(2,1)}, bf16[128,4096]{1,0:T(8,128)(2,1)}) custom-call(s32[4,32]{1,0:T(4,128)} %bitcast.26, bf16[8,2,2,32,1024]{4,3,2,1,0:T(8,128)(2,1)} %all-to-all-done.returned), custom_call_target="tpu_custom_call" | custom-call | bytes 4194304 | tf_op jit(solution)/shard_map/collect_0/pallas_call | solution.py:484
  128.3 17.5 %collective-permute-done.10 = bf16[2,1616,128]{2,1,0:T(8,128)(2,1)} collective-permute-done((bf16[2,1616,128]{2,1,0:T(8,128)(2,1)}, bf16[2,1616,128]{2,1,0:T(8,128)(2,1)}, u32[]{:S(2)}, u32[]{:S(2)}) %collective-permute-start.10) | collective-permute-done | bytes 827424 | tf_op jit(solution)/shard_map/ppermute | solution.py:397
  145.8 2.6 %fusion.5 = (bf16[1,1601,128]{2,1,0:T(8,128)(2,1)}, bf16[1,1601,128]{2,1,0:T(8,128)(2,1)}) fusion(bf16[2,1616,128]{2,1,0:T(8,128)(2,1)} %collective-permute-done.10, bf16[1616,128]{1,0:T(8,128)(2,1)} %copy-done.7, bf16[2,1616,128]{2,1,0:T(8,128)(2,1)S(1)} %copy-done.4, bf16[1616,128]{1,0:T(8,128)(2,1)} %copy-done.6), kind=kLoop, calls=%fused_computation.9 | loop fusion | flops 2459136 | bytes 3278848 | tf_op jit(solution)/shard_map/broadcast_in_dim | solution.py:543
  148.3 2.8 %collect_2.1 = (bf16[128,4096]{1,0:T(8,128)(2,1)}, bf16[128,4096]{1,0:T(8,128)(2,1)}) custom-call(s32[4,32]{1,0:T(4,128)} %bitcast.27, bf16[8,2,2,32,1024]{4,3,2,1,0:T(8,128)(2,1)} %all-to-all-done.2.returned, bf16[128,4096]{1,0:T(8,128)(2,1)} %get-tuple-element.75.refs_0_, ...), custom_call_target="tpu_custom_call", output_to_operand_aliasing={{0}: (2, {}), {1}: (3, {})} | custom-call | bytes 4194304 | tf_op jit(solution)/shard_map/collect_2/pallas_call | solution.py:484
  (21 shorter events, 0.0 us)
Async XLA Ops:
  3.5 4.9 %collective-permute-start = (bf16[2,2,32,1024]{3,2,1,0:T(8,128)(2,1)}, bf16[2,2,32,1024]{3,2,1,0:T(8,128)(2,1)S(1)}, u32[]{:S(2)}, u32[]{:S(2)}) collective-permute-start(bf16[2,2,32,1024]{3,2,1,0:T(8,128)(2,1)} %get-tuple-element.47), channel_id=1, source_target_pairs={{0,1},{1,0},{2,3},{3,2},{4,5},{5,4},{6,7},{7,6},{8,9},{9,8},{10,11... | collective-permute-start | bytes 786440 | tf_op jit(solution)/shard_map/ppermute | solution.py:397
  4.0 9.9 %collective-permute-start.1 = (bf16[2,2,32,1024]{3,2,1,0:T(8,128)(2,1)}, bf16[2,2,32,1024]{3,2,1,0:T(8,128)(2,1)S(1)}, u32[]{:S(2)}, u32[]{:S(2)}) collective-permute-start(bf16[2,2,32,1024]{3,2,1,0:T(8,128)(2,1)} %get-tuple-element.48), channel_id=1, source_target_pairs={{0,2},{1,3},{2,0},{3,1},{4,6},{5,7},{6,4},{7,5},{8,10},{9,11},{10,... | collective-permute-start | bytes 786440 | tf_op jit(solution)/shard_map/ppermute | solution.py:397
  6.5 16.2 %collective-permute-start.2 = (bf16[2,2,32,1024]{3,2,1,0:T(8,128)(2,1)}, bf16[2,2,32,1024]{3,2,1,0:T(8,128)(2,1)S(1)}, u32[]{:S(2)}, u32[]{:S(2)}) collective-permute-start(bf16[2,2,32,1024]{3,2,1,0:T(8,128)(2,1)} %get-tuple-element.49), channel_id=1, source_target_pairs={{0,3},{1,2},{2,1},{3,0},{4,7},{5,6},{6,5},{7,4},{8,11},{9,10},{10,... | collective-permute-start | bytes 786440 | tf_op jit(solution)/shard_map/ppermute | solution.py:397
  6.6 16.1 %collective-permute-start.3 = (bf16[2,2,32,1024]{3,2,1,0:T(8,128)(2,1)}, bf16[2,2,32,1024]{3,2,1,0:T(8,128)(2,1)}, u32[]{:S(2)}, u32[]{:S(2)}) collective-permute-start(bf16[2,2,32,1024]{3,2,1,0:T(8,128)(2,1)} %get-tuple-element.50), channel_id=1, source_target_pairs={{0,4},{1,5},{2,6},{3,7},{4,0},{5,1},{6,2},{7,3},{8,12},{9,13},{10,... | collective-permute-start | bytes 786440 | tf_op jit(solution)/shard_map/ppermute | solution.py:397
  8.4 23.2 %collective-permute-start.4 = (bf16[2,2,32,1024]{3,2,1,0:T(8,128)(2,1)}, bf16[2,2,32,1024]{3,2,1,0:T(8,128)(2,1)}, u32[]{:S(2)}, u32[]{:S(2)}) collective-permute-start(bf16[2,2,32,1024]{3,2,1,0:T(8,128)(2,1)} %get-tuple-element.51), channel_id=1, source_target_pairs={{0,5},{1,4},{2,7},{3,6},{4,1},{5,0},{6,3},{7,2},{8,13},{9,12},{10,... | collective-permute-start | bytes 786440 | tf_op jit(solution)/shard_map/ppermute | solution.py:397
  8.4 14.3 %copy-start = (bf16[2,2,32,1024]{3,2,1,0:T(8,128)(2,1)}, bf16[2,2,32,1024]{3,2,1,0:T(8,128)(2,1)S(1)}, u32[]{:S(2)}) copy-start(bf16[2,2,32,1024]{3,2,1,0:T(8,128)(2,1)S(1)} %collective-permute-done.refs_1_) | copy-start | bytes 786436
  8.4 23.2 %collective-permute-start.5 = (bf16[2,2,32,1024]{3,2,1,0:T(8,128)(2,1)}, bf16[2,2,32,1024]{3,2,1,0:T(8,128)(2,1)}, u32[]{:S(2)}, u32[]{:S(2)}) collective-permute-start(bf16[2,2,32,1024]{3,2,1,0:T(8,128)(2,1)} %get-tuple-element.52), channel_id=1, source_target_pairs={{0,6},{1,7},{2,4},{3,5},{4,2},{5,3},{6,0},{7,1},{8,14},{9,15},{10,... | collective-permute-start | bytes 786440 | tf_op jit(solution)/shard_map/ppermute | solution.py:397
  13.9 8.8 %copy-start.1 = (bf16[2,2,32,1024]{3,2,1,0:T(8,128)(2,1)}, bf16[2,2,32,1024]{3,2,1,0:T(8,128)(2,1)S(1)}, u32[]{:S(2)}) copy-start(bf16[2,2,32,1024]{3,2,1,0:T(8,128)(2,1)S(1)} %collective-permute-done.1.refs_2_) | copy-start | bytes 786436
  13.9 17.7 %collective-permute-start.6 = (bf16[2,2,32,1024]{3,2,1,0:T(8,128)(2,1)}, bf16[2,2,32,1024]{3,2,1,0:T(8,128)(2,1)}, u32[]{:S(2)}, u32[]{:S(2)}) collective-permute-start(bf16[2,2,32,1024]{3,2,1,0:T(8,128)(2,1)} %get-tuple-element.53), channel_id=1, source_target_pairs={{0,7},{1,6},{2,5},{3,4},{4,3},{5,2},{6,1},{7,0},{8,15},{9,14},{10,... | collective-permute-start | bytes 786440 | tf_op jit(solution)/shard_map/ppermute | solution.py:397
  22.7 8.9 %copy-start.2 = (bf16[2,2,32,1024]{3,2,1,0:T(8,128)(2,1)}, bf16[2,2,32,1024]{3,2,1,0:T(8,128)(2,1)S(1)}, u32[]{:S(2)}) copy-start(bf16[2,2,32,1024]{3,2,1,0:T(8,128)(2,1)S(1)} %collective-permute-done.2.refs_3_) | copy-start | bytes 786436
  31.6 32.8 %all-to-all-start.1 = ((bf16[8,2,2,32,1024]{4,3,2,1,0:T(8,128)(2,1)}), bf16[8,2,2,32,1024]{4,3,2,1,0:T(8,128)(2,1)}, u32[]{:S(2)}, u32[]{:S(2)}) async-start(bf16[8,2,2,32,1024]{4,3,2,1,0:T(8,128)(2,1)} %get-tuple-element.69), calls=%async_computation.1 | async-start | bytes 4194304 | tf_op jit(solution)/shard_map/all_to_all | solution.py:501
  49.1 21.2 %collective-permute-start.7 = (bf16[2,1616,128]{2,1,0:T(8,128)(2,1)}, bf16[2,1616,128]{2,1,0:T(8,128)(2,1)S(1)}, u32[]{:S(2)}, u32[]{:S(2)}) collective-permute-start(bf16[2,1616,128]{2,1,0:T(8,128)(2,1)} %get-tuple-element.65), channel_id=1, source_target_pairs={{0,8},{8,0},{16,24},{24,16},{1,9},{9,1},{17,25},{25,17},{2,10},{10... | collective-permute-start | bytes 2482184 | tf_op jit(solution)/shard_map/ppermute | solution.py:397
  64.4 5.8 %copy-start.3 = (bf16[2,1616,128]{2,1,0:T(8,128)(2,1)S(1)}, bf16[2,1616,128]{2,1,0:T(8,128)(2,1)}, u32[]{:S(2)}) copy-start(bf16[2,1616,128]{2,1,0:T(8,128)(2,1)} %get-tuple-element.67) | copy-start | bytes 2482180
  64.4 33.5 %all-to-all-start = ((bf16[8,2,2,32,1024]{4,3,2,1,0:T(8,128)(2,1)}), bf16[8,2,2,32,1024]{4,3,2,1,0:T(8,128)(2,1)}, u32[]{:S(2)}, u32[]{:S(2)}) async-start(bf16[8,2,2,32,1024]{4,3,2,1,0:T(8,128)(2,1)} %get-tuple-element.64), calls=%async_computation | async-start | bytes 4194304 | tf_op jit(solution)/shard_map/all_to_all | solution.py:501
  71.4 26.6 %collective-permute-start.8 = (bf16[1616,128]{1,0:T(8,128)(2,1)}, bf16[1616,128]{1,0:T(8,128)(2,1)S(1)}, u32[]{:S(2)}, u32[]{:S(2)}) collective-permute-start(bf16[1616,128]{1,0:T(8,128)(2,1)} %get-tuple-element.87), channel_id=1, source_target_pairs={{0,16},{8,24},{16,0},{24,8},{1,17},{9,25},{17,1},{25,9},{2,18},{10... | collective-permute-start | bytes 1241096 | tf_op jit(solution)/shard_map/ppermute | solution.py:397
  97.9 0.8 copy-start.6
  98.0 5.1 %copy-start.5 = (bf16[1616,128]{1,0:T(8,128)(2,1)S(1)}, bf16[1616,128]{1,0:T(8,128)(2,1)}, u32[]{:S(2)}) copy-start(bf16[1616,128]{1,0:T(8,128)(2,1)} %get-tuple-element.86) | copy-start | bytes 1241092
  98.7 49.6 %all-to-all-start.2 = ((bf16[8,2,2,32,1024]{4,3,2,1,0:T(8,128)(2,1)}), bf16[8,2,2,32,1024]{4,3,2,1,0:T(8,128)(2,1)}, u32[]{:S(2)}, u32[]{:S(2)}) async-start(bf16[8,2,2,32,1024]{4,3,2,1,0:T(8,128)(2,1)} %get-tuple-element.73), calls=%async_computation.2 | async-start | bytes 4194304 | tf_op jit(solution)/shard_map/all_to_all | solution.py:501
  103.1 42.7 %copy-start.4 = (bf16[2,1616,128]{2,1,0:T(8,128)(2,1)S(1)}, bf16[2,1616,128]{2,1,0:T(8,128)(2,1)}, u32[]{:S(2)}) copy-start(bf16[2,1616,128]{2,1,0:T(8,128)(2,1)} %get-tuple-element.79) | copy-start | bytes 2482180
  103.1 21.6 %collective-permute-start.9 = (bf16[1616,128]{1,0:T(8,128)(2,1)S(1)}, bf16[1616,128]{1,0:T(8,128)(2,1)S(1)}, u32[]{:S(2)}, u32[]{:S(2)}) collective-permute-start(bf16[1616,128]{1,0:T(8,128)(2,1)S(1)} %copy-done.5), channel_id=1, source_target_pairs={{0,16},{8,24},{16,0},{24,8},{1,17},{9,25},{17,1},{25,9},{2,18},{10... | collective-permute-start | bytes 1241096 | tf_op jit(solution)/shard_map/ppermute | solution.py:397
  124.7 0.7 copy-start.7
  125.5 20.3 %collective-permute-start.10 = (bf16[2,1616,128]{2,1,0:T(8,128)(2,1)}, bf16[2,1616,128]{2,1,0:T(8,128)(2,1)}, u32[]{:S(2)}, u32[]{:S(2)}) collective-permute-start(bf16[2,1616,128]{2,1,0:T(8,128)(2,1)} %get-tuple-element.81), channel_id=1, source_target_pairs={{0,8},{8,0},{16,24},{24,16},{1,9},{9,1},{17,25},{25,17},{2,10},{10... | collective-permute-start | bytes 2482184 | tf_op jit(solution)/shard_map/ppermute | solution.py:397

commit v13 on v12

--- a/solution.py
+++ b/solution.py
@@ -518,22 +518,27 @@
     grads.append(last)
     if butterfly:
         passed, last = lax.optimization_barrier((passed, last))
-        pair = [(last[j].astype(f32) + passed[j].astype(f32)).astype(bf16) for j in range(2)]
+        half = padded // 32 * 16
+        cuts = [(0, 0, padded), (1, 0, half), (1, half, padded)]
+        pair = [
+            (last[j, a:b].astype(f32) + passed[j, a:b].astype(f32)).astype(bf16)
+            for j, a, b in cuts
+        ]
         pair = [xor_permute(one, "seq", 2) for one in pair]
     answer = exchange(returned)
     received_later, returned = lax.optimization_barrier((received_later, returned))
     returned, *more = attend(second, 0, [received_later], [])
     if butterfly:
-        pair[0], returned = lax.optimization_barrier((pair[0], returned))
+        *pair[:2], returned = lax.optimization_barrier((*pair[:2], returned))
     answer, returned = lax.optimization_barrier((answer, returned))
     answer_later = exchange(returned)
     if butterfly:
-        pair[1], turn_two = lax.optimization_barrier((pair[1], more[0]))
-        near = xor_permute(turn_two, "seq", 1)
-    half = collect(first, answer, [])
-    attended, grad_queries = collect(second, answer_later, half)
+        near = xor_permute(more[0], "seq", 1)
+    early = collect(first, answer, [])
+    attended, grad_queries = collect(second, answer_later, early)
 
     if butterfly:
+        pair = [pair[0], jnp.concatenate(pair[1:], axis=0)]
         summed = [
             sum(
                 term[:tokens].astype(f32) for term in (more[1][j], near[j], pair[j])

time: 151 us -> 136 us (0.901)
  Pallas kernels: 65.4 us -> 51.8 us
  waiting for transfers between devices: 52 us -> 44.5 us
  starting transfers between devices: 27.7 us -> 31.9 us
  other arithmetic: 3.69 us -> 6.04 us
    pallas_call x3, Pallas kernels: 50 us -> 36.4 us  [attend(): pl.pallas_call(functools.partial(attend_kernel, turns, offset, len(before...]
    ppermute x11 -> x12, waiting for transfers between devices: 52 us -> 39.2 us  [xor_permute(): return lax.ppermute(array, axis, [(i, i ^ k) for i in range(size)])]
    all_to_all x3, waiting for transfers between devices: 0.01 us -> 5.32 us  [exchange(): return lax.all_to_all(array, 'enc', split_axis=0, concat_axis=0, tiled=True)]
    ppermute x11 -> x12, starting transfers between devices: 14.5 us -> 18.2 us  [xor_permute(): return lax.ppermute(array, axis, [(i, i ^ k) for i in range(size)])]
    convert_element_type x1 -> x3, other arithmetic: 1.1 us -> 3.27 us  [per_device(): (last[j, a:b].astype(f32) + passed[j, a:b].astype(f32)).astype(bf16)]
  transfers between devices with their start and end apart: 14 -> 15, of which waited for: 5 -> 7; matrix products, arithmetic and copies ran while one was open for 2% -> 4% of each run, Pallas kernels for 39% -> 34%
where the time goes in v13:
time: 136 us; the launch traced here: 135 us
  Pallas kernels  51.8 us (38%)
  waiting for transfers between devices  44.5 us (33%)
  starting transfers between devices  31.9 us (23%)
  other arithmetic  6.04 us (4%)
    ppermute x12, waiting for transfers between devices, xor_permute(): return lax.ppermute(array, axis, [(i, i ^ k) for i in range(size)])  39.2 us
    pallas_call x3, Pallas kernels, attend(): pl.pallas_call(functools.partial(attend_kernel, turns, offset, len(before...  36.4 us
    ppermute x12, starting transfers between devices, xor_permute(): return lax.ppermute(array, axis, [(i, i ^ k) for i in range(size)])  18.2 us
    all_to_all x3, starting transfers between devices, exchange(): return lax.all_to_all(array, 'enc', split_axis=0, concat_axis=0, tiled=True)  13.8 us
    pallas_call x2, Pallas kernels, route(): pl.pallas_call(functools.partial(route_kernel, turns, not prepares, n_seg...  9.77 us
    pallas_call x2, Pallas kernels, collect(): pl.pallas_call(functools.partial(collect_kernel, turns, n_seg, seg_rows),...  5.64 us
    all_to_all x3, waiting for transfers between devices, exchange(): return lax.all_to_all(array, 'enc', split_axis=0, concat_axis=0, tiled=True)  5.32 us
    convert_element_type x3, other arithmetic, per_device(): (last[j, a:b].astype(f32) + passed[j, a:b].astype(f32)).astype(bf16)  3.27 us
  transfers between devices with their start and end apart: 15, of which 7 were waited for; matrix products, arithmetic and copies ran while one was open for 4% of the time, Pallas kernels for 34%

profile of v13, /device:TPU:0, one launch (start us, length us, event | category | flops | bytes accessed | tf_op | source)
XLA Modules:
  0.0 135.2 jit_solution(2001656023222123921)
XLA Ops:
  0.6 2.8 %route_0.1 = (bf16[2,2,32,1024]{3,2,1,0:T(8,128)(2,1)}, bf16[2,2,32,1024]{3,2,1,0:T(8,128)(2,1)}, bf16[2,2,32,1024]{3,2,1,0:T(8,128)(2,1)}, bf16[2,2,32,1024]{3,...) custom-call(s32[4,32]{1,0:T(4,128)} %bitcast.23, ...), custom_call_target="tpu_custom_call" | custom-call | bytes 2097152 | tf_op jit(solution)/shard_map/route_0/pallas_call | solution.py:422
  3.5 0.5 collective-permute-start
  4.0 2.6 %collective-permute-start.1 = (bf16[2,2,32,1024]{3,2,1,0:T(8,128)(2,1)}, bf16[2,2,32,1024]{3,2,1,0:T(8,128)(2,1)S(1)}, u32[]{:S(2)}, u32[]{:S(2)}) collective-permute-start(bf16[2,2,32,1024]{3,2,1,0:T(8,128)(2,1)} %get-tuple-element.47), channel_id=1, source_target_pairs={{0,2},{1,3},{2,0},{3,1},{4,6},{5,7},{6,4},{7,5},{8,10},{9,11},{10,... | collective-permute-start | bytes 786440 | tf_op jit(solution)/shard_map/ppermute | solution.py:397
  6.5 0.1 collective-permute-start.2
  6.6 1.8 %collective-permute-start.3 = (bf16[2,2,32,1024]{3,2,1,0:T(8,128)(2,1)}, bf16[2,2,32,1024]{3,2,1,0:T(8,128)(2,1)}, u32[]{:S(2)}, u32[]{:S(2)}) collective-permute-start(bf16[2,2,32,1024]{3,2,1,0:T(8,128)(2,1)} %get-tuple-element.49), channel_id=1, source_target_pairs={{0,4},{1,5},{2,6},{3,7},{4,0},{5,1},{6,2},{7,3},{8,12},{9,13},{10,... | collective-permute-start | bytes 786440 | tf_op jit(solution)/shard_map/ppermute | solution.py:397
  8.4 2.6 %collective-permute-start.5 = (bf16[2,2,32,1024]{3,2,1,0:T(8,128)(2,1)}, bf16[2,2,32,1024]{3,2,1,0:T(8,128)(2,1)}, u32[]{:S(2)}, u32[]{:S(2)}) collective-permute-start(bf16[2,2,32,1024]{3,2,1,0:T(8,128)(2,1)} %get-tuple-element.51), channel_id=1, source_target_pairs={{0,6},{1,7},{2,4},{3,5},{4,2},{5,3},{6,0},{7,1},{8,14},{9,15},{10,... | collective-permute-start | bytes 786440 | tf_op jit(solution)/shard_map/ppermute | solution.py:397
  11.0 2.9 %collective-permute-done.1.refs_2_ = bf16[2,2,32,1024]{3,2,1,0:T(8,128)(2,1)S(1)} collective-permute-done((bf16[2,2,32,1024]{3,2,1,0:T(8,128)(2,1)}, bf16[2,2,32,1024]{3,2,1,0:T(8,128)(2,1)S(1)}, u32[]{:S(2)}, u32[]{:S(2)}) %collective-permute-start.1) | collective-permute-done | bytes 262176 | tf_op jit(solution)/shard_map/ppermute | solution.py:397
  13.9 1.8 %collective-permute-start.6 = (bf16[2,2,32,1024]{3,2,1,0:T(8,128)(2,1)}, bf16[2,2,32,1024]{3,2,1,0:T(8,128)(2,1)}, u32[]{:S(2)}, u32[]{:S(2)}) collective-permute-start(bf16[2,2,32,1024]{3,2,1,0:T(8,128)(2,1)} %get-tuple-element.52), channel_id=1, source_target_pairs={{0,7},{1,6},{2,5},{3,4},{4,3},{5,2},{6,1},{7,0},{8,15},{9,14},{10,... | collective-permute-start | bytes 786440 | tf_op jit(solution)/shard_map/ppermute | solution.py:397
  15.7 6.9 %route_2.1 = (bf16[8,2,2,32,1024]{4,3,2,1,0:T(8,128)(2,1)}, bf16[4,2,1616,128]{3,2,1,0:T(8,128)(2,1)}, bf16[4,2,128,1616]{3,2,1,0:T(8,128)(2,1)}) custom-call(s32[4,32]{1,0:T(4,128)} %bitcast.24, bf16[128,4096]{1,0:T(8,128)(2,1)} %q_hbm.3, bf16[128,4096]{1,0:T(8,128)(2,1)} %g_hbm.3, bf16[1,1601,512]{2,1,0:T(8,128)(2,1)} %refs_0_.1, bf16[1,1601,512]{2,1,0:T(8,128)(2,1)} %refs_1_.1), custom_call_target="tpu_custom_call" | custom-call | bytes 12582912 | tf_op jit(solution)/shard_map/route_2/pallas_call | solution.py:422
  22.7 8.9 %collective-permute-done.4.refs_5_ = bf16[2,2,32,1024]{3,2,1,0:T(8,128)(2,1)} collective-permute-done((bf16[2,2,32,1024]{3,2,1,0:T(8,128)(2,1)}, bf16[2,2,32,1024]{3,2,1,0:T(8,128)(2,1)}, u32[]{:S(2)}, u32[]{:S(2)}) %collective-permute-start.4) | collective-permute-done | bytes 262176 | tf_op jit(solution)/shard_map/ppermute | solution.py:397
  31.6 4.4 %all-to-all-start.1 = ((bf16[8,2,2,32,1024]{4,3,2,1,0:T(8,128)(2,1)}), bf16[8,2,2,32,1024]{4,3,2,1,0:T(8,128)(2,1)}, u32[]{:S(2)}, u32[]{:S(2)}) async-start(bf16[8,2,2,32,1024]{4,3,2,1,0:T(8,128)(2,1)} %get-tuple-element.68), calls=%async_computation.1 | async-start | bytes 4194304 | tf_op jit(solution)/shard_map/all_to_all | solution.py:501
  36.0 9.6 %attend_0.1 = (bf16[8,2,2,32,1024]{4,3,2,1,0:T(8,128)(2,1)}, bf16[2,1616,128]{2,1,0:T(8,128)(2,1)}) custom-call(s32[4,32]{1,0:T(4,128)} %bitcast.25, bf16[4,2,1616,128]{3,2,1,0:T(8,128)(2,1)} %get-tuple-element.43.caches, bf16[4,2,128,1616]{3,2,1,0:T(8,128)(2,1)} %get-tuple-element.44.turned_caches, bf16[2,2,32,1024]{3,2,1,0:T(8,128)(2,1)} %get-tuple-element.54.refs_0_, ...), custom_call_target="tpu_custom_call" | custom-call | flops 314769408 | bytes 1048576 | tf_op jit(solution)/shard_map/attend_0/pallas_call | solution.py:449
  45.6 2.0 %collective-permute-start.7 = (bf16[2,1616,128]{2,1,0:T(8,128)(2,1)}, bf16[2,1616,128]{2,1,0:T(8,128)(2,1)S(1)}, u32[]{:S(2)}, u32[]{:S(2)}) collective-permute-start(bf16[2,1616,128]{2,1,0:T(8,128)(2,1)} %get-tuple-element.64), channel_id=1, source_target_pairs={{0,8},{8,0},{16,24},{24,16},{1,9},{9,1},{17,25},{25,17},{2,10},{10... | collective-permute-start | bytes 2482184 | tf_op jit(solution)/shard_map/ppermute | solution.py:397
  47.7 9.8 %attend_1.1 = (bf16[8,2,2,32,1024]{4,3,2,1,0:T(8,128)(2,1)}, bf16[2,1616,128]{2,1,0:T(8,128)(2,1)}) custom-call(s32[4,32]{1,0:T(4,128)} %bitcast.26, bf16[4,2,1616,128]{3,2,1,0:T(8,128)(2,1)} %get-tuple-element.43.caches, bf16[4,2,128,1616]{3,2,1,0:T(8,128)(2,1)} %get-tuple-element.44.turned_caches, ...), custom_call_target="tpu_custom_call", output_to_operand_aliasing={{0}: (11, {})} | custom-call | flops 314769408 | bytes 1048576 | tf_op jit(solution)/shard_map/attend_1/pallas_call | solution.py:449
  57.5 5.3 %all-to-all-done.1.refs_0_ = bf16[8,2,2,32,1024]{4,3,2,1,0:T(8,128)(2,1)} async-done(((bf16[8,2,2,32,1024]{4,3,2,1,0:T(8,128)(2,1)}), bf16[8,2,2,32,1024]{4,3,2,1,0:T(8,128)(2,1)}, u32[]{:S(2)}, u32[]{:S(2)}) %all-to-all-start.1) | async-done | bytes 2097184 | tf_op jit(solution)/shard_map/all_to_all | solution.py:501
  62.8 5.0 %all-to-all-start = ((bf16[8,2,2,32,1024]{4,3,2,1,0:T(8,128)(2,1)}), bf16[8,2,2,32,1024]{4,3,2,1,0:T(8,128)(2,1)}, u32[]{:S(2)}, u32[]{:S(2)}) async-start(bf16[8,2,2,32,1024]{4,3,2,1,0:T(8,128)(2,1)} %get-tuple-element.63), calls=%async_computation | async-start | bytes 4194304 | tf_op jit(solution)/shard_map/all_to_all | solution.py:501
  67.8 0.7 fusion.6
  68.6 2.7 %collective-permute-start.9 = (bf16[800,128]{1,0:T(8,128)(2,1)}, bf16[800,128]{1,0:T(8,128)(2,1)}, u32[]{:S(2)}, u32[]{:S(2)}) collective-permute-start(bf16[800,128]{1,0:T(8,128)(2,1)} %fusion.6), channel_id=1, source_target_pairs={{0,16},{8,24},{16,0},{24,8},{1,17},{9,25},{17,1},{25,9},{2,18},{10... | collective-permute-start | bytes 614408 | tf_op jit(solution)/shard_map/ppermute | solution.py:397
  71.2 0.9 fusion.2
  72.1 0.3 collective-permute-start.8
  72.4 16.9 %attend_2.1 = (bf16[8,2,2,32,1024]{4,3,2,1,0:T(8,128)(2,1)}, bf16[2,1616,128]{2,1,0:T(8,128)(2,1)}, bf16[2,1616,128]{2,1,0:T(8,128)(2,1)}) custom-call(s32[4,32]{1,0:T(4,128)} %bitcast.27, bf16[4,2,1616,128]{3,2,1,0:T(8,128)(2,1)} %get-tuple-element.43.caches, bf16[4,2,128,1616]{3,2,1,0:T(8,128)(2,1)} %get-tuple-element.44.turned_caches, ...), custom_call_target="tpu_custom_call" | custom-call | flops 7554465792 | bytes 8388608 | tf_op jit(solution)/shard_map/attend_2/pallas_call | solution.py:449
  89.3 1.6 %collective-permute-done.9 = bf16[800,128]{1,0:T(8,128)(2,1)} collective-permute-done((bf16[800,128]{1,0:T(8,128)(2,1)}, bf16[800,128]{1,0:T(8,128)(2,1)}, u32[]{:S(2)}, u32[]{:S(2)}) %collective-permute-start.9) | collective-permute-done | bytes 204832 | tf_op jit(solution)/shard_map/ppermute | solution.py:397
  90.9 8.5 %collective-permute-done.8 = bf16[1616,128]{1,0:T(8,128)(2,1)} collective-permute-done((bf16[1616,128]{1,0:T(8,128)(2,1)}, bf16[1616,128]{1,0:T(8,128)(2,1)}, u32[]{:S(2)}, u32[]{:S(2)}) %collective-permute-start.8) | collective-permute-done | bytes 413728 | tf_op jit(solution)/shard_map/ppermute | solution.py:397
  99.4 4.4 %all-to-all-start.2 = ((bf16[8,2,2,32,1024]{4,3,2,1,0:T(8,128)(2,1)}), bf16[8,2,2,32,1024]{4,3,2,1,0:T(8,128)(2,1)}, u32[]{:S(2)}, u32[]{:S(2)}) async-start(bf16[8,2,2,32,1024]{4,3,2,1,0:T(8,128)(2,1)} %get-tuple-element.72), calls=%async_computation.2 | async-start | bytes 4194304 | tf_op jit(solution)/shard_map/all_to_all | solution.py:501
  103.8 0.5 collective-permute-start.10
  104.3 1.7 %fusion.5 = bf16[816,128]{1,0:T(8,128)(2,1)} fusion(bf16[2,1616,128]{2,1,0:T(8,128)(2,1)S(1)} %collective-permute-done.7, bf16[2,1616,128]{2,1,0:T(8,128)(2,1)} %get-tuple-element.66), kind=kLoop, calls=%fused_computation.11 | loop fusion | flops 417792 | bytes 626688 | tf_op jit(solution)/shard_map/convert_element_type | solution.py:524
  105.9 3.4 %collective-permute-start.11 = (bf16[816,128]{1,0:T(8,128)(2,1)}, bf16[816,128]{1,0:T(8,128)(2,1)S(1)}, u32[]{:S(2)}, u32[]{:S(2)}) collective-permute-start(bf16[816,128]{1,0:T(8,128)(2,1)} %fusion.5), channel_id=1, source_target_pairs={{0,16},{8,24},{16,0},{24,8},{1,17},{9,25},{17,1},{25,9},{2,18},{10... | collective-permute-start | bytes 626696 | tf_op jit(solution)/shard_map/ppermute | solution.py:397
  109.3 2.8 %collect_0.1 = (bf16[128,4096]{1,0:T(8,128)(2,1)}, bf16[128,4096]{1,0:T(8,128)(2,1)}) custom-call(s32[4,32]{1,0:T(4,128)} %bitcast.28, bf16[8,2,2,32,1024]{4,3,2,1,0:T(8,128)(2,1)} %all-to-all-done.returned), custom_call_target="tpu_custom_call" | custom-call | bytes 4194304 | tf_op jit(solution)/shard_map/collect_0/pallas_call | solution.py:484
  112.1 15.3 %collective-permute-done.11 = bf16[816,128]{1,0:T(8,128)(2,1)S(1)} collective-permute-done((bf16[816,128]{1,0:T(8,128)(2,1)}, bf16[816,128]{1,0:T(8,128)(2,1)S(1)}, u32[]{:S(2)}, u32[]{:S(2)}) %collective-permute-start.11) | collective-permute-done | bytes 208928 | tf_op jit(solution)/shard_map/ppermute | solution.py:397
  127.4 2.0 %collective-permute-done.10 = bf16[2,1616,128]{2,1,0:T(8,128)(2,1)} collective-permute-done((bf16[2,1616,128]{2,1,0:T(8,128)(2,1)}, bf16[2,1616,128]{2,1,0:T(8,128)(2,1)}, u32[]{:S(2)}, u32[]{:S(2)}) %collective-permute-start.10) | collective-permute-done | bytes 827424 | tf_op jit(solution)/shard_map/ppermute | solution.py:397
  129.4 2.8 %fusion.4 = (bf16[1,1601,128]{2,1,0:T(8,128)(2,1)}, bf16[1,1601,128]{2,1,0:T(8,128)(2,1)}) fusion(bf16[816,128]{1,0:T(8,128)(2,1)S(1)} %collective-permute-done.11, bf16[800,128]{1,0:T(8,128)(2,1)} %collective-permute-done.9, bf16[2,1616,128]{2,1,0:T(8,128)(2,1)} %collective-permute-done.10, bf16[2,1616,128]{2,1,0:T(8,128)(2,1)} %get-tuple-element.78, ...), kind=kLoop, calls=%fused_computation.8 | loop fusion | flops 3073920 | bytes 3282688 | tf_op jit(solution)/shard_map/broadcast_in_dim | solution.py:548
  132.2 2.8 %collect_2.1 = (bf16[128,4096]{1,0:T(8,128)(2,1)}, bf16[128,4096]{1,0:T(8,128)(2,1)}) custom-call(s32[4,32]{1,0:T(4,128)} %bitcast.29, bf16[8,2,2,32,1024]{4,3,2,1,0:T(8,128)(2,1)} %all-to-all-done.2.returned, bf16[128,4096]{1,0:T(8,128)(2,1)} %get-tuple-element.74.refs_0_, ...), custom_call_target="tpu_custom_call", output_to_operand_aliasing={{0}: (2, {}), {1}: (3, {})} | custom-call | bytes 4194304 | tf_op jit(solution)/shard_map/collect_2/pallas_call | solution.py:484
  (17 shorter events, 0.0 us)
Async XLA Ops:
  3.5 4.9 %collective-permute-start = (bf16[2,2,32,1024]{3,2,1,0:T(8,128)(2,1)}, bf16[2,2,32,1024]{3,2,1,0:T(8,128)(2,1)S(1)}, u32[]{:S(2)}, u32[]{:S(2)}) collective-permute-start(bf16[2,2,32,1024]{3,2,1,0:T(8,128)(2,1)} %get-tuple-element.46), channel_id=1, source_target_pairs={{0,1},{1,0},{2,3},{3,2},{4,5},{5,4},{6,7},{7,6},{8,9},{9,8},{10,11... | collective-permute-start | bytes 786440 | tf_op jit(solution)/shard_map/ppermute | solution.py:397
  4.0 9.9 %collective-permute-start.1 = (bf16[2,2,32,1024]{3,2,1,0:T(8,128)(2,1)}, bf16[2,2,32,1024]{3,2,1,0:T(8,128)(2,1)S(1)}, u32[]{:S(2)}, u32[]{:S(2)}) collective-permute-start(bf16[2,2,32,1024]{3,2,1,0:T(8,128)(2,1)} %get-tuple-element.47), channel_id=1, source_target_pairs={{0,2},{1,3},{2,0},{3,1},{4,6},{5,7},{6,4},{7,5},{8,10},{9,11},{10,... | collective-permute-start | bytes 786440 | tf_op jit(solution)/shard_map/ppermute | solution.py:397
  6.5 16.2 %collective-permute-start.2 = (bf16[2,2,32,1024]{3,2,1,0:T(8,128)(2,1)}, bf16[2,2,32,1024]{3,2,1,0:T(8,128)(2,1)S(1)}, u32[]{:S(2)}, u32[]{:S(2)}) collective-permute-start(bf16[2,2,32,1024]{3,2,1,0:T(8,128)(2,1)} %get-tuple-element.48), channel_id=1, source_target_pairs={{0,3},{1,2},{2,1},{3,0},{4,7},{5,6},{6,5},{7,4},{8,11},{9,10},{10,... | collective-permute-start | bytes 786440 | tf_op jit(solution)/shard_map/ppermute | solution.py:397
  6.6 16.1 %collective-permute-start.3 = (bf16[2,2,32,1024]{3,2,1,0:T(8,128)(2,1)}, bf16[2,2,32,1024]{3,2,1,0:T(8,128)(2,1)}, u32[]{:S(2)}, u32[]{:S(2)}) collective-permute-start(bf16[2,2,32,1024]{3,2,1,0:T(8,128)(2,1)} %get-tuple-element.49), channel_id=1, source_target_pairs={{0,4},{1,5},{2,6},{3,7},{4,0},{5,1},{6,2},{7,3},{8,12},{9,13},{10,... | collective-permute-start | bytes 786440 | tf_op jit(solution)/shard_map/ppermute | solution.py:397
  8.4 23.2 %collective-permute-start.4 = (bf16[2,2,32,1024]{3,2,1,0:T(8,128)(2,1)}, bf16[2,2,32,1024]{3,2,1,0:T(8,128)(2,1)}, u32[]{:S(2)}, u32[]{:S(2)}) collective-permute-start(bf16[2,2,32,1024]{3,2,1,0:T(8,128)(2,1)} %get-tuple-element.50), channel_id=1, source_target_pairs={{0,5},{1,4},{2,7},{3,6},{4,1},{5,0},{6,3},{7,2},{8,13},{9,12},{10,... | collective-permute-start | bytes 786440 | tf_op jit(solution)/shard_map/ppermute | solution.py:397
  8.4 14.3 %copy-start = (bf16[2,2,32,1024]{3,2,1,0:T(8,128)(2,1)}, bf16[2,2,32,1024]{3,2,1,0:T(8,128)(2,1)S(1)}, u32[]{:S(2)}) copy-start(bf16[2,2,32,1024]{3,2,1,0:T(8,128)(2,1)S(1)} %collective-permute-done.refs_1_) | copy-start | bytes 786436
  8.4 23.2 %collective-permute-start.5 = (bf16[2,2,32,1024]{3,2,1,0:T(8,128)(2,1)}, bf16[2,2,32,1024]{3,2,1,0:T(8,128)(2,1)}, u32[]{:S(2)}, u32[]{:S(2)}) collective-permute-start(bf16[2,2,32,1024]{3,2,1,0:T(8,128)(2,1)} %get-tuple-element.51), channel_id=1, source_target_pairs={{0,6},{1,7},{2,4},{3,5},{4,2},{5,3},{6,0},{7,1},{8,14},{9,15},{10,... | collective-permute-start | bytes 786440 | tf_op jit(solution)/shard_map/ppermute | solution.py:397
  13.9 8.8 %copy-start.1 = (bf16[2,2,32,1024]{3,2,1,0:T(8,128)(2,1)}, bf16[2,2,32,1024]{3,2,1,0:T(8,128)(2,1)S(1)}, u32[]{:S(2)}) copy-start(bf16[2,2,32,1024]{3,2,1,0:T(8,128)(2,1)S(1)} %collective-permute-done.1.refs_2_) | copy-start | bytes 786436
  13.9 17.7 %collective-permute-start.6 = (bf16[2,2,32,1024]{3,2,1,0:T(8,128)(2,1)}, bf16[2,2,32,1024]{3,2,1,0:T(8,128)(2,1)}, u32[]{:S(2)}, u32[]{:S(2)}) collective-permute-start(bf16[2,2,32,1024]{3,2,1,0:T(8,128)(2,1)} %get-tuple-element.52), channel_id=1, source_target_pairs={{0,7},{1,6},{2,5},{3,4},{4,3},{5,2},{6,1},{7,0},{8,15},{9,14},{10,... | collective-permute-start | bytes 786440 | tf_op jit(solution)/shard_map/ppermute | solution.py:397
  22.7 8.9 %copy-start.2 = (bf16[2,2,32,1024]{3,2,1,0:T(8,128)(2,1)}, bf16[2,2,32,1024]{3,2,1,0:T(8,128)(2,1)S(1)}, u32[]{:S(2)}) copy-start(bf16[2,2,32,1024]{3,2,1,0:T(8,128)(2,1)S(1)} %collective-permute-done.2.refs_3_) | copy-start | bytes 786436
  31.6 31.2 %all-to-all-start.1 = ((bf16[8,2,2,32,1024]{4,3,2,1,0:T(8,128)(2,1)}), bf16[8,2,2,32,1024]{4,3,2,1,0:T(8,128)(2,1)}, u32[]{:S(2)}, u32[]{:S(2)}) async-start(bf16[8,2,2,32,1024]{4,3,2,1,0:T(8,128)(2,1)} %get-tuple-element.68), calls=%async_computation.1 | async-start | bytes 4194304 | tf_op jit(solution)/shard_map/all_to_all | solution.py:501
  45.6 22.2 %collective-permute-start.7 = (bf16[2,1616,128]{2,1,0:T(8,128)(2,1)}, bf16[2,1616,128]{2,1,0:T(8,128)(2,1)S(1)}, u32[]{:S(2)}, u32[]{:S(2)}) collective-permute-start(bf16[2,1616,128]{2,1,0:T(8,128)(2,1)} %get-tuple-element.64), channel_id=1, source_target_pairs={{0,8},{8,0},{16,24},{24,16},{1,9},{9,1},{17,25},{25,17},{2,10},{10... | collective-permute-start | bytes 2482184 | tf_op jit(solution)/shard_map/ppermute | solution.py:397
  62.8 5.0 %copy-start.3 = (bf16[2,1616,128]{2,1,0:T(8,128)(2,1)S(1)}, bf16[2,1616,128]{2,1,0:T(8,128)(2,1)}, u32[]{:S(2)}) copy-start(bf16[2,1616,128]{2,1,0:T(8,128)(2,1)} %get-tuple-element.66) | copy-start | bytes 2482180
  62.8 36.6 %all-to-all-start = ((bf16[8,2,2,32,1024]{4,3,2,1,0:T(8,128)(2,1)}), bf16[8,2,2,32,1024]{4,3,2,1,0:T(8,128)(2,1)}, u32[]{:S(2)}, u32[]{:S(2)}) async-start(bf16[8,2,2,32,1024]{4,3,2,1,0:T(8,128)(2,1)} %get-tuple-element.63), calls=%async_computation | async-start | bytes 4194304 | tf_op jit(solution)/shard_map/all_to_all | solution.py:501
  68.6 22.3 %collective-permute-start.9 = (bf16[800,128]{1,0:T(8,128)(2,1)}, bf16[800,128]{1,0:T(8,128)(2,1)}, u32[]{:S(2)}, u32[]{:S(2)}) collective-permute-start(bf16[800,128]{1,0:T(8,128)(2,1)} %fusion.6), channel_id=1, source_target_pairs={{0,16},{8,24},{16,0},{24,8},{1,17},{9,25},{17,1},{25,9},{2,18},{10... | collective-permute-start | bytes 614408 | tf_op jit(solution)/shard_map/ppermute | solution.py:397
  72.1 27.3 %collective-permute-start.8 = (bf16[1616,128]{1,0:T(8,128)(2,1)}, bf16[1616,128]{1,0:T(8,128)(2,1)}, u32[]{:S(2)}, u32[]{:S(2)}) collective-permute-start(bf16[1616,128]{1,0:T(8,128)(2,1)} %fusion.2), channel_id=1, source_target_pairs={{0,16},{8,24},{16,0},{24,8},{1,17},{9,25},{17,1},{25,9},{2,18},{10... | collective-permute-start | bytes 1241096 | tf_op jit(solution)/shard_map/ppermute | solution.py:397
  99.4 32.8 %all-to-all-start.2 = ((bf16[8,2,2,32,1024]{4,3,2,1,0:T(8,128)(2,1)}), bf16[8,2,2,32,1024]{4,3,2,1,0:T(8,128)(2,1)}, u32[]{:S(2)}, u32[]{:S(2)}) async-start(bf16[8,2,2,32,1024]{4,3,2,1,0:T(8,128)(2,1)} %get-tuple-element.72), calls=%async_computation.2 | async-start | bytes 4194304 | tf_op jit(solution)/shard_map/all_to_all | solution.py:501
  103.8 25.6 %collective-permute-start.10 = (bf16[2,1616,128]{2,1,0:T(8,128)(2,1)}, bf16[2,1616,128]{2,1,0:T(8,128)(2,1)}, u32[]{:S(2)}, u32[]{:S(2)}) collective-permute-start(bf16[2,1616,128]{2,1,0:T(8,128)(2,1)} %get-tuple-element.79), channel_id=1, source_target_pairs={{0,8},{8,0},{16,24},{24,16},{1,9},{9,1},{17,25},{25,17},{2,10},{10... | collective-permute-start | bytes 2482184 | tf_op jit(solution)/shard_map/ppermute | solution.py:397
  105.9 21.5 %collective-permute-start.11 = (bf16[816,128]{1,0:T(8,128)(2,1)}, bf16[816,128]{1,0:T(8,128)(2,1)S(1)}, u32[]{:S(2)}, u32[]{:S(2)}) collective-permute-start(bf16[816,128]{1,0:T(8,128)(2,1)} %fusion.5), channel_id=1, source_target_pairs={{0,16},{8,24},{16,0},{24,8},{1,17},{9,25},{17,1},{25,9},{2,18},{10... | collective-permute-start | bytes 626696 | tf_op jit(solution)/shard_map/ppermute | solution.py:397

commit v14 on v13

--- a/solution.py
+++ b/solution.py
@@ -48,8 +48,8 @@
                     )
                 )
 
-    def leaving(r, target):
-        return pltpu.make_async_copy(stage.at[r], target, out_sems.at[r])
+    def leaving(r, i, target):
+        return pltpu.make_async_copy(stage.at[r, i], target, out_sems.at[r, i])
 
     for copies in arriving:
         for copy in copies:
@@ -58,14 +58,17 @@
         for copy in copies:
             copy.wait()
         if apart:
-            for k, out in enumerate(refs[:-3]):
+            peers = len(refs[:-3]) // len(turns)
+            for k in range(peers):
 
                 @pl.when(reads[r, row] == me ^ k)
                 def _():
-                    leaving(r, out).start()
+                    for i in range(len(turns)):
+                        leaving(r, i, refs[i * peers + k]).start()
 
         else:
-            leaving(r, refs[2].at[reads[r, row]]).start()
+            for i in range(len(turns)):
+                leaving(r, i, refs[2].at[reads[r, row], i]).start()
     if not apart:
         k_in, v_in, _, *targets = refs[:5]
         straight, turned, cache_sems = more
@@ -79,7 +82,8 @@
         for copy in copies:
             copy.wait()
     for r in range(n_seg):
-        leaving(r, refs[0] if apart else refs[2].at[0]).wait()
+        for i in range(len(turns)):
+            leaving(r, i, refs[0] if apart else refs[2].at[0, 0]).wait()
 
 
 def collect_kernel(turns, n_seg, seg_rows, reads, returned, *refs):
@@ -186,8 +190,8 @@
     ]
 
     def arriving(i, slot, k):
-        source = received[k] if len(received) > 1 else received[0].at[me ^ k]
-        return pltpu.make_async_copy(source.at[offset + i], inbox.at[i, slot], in_sems.at[i, slot])
+        source = received[k] if len(received) > 1 else received[0].at[me ^ k, offset + i]
+        return pltpu.make_async_copy(source, inbox.at[i, slot], in_sems.at[i, slot])
 
     def leaving(i, slot, owner):
         return pltpu.make_async_copy(
@@ -410,7 +414,7 @@
     bf16, f32 = jnp.bfloat16, jnp.float32
     chunks = [tuple(range(i, i + PER_CHUNK)) for i in range(0, KVH, PER_CHUNK)]
     message = jax.ShapeDtypeStruct((peers, PER_CHUNK, 2, seg_rows, WIDTH), bf16)
-    part = jax.ShapeDtypeStruct((PER_CHUNK, 2, seg_rows, WIDTH), bf16)
+    part = jax.ShapeDtypeStruct((2, seg_rows, WIDTH), bf16)
 
     caches = [
         jax.ShapeDtypeStruct((KVH, 2, padded, HD), bf16),
@@ -418,7 +422,7 @@
     ]
 
     def route(turns, prepares):
-        outputs = [message] + caches if prepares else [part] * peers
+        outputs = [message] + caches if prepares else [part] * peers * len(turns)
         return pl.pallas_call(
             functools.partial(route_kernel, turns, not prepares, n_seg, seg_rows, tokens),
             out_shape=outputs,
@@ -427,7 +431,7 @@
             scratch_shapes=[
                 pltpu.VMEM((n_seg, PER_CHUNK, 2, seg_rows, WIDTH), bf16),
                 pltpu.SemaphoreType.DMA((n_seg, PER_CHUNK, 2)),
-                pltpu.SemaphoreType.DMA((n_seg,)),
+                pltpu.SemaphoreType.DMA((n_seg, PER_CHUNK)),
             ]
             + [
                 pltpu.VMEM((KVH, 2, padded, HD), bf16),
@@ -506,15 +510,16 @@
         return [arrived[k] for k in range(peers)]
 
     first, second = chunks
-    received = exchange_apart(route(first, 0))
+    apart = route(first, 0)
+    received = [exchange_apart(apart[i * peers : (i + 1) * peers]) for i in range(PER_CHUNK)]
     routed, *prepared = route(second, 1)
-    *received, routed = lax.optimization_barrier((*received, routed))
+    butterfly = n_seq == KVH
+    returned, *grads = attend(first[:1], 0, received[0], [])
+    *received[1], grads[0], routed = lax.optimization_barrier((*received[1], grads[0], routed))
     received_later = exchange(routed)
-    butterfly = n_seq == KVH
-    returned, *grads = attend(first[:1], 0, received, [])
     if butterfly:
         passed = xor_permute(grads[0], "seq", 1)
-    returned, last = attend(first[1:], 1, received, [returned])
+    returned, last = attend(first[1:], 1, received[1], [returned])
     grads.append(last)
     if butterfly:
         passed, last = lax.optimization_barrier((passed, last))
@@ -524,6 +529,7 @@
             (last[j, a:b].astype(f32) + passed[j, a:b].astype(f32)).astype(bf16)
             for j, a, b in cuts
         ]
+        returned, *pair = lax.optimization_barrier((returned, *pair))
         pair = [xor_permute(one, "seq", 2) for one in pair]
     answer = exchange(returned)
     received_later, returned = lax.optimization_barrier((received_later, returned))

time: 136 us -> 150 us (1.10)
  starting transfers between devices: 31.9 us -> 45.1 us
  Pallas kernels: 51.8 us -> 48.3 us
  other arithmetic: 6.04 us -> 7.83 us
    ppermute x12 -> x19, starting transfers between devices: 18.2 us -> 30.7 us  [xor_permute(): return lax.ppermute(array, axis, [(i, i ^ k) for i in range(size)])]
    ppermute x12 -> x19, waiting for transfers between devices: 39.2 us -> 44 us  [xor_permute(): return lax.ppermute(array, axis, [(i, i ^ k) for i in range(size)])]
    all_to_all x3, waiting for transfers between devices: 5.32 us -> 1.04 us  [exchange(): return lax.all_to_all(array, 'enc', split_axis=0, concat_axis=0, tiled=True)]
    pallas_call x3, Pallas kernels: 36.4 us -> 32.8 us  [attend(): pl.pallas_call(functools.partial(attend_kernel, turns, offset, len(before...]
    convert_element_type x3, other arithmetic: 3.27 us -> 5.2 us  [per_device(): (last[j, a:b].astype(f32) + passed[j, a:b].astype(f32)).astype(bf16)]
  transfers between devices with their start and end apart: 15 -> 22, of which waited for: 7 -> 8; matrix products, arithmetic and copies ran while one was open for 4% -> 5% of each run, Pallas kernels for 34% -> 29%
where the time goes in v14:
time: 150 us; the launch traced here: 149 us
  Pallas kernels  48.3 us (32%)
  starting transfers between devices  45.1 us (30%)
  waiting for transfers between devices  45.1 us (30%)
  other arithmetic  7.83 us (5%)
    ppermute x19, waiting for transfers between devices, xor_permute(): return lax.ppermute(array, axis, [(i, i ^ k) for i in range(size)])  44 us
    pallas_call x3, Pallas kernels, attend(): pl.pallas_call(functools.partial(attend_kernel, turns, offset, len(before...  32.8 us
    ppermute x19, starting transfers between devices, xor_permute(): return lax.ppermute(array, axis, [(i, i ^ k) for i in range(size)])  30.7 us
    all_to_all x3, starting transfers between devices, exchange(): return lax.all_to_all(array, 'enc', split_axis=0, concat_axis=0, tiled=True)  14.3 us
    pallas_call x2, Pallas kernels, route(): pl.pallas_call(functools.partial(route_kernel, turns, not prepares, n_seg...  9.87 us
    pallas_call x2, Pallas kernels, collect(): pl.pallas_call(functools.partial(collect_kernel, turns, n_seg, seg_rows),...  5.64 us
    convert_element_type x3, other arithmetic, per_device(): (last[j, a:b].astype(f32) + passed[j, a:b].astype(f32)).astype(bf16)  5.2 us
  transfers between devices with their start and end apart: 22, of which 8 were waited for; matrix products, arithmetic and copies ran while one was open for 5% of the time, Pallas kernels for 29%

profile of v14, /device:TPU:0, one launch (start us, length us, event | category | flops | bytes accessed | tf_op | source)
XLA Modules:
  0.0 148.7 jit_solution(833288552033137460)
XLA Ops:
  0.6 2.9 %route_0.1 = (bf16[2,32,1024]{2,1,0:T(8,128)(2,1)}, bf16[2,32,1024]{2,1,0:T(8,128)(2,1)}, bf16[2,32,1024]{2,1,0:T(8,128)(2,1)}, bf16[2,32,1024]{2,1,0:T(8,128)(2...) custom-call(s32[4,32]{1,0:T(4,128)} %bitcast.23, ...), custom_call_target="tpu_custom_call" | custom-call | bytes 2097152 | tf_op jit(solution)/shard_map/route_0/pallas_call | solution.py:426
  4.0 2.6 %collective-permute-start.1 = (bf16[2,32,1024]{2,1,0:T(8,128)(2,1)}, bf16[2,32,1024]{2,1,0:T(8,128)(2,1)}, u32[]{:S(2)}, u32[]{:S(2)}) collective-permute-start(bf16[2,32,1024]{2,1,0:T(8,128)(2,1)} %get-tuple-element.60), channel_id=1, source_target_pairs={{0,2},{1,3},{2,0},{3,1},{4,6},{5,7},{6,4},{7,5},{8,10},{9,11},{10,... | collective-permute-start | bytes 393224 | tf_op jit(solution)/shard_map/ppermute | solution.py:401
  7.0 1.4 collective-permute-start.9
  8.5 1.5 %collective-permute-start.10 = (bf16[2,32,1024]{2,1,0:T(8,128)(2,1)}, bf16[2,32,1024]{2,1,0:T(8,128)(2,1)S(1)}, u32[]{:S(2)}, u32[]{:S(2)}) collective-permute-start(bf16[2,32,1024]{2,1,0:T(8,128)(2,1)} %get-tuple-element.70), channel_id=1, source_target_pairs={{0,4},{1,5},{2,6},{3,7},{4,0},{5,1},{6,2},{7,3},{8,12},{9,13},{10,... | collective-permute-start | bytes 393224 | tf_op jit(solution)/shard_map/ppermute | solution.py:401
  12.1 2.2 %collective-permute-start.12 = (bf16[2,32,1024]{2,1,0:T(8,128)(2,1)}, bf16[2,32,1024]{2,1,0:T(8,128)(2,1)}, u32[]{:S(2)}, u32[]{:S(2)}) collective-permute-start(bf16[2,32,1024]{2,1,0:T(8,128)(2,1)} %get-tuple-element.72), channel_id=1, source_target_pairs={{0,6},{1,7},{2,4},{3,5},{4,2},{5,3},{6,0},{7,1},{8,14},{9,15},{10,... | collective-permute-start | bytes 393224 | tf_op jit(solution)/shard_map/ppermute | solution.py:401
  14.2 1.4 collective-permute-start.13
  16.3 2.2 %collective-permute-start.2 = (bf16[2,32,1024]{2,1,0:T(8,128)(2,1)}, bf16[2,32,1024]{2,1,0:T(8,128)(2,1)S(1)}, u32[]{:S(2)}, u32[]{:S(2)}) collective-permute-start(bf16[2,32,1024]{2,1,0:T(8,128)(2,1)} %get-tuple-element.61), channel_id=1, source_target_pairs={{0,3},{1,2},{2,1},{3,0},{4,7},{5,6},{6,5},{7,4},{8,11},{9,10},{10,... | collective-permute-start | bytes 393224 | tf_op jit(solution)/shard_map/ppermute | solution.py:401
  18.5 1.5 %collective-permute-start.3 = (bf16[2,32,1024]{2,1,0:T(8,128)(2,1)}, bf16[2,32,1024]{2,1,0:T(8,128)(2,1)S(1)}, u32[]{:S(2)}, u32[]{:S(2)}) collective-permute-start(bf16[2,32,1024]{2,1,0:T(8,128)(2,1)} %get-tuple-element.62), channel_id=1, source_target_pairs={{0,4},{1,5},{2,6},{3,7},{4,0},{5,1},{6,2},{7,3},{8,12},{9,13},{10,... | collective-permute-start | bytes 393224 | tf_op jit(solution)/shard_map/ppermute | solution.py:401
  20.1 3.8 %collective-permute-start.4 = (bf16[2,32,1024]{2,1,0:T(8,128)(2,1)}, bf16[2,32,1024]{2,1,0:T(8,128)(2,1)}, u32[]{:S(2)}, u32[]{:S(2)}) collective-permute-start(bf16[2,32,1024]{2,1,0:T(8,128)(2,1)} %get-tuple-element.63), channel_id=1, source_target_pairs={{0,5},{1,4},{2,7},{3,6},{4,1},{5,0},{6,3},{7,2},{8,13},{9,12},{10,... | collective-permute-start | bytes 393224 | tf_op jit(solution)/shard_map/ppermute | solution.py:401
  23.8 1.7 %collective-permute-start.5 = (bf16[2,32,1024]{2,1,0:T(8,128)(2,1)}, bf16[2,32,1024]{2,1,0:T(8,128)(2,1)}, u32[]{:S(2)}, u32[]{:S(2)}) collective-permute-start(bf16[2,32,1024]{2,1,0:T(8,128)(2,1)} %get-tuple-element.64), channel_id=1, source_target_pairs={{0,6},{1,7},{2,4},{3,5},{4,2},{5,3},{6,0},{7,1},{8,14},{9,15},{10,... | collective-permute-start | bytes 393224 | tf_op jit(solution)/shard_map/ppermute | solution.py:401
  25.5 1.9 %collective-permute-start.6 = (bf16[2,32,1024]{2,1,0:T(8,128)(2,1)}, bf16[2,32,1024]{2,1,0:T(8,128)(2,1)}, u32[]{:S(2)}, u32[]{:S(2)}) collective-permute-start(bf16[2,32,1024]{2,1,0:T(8,128)(2,1)} %get-tuple-element.65), channel_id=1, source_target_pairs={{0,7},{1,6},{2,5},{3,4},{4,3},{5,2},{6,1},{7,0},{8,15},{9,14},{10,... | collective-permute-start | bytes 393224 | tf_op jit(solution)/shard_map/ppermute | solution.py:401
  27.4 7.0 %route_2.1 = (bf16[8,2,2,32,1024]{4,3,2,1,0:T(8,128)(2,1)}, bf16[4,2,1616,128]{3,2,1,0:T(8,128)(2,1)}, bf16[4,2,128,1616]{3,2,1,0:T(8,128)(2,1)}) custom-call(s32[4,32]{1,0:T(4,128)} %bitcast.24, bf16[128,4096]{1,0:T(8,128)(2,1)} %q_hbm.3, bf16[128,4096]{1,0:T(8,128)(2,1)} %g_hbm.3, bf16[1,1601,512]{2,1,0:T(8,128)(2,1)} %refs_0_.1, bf16[1,1601,512]{2,1,0:T(8,128)(2,1)} %refs_1_.1), custom_call_target="tpu_custom_call" | custom-call | bytes 12582912 | tf_op jit(solution)/shard_map/route_2/pallas_call | solution.py:426
  34.5 9.6 %attend_0.1 = (bf16[8,2,2,32,1024]{4,3,2,1,0:T(8,128)(2,1)}, bf16[2,1616,128]{2,1,0:T(8,128)(2,1)}) custom-call(s32[4,32]{1,0:T(4,128)} %bitcast.25, bf16[4,2,1616,128]{3,2,1,0:T(8,128)(2,1)} %get-tuple-element.56.caches, bf16[4,2,128,1616]{3,2,1,0:T(8,128)(2,1)} %get-tuple-element.57.turned_caches, bf16[2,32,1024]{2,1,0:T(8,128)(2,1)} %get-tuple-element.66.refs_0_, ...), custom_call_target="tpu_custom_call" | custom-call | flops 314769408 | bytes 1048576 | tf_op jit(solution)/shard_map/attend_0/pallas_call | solution.py:453
  44.7 5.7 %all-to-all-start.1 = ((bf16[8,2,2,32,1024]{4,3,2,1,0:T(8,128)(2,1)}), bf16[8,2,2,32,1024]{4,3,2,1,0:T(8,128)(2,1)}, u32[]{:S(2)}, u32[]{:S(2)}) async-start(bf16[8,2,2,32,1024]{4,3,2,1,0:T(8,128)(2,1)} %get-tuple-element.93), calls=%async_computation.1 | async-start | bytes 4194304 | tf_op jit(solution)/shard_map/all_to_all | solution.py:505
  50.4 1.7 %collective-permute-start.14 = (bf16[2,1616,128]{2,1,0:T(8,128)(2,1)}, bf16[2,1616,128]{2,1,0:T(8,128)(2,1)S(1)}, u32[]{:S(2)}, u32[]{:S(2)}) collective-permute-start(bf16[2,1616,128]{2,1,0:T(8,128)(2,1)} %get-tuple-element.86), channel_id=1, source_target_pairs={{0,8},{8,0},{16,24},{24,16},{1,9},{9,1},{17,25},{25,17},{2,10},{10... | collective-permute-start | bytes 2482184 | tf_op jit(solution)/shard_map/ppermute | solution.py:401
  52.1 9.7 %attend_1.1 = (bf16[8,2,2,32,1024]{4,3,2,1,0:T(8,128)(2,1)}, bf16[2,1616,128]{2,1,0:T(8,128)(2,1)}) custom-call(s32[4,32]{1,0:T(4,128)} %bitcast.26, bf16[4,2,1616,128]{3,2,1,0:T(8,128)(2,1)} %get-tuple-element.56.caches, bf16[4,2,128,1616]{3,2,1,0:T(8,128)(2,1)} %get-tuple-element.57.turned_caches, ...), custom_call_target="tpu_custom_call", output_to_operand_aliasing={{0}: (11, {})} | custom-call | flops 314769408 | bytes 1048576 | tf_op jit(solution)/shard_map/attend_1/pallas_call | solution.py:453
  61.9 9.4 %collective-permute-done.14 = bf16[2,1616,128]{2,1,0:T(8,128)(2,1)S(1)} collective-permute-done((bf16[2,1616,128]{2,1,0:T(8,128)(2,1)}, bf16[2,1616,128]{2,1,0:T(8,128)(2,1)S(1)}, u32[]{:S(2)}, u32[]{:S(2)}) %collective-permute-start.14) | collective-permute-done | bytes 827424 | tf_op jit(solution)/shard_map/ppermute | solution.py:401
  71.2 1.7 %fusion.6 = bf16[800,128]{1,0:T(8,128)(2,1)} fusion(bf16[2,1616,128]{2,1,0:T(8,128)(2,1)S(1)} %collective-permute-done.14, bf16[2,1616,128]{2,1,0:T(8,128)(2,1)} %get-tuple-element.88), kind=kLoop, calls=%fused_computation.12 | loop fusion | flops 409600 | bytes 614400 | tf_op jit(solution)/shard_map/convert_element_type | solution.py:529
  72.9 1.7 %fusion.5 = bf16[816,128]{1,0:T(8,128)(2,1)} fusion(bf16[2,1616,128]{2,1,0:T(8,128)(2,1)S(1)} %collective-permute-done.14, bf16[2,1616,128]{2,1,0:T(8,128)(2,1)} %get-tuple-element.88), kind=kLoop, calls=%fused_computation.11 | loop fusion | flops 417792 | bytes 626688 | tf_op jit(solution)/shard_map/convert_element_type | solution.py:529
  74.6 1.9 %fusion.2 = bf16[1616,128]{1,0:T(8,128)(2,1)} fusion(bf16[2,1616,128]{2,1,0:T(8,128)(2,1)S(1)} %collective-permute-done.14, bf16[2,1616,128]{2,1,0:T(8,128)(2,1)} %get-tuple-element.88), kind=kLoop, calls=%fused_computation.6 | loop fusion | flops 827392 | bytes 1241088 | tf_op jit(solution)/shard_map/convert_element_type | solution.py:529
  77.5 4.3 %all-to-all-start = ((bf16[8,2,2,32,1024]{4,3,2,1,0:T(8,128)(2,1)}), bf16[8,2,2,32,1024]{4,3,2,1,0:T(8,128)(2,1)}, u32[]{:S(2)}, u32[]{:S(2)}) async-start(bf16[8,2,2,32,1024]{4,3,2,1,0:T(8,128)(2,1)} %get-tuple-element.90), calls=%async_computation | async-start | bytes 4194304 | tf_op jit(solution)/shard_map/all_to_all | solution.py:505
  81.8 2.7 %collective-permute-start.16 = (bf16[800,128]{1,0:T(8,128)(2,1)}, bf16[800,128]{1,0:T(8,128)(2,1)S(1)}, u32[]{:S(2)}, u32[]{:S(2)}) collective-permute-start(bf16[800,128]{1,0:T(8,128)(2,1)} %fusion.6), channel_id=1, source_target_pairs={{0,16},{8,24},{16,0},{24,8},{1,17},{9,25},{17,1},{25,9},{2,18},{10... | collective-permute-start | bytes 614408 | tf_op jit(solution)/shard_map/ppermute | solution.py:401
  84.8 13.4 %attend_2.1 = (bf16[8,2,2,32,1024]{4,3,2,1,0:T(8,128)(2,1)}, bf16[2,1616,128]{2,1,0:T(8,128)(2,1)}, bf16[2,1616,128]{2,1,0:T(8,128)(2,1)}) custom-call(s32[4,32]{1,0:T(4,128)} %bitcast.27, bf16[4,2,1616,128]{3,2,1,0:T(8,128)(2,1)} %get-tuple-element.56.caches, bf16[4,2,128,1616]{3,2,1,0:T(8,128)(2,1)} %get-tuple-element.57.turned_caches, ...), custom_call_target="tpu_custom_call" | custom-call | flops 7554465792 | bytes 8388608 | tf_op jit(solution)/shard_map/attend_2/pallas_call | solution.py:453
  98.3 5.9 %collective-permute-done.16 = bf16[800,128]{1,0:T(8,128)(2,1)S(1)} collective-permute-done((bf16[800,128]{1,0:T(8,128)(2,1)}, bf16[800,128]{1,0:T(8,128)(2,1)S(1)}, u32[]{:S(2)}, u32[]{:S(2)}) %collective-permute-start.16) | collective-permute-done | bytes 204832 | tf_op jit(solution)/shard_map/ppermute | solution.py:401
  104.2 8.3 %collective-permute-done.15 = bf16[1616,128]{1,0:T(8,128)(2,1)S(1)} collective-permute-done((bf16[1616,128]{1,0:T(8,128)(2,1)}, bf16[1616,128]{1,0:T(8,128)(2,1)S(1)}, u32[]{:S(2)}, u32[]{:S(2)}) %collective-permute-start.15) | collective-permute-done | bytes 413728 | tf_op jit(solution)/shard_map/ppermute | solution.py:401
  113.2 4.3 %all-to-all-start.2 = ((bf16[8,2,2,32,1024]{4,3,2,1,0:T(8,128)(2,1)}), bf16[8,2,2,32,1024]{4,3,2,1,0:T(8,128)(2,1)}, u32[]{:S(2)}, u32[]{:S(2)}) async-start(bf16[8,2,2,32,1024]{4,3,2,1,0:T(8,128)(2,1)} %get-tuple-element.97), calls=%async_computation.2 | async-start | bytes 4194304 | tf_op jit(solution)/shard_map/all_to_all | solution.py:505
  118.4 3.3 %collective-permute-start.18 = (bf16[816,128]{1,0:T(8,128)(2,1)}, bf16[816,128]{1,0:T(8,128)(2,1)}, u32[]{:S(2)}, u32[]{:S(2)}) collective-permute-start(bf16[816,128]{1,0:T(8,128)(2,1)} %fusion.5), channel_id=1, source_target_pairs={{0,16},{8,24},{16,0},{24,8},{1,17},{9,25},{17,1},{25,9},{2,18},{10... | collective-permute-start | bytes 626696 | tf_op jit(solution)/shard_map/ppermute | solution.py:401
  121.6 2.8 %collect_0.1 = (bf16[128,4096]{1,0:T(8,128)(2,1)}, bf16[128,4096]{1,0:T(8,128)(2,1)}) custom-call(s32[4,32]{1,0:T(4,128)} %bitcast.28, bf16[8,2,2,32,1024]{4,3,2,1,0:T(8,128)(2,1)} %all-to-all-done.returned), custom_call_target="tpu_custom_call" | custom-call | bytes 4194304 | tf_op jit(solution)/shard_map/collect_0/pallas_call | solution.py:488
  124.5 16.8 %collective-permute-done.18 = bf16[816,128]{1,0:T(8,128)(2,1)} collective-permute-done((bf16[816,128]{1,0:T(8,128)(2,1)}, bf16[816,128]{1,0:T(8,128)(2,1)}, u32[]{:S(2)}, u32[]{:S(2)}) %collective-permute-start.18) | collective-permute-done | bytes 208928 | tf_op jit(solution)/shard_map/ppermute | solution.py:401
  141.3 1.7 %collective-permute-done.17 = bf16[2,1616,128]{2,1,0:T(8,128)(2,1)} collective-permute-done((bf16[2,1616,128]{2,1,0:T(8,128)(2,1)}, bf16[2,1616,128]{2,1,0:T(8,128)(2,1)}, u32[]{:S(2)}, u32[]{:S(2)}) %collective-permute-start.17) | collective-permute-done | bytes 827424 | tf_op jit(solution)/shard_map/ppermute | solution.py:401
  143.0 2.6 %fusion.4 = (bf16[1,1601,128]{2,1,0:T(8,128)(2,1)}, bf16[1,1601,128]{2,1,0:T(8,128)(2,1)}) fusion(bf16[816,128]{1,0:T(8,128)(2,1)} %collective-permute-done.18, bf16[800,128]{1,0:T(8,128)(2,1)} %copy-done.2, bf16[2,1616,128]{2,1,0:T(8,128)(2,1)} %collective-permute-done.17, bf16[2,1616,128]{2,1,0:T(8,128)(2,1)S(1)} %copy-done, bf16[1616,128]{1,0:T(8,128)(2,1)} %copy-done.1), kind=kLoop, calls=%fused_computation.8 | loop fusion | flops 3073920 | bytes 3282688 | tf_op jit(solution)/shard_map/broadcast_in_dim | solution.py:554
  145.7 2.8 %collect_2.1 = (bf16[128,4096]{1,0:T(8,128)(2,1)}, bf16[128,4096]{1,0:T(8,128)(2,1)}) custom-call(s32[4,32]{1,0:T(4,128)} %bitcast.29, bf16[8,2,2,32,1024]{4,3,2,1,0:T(8,128)(2,1)} %all-to-all-done.2.returned, bf16[128,4096]{1,0:T(8,128)(2,1)} %get-tuple-element.99.refs_0_, ...), custom_call_target="tpu_custom_call", output_to_operand_aliasing={{0}: (2, {}), {1}: (3, {})} | custom-call | bytes 4194304 | tf_op jit(solution)/shard_map/collect_2/pallas_call | solution.py:488
  (43 shorter events, 7.3 us)
Async XLA Ops:
  3.5 4.9 %collective-permute-start = (bf16[2,32,1024]{2,1,0:T(8,128)(2,1)}, bf16[2,32,1024]{2,1,0:T(8,128)(2,1)S(1)}, u32[]{:S(2)}, u32[]{:S(2)}) collective-permute-start(bf16[2,32,1024]{2,1,0:T(8,128)(2,1)} %get-tuple-element.59), channel_id=1, source_target_pairs={{0,1},{1,0},{2,3},{3,2},{4,5},{5,4},{6,7},{7,6},{8,9},{9,8},{10,11... | collective-permute-start | bytes 393224 | tf_op jit(solution)/shard_map/ppermute | solution.py:401
  4.0 7.2 %collective-permute-start.1 = (bf16[2,32,1024]{2,1,0:T(8,128)(2,1)}, bf16[2,32,1024]{2,1,0:T(8,128)(2,1)}, u32[]{:S(2)}, u32[]{:S(2)}) collective-permute-start(bf16[2,32,1024]{2,1,0:T(8,128)(2,1)} %get-tuple-element.60), channel_id=1, source_target_pairs={{0,2},{1,3},{2,0},{3,1},{4,6},{5,7},{6,4},{7,5},{8,10},{9,11},{10,... | collective-permute-start | bytes 393224 | tf_op jit(solution)/shard_map/ppermute | solution.py:401
  6.6 5.5 %collective-permute-start.7 = (bf16[2,32,1024]{2,1,0:T(8,128)(2,1)}, bf16[2,32,1024]{2,1,0:T(8,128)(2,1)S(1)}, u32[]{:S(2)}, u32[]{:S(2)}) collective-permute-start(bf16[2,32,1024]{2,1,0:T(8,128)(2,1)} %get-tuple-element.67), channel_id=1, source_target_pairs={{0,1},{1,0},{2,3},{3,2},{4,5},{5,4},{6,7},{7,6},{8,9},{9,8},{10,11... | collective-permute-start | bytes 393224 | tf_op jit(solution)/shard_map/ppermute | solution.py:401
  6.8 7.5 %collective-permute-start.8 = (bf16[2,32,1024]{2,1,0:T(8,128)(2,1)}, bf16[2,32,1024]{2,1,0:T(8,128)(2,1)S(1)}, u32[]{:S(2)}, u32[]{:S(2)}) collective-permute-start(bf16[2,32,1024]{2,1,0:T(8,128)(2,1)} %get-tuple-element.68), channel_id=1, source_target_pairs={{0,2},{1,3},{2,0},{3,1},{4,6},{5,7},{6,4},{7,5},{8,10},{9,11},{10,... | collective-permute-start | bytes 393224 | tf_op jit(solution)/shard_map/ppermute | solution.py:401
  7.0 9.3 %collective-permute-start.9 = (bf16[2,32,1024]{2,1,0:T(8,128)(2,1)}, bf16[2,32,1024]{2,1,0:T(8,128)(2,1)S(1)}, u32[]{:S(2)}, u32[]{:S(2)}) collective-permute-start(bf16[2,32,1024]{2,1,0:T(8,128)(2,1)} %get-tuple-element.69), channel_id=1, source_target_pairs={{0,3},{1,2},{2,1},{3,0},{4,7},{5,6},{6,5},{7,4},{8,11},{9,10},{10,... | collective-permute-start | bytes 393224 | tf_op jit(solution)/shard_map/ppermute | solution.py:401
  8.5 26.0 %copy-start.3 = (bf16[2,32,1024]{2,1,0:T(8,128)(2,1)}, bf16[2,32,1024]{2,1,0:T(8,128)(2,1)S(1)}, u32[]{:S(2)}) copy-start(bf16[2,32,1024]{2,1,0:T(8,128)(2,1)S(1)} %collective-permute-done.refs_1_) | copy-start | bytes 393220
  8.5 10.1 %collective-permute-start.10 = (bf16[2,32,1024]{2,1,0:T(8,128)(2,1)}, bf16[2,32,1024]{2,1,0:T(8,128)(2,1)S(1)}, u32[]{:S(2)}, u32[]{:S(2)}) collective-permute-start(bf16[2,32,1024]{2,1,0:T(8,128)(2,1)} %get-tuple-element.70), channel_id=1, source_target_pairs={{0,4},{1,5},{2,6},{3,7},{4,0},{5,1},{6,2},{7,3},{8,12},{9,13},{10,... | collective-permute-start | bytes 393224 | tf_op jit(solution)/shard_map/ppermute | solution.py:401
  11.3 8.8 %collective-permute-start.11 = (bf16[2,32,1024]{2,1,0:T(8,128)(2,1)}, bf16[2,32,1024]{2,1,0:T(8,128)(2,1)}, u32[]{:S(2)}, u32[]{:S(2)}) collective-permute-start(bf16[2,32,1024]{2,1,0:T(8,128)(2,1)} %get-tuple-element.71), channel_id=1, source_target_pairs={{0,5},{1,4},{2,7},{3,6},{4,1},{5,0},{6,3},{7,2},{8,13},{9,12},{10,... | collective-permute-start | bytes 393224 | tf_op jit(solution)/shard_map/ppermute | solution.py:401
  12.0 22.4 %copy-start.4 = (bf16[2,32,1024]{2,1,0:T(8,128)(2,1)}, bf16[2,32,1024]{2,1,0:T(8,128)(2,1)S(1)}, u32[]{:S(2)}) copy-start(bf16[2,32,1024]{2,1,0:T(8,128)(2,1)S(1)} %collective-permute-done.7.refs_1_) | copy-start | bytes 393220
  12.1 11.8 %collective-permute-start.12 = (bf16[2,32,1024]{2,1,0:T(8,128)(2,1)}, bf16[2,32,1024]{2,1,0:T(8,128)(2,1)}, u32[]{:S(2)}, u32[]{:S(2)}) collective-permute-start(bf16[2,32,1024]{2,1,0:T(8,128)(2,1)} %get-tuple-element.72), channel_id=1, source_target_pairs={{0,6},{1,7},{2,4},{3,5},{4,2},{5,3},{6,0},{7,1},{8,14},{9,15},{10,... | collective-permute-start | bytes 393224 | tf_op jit(solution)/shard_map/ppermute | solution.py:401
  14.2 20.2 %copy-start.5 = (bf16[2,32,1024]{2,1,0:T(8,128)(2,1)}, bf16[2,32,1024]{2,1,0:T(8,128)(2,1)S(1)}, u32[]{:S(2)}) copy-start(bf16[2,32,1024]{2,1,0:T(8,128)(2,1)S(1)} %collective-permute-done.8.refs_2_) | copy-start | bytes 393220
  14.2 11.3 %collective-permute-start.13 = (bf16[2,32,1024]{2,1,0:T(8,128)(2,1)}, bf16[2,32,1024]{2,1,0:T(8,128)(2,1)}, u32[]{:S(2)}, u32[]{:S(2)}) collective-permute-start(bf16[2,32,1024]{2,1,0:T(8,128)(2,1)} %get-tuple-element.73), channel_id=1, source_target_pairs={{0,7},{1,6},{2,5},{3,4},{4,3},{5,2},{6,1},{7,0},{8,15},{9,14},{10,... | collective-permute-start | bytes 393224 | tf_op jit(solution)/shard_map/ppermute | solution.py:401
  16.3 18.1 %copy-start.7 = (bf16[2,32,1024]{2,1,0:T(8,128)(2,1)}, bf16[2,32,1024]{2,1,0:T(8,128)(2,1)S(1)}, u32[]{:S(2)}) copy-start(bf16[2,32,1024]{2,1,0:T(8,128)(2,1)S(1)} %collective-permute-done.9.refs_3_) | copy-start | bytes 393220
  16.3 27.7 %collective-permute-start.2 = (bf16[2,32,1024]{2,1,0:T(8,128)(2,1)}, bf16[2,32,1024]{2,1,0:T(8,128)(2,1)S(1)}, u32[]{:S(2)}, u32[]{:S(2)}) collective-permute-start(bf16[2,32,1024]{2,1,0:T(8,128)(2,1)} %get-tuple-element.61), channel_id=1, source_target_pairs={{0,3},{1,2},{2,1},{3,0},{4,7},{5,6},{6,5},{7,4},{8,11},{9,10},{10,... | collective-permute-start | bytes 393224 | tf_op jit(solution)/shard_map/ppermute | solution.py:401
  18.5 15.9 %copy-start.9 = (bf16[2,32,1024]{2,1,0:T(8,128)(2,1)}, bf16[2,32,1024]{2,1,0:T(8,128)(2,1)S(1)}, u32[]{:S(2)}) copy-start(bf16[2,32,1024]{2,1,0:T(8,128)(2,1)S(1)} %collective-permute-done.10.refs_4_) | copy-start | bytes 393220
  18.5 25.5 %collective-permute-start.3 = (bf16[2,32,1024]{2,1,0:T(8,128)(2,1)}, bf16[2,32,1024]{2,1,0:T(8,128)(2,1)S(1)}, u32[]{:S(2)}, u32[]{:S(2)}) collective-permute-start(bf16[2,32,1024]{2,1,0:T(8,128)(2,1)} %get-tuple-element.62), channel_id=1, source_target_pairs={{0,4},{1,5},{2,6},{3,7},{4,0},{5,1},{6,2},{7,3},{8,12},{9,13},{10,... | collective-permute-start | bytes 393224 | tf_op jit(solution)/shard_map/ppermute | solution.py:401
  20.1 24.0 %collective-permute-start.4 = (bf16[2,32,1024]{2,1,0:T(8,128)(2,1)}, bf16[2,32,1024]{2,1,0:T(8,128)(2,1)}, u32[]{:S(2)}, u32[]{:S(2)}) collective-permute-start(bf16[2,32,1024]{2,1,0:T(8,128)(2,1)} %get-tuple-element.63), channel_id=1, source_target_pairs={{0,5},{1,4},{2,7},{3,6},{4,1},{5,0},{6,3},{7,2},{8,13},{9,12},{10,... | collective-permute-start | bytes 393224 | tf_op jit(solution)/shard_map/ppermute | solution.py:401
  23.8 20.3 %collective-permute-start.5 = (bf16[2,32,1024]{2,1,0:T(8,128)(2,1)}, bf16[2,32,1024]{2,1,0:T(8,128)(2,1)}, u32[]{:S(2)}, u32[]{:S(2)}) collective-permute-start(bf16[2,32,1024]{2,1,0:T(8,128)(2,1)} %get-tuple-element.64), channel_id=1, source_target_pairs={{0,6},{1,7},{2,4},{3,5},{4,2},{5,3},{6,0},{7,1},{8,14},{9,15},{10,... | collective-permute-start | bytes 393224 | tf_op jit(solution)/shard_map/ppermute | solution.py:401
  25.5 18.6 %collective-permute-start.6 = (bf16[2,32,1024]{2,1,0:T(8,128)(2,1)}, bf16[2,32,1024]{2,1,0:T(8,128)(2,1)}, u32[]{:S(2)}, u32[]{:S(2)}) collective-permute-start(bf16[2,32,1024]{2,1,0:T(8,128)(2,1)} %get-tuple-element.65), channel_id=1, source_target_pairs={{0,7},{1,6},{2,5},{3,4},{4,3},{5,2},{6,1},{7,0},{8,15},{9,14},{10,... | collective-permute-start | bytes 393224 | tf_op jit(solution)/shard_map/ppermute | solution.py:401
  44.0 0.7 copy-start.6
  44.1 0.7 copy-start.8
  44.7 32.7 %all-to-all-start.1 = ((bf16[8,2,2,32,1024]{4,3,2,1,0:T(8,128)(2,1)}), bf16[8,2,2,32,1024]{4,3,2,1,0:T(8,128)(2,1)}, u32[]{:S(2)}, u32[]{:S(2)}) async-start(bf16[8,2,2,32,1024]{4,3,2,1,0:T(8,128)(2,1)} %get-tuple-element.93), calls=%async_computation.1 | async-start | bytes 4194304 | tf_op jit(solution)/shard_map/all_to_all | solution.py:505
  50.4 20.8 %collective-permute-start.14 = (bf16[2,1616,128]{2,1,0:T(8,128)(2,1)}, bf16[2,1616,128]{2,1,0:T(8,128)(2,1)S(1)}, u32[]{:S(2)}, u32[]{:S(2)}) collective-permute-start(bf16[2,1616,128]{2,1,0:T(8,128)(2,1)} %get-tuple-element.86), channel_id=1, source_target_pairs={{0,8},{8,0},{16,24},{24,16},{1,9},{9,1},{17,25},{25,17},{2,10},{10... | collective-permute-start | bytes 2482184 | tf_op jit(solution)/shard_map/ppermute | solution.py:401
  77.5 34.9 %all-to-all-start = ((bf16[8,2,2,32,1024]{4,3,2,1,0:T(8,128)(2,1)}), bf16[8,2,2,32,1024]{4,3,2,1,0:T(8,128)(2,1)}, u32[]{:S(2)}, u32[]{:S(2)}) async-start(bf16[8,2,2,32,1024]{4,3,2,1,0:T(8,128)(2,1)} %get-tuple-element.90), calls=%async_computation | async-start | bytes 4194304 | tf_op jit(solution)/shard_map/all_to_all | solution.py:505
  81.8 22.3 %collective-permute-start.16 = (bf16[800,128]{1,0:T(8,128)(2,1)}, bf16[800,128]{1,0:T(8,128)(2,1)S(1)}, u32[]{:S(2)}, u32[]{:S(2)}) collective-permute-start(bf16[800,128]{1,0:T(8,128)(2,1)} %fusion.6), channel_id=1, source_target_pairs={{0,16},{8,24},{16,0},{24,8},{1,17},{9,25},{17,1},{25,9},{2,18},{10... | collective-permute-start | bytes 614408 | tf_op jit(solution)/shard_map/ppermute | solution.py:401
  84.5 27.9 %collective-permute-start.15 = (bf16[1616,128]{1,0:T(8,128)(2,1)}, bf16[1616,128]{1,0:T(8,128)(2,1)S(1)}, u32[]{:S(2)}, u32[]{:S(2)}) collective-permute-start(bf16[1616,128]{1,0:T(8,128)(2,1)} %fusion.2), channel_id=1, source_target_pairs={{0,16},{8,24},{16,0},{24,8},{1,17},{9,25},{17,1},{25,9},{2,18},{10... | collective-permute-start | bytes 1241096 | tf_op jit(solution)/shard_map/ppermute | solution.py:401
  104.2 8.3 %copy-start.2 = (bf16[800,128]{1,0:T(8,128)(2,1)}, bf16[800,128]{1,0:T(8,128)(2,1)S(1)}, u32[]{:S(2)}) copy-start(bf16[800,128]{1,0:T(8,128)(2,1)S(1)} %collective-permute-done.16) | copy-start | bytes 614404
  112.4 0.8 copy-start.1
  113.2 32.5 %all-to-all-start.2 = ((bf16[8,2,2,32,1024]{4,3,2,1,0:T(8,128)(2,1)}), bf16[8,2,2,32,1024]{4,3,2,1,0:T(8,128)(2,1)}, u32[]{:S(2)}, u32[]{:S(2)}) async-start(bf16[8,2,2,32,1024]{4,3,2,1,0:T(8,128)(2,1)} %get-tuple-element.97), calls=%async_computation.2 | async-start | bytes 4194304 | tf_op jit(solution)/shard_map/all_to_all | solution.py:505
  117.5 25.5 %copy-start = (bf16[2,1616,128]{2,1,0:T(8,128)(2,1)S(1)}, bf16[2,1616,128]{2,1,0:T(8,128)(2,1)}, u32[]{:S(2)}) copy-start(bf16[2,1616,128]{2,1,0:T(8,128)(2,1)} %get-tuple-element.103) | copy-start | bytes 2482180
  117.5 25.5 %collective-permute-start.17 = (bf16[2,1616,128]{2,1,0:T(8,128)(2,1)}, bf16[2,1616,128]{2,1,0:T(8,128)(2,1)}, u32[]{:S(2)}, u32[]{:S(2)}) collective-permute-start(bf16[2,1616,128]{2,1,0:T(8,128)(2,1)} %get-tuple-element.104), channel_id=1, source_target_pairs={{0,8},{8,0},{16,24},{24,16},{1,9},{9,1},{17,25},{25,17},{2,10},{10... | collective-permute-start | bytes 2482184 | tf_op jit(solution)/shard_map/ppermute | solution.py:401
  118.4 22.9 %collective-permute-start.18 = (bf16[816,128]{1,0:T(8,128)(2,1)}, bf16[816,128]{1,0:T(8,128)(2,1)}, u32[]{:S(2)}, u32[]{:S(2)}) collective-permute-start(bf16[816,128]{1,0:T(8,128)(2,1)} %fusion.5), channel_id=1, source_target_pairs={{0,16},{8,24},{16,0},{24,8},{1,17},{9,25},{17,1},{25,9},{2,18},{10... | collective-permute-start | bytes 626696 | tf_op jit(solution)/shard_map/ppermute | solution.py:401

commit v15 on v13

--- a/solution.py
+++ b/solution.py
@@ -194,8 +194,8 @@
             outbox.at[i, slot], returned.at[owner, offset + i], out_sems.at[i, slot]
         )
 
-    def handing(i):
-        return pltpu.make_async_copy(staged.at[i], grads[i], grad_sems.at[i])
+    def handing(i, j):
+        return pltpu.make_async_copy(staged.at[i, j], grads[i].at[j], grad_sems.at[i, j])
 
     for copies in kv_copies:
         copies[0].start()
@@ -236,6 +236,7 @@
 
     def forward(u, i, slot, weights):
         source = jnp.minimum(slot, count - 1)
+        own = slice(u * lanes, (u + 1) * lanes)
         q_turned = stacked(i, source, 0).astype(f32).T.astype(bf16)
         tops, totals, outs = [], [], []
 
@@ -255,9 +256,9 @@
             for c, d in slices(a, b):
                 piece = jnp.exp2((scores[u, c:d, :] - tops[0]) * (SCALE * LOG2E))
                 totals.append(folded(piece, jnp.sum))
-                weights[u, c:d, :] = piece.astype(bf16)
+                weights[c:d, own] = piece.astype(bf16)
             outs.append(
-                jnp.dot(turned[i, 1, :, a:b], weights[u, a:b, :], preferred_element_type=f32)
+                jnp.dot(turned[i, 1, :, a:b], weights[a:b, own], preferred_element_type=f32)
             )
 
         def finish():
@@ -275,30 +276,26 @@
 
     def backward(u, i, slot, weights, delta, g_turned, g):
         q = stacked(i, jnp.minimum(slot, count - 1), 0)
+        own = slice(u * lanes, (u + 1) * lanes)
         turned_dq = []
 
         def values_part(a, b):
             dprob = jnp.dot(straight[i, 1, a:b, :], g_turned, preferred_element_type=f32)
             for c, d in slices(a, b):
-                piece = weights[u, c:d, :].astype(f32) * (dprob[c - a : d - a, :] - delta)
-                dscores[u, c:d, :] = piece.astype(bf16)
-
-        def values_sum():
-            sums[i, 1] += jnp.dot(weights[u], g, preferred_element_type=f32)
-
-        def keys_sum():
-            sums[i, 0] += jnp.dot(dscores[u], q, preferred_element_type=f32)
+                piece = weights[c:d, own].astype(f32) * (dprob[c - a : d - a, :] - delta)
+                dscores[c:d, own] = piece.astype(bf16)
 
         def queries_part(a, b):
             turned_dq.append(
-                jnp.dot(turned[i, 0, :, a:b], dscores[u, a:b, :], preferred_element_type=f32)
+                jnp.dot(turned[i, 0, :, a:b], dscores[a:b, own], preferred_element_type=f32)
             )
 
         def finish():
             store(i, slot, 1, functools.reduce(jnp.add, turned_dq) * SCALE)
 
-        return values_part, values_sum, keys_sum, queries_part, finish
-
+        return values_part, (q, g), queries_part, finish
+
+    heads = range(len(turns))
     paired = len(turns) == 2
     steps = count if paired else (count + 1) // 2
 
@@ -326,13 +323,20 @@
         for a, b in pieces:
             for values_part, *_ in behind:
                 values_part(a, b)
-        for _, values_sum, keys_sum, _, _ in behind:
-            values_sum()
-            keys_sum()
+        rows = [both for _, both, _, _ in behind]
+        for j, left in ((1, weights), (0, dscores)):
+            for i in heads:
+                own = slice(i * lanes, (i + 1) * lanes) if paired else slice(None)
+                right = rows[i][j] if paired else jnp.concatenate([r[j] for r in rows], axis=0)
+                sums[i, j] += jnp.dot(left[:, own], right, preferred_element_type=f32)
+            if last:
+                for i in heads:
+                    staged[i, j] = (sums[i, j] * (1.0 if j else SCALE)).astype(bf16)
+                    handing(i, j).start()
         for a, b in pieces:
             for _, weigh, _ in ahead:
                 weigh(a, b)
-            for _, _, _, queries_part, _ in behind:
+            for _, _, queries_part, _ in behind:
                 queries_part(a, b)
         for *_, finish in behind:
             finish()
@@ -345,8 +349,6 @@
                 leaving(i, slot, owners[slot]).start()
 
         return carry
-
-    heads = range(len(turns))
 
     @pl.when(count > 0)
     def _():
@@ -367,10 +369,6 @@
             kv_copies[i][3].wait()
         carry = lax.fori_loop(0, steps - 1, one_step, carry)
         one_step(steps - 1, carry, last=True)
-        for i in heads:
-            staged[i, 0] = (sums[i, 0] * SCALE).astype(bf16)
-            staged[i, 1] = sums[i, 1].astype(bf16)
-            handing(i).start()
 
     @pl.when(count == 0)
     def _():
@@ -378,7 +376,8 @@
         for i in range(len(turns)):
             for copy in kv_copies[i]:
                 copy.wait()
-            handing(i).start()
+            for j in range(2):
+                handing(i, j).start()
 
     for i in range(len(turns)):
         for slot in range(slots):
@@ -387,7 +386,8 @@
             def _():
                 leaving(i, slot, 0).wait()
 
-        handing(i).wait()
+        for j in range(2):
+            handing(i, j).wait()
 
 
 def xor_permute(array, axis, k):
@@ -460,15 +460,15 @@
                 pltpu.VMEM((len(turns), slots, 2, seg_rows, WIDTH), bf16),
                 pltpu.VMEM((len(turns), room, 2, seg_rows, WIDTH), bf16),
                 pltpu.VMEM((2, padded, lanes), f32),
-                pltpu.VMEM((2, 2, padded, lanes), bf16),
-                pltpu.VMEM((2, padded, lanes), bf16),
+                pltpu.VMEM((2, padded, 2 * lanes), bf16),
+                pltpu.VMEM((padded, 2 * lanes), bf16),
                 pltpu.VMEM((len(turns), 2, padded, HD), f32),
                 pltpu.VMEM((len(turns), 2, padded, HD), bf16),
                 pltpu.SMEM((slots,), jnp.int32),
                 pltpu.SemaphoreType.DMA((len(turns), 4)),
                 pltpu.SemaphoreType.DMA((len(turns), slots)),
                 pltpu.SemaphoreType.DMA((len(turns), slots)),
-                pltpu.SemaphoreType.DMA((len(turns),)),
+                pltpu.SemaphoreType.DMA((len(turns), 2)),
             ],
             compiler_params=pltpu.CompilerParams(vmem_limit_bytes=VMEM_BYTES),
             cost_estimate=pl.CostEstimate(

time: 136 us -> 137 us (level)
  Pallas kernels: 51.8 us -> 66.5 us
  waiting for transfers between devices: 44.5 us -> 31.7 us
    pallas_call x3, Pallas kernels: 36.4 us -> 51.1 us  [attend(): pl.pallas_call(functools.partial(attend_kernel, turns, offset, len(before...]
    ppermute x12, waiting for transfers between devices: 39.2 us -> 31.7 us  [xor_permute(): return lax.ppermute(array, axis, [(i, i ^ k) for i in range(size)])]
    all_to_all x3, waiting for transfers between devices: 5.32 us -> 0.01 us  [exchange(): return lax.all_to_all(array, 'enc', split_axis=0, concat_axis=0, tiled=True)]
  transfers between devices with their start and end apart: 15 -> 15, of which waited for: 7 -> 5; matrix products, arithmetic and copies ran while one was open for 4% -> 4% of each run, Pallas kernels for 34% -> 45%
where the time goes in v15:
time: 137 us; the launch traced here: 136 us
  Pallas kernels  66.5 us (49%)
  waiting for transfers between devices  31.7 us (23%)
  starting transfers between devices  30.8 us (22%)
  other arithmetic  6.04 us (4%)
    pallas_call x3, Pallas kernels, attend(): pl.pallas_call(functools.partial(attend_kernel, turns, offset, len(before...  51.1 us
    ppermute x12, waiting for transfers between devices, xor_permute(): return lax.ppermute(array, axis, [(i, i ^ k) for i in range(size)])  31.7 us
    ppermute x12, starting transfers between devices, xor_permute(): return lax.ppermute(array, axis, [(i, i ^ k) for i in range(size)])  17.6 us
    all_to_all x3, starting transfers between devices, exchange(): return lax.all_to_all(array, 'enc', split_axis=0, concat_axis=0, tiled=True)  13.2 us
    pallas_call x2, Pallas kernels, route(): pl.pallas_call(functools.partial(route_kernel, turns, not prepares, n_seg...  9.75 us
    pallas_call x2, Pallas kernels, collect(): pl.pallas_call(functools.partial(collect_kernel, turns, n_seg, seg_rows),...  5.64 us
    convert_element_type x3, other arithmetic, per_device(): (last[j, a:b].astype(f32) + passed[j, a:b].astype(f32)).astype(bf16)  3.27 us
    broadcast_in_dim x1, other arithmetic, per_device(): return (attended, grad_queries, summed[0][None], summed[1][None])  2.77 us
  transfers between devices with their start and end apart: 15, of which 5 were waited for; matrix products, arithmetic and copies ran while one was open for 4% of the time, Pallas kernels for 45%

profile of v15, /device:TPU:0, one launch (start us, length us, event | category | flops | bytes accessed | tf_op | source)
XLA Modules:
  0.0 136.1 jit_solution(13785105906024014650)
XLA Ops:
  0.6 2.8 %route_0.1 = (bf16[2,2,32,1024]{3,2,1,0:T(8,128)(2,1)}, bf16[2,2,32,1024]{3,2,1,0:T(8,128)(2,1)}, bf16[2,2,32,1024]{3,2,1,0:T(8,128)(2,1)}, bf16[2,2,32,1024]{3,...) custom-call(s32[4,32]{1,0:T(4,128)} %bitcast.23, ...), custom_call_target="tpu_custom_call" | custom-call | bytes 2097152 | tf_op jit(solution)/shard_map/route_0/pallas_call | solution.py:422
  3.4 0.5 collective-permute-start
  4.0 2.6 %collective-permute-start.1 = (bf16[2,2,32,1024]{3,2,1,0:T(8,128)(2,1)}, bf16[2,2,32,1024]{3,2,1,0:T(8,128)(2,1)S(1)}, u32[]{:S(2)}, u32[]{:S(2)}) collective-permute-start(bf16[2,2,32,1024]{3,2,1,0:T(8,128)(2,1)} %get-tuple-element.47), channel_id=1, source_target_pairs={{0,2},{1,3},{2,0},{3,1},{4,6},{5,7},{6,4},{7,5},{8,10},{9,11},{10,... | collective-permute-start | bytes 786440 | tf_op jit(solution)/shard_map/ppermute | solution.py:397
  6.6 0.1 collective-permute-start.2
  6.6 1.8 %collective-permute-start.3 = (bf16[2,2,32,1024]{3,2,1,0:T(8,128)(2,1)}, bf16[2,2,32,1024]{3,2,1,0:T(8,128)(2,1)}, u32[]{:S(2)}, u32[]{:S(2)}) collective-permute-start(bf16[2,2,32,1024]{3,2,1,0:T(8,128)(2,1)} %get-tuple-element.49), channel_id=1, source_target_pairs={{0,4},{1,5},{2,6},{3,7},{4,0},{5,1},{6,2},{7,3},{8,12},{9,13},{10,... | collective-permute-start | bytes 786440 | tf_op jit(solution)/shard_map/ppermute | solution.py:397
  8.4 0.0 collective-permute-start.4
  8.4 2.6 %collective-permute-start.5 = (bf16[2,2,32,1024]{3,2,1,0:T(8,128)(2,1)}, bf16[2,2,32,1024]{3,2,1,0:T(8,128)(2,1)}, u32[]{:S(2)}, u32[]{:S(2)}) collective-permute-start(bf16[2,2,32,1024]{3,2,1,0:T(8,128)(2,1)} %get-tuple-element.51), channel_id=1, source_target_pairs={{0,6},{1,7},{2,4},{3,5},{4,2},{5,3},{6,0},{7,1},{8,14},{9,15},{10,... | collective-permute-start | bytes 786440 | tf_op jit(solution)/shard_map/ppermute | solution.py:397
  11.0 2.9 %collective-permute-done.1.refs_2_ = bf16[2,2,32,1024]{3,2,1,0:T(8,128)(2,1)S(1)} collective-permute-done((bf16[2,2,32,1024]{3,2,1,0:T(8,128)(2,1)}, bf16[2,2,32,1024]{3,2,1,0:T(8,128)(2,1)S(1)}, u32[]{:S(2)}, u32[]{:S(2)}) %collective-permute-start.1) | collective-permute-done | bytes 262176 | tf_op jit(solution)/shard_map/ppermute | solution.py:397
  13.9 1.8 %collective-permute-start.6 = (bf16[2,2,32,1024]{3,2,1,0:T(8,128)(2,1)}, bf16[2,2,32,1024]{3,2,1,0:T(8,128)(2,1)}, u32[]{:S(2)}, u32[]{:S(2)}) collective-permute-start(bf16[2,2,32,1024]{3,2,1,0:T(8,128)(2,1)} %get-tuple-element.52), channel_id=1, source_target_pairs={{0,7},{1,6},{2,5},{3,4},{4,3},{5,2},{6,1},{7,0},{8,15},{9,14},{10,... | collective-permute-start | bytes 786440 | tf_op jit(solution)/shard_map/ppermute | solution.py:397
  15.7 6.9 %route_2.1 = (bf16[8,2,2,32,1024]{4,3,2,1,0:T(8,128)(2,1)}, bf16[4,2,1616,128]{3,2,1,0:T(8,128)(2,1)}, bf16[4,2,128,1616]{3,2,1,0:T(8,128)(2,1)}) custom-call(s32[4,32]{1,0:T(4,128)} %bitcast.24, bf16[128,4096]{1,0:T(8,128)(2,1)} %q_hbm.3, bf16[128,4096]{1,0:T(8,128)(2,1)} %g_hbm.3, bf16[1,1601,512]{2,1,0:T(8,128)(2,1)} %refs_0_.1, bf16[1,1601,512]{2,1,0:T(8,128)(2,1)} %refs_1_.1), custom_call_target="tpu_custom_call" | custom-call | bytes 12582912 | tf_op jit(solution)/shard_map/route_2/pallas_call | solution.py:422
  22.7 8.9 %collective-permute-done.4.refs_5_ = bf16[2,2,32,1024]{3,2,1,0:T(8,128)(2,1)} collective-permute-done((bf16[2,2,32,1024]{3,2,1,0:T(8,128)(2,1)}, bf16[2,2,32,1024]{3,2,1,0:T(8,128)(2,1)}, u32[]{:S(2)}, u32[]{:S(2)}) %collective-permute-start.4) | collective-permute-done | bytes 262176 | tf_op jit(solution)/shard_map/ppermute | solution.py:397
  31.6 4.4 %all-to-all-start.1 = ((bf16[8,2,2,32,1024]{4,3,2,1,0:T(8,128)(2,1)}), bf16[8,2,2,32,1024]{4,3,2,1,0:T(8,128)(2,1)}, u32[]{:S(2)}, u32[]{:S(2)}) async-start(bf16[8,2,2,32,1024]{4,3,2,1,0:T(8,128)(2,1)} %get-tuple-element.68), calls=%async_computation.1 | async-start | bytes 4194304 | tf_op jit(solution)/shard_map/all_to_all | solution.py:501
  36.0 13.3 %attend_0.1 = (bf16[8,2,2,32,1024]{4,3,2,1,0:T(8,128)(2,1)}, bf16[2,1616,128]{2,1,0:T(8,128)(2,1)}) custom-call(s32[4,32]{1,0:T(4,128)} %bitcast.25, bf16[4,2,1616,128]{3,2,1,0:T(8,128)(2,1)} %get-tuple-element.43.caches, bf16[4,2,128,1616]{3,2,1,0:T(8,128)(2,1)} %get-tuple-element.44.turned_caches, bf16[2,2,32,1024]{3,2,1,0:T(8,128)(2,1)} %get-tuple-element.54.refs_0_, ...), custom_call_target="tpu_custom_call" | custom-call | flops 314769408 | bytes 1048576 | tf_op jit(solution)/shard_map/attend_0/pallas_call | solution.py:449
  49.3 2.1 %collective-permute-start.7 = (bf16[2,1616,128]{2,1,0:T(8,128)(2,1)}, bf16[2,1616,128]{2,1,0:T(8,128)(2,1)S(1)}, u32[]{:S(2)}, u32[]{:S(2)}) collective-permute-start(bf16[2,1616,128]{2,1,0:T(8,128)(2,1)} %get-tuple-element.64), channel_id=1, source_target_pairs={{0,8},{8,0},{16,24},{24,16},{1,9},{9,1},{17,25},{25,17},{2,10},{10... | collective-permute-start | bytes 2482184 | tf_op jit(solution)/shard_map/ppermute | solution.py:397
  51.3 13.4 %attend_1.1 = (bf16[8,2,2,32,1024]{4,3,2,1,0:T(8,128)(2,1)}, bf16[2,1616,128]{2,1,0:T(8,128)(2,1)}) custom-call(s32[4,32]{1,0:T(4,128)} %bitcast.26, bf16[4,2,1616,128]{3,2,1,0:T(8,128)(2,1)} %get-tuple-element.43.caches, bf16[4,2,128,1616]{3,2,1,0:T(8,128)(2,1)} %get-tuple-element.44.turned_caches, ...), custom_call_target="tpu_custom_call", output_to_operand_aliasing={{0}: (11, {})} | custom-call | flops 314769408 | bytes 1048576 | tf_op jit(solution)/shard_map/attend_1/pallas_call | solution.py:449
  64.8 0.0 copy-start.3
  64.8 4.5 %all-to-all-start = ((bf16[8,2,2,32,1024]{4,3,2,1,0:T(8,128)(2,1)}), bf16[8,2,2,32,1024]{4,3,2,1,0:T(8,128)(2,1)}, u32[]{:S(2)}, u32[]{:S(2)}) async-start(bf16[8,2,2,32,1024]{4,3,2,1,0:T(8,128)(2,1)} %get-tuple-element.63), calls=%async_computation | async-start | bytes 4194304 | tf_op jit(solution)/shard_map/all_to_all | solution.py:501
  69.3 0.7 fusion.6
  70.0 2.5 %collective-permute-start.9 = (bf16[800,128]{1,0:T(8,128)(2,1)}, bf16[800,128]{1,0:T(8,128)(2,1)}, u32[]{:S(2)}, u32[]{:S(2)}) collective-permute-start(bf16[800,128]{1,0:T(8,128)(2,1)} %fusion.6), channel_id=1, source_target_pairs={{0,16},{8,24},{16,0},{24,8},{1,17},{9,25},{17,1},{25,9},{2,18},{10... | collective-permute-start | bytes 614408 | tf_op jit(solution)/shard_map/ppermute | solution.py:397
  72.6 0.9 fusion.2
  73.4 0.4 collective-permute-start.8
  73.8 24.5 %attend_2.1 = (bf16[8,2,2,32,1024]{4,3,2,1,0:T(8,128)(2,1)}, bf16[2,1616,128]{2,1,0:T(8,128)(2,1)}, bf16[2,1616,128]{2,1,0:T(8,128)(2,1)}) custom-call(s32[4,32]{1,0:T(4,128)} %bitcast.27, bf16[4,2,1616,128]{3,2,1,0:T(8,128)(2,1)} %get-tuple-element.43.caches, bf16[4,2,128,1616]{3,2,1,0:T(8,128)(2,1)} %get-tuple-element.44.turned_caches, ...), custom_call_target="tpu_custom_call" | custom-call | flops 7554465792 | bytes 8388608 | tf_op jit(solution)/shard_map/attend_2/pallas_call | solution.py:449
  98.3 2.2 %collective-permute-done.8 = bf16[1616,128]{1,0:T(8,128)(2,1)} collective-permute-done((bf16[1616,128]{1,0:T(8,128)(2,1)}, bf16[1616,128]{1,0:T(8,128)(2,1)}, u32[]{:S(2)}, u32[]{:S(2)}) %collective-permute-start.8) | collective-permute-done | bytes 413728 | tf_op jit(solution)/shard_map/ppermute | solution.py:397
  100.5 4.3 %all-to-all-start.2 = ((bf16[8,2,2,32,1024]{4,3,2,1,0:T(8,128)(2,1)}), bf16[8,2,2,32,1024]{4,3,2,1,0:T(8,128)(2,1)}, u32[]{:S(2)}, u32[]{:S(2)}) async-start(bf16[8,2,2,32,1024]{4,3,2,1,0:T(8,128)(2,1)} %get-tuple-element.72), calls=%async_computation.2 | async-start | bytes 4194304 | tf_op jit(solution)/shard_map/all_to_all | solution.py:501
  104.9 0.1 collective-permute-start.10
  104.9 1.7 %fusion.5 = bf16[816,128]{1,0:T(8,128)(2,1)} fusion(bf16[2,1616,128]{2,1,0:T(8,128)(2,1)S(1)} %collective-permute-done.7, bf16[2,1616,128]{2,1,0:T(8,128)(2,1)} %get-tuple-element.66), kind=kLoop, calls=%fused_computation.11 | loop fusion | flops 417792 | bytes 626688 | tf_op jit(solution)/shard_map/convert_element_type | solution.py:524
  106.6 3.2 %collective-permute-start.11 = (bf16[816,128]{1,0:T(8,128)(2,1)}, bf16[816,128]{1,0:T(8,128)(2,1)S(1)}, u32[]{:S(2)}, u32[]{:S(2)}) collective-permute-start(bf16[816,128]{1,0:T(8,128)(2,1)} %fusion.5), channel_id=1, source_target_pairs={{0,16},{8,24},{16,0},{24,8},{1,17},{9,25},{17,1},{25,9},{2,18},{10... | collective-permute-start | bytes 626696 | tf_op jit(solution)/shard_map/ppermute | solution.py:397
  109.8 2.8 %collect_0.1 = (bf16[128,4096]{1,0:T(8,128)(2,1)}, bf16[128,4096]{1,0:T(8,128)(2,1)}) custom-call(s32[4,32]{1,0:T(4,128)} %bitcast.28, bf16[8,2,2,32,1024]{4,3,2,1,0:T(8,128)(2,1)} %all-to-all-done.returned), custom_call_target="tpu_custom_call" | custom-call | bytes 4194304 | tf_op jit(solution)/shard_map/collect_0/pallas_call | solution.py:484
  112.6 15.5 %collective-permute-done.11 = bf16[816,128]{1,0:T(8,128)(2,1)S(1)} collective-permute-done((bf16[816,128]{1,0:T(8,128)(2,1)}, bf16[816,128]{1,0:T(8,128)(2,1)S(1)}, u32[]{:S(2)}, u32[]{:S(2)}) %collective-permute-start.11) | collective-permute-done | bytes 208928 | tf_op jit(solution)/shard_map/ppermute | solution.py:397
  128.2 2.2 %collective-permute-done.10 = bf16[2,1616,128]{2,1,0:T(8,128)(2,1)} collective-permute-done((bf16[2,1616,128]{2,1,0:T(8,128)(2,1)}, bf16[2,1616,128]{2,1,0:T(8,128)(2,1)}, u32[]{:S(2)}, u32[]{:S(2)}) %collective-permute-start.10) | collective-permute-done | bytes 827424 | tf_op jit(solution)/shard_map/ppermute | solution.py:397
  130.4 2.8 %fusion.4 = (bf16[1,1601,128]{2,1,0:T(8,128)(2,1)}, bf16[1,1601,128]{2,1,0:T(8,128)(2,1)}) fusion(bf16[816,128]{1,0:T(8,128)(2,1)S(1)} %collective-permute-done.11, bf16[800,128]{1,0:T(8,128)(2,1)} %collective-permute-done.9, bf16[2,1616,128]{2,1,0:T(8,128)(2,1)} %collective-permute-done.10, bf16[2,1616,128]{2,1,0:T(8,128)(2,1)} %get-tuple-element.78, ...), kind=kLoop, calls=%fused_computation.8 | loop fusion | flops 3073920 | bytes 3282688 | tf_op jit(solution)/shard_map/broadcast_in_dim | solution.py:548
  133.1 2.8 %collect_2.1 = (bf16[128,4096]{1,0:T(8,128)(2,1)}, bf16[128,4096]{1,0:T(8,128)(2,1)}) custom-call(s32[4,32]{1,0:T(4,128)} %bitcast.29, bf16[8,2,2,32,1024]{4,3,2,1,0:T(8,128)(2,1)} %all-to-all-done.2.returned, bf16[128,4096]{1,0:T(8,128)(2,1)} %get-tuple-element.74.refs_0_, ...), custom_call_target="tpu_custom_call", output_to_operand_aliasing={{0}: (2, {}), {1}: (3, {})} | custom-call | bytes 4194304 | tf_op jit(solution)/shard_map/collect_2/pallas_call | solution.py:484
  (17 shorter events, 0.0 us)
Async XLA Ops:
  3.4 4.9 %collective-permute-start = (bf16[2,2,32,1024]{3,2,1,0:T(8,128)(2,1)}, bf16[2,2,32,1024]{3,2,1,0:T(8,128)(2,1)S(1)}, u32[]{:S(2)}, u32[]{:S(2)}) collective-permute-start(bf16[2,2,32,1024]{3,2,1,0:T(8,128)(2,1)} %get-tuple-element.46), channel_id=1, source_target_pairs={{0,1},{1,0},{2,3},{3,2},{4,5},{5,4},{6,7},{7,6},{8,9},{9,8},{10,11... | collective-permute-start | bytes 786440 | tf_op jit(solution)/shard_map/ppermute | solution.py:397
  4.0 9.9 %collective-permute-start.1 = (bf16[2,2,32,1024]{3,2,1,0:T(8,128)(2,1)}, bf16[2,2,32,1024]{3,2,1,0:T(8,128)(2,1)S(1)}, u32[]{:S(2)}, u32[]{:S(2)}) collective-permute-start(bf16[2,2,32,1024]{3,2,1,0:T(8,128)(2,1)} %get-tuple-element.47), channel_id=1, source_target_pairs={{0,2},{1,3},{2,0},{3,1},{4,6},{5,7},{6,4},{7,5},{8,10},{9,11},{10,... | collective-permute-start | bytes 786440 | tf_op jit(solution)/shard_map/ppermute | solution.py:397
  6.6 16.1 %collective-permute-start.2 = (bf16[2,2,32,1024]{3,2,1,0:T(8,128)(2,1)}, bf16[2,2,32,1024]{3,2,1,0:T(8,128)(2,1)S(1)}, u32[]{:S(2)}, u32[]{:S(2)}) collective-permute-start(bf16[2,2,32,1024]{3,2,1,0:T(8,128)(2,1)} %get-tuple-element.48), channel_id=1, source_target_pairs={{0,3},{1,2},{2,1},{3,0},{4,7},{5,6},{6,5},{7,4},{8,11},{9,10},{10,... | collective-permute-start | bytes 786440 | tf_op jit(solution)/shard_map/ppermute | solution.py:397
  6.6 16.1 %collective-permute-start.3 = (bf16[2,2,32,1024]{3,2,1,0:T(8,128)(2,1)}, bf16[2,2,32,1024]{3,2,1,0:T(8,128)(2,1)}, u32[]{:S(2)}, u32[]{:S(2)}) collective-permute-start(bf16[2,2,32,1024]{3,2,1,0:T(8,128)(2,1)} %get-tuple-element.49), channel_id=1, source_target_pairs={{0,4},{1,5},{2,6},{3,7},{4,0},{5,1},{6,2},{7,3},{8,12},{9,13},{10,... | collective-permute-start | bytes 786440 | tf_op jit(solution)/shard_map/ppermute | solution.py:397
  8.4 23.2 %collective-permute-start.4 = (bf16[2,2,32,1024]{3,2,1,0:T(8,128)(2,1)}, bf16[2,2,32,1024]{3,2,1,0:T(8,128)(2,1)}, u32[]{:S(2)}, u32[]{:S(2)}) collective-permute-start(bf16[2,2,32,1024]{3,2,1,0:T(8,128)(2,1)} %get-tuple-element.50), channel_id=1, source_target_pairs={{0,5},{1,4},{2,7},{3,6},{4,1},{5,0},{6,3},{7,2},{8,13},{9,12},{10,... | collective-permute-start | bytes 786440 | tf_op jit(solution)/shard_map/ppermute | solution.py:397
  8.4 14.3 %copy-start = (bf16[2,2,32,1024]{3,2,1,0:T(8,128)(2,1)}, bf16[2,2,32,1024]{3,2,1,0:T(8,128)(2,1)S(1)}, u32[]{:S(2)}) copy-start(bf16[2,2,32,1024]{3,2,1,0:T(8,128)(2,1)S(1)} %collective-permute-done.refs_1_) | copy-start | bytes 786436
  8.4 23.2 %collective-permute-start.5 = (bf16[2,2,32,1024]{3,2,1,0:T(8,128)(2,1)}, bf16[2,2,32,1024]{3,2,1,0:T(8,128)(2,1)}, u32[]{:S(2)}, u32[]{:S(2)}) collective-permute-start(bf16[2,2,32,1024]{3,2,1,0:T(8,128)(2,1)} %get-tuple-element.51), channel_id=1, source_target_pairs={{0,6},{1,7},{2,4},{3,5},{4,2},{5,3},{6,0},{7,1},{8,14},{9,15},{10,... | collective-permute-start | bytes 786440 | tf_op jit(solution)/shard_map/ppermute | solution.py:397
  13.9 8.8 %copy-start.1 = (bf16[2,2,32,1024]{3,2,1,0:T(8,128)(2,1)}, bf16[2,2,32,1024]{3,2,1,0:T(8,128)(2,1)S(1)}, u32[]{:S(2)}) copy-start(bf16[2,2,32,1024]{3,2,1,0:T(8,128)(2,1)S(1)} %collective-permute-done.1.refs_2_) | copy-start | bytes 786436
  13.9 17.7 %collective-permute-start.6 = (bf16[2,2,32,1024]{3,2,1,0:T(8,128)(2,1)}, bf16[2,2,32,1024]{3,2,1,0:T(8,128)(2,1)}, u32[]{:S(2)}, u32[]{:S(2)}) collective-permute-start(bf16[2,2,32,1024]{3,2,1,0:T(8,128)(2,1)} %get-tuple-element.52), channel_id=1, source_target_pairs={{0,7},{1,6},{2,5},{3,4},{4,3},{5,2},{6,1},{7,0},{8,15},{9,14},{10,... | collective-permute-start | bytes 786440 | tf_op jit(solution)/shard_map/ppermute | solution.py:397
  22.7 8.9 %copy-start.2 = (bf16[2,2,32,1024]{3,2,1,0:T(8,128)(2,1)}, bf16[2,2,32,1024]{3,2,1,0:T(8,128)(2,1)S(1)}, u32[]{:S(2)}) copy-start(bf16[2,2,32,1024]{3,2,1,0:T(8,128)(2,1)S(1)} %collective-permute-done.2.refs_3_) | copy-start | bytes 786436
  31.6 33.1 %all-to-all-start.1 = ((bf16[8,2,2,32,1024]{4,3,2,1,0:T(8,128)(2,1)}), bf16[8,2,2,32,1024]{4,3,2,1,0:T(8,128)(2,1)}, u32[]{:S(2)}, u32[]{:S(2)}) async-start(bf16[8,2,2,32,1024]{4,3,2,1,0:T(8,128)(2,1)} %get-tuple-element.68), calls=%async_computation.1 | async-start | bytes 4194304 | tf_op jit(solution)/shard_map/all_to_all | solution.py:501
  49.3 20.0 %collective-permute-start.7 = (bf16[2,1616,128]{2,1,0:T(8,128)(2,1)}, bf16[2,1616,128]{2,1,0:T(8,128)(2,1)S(1)}, u32[]{:S(2)}, u32[]{:S(2)}) collective-permute-start(bf16[2,1616,128]{2,1,0:T(8,128)(2,1)} %get-tuple-element.64), channel_id=1, source_target_pairs={{0,8},{8,0},{16,24},{24,16},{1,9},{9,1},{17,25},{25,17},{2,10},{10... | collective-permute-start | bytes 2482184 | tf_op jit(solution)/shard_map/ppermute | solution.py:397
  64.8 4.5 %copy-start.3 = (bf16[2,1616,128]{2,1,0:T(8,128)(2,1)S(1)}, bf16[2,1616,128]{2,1,0:T(8,128)(2,1)}, u32[]{:S(2)}) copy-start(bf16[2,1616,128]{2,1,0:T(8,128)(2,1)} %get-tuple-element.66) | copy-start | bytes 2482180
  64.8 35.7 %all-to-all-start = ((bf16[8,2,2,32,1024]{4,3,2,1,0:T(8,128)(2,1)}), bf16[8,2,2,32,1024]{4,3,2,1,0:T(8,128)(2,1)}, u32[]{:S(2)}, u32[]{:S(2)}) async-start(bf16[8,2,2,32,1024]{4,3,2,1,0:T(8,128)(2,1)} %get-tuple-element.63), calls=%async_computation | async-start | bytes 4194304 | tf_op jit(solution)/shard_map/all_to_all | solution.py:501
  70.0 28.3 %collective-permute-start.9 = (bf16[800,128]{1,0:T(8,128)(2,1)}, bf16[800,128]{1,0:T(8,128)(2,1)}, u32[]{:S(2)}, u32[]{:S(2)}) collective-permute-start(bf16[800,128]{1,0:T(8,128)(2,1)} %fusion.6), channel_id=1, source_target_pairs={{0,16},{8,24},{16,0},{24,8},{1,17},{9,25},{17,1},{25,9},{2,18},{10... | collective-permute-start | bytes 614408 | tf_op jit(solution)/shard_map/ppermute | solution.py:397
  73.4 27.1 %collective-permute-start.8 = (bf16[1616,128]{1,0:T(8,128)(2,1)}, bf16[1616,128]{1,0:T(8,128)(2,1)}, u32[]{:S(2)}, u32[]{:S(2)}) collective-permute-start(bf16[1616,128]{1,0:T(8,128)(2,1)} %fusion.2), channel_id=1, source_target_pairs={{0,16},{8,24},{16,0},{24,8},{1,17},{9,25},{17,1},{25,9},{2,18},{10... | collective-permute-start | bytes 1241096 | tf_op jit(solution)/shard_map/ppermute | solution.py:397
  100.5 32.6 %all-to-all-start.2 = ((bf16[8,2,2,32,1024]{4,3,2,1,0:T(8,128)(2,1)}), bf16[8,2,2,32,1024]{4,3,2,1,0:T(8,128)(2,1)}, u32[]{:S(2)}, u32[]{:S(2)}) async-start(bf16[8,2,2,32,1024]{4,3,2,1,0:T(8,128)(2,1)} %get-tuple-element.72), calls=%async_computation.2 | async-start | bytes 4194304 | tf_op jit(solution)/shard_map/all_to_all | solution.py:501
  104.9 25.5 %collective-permute-start.10 = (bf16[2,1616,128]{2,1,0:T(8,128)(2,1)}, bf16[2,1616,128]{2,1,0:T(8,128)(2,1)}, u32[]{:S(2)}, u32[]{:S(2)}) collective-permute-start(bf16[2,1616,128]{2,1,0:T(8,128)(2,1)} %get-tuple-element.79), channel_id=1, source_target_pairs={{0,8},{8,0},{16,24},{24,16},{1,9},{9,1},{17,25},{25,17},{2,10},{10... | collective-permute-start | bytes 2482184 | tf_op jit(solution)/shard_map/ppermute | solution.py:397
  106.6 21.5 %collective-permute-start.11 = (bf16[816,128]{1,0:T(8,128)(2,1)}, bf16[816,128]{1,0:T(8,128)(2,1)S(1)}, u32[]{:S(2)}, u32[]{:S(2)}) collective-permute-start(bf16[816,128]{1,0:T(8,128)(2,1)} %fusion.5), channel_id=1, source_target_pairs={{0,16},{8,24},{16,0},{24,8},{1,17},{9,25},{17,1},{25,9},{2,18},{10... | collective-permute-start | bytes 626696 | tf_op jit(solution)/shard_map/ppermute | solution.py:397

commit v16 on v13

--- a/solution.py
+++ b/solution.py
@@ -14,7 +14,7 @@
 WIDTH = GROUP * HD
 SCALE = HD ** (-0.5)
 LOG2E = 1.4426950408889634
-CHUNK = 512
+CHUNK = 1024
 SLICE = 128
 LOWEST = -3.0e38
 PER_CHUNK = 2
@@ -492,7 +492,7 @@
                 pltpu.SemaphoreType.DMA((PER_CHUNK, 2, n_seg)),
                 pltpu.SemaphoreType.DMA((PER_CHUNK, 2)),
             ],
-            compiler_params=pltpu.CompilerParams(vmem_limit_bytes=VMEM_BYTES),
+            compiler_params=pltpu.CompilerParams(vmem_limit_bytes=8 << 20),
             cost_estimate=pl.CostEstimate(flops=0, bytes_accessed=4 << 20, transcendentals=0),
             name=f"collect_{turns[0]}",
         )(by_segment, returned, *before)

time: 136 us -> 136 us (level)
  waiting for transfers between devices: 44.5 us -> 49.9 us
  Pallas kernels: 51.8 us -> 47.9 us
    ppermute x12, waiting for transfers between devices: 39.2 us -> 44.4 us  [xor_permute(): return lax.ppermute(array, axis, [(i, i ^ k) for i in range(size)])]
    pallas_call x3, Pallas kernels: 36.4 us -> 32.4 us  [attend(): pl.pallas_call(functools.partial(attend_kernel, turns, offset, len(before...]
  transfers between devices with their start and end apart: 15 -> 15, of which waited for: 7 -> 7; matrix products, arithmetic and copies ran while one was open for 4% -> 4% of each run, Pallas kernels for 34% -> 31%
where the time goes in v16:
time: 136 us; the launch traced here: 135 us
  waiting for transfers between devices  49.9 us (37%)
  Pallas kernels  47.9 us (35%)
  starting transfers between devices  31.3 us (23%)
  other arithmetic  4.98 us (4%)
    ppermute x12, waiting for transfers between devices, xor_permute(): return lax.ppermute(array, axis, [(i, i ^ k) for i in range(size)])  44.4 us
    pallas_call x3, Pallas kernels, attend(): pl.pallas_call(functools.partial(attend_kernel, turns, offset, len(before...  32.4 us
    ppermute x12, starting transfers between devices, xor_permute(): return lax.ppermute(array, axis, [(i, i ^ k) for i in range(size)])  17.5 us
    all_to_all x3, starting transfers between devices, exchange(): return lax.all_to_all(array, 'enc', split_axis=0, concat_axis=0, tiled=True)  13.8 us
    pallas_call x2, Pallas kernels, route(): pl.pallas_call(functools.partial(route_kernel, turns, not prepares, n_seg...  9.75 us
    pallas_call x2, Pallas kernels, collect(): pl.pallas_call(functools.partial(collect_kernel, turns, n_seg, seg_rows),...  5.77 us
    all_to_all x3, waiting for transfers between devices, exchange(): return lax.all_to_all(array, 'enc', split_axis=0, concat_axis=0, tiled=True)  5.5 us
  transfers between devices with their start and end apart: 15, of which 7 were waited for; matrix products, arithmetic and copies ran while one was open for 4% of the time, Pallas kernels for 31%

profile of v16, /device:TPU:0, one launch (start us, length us, event | category | flops | bytes accessed | tf_op | source)
XLA Modules:
  0.0 135.1 jit_solution(2521493482228081245)
XLA Ops:
  0.6 2.8 %route_0.1 = (bf16[2,2,32,1024]{3,2,1,0:T(8,128)(2,1)}, bf16[2,2,32,1024]{3,2,1,0:T(8,128)(2,1)}, bf16[2,2,32,1024]{3,2,1,0:T(8,128)(2,1)}, bf16[2,2,32,1024]{3,...) custom-call(s32[4,32]{1,0:T(4,128)} %bitcast.23, ...), custom_call_target="tpu_custom_call" | custom-call | bytes 2097152 | tf_op jit(solution)/shard_map/route_0/pallas_call | solution.py:422
  3.5 0.5 collective-permute-start
  4.0 2.6 %collective-permute-start.1 = (bf16[2,2,32,1024]{3,2,1,0:T(8,128)(2,1)}, bf16[2,2,32,1024]{3,2,1,0:T(8,128)(2,1)S(1)}, u32[]{:S(2)}, u32[]{:S(2)}) collective-permute-start(bf16[2,2,32,1024]{3,2,1,0:T(8,128)(2,1)} %get-tuple-element.47), channel_id=1, source_target_pairs={{0,2},{1,3},{2,0},{3,1},{4,6},{5,7},{6,4},{7,5},{8,10},{9,11},{10,... | collective-permute-start | bytes 786440 | tf_op jit(solution)/shard_map/ppermute | solution.py:397
  6.5 0.1 collective-permute-start.2
  6.6 1.8 %collective-permute-start.3 = (bf16[2,2,32,1024]{3,2,1,0:T(8,128)(2,1)}, bf16[2,2,32,1024]{3,2,1,0:T(8,128)(2,1)}, u32[]{:S(2)}, u32[]{:S(2)}) collective-permute-start(bf16[2,2,32,1024]{3,2,1,0:T(8,128)(2,1)} %get-tuple-element.49), channel_id=1, source_target_pairs={{0,4},{1,5},{2,6},{3,7},{4,0},{5,1},{6,2},{7,3},{8,12},{9,13},{10,... | collective-permute-start | bytes 786440 | tf_op jit(solution)/shard_map/ppermute | solution.py:397
  8.4 2.6 %collective-permute-start.5 = (bf16[2,2,32,1024]{3,2,1,0:T(8,128)(2,1)}, bf16[2,2,32,1024]{3,2,1,0:T(8,128)(2,1)}, u32[]{:S(2)}, u32[]{:S(2)}) collective-permute-start(bf16[2,2,32,1024]{3,2,1,0:T(8,128)(2,1)} %get-tuple-element.51), channel_id=1, source_target_pairs={{0,6},{1,7},{2,4},{3,5},{4,2},{5,3},{6,0},{7,1},{8,14},{9,15},{10,... | collective-permute-start | bytes 786440 | tf_op jit(solution)/shard_map/ppermute | solution.py:397
  11.0 2.9 %collective-permute-done.1.refs_2_ = bf16[2,2,32,1024]{3,2,1,0:T(8,128)(2,1)S(1)} collective-permute-done((bf16[2,2,32,1024]{3,2,1,0:T(8,128)(2,1)}, bf16[2,2,32,1024]{3,2,1,0:T(8,128)(2,1)S(1)}, u32[]{:S(2)}, u32[]{:S(2)}) %collective-permute-start.1) | collective-permute-done | bytes 262176 | tf_op jit(solution)/shard_map/ppermute | solution.py:397
  13.9 1.8 %collective-permute-start.6 = (bf16[2,2,32,1024]{3,2,1,0:T(8,128)(2,1)}, bf16[2,2,32,1024]{3,2,1,0:T(8,128)(2,1)}, u32[]{:S(2)}, u32[]{:S(2)}) collective-permute-start(bf16[2,2,32,1024]{3,2,1,0:T(8,128)(2,1)} %get-tuple-element.52), channel_id=1, source_target_pairs={{0,7},{1,6},{2,5},{3,4},{4,3},{5,2},{6,1},{7,0},{8,15},{9,14},{10,... | collective-permute-start | bytes 786440 | tf_op jit(solution)/shard_map/ppermute | solution.py:397
  15.7 6.9 %route_2.1 = (bf16[8,2,2,32,1024]{4,3,2,1,0:T(8,128)(2,1)}, bf16[4,2,1616,128]{3,2,1,0:T(8,128)(2,1)}, bf16[4,2,128,1616]{3,2,1,0:T(8,128)(2,1)}) custom-call(s32[4,32]{1,0:T(4,128)} %bitcast.24, bf16[128,4096]{1,0:T(8,128)(2,1)} %q_hbm.3, bf16[128,4096]{1,0:T(8,128)(2,1)} %g_hbm.3, bf16[1,1601,512]{2,1,0:T(8,128)(2,1)} %refs_0_.1, bf16[1,1601,512]{2,1,0:T(8,128)(2,1)} %refs_1_.1), custom_call_target="tpu_custom_call" | custom-call | bytes 12582912 | tf_op jit(solution)/shard_map/route_2/pallas_call | solution.py:422
  22.7 8.9 %collective-permute-done.4.refs_5_ = bf16[2,2,32,1024]{3,2,1,0:T(8,128)(2,1)} collective-permute-done((bf16[2,2,32,1024]{3,2,1,0:T(8,128)(2,1)}, bf16[2,2,32,1024]{3,2,1,0:T(8,128)(2,1)}, u32[]{:S(2)}, u32[]{:S(2)}) %collective-permute-start.4) | collective-permute-done | bytes 262176 | tf_op jit(solution)/shard_map/ppermute | solution.py:397
  31.6 4.4 %all-to-all-start.1 = ((bf16[8,2,2,32,1024]{4,3,2,1,0:T(8,128)(2,1)}), bf16[8,2,2,32,1024]{4,3,2,1,0:T(8,128)(2,1)}, u32[]{:S(2)}, u32[]{:S(2)}) async-start(bf16[8,2,2,32,1024]{4,3,2,1,0:T(8,128)(2,1)} %get-tuple-element.68), calls=%async_computation.1 | async-start | bytes 4194304 | tf_op jit(solution)/shard_map/all_to_all | solution.py:501
  36.0 9.5 %attend_0.1 = (bf16[8,2,2,32,1024]{4,3,2,1,0:T(8,128)(2,1)}, bf16[2,1616,128]{2,1,0:T(8,128)(2,1)}) custom-call(s32[4,32]{1,0:T(4,128)} %bitcast.25, bf16[4,2,1616,128]{3,2,1,0:T(8,128)(2,1)} %get-tuple-element.43.caches, bf16[4,2,128,1616]{3,2,1,0:T(8,128)(2,1)} %get-tuple-element.44.turned_caches, bf16[2,2,32,1024]{3,2,1,0:T(8,128)(2,1)} %get-tuple-element.54.refs_0_, ...), custom_call_target="tpu_custom_call" | custom-call | flops 314769408 | bytes 1048576 | tf_op jit(solution)/shard_map/attend_0/pallas_call | solution.py:449
  45.6 2.0 %collective-permute-start.7 = (bf16[2,1616,128]{2,1,0:T(8,128)(2,1)}, bf16[2,1616,128]{2,1,0:T(8,128)(2,1)S(1)}, u32[]{:S(2)}, u32[]{:S(2)}) collective-permute-start(bf16[2,1616,128]{2,1,0:T(8,128)(2,1)} %get-tuple-element.64), channel_id=1, source_target_pairs={{0,8},{8,0},{16,24},{24,16},{1,9},{9,1},{17,25},{25,17},{2,10},{10... | collective-permute-start | bytes 2482184 | tf_op jit(solution)/shard_map/ppermute | solution.py:397
  47.6 9.7 %attend_1.1 = (bf16[8,2,2,32,1024]{4,3,2,1,0:T(8,128)(2,1)}, bf16[2,1616,128]{2,1,0:T(8,128)(2,1)}) custom-call(s32[4,32]{1,0:T(4,128)} %bitcast.26, bf16[4,2,1616,128]{3,2,1,0:T(8,128)(2,1)} %get-tuple-element.43.caches, bf16[4,2,128,1616]{3,2,1,0:T(8,128)(2,1)} %get-tuple-element.44.turned_caches, ...), custom_call_target="tpu_custom_call", output_to_operand_aliasing={{0}: (11, {})} | custom-call | flops 314769408 | bytes 1048576 | tf_op jit(solution)/shard_map/attend_1/pallas_call | solution.py:449
  57.3 5.5 %all-to-all-done.1.refs_0_ = bf16[8,2,2,32,1024]{4,3,2,1,0:T(8,128)(2,1)} async-done(((bf16[8,2,2,32,1024]{4,3,2,1,0:T(8,128)(2,1)}), bf16[8,2,2,32,1024]{4,3,2,1,0:T(8,128)(2,1)}, u32[]{:S(2)}, u32[]{:S(2)}) %all-to-all-start.1) | async-done | bytes 2097184 | tf_op jit(solution)/shard_map/all_to_all | solution.py:501
  62.8 5.4 %all-to-all-start = ((bf16[8,2,2,32,1024]{4,3,2,1,0:T(8,128)(2,1)}), bf16[8,2,2,32,1024]{4,3,2,1,0:T(8,128)(2,1)}, u32[]{:S(2)}, u32[]{:S(2)}) async-start(bf16[8,2,2,32,1024]{4,3,2,1,0:T(8,128)(2,1)} %get-tuple-element.63), calls=%async_computation | async-start | bytes 4194304 | tf_op jit(solution)/shard_map/all_to_all | solution.py:501
  68.2 0.7 fusion.6
  69.0 2.6 %collective-permute-start.9 = (bf16[800,128]{1,0:T(8,128)(2,1)}, bf16[800,128]{1,0:T(8,128)(2,1)}, u32[]{:S(2)}, u32[]{:S(2)}) collective-permute-start(bf16[800,128]{1,0:T(8,128)(2,1)} %fusion.6), channel_id=1, source_target_pairs={{0,16},{8,24},{16,0},{24,8},{1,17},{9,25},{17,1},{25,9},{2,18},{10... | collective-permute-start | bytes 614408 | tf_op jit(solution)/shard_map/ppermute | solution.py:397
  71.6 0.9 fusion.2
  72.4 0.3 collective-permute-start.8
  72.8 13.2 %attend_2.1 = (bf16[8,2,2,32,1024]{4,3,2,1,0:T(8,128)(2,1)}, bf16[2,1616,128]{2,1,0:T(8,128)(2,1)}, bf16[2,1616,128]{2,1,0:T(8,128)(2,1)}) custom-call(s32[4,32]{1,0:T(4,128)} %bitcast.27, bf16[4,2,1616,128]{3,2,1,0:T(8,128)(2,1)} %get-tuple-element.43.caches, bf16[4,2,128,1616]{3,2,1,0:T(8,128)(2,1)} %get-tuple-element.44.turned_caches, ...), custom_call_target="tpu_custom_call" | custom-call | flops 7554465792 | bytes 8388608 | tf_op jit(solution)/shard_map/attend_2/pallas_call | solution.py:449
  85.9 5.2 %collective-permute-done.9 = bf16[800,128]{1,0:T(8,128)(2,1)} collective-permute-done((bf16[800,128]{1,0:T(8,128)(2,1)}, bf16[800,128]{1,0:T(8,128)(2,1)}, u32[]{:S(2)}, u32[]{:S(2)}) %collective-permute-start.9) | collective-permute-done | bytes 204832 | tf_op jit(solution)/shard_map/ppermute | solution.py:397
  91.1 8.9 %collective-permute-done.8 = bf16[1616,128]{1,0:T(8,128)(2,1)} collective-permute-done((bf16[1616,128]{1,0:T(8,128)(2,1)}, bf16[1616,128]{1,0:T(8,128)(2,1)}, u32[]{:S(2)}, u32[]{:S(2)}) %collective-permute-start.8) | collective-permute-done | bytes 413728 | tf_op jit(solution)/shard_map/ppermute | solution.py:397
  100.0 4.0 %all-to-all-start.2 = ((bf16[8,2,2,32,1024]{4,3,2,1,0:T(8,128)(2,1)}), bf16[8,2,2,32,1024]{4,3,2,1,0:T(8,128)(2,1)S(1)}, u32[]{:S(2)}, u32[]{:S(2)}) async-start(bf16[8,2,2,32,1024]{4,3,2,1,0:T(8,128)(2,1)} %get-tuple-element.72), calls=%async_computation.2 | async-start | bytes 4194304 | tf_op jit(solution)/shard_map/all_to_all | solution.py:501
  104.0 0.1 collective-permute-start.10
  104.1 1.1 fusion.5
  105.1 3.2 %collective-permute-start.11 = (bf16[816,128]{1,0:T(8,128)(2,1)S(1)}, bf16[816,128]{1,0:T(8,128)(2,1)S(1)}, u32[]{:S(2)}, u32[]{:S(2)}) collective-permute-start(bf16[816,128]{1,0:T(8,128)(2,1)S(1)} %fusion.5), channel_id=1, source_target_pairs={{0,16},{8,24},{16,0},{24,8},{1,17},{9,25},{17,1},{25,9},{2,18},{10... | collective-permute-start | bytes 626696 | tf_op jit(solution)/shard_map/ppermute | solution.py:397
  108.3 2.7 %collect_0.1 = (bf16[128,4096]{1,0:T(8,128)(2,1)}, bf16[128,4096]{1,0:T(8,128)(2,1)}) custom-call(s32[4,32]{1,0:T(4,128)S(1)} %bitcast.28, bf16[8,2,2,32,1024]{4,3,2,1,0:T(8,128)(2,1)} %all-to-all-done.returned), custom_call_target="tpu_custom_call" | custom-call | bytes 4194304 | tf_op jit(solution)/shard_map/collect_0/pallas_call | solution.py:484
  111.0 16.3 %collective-permute-done.11 = bf16[816,128]{1,0:T(8,128)(2,1)S(1)} collective-permute-done((bf16[816,128]{1,0:T(8,128)(2,1)S(1)}, bf16[816,128]{1,0:T(8,128)(2,1)S(1)}, u32[]{:S(2)}, u32[]{:S(2)}) %collective-permute-start.11) | collective-permute-done | bytes 208928 | tf_op jit(solution)/shard_map/ppermute | solution.py:397
  127.3 2.2 %collective-permute-done.10 = bf16[2,1616,128]{2,1,0:T(8,128)(2,1)S(1)} collective-permute-done((bf16[2,1616,128]{2,1,0:T(8,128)(2,1)}, bf16[2,1616,128]{2,1,0:T(8,128)(2,1)S(1)}, u32[]{:S(2)}, u32[]{:S(2)}) %collective-permute-start.10) | collective-permute-done | bytes 827424 | tf_op jit(solution)/shard_map/ppermute | solution.py:397
  129.5 2.3 %fusion.4 = (bf16[1,1601,128]{2,1,0:T(8,128)(2,1)}, bf16[1,1601,128]{2,1,0:T(8,128)(2,1)}) fusion(bf16[816,128]{1,0:T(8,128)(2,1)S(1)} %collective-permute-done.11, bf16[800,128]{1,0:T(8,128)(2,1)} %collective-permute-done.9, bf16[2,1616,128]{2,1,0:T(8,128)(2,1)S(1)} %collective-permute-done.10, bf16[2,1616,128]{2,1,0:T(8,128)(2,1)S(1)} %copy-done.5, ...), kind=kLoop, calls=%fused_computation.8 | loop fusion | flops 3073920 | bytes 3282688 | tf_op jit(solution)/shard_map/broadcast_in_dim | solution.py:548
  131.8 3.1 %collect_2.1 = (bf16[128,4096]{1,0:T(8,128)(2,1)}, bf16[128,4096]{1,0:T(8,128)(2,1)}) custom-call(s32[4,32]{1,0:T(4,128)S(1)} %bitcast.29, bf16[8,2,2,32,1024]{4,3,2,1,0:T(8,128)(2,1)S(1)} %all-to-all-done.2.returned, bf16[128,4096]{1,0:T(8,128)(2,1)} %get-tuple-element.74.refs_0_, ...), custom_call_target="tpu_custom_call", output_to_operand_aliasing={{0}: (2, {}), {1}: (3, {})} | custom-call | bytes 4194304 | tf_op jit(solution)/shard_map/collect_2/pallas_call | solution.py:484
  (21 shorter events, 0.0 us)
Async XLA Ops:
  3.5 4.9 %collective-permute-start = (bf16[2,2,32,1024]{3,2,1,0:T(8,128)(2,1)}, bf16[2,2,32,1024]{3,2,1,0:T(8,128)(2,1)S(1)}, u32[]{:S(2)}, u32[]{:S(2)}) collective-permute-start(bf16[2,2,32,1024]{3,2,1,0:T(8,128)(2,1)} %get-tuple-element.46), channel_id=1, source_target_pairs={{0,1},{1,0},{2,3},{3,2},{4,5},{5,4},{6,7},{7,6},{8,9},{9,8},{10,11... | collective-permute-start | bytes 786440 | tf_op jit(solution)/shard_map/ppermute | solution.py:397
  4.0 9.9 %collective-permute-start.1 = (bf16[2,2,32,1024]{3,2,1,0:T(8,128)(2,1)}, bf16[2,2,32,1024]{3,2,1,0:T(8,128)(2,1)S(1)}, u32[]{:S(2)}, u32[]{:S(2)}) collective-permute-start(bf16[2,2,32,1024]{3,2,1,0:T(8,128)(2,1)} %get-tuple-element.47), channel_id=1, source_target_pairs={{0,2},{1,3},{2,0},{3,1},{4,6},{5,7},{6,4},{7,5},{8,10},{9,11},{10,... | collective-permute-start | bytes 786440 | tf_op jit(solution)/shard_map/ppermute | solution.py:397
  6.5 16.2 %collective-permute-start.2 = (bf16[2,2,32,1024]{3,2,1,0:T(8,128)(2,1)}, bf16[2,2,32,1024]{3,2,1,0:T(8,128)(2,1)S(1)}, u32[]{:S(2)}, u32[]{:S(2)}) collective-permute-start(bf16[2,2,32,1024]{3,2,1,0:T(8,128)(2,1)} %get-tuple-element.48), channel_id=1, source_target_pairs={{0,3},{1,2},{2,1},{3,0},{4,7},{5,6},{6,5},{7,4},{8,11},{9,10},{10,... | collective-permute-start | bytes 786440 | tf_op jit(solution)/shard_map/ppermute | solution.py:397
  6.6 16.1 %collective-permute-start.3 = (bf16[2,2,32,1024]{3,2,1,0:T(8,128)(2,1)}, bf16[2,2,32,1024]{3,2,1,0:T(8,128)(2,1)}, u32[]{:S(2)}, u32[]{:S(2)}) collective-permute-start(bf16[2,2,32,1024]{3,2,1,0:T(8,128)(2,1)} %get-tuple-element.49), channel_id=1, source_target_pairs={{0,4},{1,5},{2,6},{3,7},{4,0},{5,1},{6,2},{7,3},{8,12},{9,13},{10,... | collective-permute-start | bytes 786440 | tf_op jit(solution)/shard_map/ppermute | solution.py:397
  8.4 23.2 %collective-permute-start.4 = (bf16[2,2,32,1024]{3,2,1,0:T(8,128)(2,1)}, bf16[2,2,32,1024]{3,2,1,0:T(8,128)(2,1)}, u32[]{:S(2)}, u32[]{:S(2)}) collective-permute-start(bf16[2,2,32,1024]{3,2,1,0:T(8,128)(2,1)} %get-tuple-element.50), channel_id=1, source_target_pairs={{0,5},{1,4},{2,7},{3,6},{4,1},{5,0},{6,3},{7,2},{8,13},{9,12},{10,... | collective-permute-start | bytes 786440 | tf_op jit(solution)/shard_map/ppermute | solution.py:397
  8.4 14.3 %copy-start.1 = (bf16[2,2,32,1024]{3,2,1,0:T(8,128)(2,1)}, bf16[2,2,32,1024]{3,2,1,0:T(8,128)(2,1)S(1)}, u32[]{:S(2)}) copy-start(bf16[2,2,32,1024]{3,2,1,0:T(8,128)(2,1)S(1)} %collective-permute-done.refs_1_) | copy-start | bytes 786436
  8.4 23.2 %collective-permute-start.5 = (bf16[2,2,32,1024]{3,2,1,0:T(8,128)(2,1)}, bf16[2,2,32,1024]{3,2,1,0:T(8,128)(2,1)}, u32[]{:S(2)}, u32[]{:S(2)}) collective-permute-start(bf16[2,2,32,1024]{3,2,1,0:T(8,128)(2,1)} %get-tuple-element.51), channel_id=1, source_target_pairs={{0,6},{1,7},{2,4},{3,5},{4,2},{5,3},{6,0},{7,1},{8,14},{9,15},{10,... | collective-permute-start | bytes 786440 | tf_op jit(solution)/shard_map/ppermute | solution.py:397
  13.9 8.8 %copy-start.2 = (bf16[2,2,32,1024]{3,2,1,0:T(8,128)(2,1)}, bf16[2,2,32,1024]{3,2,1,0:T(8,128)(2,1)S(1)}, u32[]{:S(2)}) copy-start(bf16[2,2,32,1024]{3,2,1,0:T(8,128)(2,1)S(1)} %collective-permute-done.1.refs_2_) | copy-start | bytes 786436
  13.9 17.7 %collective-permute-start.6 = (bf16[2,2,32,1024]{3,2,1,0:T(8,128)(2,1)}, bf16[2,2,32,1024]{3,2,1,0:T(8,128)(2,1)}, u32[]{:S(2)}, u32[]{:S(2)}) collective-permute-start(bf16[2,2,32,1024]{3,2,1,0:T(8,128)(2,1)} %get-tuple-element.52), channel_id=1, source_target_pairs={{0,7},{1,6},{2,5},{3,4},{4,3},{5,2},{6,1},{7,0},{8,15},{9,14},{10,... | collective-permute-start | bytes 786440 | tf_op jit(solution)/shard_map/ppermute | solution.py:397
  22.7 8.9 %copy-start.3 = (bf16[2,2,32,1024]{3,2,1,0:T(8,128)(2,1)}, bf16[2,2,32,1024]{3,2,1,0:T(8,128)(2,1)S(1)}, u32[]{:S(2)}) copy-start(bf16[2,2,32,1024]{3,2,1,0:T(8,128)(2,1)S(1)} %collective-permute-done.2.refs_3_) | copy-start | bytes 786436
  31.6 31.2 %all-to-all-start.1 = ((bf16[8,2,2,32,1024]{4,3,2,1,0:T(8,128)(2,1)}), bf16[8,2,2,32,1024]{4,3,2,1,0:T(8,128)(2,1)}, u32[]{:S(2)}, u32[]{:S(2)}) async-start(bf16[8,2,2,32,1024]{4,3,2,1,0:T(8,128)(2,1)} %get-tuple-element.68), calls=%async_computation.1 | async-start | bytes 4194304 | tf_op jit(solution)/shard_map/all_to_all | solution.py:501
  45.6 22.7 %collective-permute-start.7 = (bf16[2,1616,128]{2,1,0:T(8,128)(2,1)}, bf16[2,1616,128]{2,1,0:T(8,128)(2,1)S(1)}, u32[]{:S(2)}, u32[]{:S(2)}) collective-permute-start(bf16[2,1616,128]{2,1,0:T(8,128)(2,1)} %get-tuple-element.64), channel_id=1, source_target_pairs={{0,8},{8,0},{16,24},{24,16},{1,9},{9,1},{17,25},{25,17},{2,10},{10... | collective-permute-start | bytes 2482184 | tf_op jit(solution)/shard_map/ppermute | solution.py:397
  62.8 5.4 %copy-start.4 = (bf16[2,1616,128]{2,1,0:T(8,128)(2,1)S(1)}, bf16[2,1616,128]{2,1,0:T(8,128)(2,1)}, u32[]{:S(2)}) copy-start(bf16[2,1616,128]{2,1,0:T(8,128)(2,1)} %get-tuple-element.66) | copy-start | bytes 2482180
  62.8 37.2 %all-to-all-start = ((bf16[8,2,2,32,1024]{4,3,2,1,0:T(8,128)(2,1)}), bf16[8,2,2,32,1024]{4,3,2,1,0:T(8,128)(2,1)}, u32[]{:S(2)}, u32[]{:S(2)}) async-start(bf16[8,2,2,32,1024]{4,3,2,1,0:T(8,128)(2,1)} %get-tuple-element.63), calls=%async_computation | async-start | bytes 4194304 | tf_op jit(solution)/shard_map/all_to_all | solution.py:501
  69.0 22.1 %collective-permute-start.9 = (bf16[800,128]{1,0:T(8,128)(2,1)}, bf16[800,128]{1,0:T(8,128)(2,1)}, u32[]{:S(2)}, u32[]{:S(2)}) collective-permute-start(bf16[800,128]{1,0:T(8,128)(2,1)} %fusion.6), channel_id=1, source_target_pairs={{0,16},{8,24},{16,0},{24,8},{1,17},{9,25},{17,1},{25,9},{2,18},{10... | collective-permute-start | bytes 614408 | tf_op jit(solution)/shard_map/ppermute | solution.py:397
  72.4 27.6 %collective-permute-start.8 = (bf16[1616,128]{1,0:T(8,128)(2,1)}, bf16[1616,128]{1,0:T(8,128)(2,1)}, u32[]{:S(2)}, u32[]{:S(2)}) collective-permute-start(bf16[1616,128]{1,0:T(8,128)(2,1)} %fusion.2), channel_id=1, source_target_pairs={{0,16},{8,24},{16,0},{24,8},{1,17},{9,25},{17,1},{25,9},{2,18},{10... | collective-permute-start | bytes 1241096 | tf_op jit(solution)/shard_map/ppermute | solution.py:397
  100.0 8.3 %copy-start = (s32[32,4]{0,1:T(4,128)S(1)}, s32[32,4]{0,1:T(4,128)}, u32[]{:S(2)}) copy-start(s32[32,4]{0,1:T(4,128)} %param.8) | copy-start | bytes 1540
  100.0 31.9 %all-to-all-start.2 = ((bf16[8,2,2,32,1024]{4,3,2,1,0:T(8,128)(2,1)}), bf16[8,2,2,32,1024]{4,3,2,1,0:T(8,128)(2,1)S(1)}, u32[]{:S(2)}, u32[]{:S(2)}) async-start(bf16[8,2,2,32,1024]{4,3,2,1,0:T(8,128)(2,1)} %get-tuple-element.72), calls=%async_computation.2 | async-start | bytes 4194304 | tf_op jit(solution)/shard_map/all_to_all | solution.py:501
  104.0 25.5 %copy-start.5 = (bf16[2,1616,128]{2,1,0:T(8,128)(2,1)S(1)}, bf16[2,1616,128]{2,1,0:T(8,128)(2,1)}, u32[]{:S(2)}) copy-start(bf16[2,1616,128]{2,1,0:T(8,128)(2,1)} %get-tuple-element.78) | copy-start | bytes 2482180
  104.0 25.5 %collective-permute-start.10 = (bf16[2,1616,128]{2,1,0:T(8,128)(2,1)}, bf16[2,1616,128]{2,1,0:T(8,128)(2,1)S(1)}, u32[]{:S(2)}, u32[]{:S(2)}) collective-permute-start(bf16[2,1616,128]{2,1,0:T(8,128)(2,1)} %get-tuple-element.79), channel_id=1, source_target_pairs={{0,8},{8,0},{16,24},{24,16},{1,9},{9,1},{17,25},{25,17},{2,10},{10... | collective-permute-start | bytes 2482184 | tf_op jit(solution)/shard_map/ppermute | solution.py:397
  105.1 22.2 %collective-permute-start.11 = (bf16[816,128]{1,0:T(8,128)(2,1)S(1)}, bf16[816,128]{1,0:T(8,128)(2,1)S(1)}, u32[]{:S(2)}, u32[]{:S(2)}) collective-permute-start(bf16[816,128]{1,0:T(8,128)(2,1)S(1)} %fusion.5), channel_id=1, source_target_pairs={{0,16},{8,24},{16,0},{24,8},{1,17},{9,25},{17,1},{25,9},{2,18},{10... | collective-permute-start | bytes 626696 | tf_op jit(solution)/shard_map/ppermute | solution.py:397

commit v17 on v16

--- a/solution.py
+++ b/solution.py
@@ -139,7 +139,7 @@
             )
 
 
-def attend_kernel(turns, offset, before, peers, seg_rows, tokens, reads, caches, turned_caches, *refs):
+def attend_kernel(turns, offset, before, order, peers, seg_rows, tokens, reads, caches, turned_caches, *refs):
     outs = 1 + len(turns)
     received, refs = refs[: len(refs) - 14 - outs], refs[len(refs) - 14 - outs :]
     received = received[: len(received) - before]
@@ -186,7 +186,7 @@
     ]
 
     def arriving(i, slot, k):
-        source = received[k] if len(received) > 1 else received[0].at[me ^ k]
+        source = received[order.index(k)] if len(received) > 1 else received[0].at[me ^ k]
         return pltpu.make_async_copy(source.at[offset + i], inbox.at[i, slot], in_sems.at[i, slot])
 
     def leaving(i, slot, owner):
@@ -448,7 +448,7 @@
         room = slots + slots % 2
         return pl.pallas_call(
             functools.partial(
-                attend_kernel, turns, offset, len(before), peers, seg_rows, tokens
+                attend_kernel, turns, offset, len(before), order, peers, seg_rows, tokens
             ),
             out_shape=[message] + [grad] * len(turns),
             in_specs=[SMEM] + [ANY] * (2 + len(received) + len(before)),
@@ -500,10 +500,10 @@
     def exchange(array):
         return lax.all_to_all(array, "enc", split_axis=0, concat_axis=0, tiled=True)
 
+    order = [0, 1] + sorted(range(2, peers), key=lambda k: (k & 1, -(k >> 1).bit_count(), k))
+
     def exchange_apart(arrays):
-        order = sorted(range(peers), key=lambda k: (-(k >> 1).bit_count(), k & 1, k))
-        arrived = {k: xor_permute(arrays[k], "enc", k) for k in order}
-        return [arrived[k] for k in range(peers)]
+        return [xor_permute(arrays[k], "enc", k) for k in order]
 
     first, second = chunks
     received = exchange_apart(route(first, 0))

time: 136 us -> 136 us (level)
  waiting for transfers between devices: 49.9 us -> 46 us
  Pallas kernels: 47.9 us -> 51.7 us
    ppermute x12, waiting for transfers between devices: 44.4 us -> 40.6 us  [xor_permute(): return lax.ppermute(array, axis, [(i, i ^ k) for i in range(size)])]
    pallas_call x3, Pallas kernels: 32.4 us -> 36.1 us  [attend(): pl.pallas_call(functools.partial(attend_kernel, turns, offset, len(before...]
  transfers between devices with their start and end apart: 15 -> 15, of which waited for: 7 -> 8; matrix products, arithmetic and copies ran while one was open for 4% -> 4% of each run, Pallas kernels for 31% -> 34%
where the time goes in v17:
time: 136 us
  Pallas kernels  51.7 us (38%)
  waiting for transfers between devices  46 us (34%)
  starting transfers between devices  32.2 us (24%)
  other arithmetic  4.91 us (4%)
    ppermute x12, waiting for transfers between devices, xor_permute(): return lax.ppermute(array, axis, [(i, i ^ k) for i in range(size)])  40.6 us
    pallas_call x3, Pallas kernels, attend(): pl.pallas_call(functools.partial(attend_kernel, turns, offset, len(before...  36.1 us
    ppermute x12, starting transfers between devices, xor_permute(): return lax.ppermute(array, axis, [(i, i ^ k) for i in range(size)])  17.3 us
    all_to_all x3, starting transfers between devices, exchange(): return lax.all_to_all(array, 'enc', split_axis=0, concat_axis=0, tiled=True)  14.9 us
    pallas_call x2, Pallas kernels, route(): pl.pallas_call(functools.partial(route_kernel, turns, not prepares, n_seg...  9.75 us
    pallas_call x2, Pallas kernels, collect(): pl.pallas_call(functools.partial(collect_kernel, turns, n_seg, seg_rows),...  5.77 us
    all_to_all x3, waiting for transfers between devices, exchange(): return lax.all_to_all(array, 'enc', split_axis=0, concat_axis=0, tiled=True)  5.4 us
  transfers between devices with their start and end apart: 15, of which 8 were waited for; matrix products, arithmetic and copies ran while one was open for 4% of the time, Pallas kernels for 34%

profile of v17, /device:TPU:0, one launch (start us, length us, event | category | flops | bytes accessed | tf_op | source)
XLA Modules:
  0.0 135.8 jit_solution(7641834755583404285)
XLA Ops:
  0.6 2.8 %route_0.1 = (bf16[2,2,32,1024]{3,2,1,0:T(8,128)(2,1)}, bf16[2,2,32,1024]{3,2,1,0:T(8,128)(2,1)}, bf16[2,2,32,1024]{3,2,1,0:T(8,128)(2,1)}, bf16[2,2,32,1024]{3,...) custom-call(s32[4,32]{1,0:T(4,128)} %bitcast.23, ...), custom_call_target="tpu_custom_call" | custom-call | bytes 2097152 | tf_op jit(solution)/shard_map/route_0/pallas_call | solution.py:422
  3.5 0.5 collective-permute-start
  4.0 3.5 %collective-permute-start.1 = (bf16[2,2,32,1024]{3,2,1,0:T(8,128)(2,1)}, bf16[2,2,32,1024]{3,2,1,0:T(8,128)(2,1)S(1)}, u32[]{:S(2)}, u32[]{:S(2)}) collective-permute-start(bf16[2,2,32,1024]{3,2,1,0:T(8,128)(2,1)} %get-tuple-element.47), channel_id=1, source_target_pairs={{0,6},{1,7},{2,4},{3,5},{4,2},{5,3},{6,0},{7,1},{8,14},{9,15},{10,... | collective-permute-start | bytes 786440 | tf_op jit(solution)/shard_map/ppermute | solution.py:397
  7.5 0.5 collective-permute-start.2
  8.2 2.0 %collective-permute-start.4 = (bf16[2,2,32,1024]{3,2,1,0:T(8,128)(2,1)}, bf16[2,2,32,1024]{3,2,1,0:T(8,128)(2,1)}, u32[]{:S(2)}, u32[]{:S(2)}) collective-permute-start(bf16[2,2,32,1024]{3,2,1,0:T(8,128)(2,1)} %get-tuple-element.50), channel_id=1, source_target_pairs={{0,7},{1,6},{2,5},{3,4},{4,3},{5,2},{6,1},{7,0},{8,15},{9,14},{10,... | collective-permute-start | bytes 786440 | tf_op jit(solution)/shard_map/ppermute | solution.py:397
  10.2 1.0 collective-permute-start.5
  11.3 3.7 %collective-permute-done.1.refs_2_ = bf16[2,2,32,1024]{3,2,1,0:T(8,128)(2,1)S(1)} collective-permute-done((bf16[2,2,32,1024]{3,2,1,0:T(8,128)(2,1)}, bf16[2,2,32,1024]{3,2,1,0:T(8,128)(2,1)S(1)}, u32[]{:S(2)}, u32[]{:S(2)}) %collective-permute-start.1) | collective-permute-done | bytes 262176 | tf_op jit(solution)/shard_map/ppermute | solution.py:397
  14.9 0.7 collective-permute-start.6
  15.7 6.9 %route_2.1 = (bf16[8,2,2,32,1024]{4,3,2,1,0:T(8,128)(2,1)}, bf16[4,2,1616,128]{3,2,1,0:T(8,128)(2,1)}, bf16[4,2,128,1616]{3,2,1,0:T(8,128)(2,1)}) custom-call(s32[4,32]{1,0:T(4,128)} %bitcast.24, bf16[128,4096]{1,0:T(8,128)(2,1)} %q_hbm.3, bf16[128,4096]{1,0:T(8,128)(2,1)} %g_hbm.3, bf16[1,1601,512]{2,1,0:T(8,128)(2,1)} %refs_0_.1, bf16[1,1601,512]{2,1,0:T(8,128)(2,1)} %refs_1_.1), custom_call_target="tpu_custom_call" | custom-call | bytes 12582912 | tf_op jit(solution)/shard_map/route_2/pallas_call | solution.py:422
  22.6 3.2 %collective-permute-done.4.refs_5_ = bf16[2,2,32,1024]{3,2,1,0:T(8,128)(2,1)} collective-permute-done((bf16[2,2,32,1024]{3,2,1,0:T(8,128)(2,1)}, bf16[2,2,32,1024]{3,2,1,0:T(8,128)(2,1)}, u32[]{:S(2)}, u32[]{:S(2)}) %collective-permute-start.4) | collective-permute-done | bytes 262176 | tf_op jit(solution)/shard_map/ppermute | solution.py:397
  25.8 5.6 %collective-permute-done.5.refs_6_ = bf16[2,2,32,1024]{3,2,1,0:T(8,128)(2,1)} collective-permute-done((bf16[2,2,32,1024]{3,2,1,0:T(8,128)(2,1)}, bf16[2,2,32,1024]{3,2,1,0:T(8,128)(2,1)}, u32[]{:S(2)}, u32[]{:S(2)}) %collective-permute-start.5) | collective-permute-done | bytes 262176 | tf_op jit(solution)/shard_map/ppermute | solution.py:397
  31.5 4.4 %all-to-all-start.1 = ((bf16[8,2,2,32,1024]{4,3,2,1,0:T(8,128)(2,1)}), bf16[8,2,2,32,1024]{4,3,2,1,0:T(8,128)(2,1)}, u32[]{:S(2)}, u32[]{:S(2)}) async-start(bf16[8,2,2,32,1024]{4,3,2,1,0:T(8,128)(2,1)} %get-tuple-element.68), calls=%async_computation.1 | async-start | bytes 4194304 | tf_op jit(solution)/shard_map/all_to_all | solution.py:501
  35.9 9.6 %attend_0.1 = (bf16[8,2,2,32,1024]{4,3,2,1,0:T(8,128)(2,1)}, bf16[2,1616,128]{2,1,0:T(8,128)(2,1)}) custom-call(s32[4,32]{1,0:T(4,128)} %bitcast.25, bf16[4,2,1616,128]{3,2,1,0:T(8,128)(2,1)} %get-tuple-element.43.caches, bf16[4,2,128,1616]{3,2,1,0:T(8,128)(2,1)} %get-tuple-element.44.turned_caches, bf16[2,2,32,1024]{3,2,1,0:T(8,128)(2,1)} %get-tuple-element.54.refs_0_, ...), custom_call_target="tpu_custom_call" | custom-call | flops 314769408 | bytes 1048576 | tf_op jit(solution)/shard_map/attend_0/pallas_call | solution.py:449
  45.5 1.8 %collective-permute-start.7 = (bf16[2,1616,128]{2,1,0:T(8,128)(2,1)}, bf16[2,1616,128]{2,1,0:T(8,128)(2,1)S(1)}, u32[]{:S(2)}, u32[]{:S(2)}) collective-permute-start(bf16[2,1616,128]{2,1,0:T(8,128)(2,1)} %get-tuple-element.64), channel_id=1, source_target_pairs={{0,8},{8,0},{16,24},{24,16},{1,9},{9,1},{17,25},{25,17},{2,10},{10... | collective-permute-start | bytes 2482184 | tf_op jit(solution)/shard_map/ppermute | solution.py:397
  47.3 9.8 %attend_1.1 = (bf16[8,2,2,32,1024]{4,3,2,1,0:T(8,128)(2,1)}, bf16[2,1616,128]{2,1,0:T(8,128)(2,1)}) custom-call(s32[4,32]{1,0:T(4,128)} %bitcast.26, bf16[4,2,1616,128]{3,2,1,0:T(8,128)(2,1)} %get-tuple-element.43.caches, bf16[4,2,128,1616]{3,2,1,0:T(8,128)(2,1)} %get-tuple-element.44.turned_caches, ...), custom_call_target="tpu_custom_call", output_to_operand_aliasing={{0}: (11, {})} | custom-call | flops 314769408 | bytes 1048576 | tf_op jit(solution)/shard_map/attend_1/pallas_call | solution.py:449
  57.1 5.4 %all-to-all-done.1.refs_0_ = bf16[8,2,2,32,1024]{4,3,2,1,0:T(8,128)(2,1)} async-done(((bf16[8,2,2,32,1024]{4,3,2,1,0:T(8,128)(2,1)}), bf16[8,2,2,32,1024]{4,3,2,1,0:T(8,128)(2,1)}, u32[]{:S(2)}, u32[]{:S(2)}) %all-to-all-start.1) | async-done | bytes 2097184 | tf_op jit(solution)/shard_map/all_to_all | solution.py:501
  62.5 5.4 %all-to-all-start = ((bf16[8,2,2,32,1024]{4,3,2,1,0:T(8,128)(2,1)}), bf16[8,2,2,32,1024]{4,3,2,1,0:T(8,128)(2,1)}, u32[]{:S(2)}, u32[]{:S(2)}) async-start(bf16[8,2,2,32,1024]{4,3,2,1,0:T(8,128)(2,1)} %get-tuple-element.63), calls=%async_computation | async-start | bytes 4194304 | tf_op jit(solution)/shard_map/all_to_all | solution.py:501
  67.9 0.7 fusion.6
  68.6 2.7 %collective-permute-start.9 = (bf16[800,128]{1,0:T(8,128)(2,1)}, bf16[800,128]{1,0:T(8,128)(2,1)}, u32[]{:S(2)}, u32[]{:S(2)}) collective-permute-start(bf16[800,128]{1,0:T(8,128)(2,1)} %fusion.6), channel_id=1, source_target_pairs={{0,16},{8,24},{16,0},{24,8},{1,17},{9,25},{17,1},{25,9},{2,18},{10... | collective-permute-start | bytes 614408 | tf_op jit(solution)/shard_map/ppermute | solution.py:397
  71.3 0.9 fusion.2
  72.4 16.7 %attend_2.1 = (bf16[8,2,2,32,1024]{4,3,2,1,0:T(8,128)(2,1)}, bf16[2,1616,128]{2,1,0:T(8,128)(2,1)}, bf16[2,1616,128]{2,1,0:T(8,128)(2,1)}) custom-call(s32[4,32]{1,0:T(4,128)} %bitcast.27, bf16[4,2,1616,128]{3,2,1,0:T(8,128)(2,1)} %get-tuple-element.43.caches, bf16[4,2,128,1616]{3,2,1,0:T(8,128)(2,1)} %get-tuple-element.44.turned_caches, ...), custom_call_target="tpu_custom_call" | custom-call | flops 7554465792 | bytes 8388608 | tf_op jit(solution)/shard_map/attend_2/pallas_call | solution.py:449
  89.1 1.7 %collective-permute-done.9 = bf16[800,128]{1,0:T(8,128)(2,1)} collective-permute-done((bf16[800,128]{1,0:T(8,128)(2,1)}, bf16[800,128]{1,0:T(8,128)(2,1)}, u32[]{:S(2)}, u32[]{:S(2)}) %collective-permute-start.9) | collective-permute-done | bytes 204832 | tf_op jit(solution)/shard_map/ppermute | solution.py:397
  90.9 8.6 %collective-permute-done.8 = bf16[1616,128]{1,0:T(8,128)(2,1)} collective-permute-done((bf16[1616,128]{1,0:T(8,128)(2,1)}, bf16[1616,128]{1,0:T(8,128)(2,1)}, u32[]{:S(2)}, u32[]{:S(2)}) %collective-permute-start.8) | collective-permute-done | bytes 413728 | tf_op jit(solution)/shard_map/ppermute | solution.py:397
  99.5 5.2 %all-to-all-start.2 = ((bf16[8,2,2,32,1024]{4,3,2,1,0:T(8,128)(2,1)}), bf16[8,2,2,32,1024]{4,3,2,1,0:T(8,128)(2,1)S(1)}, u32[]{:S(2)}, u32[]{:S(2)}) async-start(bf16[8,2,2,32,1024]{4,3,2,1,0:T(8,128)(2,1)} %get-tuple-element.72), calls=%async_computation.2 | async-start | bytes 4194304 | tf_op jit(solution)/shard_map/all_to_all | solution.py:501
  104.6 0.6 collective-permute-start.10
  105.3 1.0 fusion.5
  106.3 3.4 %collective-permute-start.11 = (bf16[816,128]{1,0:T(8,128)(2,1)S(1)}, bf16[816,128]{1,0:T(8,128)(2,1)S(1)}, u32[]{:S(2)}, u32[]{:S(2)}) collective-permute-start(bf16[816,128]{1,0:T(8,128)(2,1)S(1)} %fusion.5), channel_id=1, source_target_pairs={{0,16},{8,24},{16,0},{24,8},{1,17},{9,25},{17,1},{25,9},{2,18},{10... | collective-permute-start | bytes 626696 | tf_op jit(solution)/shard_map/ppermute | solution.py:397
  109.7 2.7 %collect_0.1 = (bf16[128,4096]{1,0:T(8,128)(2,1)}, bf16[128,4096]{1,0:T(8,128)(2,1)}) custom-call(s32[4,32]{1,0:T(4,128)S(1)} %bitcast.28, bf16[8,2,2,32,1024]{4,3,2,1,0:T(8,128)(2,1)} %all-to-all-done.returned), custom_call_target="tpu_custom_call" | custom-call | bytes 4194304 | tf_op jit(solution)/shard_map/collect_0/pallas_call | solution.py:484
  112.4 15.8 %collective-permute-done.11 = bf16[816,128]{1,0:T(8,128)(2,1)S(1)} collective-permute-done((bf16[816,128]{1,0:T(8,128)(2,1)S(1)}, bf16[816,128]{1,0:T(8,128)(2,1)S(1)}, u32[]{:S(2)}, u32[]{:S(2)}) %collective-permute-start.11) | collective-permute-done | bytes 208928 | tf_op jit(solution)/shard_map/ppermute | solution.py:397
  128.2 1.9 %collective-permute-done.10 = bf16[2,1616,128]{2,1,0:T(8,128)(2,1)S(1)} collective-permute-done((bf16[2,1616,128]{2,1,0:T(8,128)(2,1)}, bf16[2,1616,128]{2,1,0:T(8,128)(2,1)S(1)}, u32[]{:S(2)}, u32[]{:S(2)}) %collective-permute-start.10) | collective-permute-done | bytes 827424 | tf_op jit(solution)/shard_map/ppermute | solution.py:397
  130.2 2.3 %fusion.4 = (bf16[1,1601,128]{2,1,0:T(8,128)(2,1)}, bf16[1,1601,128]{2,1,0:T(8,128)(2,1)}) fusion(bf16[816,128]{1,0:T(8,128)(2,1)S(1)} %collective-permute-done.11, bf16[800,128]{1,0:T(8,128)(2,1)} %collective-permute-done.9, bf16[2,1616,128]{2,1,0:T(8,128)(2,1)S(1)} %collective-permute-done.10, bf16[2,1616,128]{2,1,0:T(8,128)(2,1)S(1)} %copy-done.5, ...), kind=kLoop, calls=%fused_computation.8 | loop fusion | flops 3073920 | bytes 3282688 | tf_op jit(solution)/shard_map/broadcast_in_dim | solution.py:548
  132.5 3.1 %collect_2.1 = (bf16[128,4096]{1,0:T(8,128)(2,1)}, bf16[128,4096]{1,0:T(8,128)(2,1)}) custom-call(s32[4,32]{1,0:T(4,128)S(1)} %bitcast.29, bf16[8,2,2,32,1024]{4,3,2,1,0:T(8,128)(2,1)S(1)} %all-to-all-done.2.returned, bf16[128,4096]{1,0:T(8,128)(2,1)} %get-tuple-element.74.refs_0_, ...), custom_call_target="tpu_custom_call", output_to_operand_aliasing={{0}: (2, {}), {1}: (3, {})} | custom-call | bytes 4194304 | tf_op jit(solution)/shard_map/collect_2/pallas_call | solution.py:484
  (21 shorter events, 0.4 us)
Async XLA Ops:
  3.5 6.8 %collective-permute-start = (bf16[2,2,32,1024]{3,2,1,0:T(8,128)(2,1)}, bf16[2,2,32,1024]{3,2,1,0:T(8,128)(2,1)S(1)}, u32[]{:S(2)}, u32[]{:S(2)}) collective-permute-start(bf16[2,2,32,1024]{3,2,1,0:T(8,128)(2,1)} %get-tuple-element.46), channel_id=1, source_target_pairs={{0,1},{1,0},{2,3},{3,2},{4,5},{5,4},{6,7},{7,6},{8,9},{9,8},{10,11... | collective-permute-start | bytes 786440 | tf_op jit(solution)/shard_map/ppermute | solution.py:397
  4.0 10.9 %collective-permute-start.1 = (bf16[2,2,32,1024]{3,2,1,0:T(8,128)(2,1)}, bf16[2,2,32,1024]{3,2,1,0:T(8,128)(2,1)S(1)}, u32[]{:S(2)}, u32[]{:S(2)}) collective-permute-start(bf16[2,2,32,1024]{3,2,1,0:T(8,128)(2,1)} %get-tuple-element.47), channel_id=1, source_target_pairs={{0,6},{1,7},{2,4},{3,5},{4,2},{5,3},{6,0},{7,1},{8,14},{9,15},{10,... | collective-permute-start | bytes 786440 | tf_op jit(solution)/shard_map/ppermute | solution.py:397
  7.5 15.1 %collective-permute-start.2 = (bf16[2,2,32,1024]{3,2,1,0:T(8,128)(2,1)}, bf16[2,2,32,1024]{3,2,1,0:T(8,128)(2,1)S(1)}, u32[]{:S(2)}, u32[]{:S(2)}) collective-permute-start(bf16[2,2,32,1024]{3,2,1,0:T(8,128)(2,1)} %get-tuple-element.48), channel_id=1, source_target_pairs={{0,2},{1,3},{2,0},{3,1},{4,6},{5,7},{6,4},{7,5},{8,10},{9,11},{10,... | collective-permute-start | bytes 786440 | tf_op jit(solution)/shard_map/ppermute | solution.py:397
  8.0 14.6 %collective-permute-start.3 = (bf16[2,2,32,1024]{3,2,1,0:T(8,128)(2,1)}, bf16[2,2,32,1024]{3,2,1,0:T(8,128)(2,1)}, u32[]{:S(2)}, u32[]{:S(2)}) collective-permute-start(bf16[2,2,32,1024]{3,2,1,0:T(8,128)(2,1)} %get-tuple-element.49), channel_id=1, source_target_pairs={{0,4},{1,5},{2,6},{3,7},{4,0},{5,1},{6,2},{7,3},{8,12},{9,13},{10,... | collective-permute-start | bytes 786440 | tf_op jit(solution)/shard_map/ppermute | solution.py:397
  8.2 17.7 %collective-permute-start.4 = (bf16[2,2,32,1024]{3,2,1,0:T(8,128)(2,1)}, bf16[2,2,32,1024]{3,2,1,0:T(8,128)(2,1)}, u32[]{:S(2)}, u32[]{:S(2)}) collective-permute-start(bf16[2,2,32,1024]{3,2,1,0:T(8,128)(2,1)} %get-tuple-element.50), channel_id=1, source_target_pairs={{0,7},{1,6},{2,5},{3,4},{4,3},{5,2},{6,1},{7,0},{8,15},{9,14},{10,... | collective-permute-start | bytes 786440 | tf_op jit(solution)/shard_map/ppermute | solution.py:397
  10.2 12.4 %copy-start.1 = (bf16[2,2,32,1024]{3,2,1,0:T(8,128)(2,1)}, bf16[2,2,32,1024]{3,2,1,0:T(8,128)(2,1)S(1)}, u32[]{:S(2)}) copy-start(bf16[2,2,32,1024]{3,2,1,0:T(8,128)(2,1)S(1)} %collective-permute-done.refs_1_) | copy-start | bytes 786436
  10.2 21.3 %collective-permute-start.5 = (bf16[2,2,32,1024]{3,2,1,0:T(8,128)(2,1)}, bf16[2,2,32,1024]{3,2,1,0:T(8,128)(2,1)}, u32[]{:S(2)}, u32[]{:S(2)}) collective-permute-start(bf16[2,2,32,1024]{3,2,1,0:T(8,128)(2,1)} %get-tuple-element.51), channel_id=1, source_target_pairs={{0,3},{1,2},{2,1},{3,0},{4,7},{5,6},{6,5},{7,4},{8,11},{9,10},{10,... | collective-permute-start | bytes 786440 | tf_op jit(solution)/shard_map/ppermute | solution.py:397
  14.9 7.7 %copy-start.2 = (bf16[2,2,32,1024]{3,2,1,0:T(8,128)(2,1)}, bf16[2,2,32,1024]{3,2,1,0:T(8,128)(2,1)S(1)}, u32[]{:S(2)}) copy-start(bf16[2,2,32,1024]{3,2,1,0:T(8,128)(2,1)S(1)} %collective-permute-done.1.refs_2_) | copy-start | bytes 786436
  14.9 16.6 %collective-permute-start.6 = (bf16[2,2,32,1024]{3,2,1,0:T(8,128)(2,1)}, bf16[2,2,32,1024]{3,2,1,0:T(8,128)(2,1)}, u32[]{:S(2)}, u32[]{:S(2)}) collective-permute-start(bf16[2,2,32,1024]{3,2,1,0:T(8,128)(2,1)} %get-tuple-element.52), channel_id=1, source_target_pairs={{0,5},{1,4},{2,7},{3,6},{4,1},{5,0},{6,3},{7,2},{8,13},{9,12},{10,... | collective-permute-start | bytes 786440 | tf_op jit(solution)/shard_map/ppermute | solution.py:397
  22.6 8.9 %copy-start.3 = (bf16[2,2,32,1024]{3,2,1,0:T(8,128)(2,1)}, bf16[2,2,32,1024]{3,2,1,0:T(8,128)(2,1)S(1)}, u32[]{:S(2)}) copy-start(bf16[2,2,32,1024]{3,2,1,0:T(8,128)(2,1)S(1)} %collective-permute-done.2.refs_3_) | copy-start | bytes 786436
  31.5 31.0 %all-to-all-start.1 = ((bf16[8,2,2,32,1024]{4,3,2,1,0:T(8,128)(2,1)}), bf16[8,2,2,32,1024]{4,3,2,1,0:T(8,128)(2,1)}, u32[]{:S(2)}, u32[]{:S(2)}) async-start(bf16[8,2,2,32,1024]{4,3,2,1,0:T(8,128)(2,1)} %get-tuple-element.68), calls=%async_computation.1 | async-start | bytes 4194304 | tf_op jit(solution)/shard_map/all_to_all | solution.py:501
  45.5 22.4 %collective-permute-start.7 = (bf16[2,1616,128]{2,1,0:T(8,128)(2,1)}, bf16[2,1616,128]{2,1,0:T(8,128)(2,1)S(1)}, u32[]{:S(2)}, u32[]{:S(2)}) collective-permute-start(bf16[2,1616,128]{2,1,0:T(8,128)(2,1)} %get-tuple-element.64), channel_id=1, source_target_pairs={{0,8},{8,0},{16,24},{24,16},{1,9},{9,1},{17,25},{25,17},{2,10},{10... | collective-permute-start | bytes 2482184 | tf_op jit(solution)/shard_map/ppermute | solution.py:397
  62.5 5.4 %copy-start.4 = (bf16[2,1616,128]{2,1,0:T(8,128)(2,1)S(1)}, bf16[2,1616,128]{2,1,0:T(8,128)(2,1)}, u32[]{:S(2)}) copy-start(bf16[2,1616,128]{2,1,0:T(8,128)(2,1)} %get-tuple-element.66) | copy-start | bytes 2482180
  62.5 37.0 %all-to-all-start = ((bf16[8,2,2,32,1024]{4,3,2,1,0:T(8,128)(2,1)}), bf16[8,2,2,32,1024]{4,3,2,1,0:T(8,128)(2,1)}, u32[]{:S(2)}, u32[]{:S(2)}) async-start(bf16[8,2,2,32,1024]{4,3,2,1,0:T(8,128)(2,1)} %get-tuple-element.63), calls=%async_computation | async-start | bytes 4194304 | tf_op jit(solution)/shard_map/all_to_all | solution.py:501
  68.6 22.2 %collective-permute-start.9 = (bf16[800,128]{1,0:T(8,128)(2,1)}, bf16[800,128]{1,0:T(8,128)(2,1)}, u32[]{:S(2)}, u32[]{:S(2)}) collective-permute-start(bf16[800,128]{1,0:T(8,128)(2,1)} %fusion.6), channel_id=1, source_target_pairs={{0,16},{8,24},{16,0},{24,8},{1,17},{9,25},{17,1},{25,9},{2,18},{10... | collective-permute-start | bytes 614408 | tf_op jit(solution)/shard_map/ppermute | solution.py:397
  72.2 27.3 %collective-permute-start.8 = (bf16[1616,128]{1,0:T(8,128)(2,1)}, bf16[1616,128]{1,0:T(8,128)(2,1)}, u32[]{:S(2)}, u32[]{:S(2)}) collective-permute-start(bf16[1616,128]{1,0:T(8,128)(2,1)} %fusion.2), channel_id=1, source_target_pairs={{0,16},{8,24},{16,0},{24,8},{1,17},{9,25},{17,1},{25,9},{2,18},{10... | collective-permute-start | bytes 1241096 | tf_op jit(solution)/shard_map/ppermute | solution.py:397
  99.5 10.2 %copy-start = (s32[32,4]{0,1:T(4,128)S(1)}, s32[32,4]{0,1:T(4,128)}, u32[]{:S(2)}) copy-start(s32[32,4]{0,1:T(4,128)} %param.8) | copy-start | bytes 1540
  99.5 33.0 %all-to-all-start.2 = ((bf16[8,2,2,32,1024]{4,3,2,1,0:T(8,128)(2,1)}), bf16[8,2,2,32,1024]{4,3,2,1,0:T(8,128)(2,1)S(1)}, u32[]{:S(2)}, u32[]{:S(2)}) async-start(bf16[8,2,2,32,1024]{4,3,2,1,0:T(8,128)(2,1)} %get-tuple-element.72), calls=%async_computation.2 | async-start | bytes 4194304 | tf_op jit(solution)/shard_map/all_to_all | solution.py:501
  104.6 25.5 %copy-start.5 = (bf16[2,1616,128]{2,1,0:T(8,128)(2,1)S(1)}, bf16[2,1616,128]{2,1,0:T(8,128)(2,1)}, u32[]{:S(2)}) copy-start(bf16[2,1616,128]{2,1,0:T(8,128)(2,1)} %get-tuple-element.78) | copy-start | bytes 2482180
  104.6 25.5 %collective-permute-start.10 = (bf16[2,1616,128]{2,1,0:T(8,128)(2,1)}, bf16[2,1616,128]{2,1,0:T(8,128)(2,1)S(1)}, u32[]{:S(2)}, u32[]{:S(2)}) collective-permute-start(bf16[2,1616,128]{2,1,0:T(8,128)(2,1)} %get-tuple-element.79), channel_id=1, source_target_pairs={{0,8},{8,0},{16,24},{24,16},{1,9},{9,1},{17,25},{25,17},{2,10},{10... | collective-permute-start | bytes 2482184 | tf_op jit(solution)/shard_map/ppermute | solution.py:397
  106.3 22.0 %collective-permute-start.11 = (bf16[816,128]{1,0:T(8,128)(2,1)S(1)}, bf16[816,128]{1,0:T(8,128)(2,1)S(1)}, u32[]{:S(2)}, u32[]{:S(2)}) collective-permute-start(bf16[816,128]{1,0:T(8,128)(2,1)S(1)} %fusion.5), channel_id=1, source_target_pairs={{0,16},{8,24},{16,0},{24,8},{1,17},{9,25},{17,1},{25,9},{2,18},{10... | collective-permute-start | bytes 626696 | tf_op jit(solution)/shard_map/ppermute | solution.py:397

commit v18 on v17

--- a/solution.py
+++ b/solution.py
@@ -518,7 +518,7 @@
     grads.append(last)
     if butterfly:
         passed, last = lax.optimization_barrier((passed, last))
-        half = padded // 32 * 16
+        half = padded // 64 * 16
         cuts = [(0, 0, padded), (1, 0, half), (1, half, padded)]
         pair = [
             (last[j, a:b].astype(f32) + passed[j, a:b].astype(f32)).astype(bf16)

time: 136 us -> 134 us (0.985)
  Pallas kernels: 51.7 us -> 61.8 us
  waiting for transfers between devices: 46 us -> 37.7 us
  starting transfers between devices: 32.2 us -> 28.8 us
    pallas_call x3, Pallas kernels: 36.1 us -> 46.3 us  [attend(): pl.pallas_call(functools.partial(attend_kernel, turns, offset, len(before...]
    all_to_all x3, waiting for transfers between devices: 5.4 us -> 0.29 us  [exchange(): return lax.all_to_all(array, 'enc', split_axis=0, concat_axis=0, tiled=True)]
    ppermute x12, waiting for transfers between devices: 40.6 us -> 37.4 us  [xor_permute(): return lax.ppermute(array, axis, [(i, i ^ k) for i in range(size)])]
    ppermute x12, starting transfers between devices: 17.3 us -> 14.9 us  [xor_permute(): return lax.ppermute(array, axis, [(i, i ^ k) for i in range(size)])]
  transfers between devices with their start and end apart: 15 -> 15, of which waited for: 8 -> 8; matrix products, arithmetic and copies ran while one was open for 4% -> 3% of each run, Pallas kernels for 34% -> 42%
where the time goes in v18:
time: 134 us
  Pallas kernels  61.8 us (46%)
  waiting for transfers between devices  37.7 us (28%)
  starting transfers between devices  28.8 us (21%)
  other arithmetic  4.25 us (3%)
    pallas_call x3, Pallas kernels, attend(): pl.pallas_call(functools.partial(attend_kernel, turns, offset, len(before...  46.3 us
    ppermute x12, waiting for transfers between devices, xor_permute(): return lax.ppermute(array, axis, [(i, i ^ k) for i in range(size)])  37.4 us
    ppermute x12, starting transfers between devices, xor_permute(): return lax.ppermute(array, axis, [(i, i ^ k) for i in range(size)])  14.9 us
    all_to_all x3, starting transfers between devices, exchange(): return lax.all_to_all(array, 'enc', split_axis=0, concat_axis=0, tiled=True)  14 us
    pallas_call x2, Pallas kernels, route(): pl.pallas_call(functools.partial(route_kernel, turns, not prepares, n_seg...  9.75 us
    pallas_call x2, Pallas kernels, collect(): pl.pallas_call(functools.partial(collect_kernel, turns, n_seg, seg_rows),...  5.77 us
  transfers between devices with their start and end apart: 15, of which 8 were waited for; matrix products, arithmetic and copies ran while one was open for 3% of the time, Pallas kernels for 42%

profile of v18, /device:TPU:0, one launch (start us, length us, event | category | flops | bytes accessed | tf_op | source)
XLA Modules:
  0.0 133.6 jit_solution(3773751122982409947)
XLA Ops:
  0.6 2.8 %route_0.1 = (bf16[2,2,32,1024]{3,2,1,0:T(8,128)(2,1)}, bf16[2,2,32,1024]{3,2,1,0:T(8,128)(2,1)}, bf16[2,2,32,1024]{3,2,1,0:T(8,128)(2,1)}, bf16[2,2,32,1024]{3,...) custom-call(s32[4,32]{1,0:T(4,128)} %bitcast.23, ...), custom_call_target="tpu_custom_call" | custom-call | bytes 2097152 | tf_op jit(solution)/shard_map/route_0/pallas_call | solution.py:422
  3.5 0.5 collective-permute-start
  4.0 3.5 %collective-permute-start.1 = (bf16[2,2,32,1024]{3,2,1,0:T(8,128)(2,1)}, bf16[2,2,32,1024]{3,2,1,0:T(8,128)(2,1)S(1)}, u32[]{:S(2)}, u32[]{:S(2)}) collective-permute-start(bf16[2,2,32,1024]{3,2,1,0:T(8,128)(2,1)} %get-tuple-element.47), channel_id=1, source_target_pairs={{0,6},{1,7},{2,4},{3,5},{4,2},{5,3},{6,0},{7,1},{8,14},{9,15},{10,... | collective-permute-start | bytes 786440 | tf_op jit(solution)/shard_map/ppermute | solution.py:397
  7.5 0.5 collective-permute-start.2
  8.0 0.1 collective-permute-start.3
  8.2 2.0 %collective-permute-start.4 = (bf16[2,2,32,1024]{3,2,1,0:T(8,128)(2,1)}, bf16[2,2,32,1024]{3,2,1,0:T(8,128)(2,1)}, u32[]{:S(2)}, u32[]{:S(2)}) collective-permute-start(bf16[2,2,32,1024]{3,2,1,0:T(8,128)(2,1)} %get-tuple-element.50), channel_id=1, source_target_pairs={{0,7},{1,6},{2,5},{3,4},{4,3},{5,2},{6,1},{7,0},{8,15},{9,14},{10,... | collective-permute-start | bytes 786440 | tf_op jit(solution)/shard_map/ppermute | solution.py:397
  10.2 1.0 collective-permute-start.5
  11.2 3.7 %collective-permute-done.1.refs_2_ = bf16[2,2,32,1024]{3,2,1,0:T(8,128)(2,1)S(1)} collective-permute-done((bf16[2,2,32,1024]{3,2,1,0:T(8,128)(2,1)}, bf16[2,2,32,1024]{3,2,1,0:T(8,128)(2,1)S(1)}, u32[]{:S(2)}, u32[]{:S(2)}) %collective-permute-start.1) | collective-permute-done | bytes 262176 | tf_op jit(solution)/shard_map/ppermute | solution.py:397
  14.9 0.7 collective-permute-start.6
  15.6 6.9 %route_2.1 = (bf16[8,2,2,32,1024]{4,3,2,1,0:T(8,128)(2,1)}, bf16[4,2,1616,128]{3,2,1,0:T(8,128)(2,1)}, bf16[4,2,128,1616]{3,2,1,0:T(8,128)(2,1)}) custom-call(s32[4,32]{1,0:T(4,128)} %bitcast.24, bf16[128,4096]{1,0:T(8,128)(2,1)} %q_hbm.3, bf16[128,4096]{1,0:T(8,128)(2,1)} %g_hbm.3, bf16[1,1601,512]{2,1,0:T(8,128)(2,1)} %refs_0_.1, bf16[1,1601,512]{2,1,0:T(8,128)(2,1)} %refs_1_.1), custom_call_target="tpu_custom_call" | custom-call | bytes 12582912 | tf_op jit(solution)/shard_map/route_2/pallas_call | solution.py:422
  22.6 3.2 %collective-permute-done.4.refs_5_ = bf16[2,2,32,1024]{3,2,1,0:T(8,128)(2,1)} collective-permute-done((bf16[2,2,32,1024]{3,2,1,0:T(8,128)(2,1)}, bf16[2,2,32,1024]{3,2,1,0:T(8,128)(2,1)}, u32[]{:S(2)}, u32[]{:S(2)}) %collective-permute-start.4) | collective-permute-done | bytes 262176 | tf_op jit(solution)/shard_map/ppermute | solution.py:397
  25.8 5.6 %collective-permute-done.5.refs_6_ = bf16[2,2,32,1024]{3,2,1,0:T(8,128)(2,1)} collective-permute-done((bf16[2,2,32,1024]{3,2,1,0:T(8,128)(2,1)}, bf16[2,2,32,1024]{3,2,1,0:T(8,128)(2,1)}, u32[]{:S(2)}, u32[]{:S(2)}) %collective-permute-start.5) | collective-permute-done | bytes 262176 | tf_op jit(solution)/shard_map/ppermute | solution.py:397
  31.5 4.4 %all-to-all-start.1 = ((bf16[8,2,2,32,1024]{4,3,2,1,0:T(8,128)(2,1)}), bf16[8,2,2,32,1024]{4,3,2,1,0:T(8,128)(2,1)}, u32[]{:S(2)}, u32[]{:S(2)}) async-start(bf16[8,2,2,32,1024]{4,3,2,1,0:T(8,128)(2,1)} %get-tuple-element.68), calls=%async_computation.1 | async-start | bytes 4194304 | tf_op jit(solution)/shard_map/all_to_all | solution.py:501
  35.8 13.0 %attend_0.1 = (bf16[8,2,2,32,1024]{4,3,2,1,0:T(8,128)(2,1)}, bf16[2,1616,128]{2,1,0:T(8,128)(2,1)}) custom-call(s32[4,32]{1,0:T(4,128)} %bitcast.25, bf16[4,2,1616,128]{3,2,1,0:T(8,128)(2,1)} %get-tuple-element.43.caches, bf16[4,2,128,1616]{3,2,1,0:T(8,128)(2,1)} %get-tuple-element.44.turned_caches, bf16[2,2,32,1024]{3,2,1,0:T(8,128)(2,1)} %get-tuple-element.54.refs_0_, ...), custom_call_target="tpu_custom_call" | custom-call | flops 314769408 | bytes 1048576 | tf_op jit(solution)/shard_map/attend_0/pallas_call | solution.py:449
  49.0 13.2 %attend_1.1 = (bf16[8,2,2,32,1024]{4,3,2,1,0:T(8,128)(2,1)}, bf16[2,1616,128]{2,1,0:T(8,128)(2,1)}) custom-call(s32[4,32]{1,0:T(4,128)} %bitcast.26, bf16[4,2,1616,128]{3,2,1,0:T(8,128)(2,1)} %get-tuple-element.43.caches, bf16[4,2,128,1616]{3,2,1,0:T(8,128)(2,1)} %get-tuple-element.44.turned_caches, ...), custom_call_target="tpu_custom_call", output_to_operand_aliasing={{0}: (11, {})} | custom-call | flops 314769408 | bytes 1048576 | tf_op jit(solution)/shard_map/attend_1/pallas_call | solution.py:449
  62.2 0.3 all-to-all-done.1.refs_0_
  62.5 4.9 %all-to-all-start = ((bf16[8,2,2,32,1024]{4,3,2,1,0:T(8,128)(2,1)}), bf16[8,2,2,32,1024]{4,3,2,1,0:T(8,128)(2,1)}, u32[]{:S(2)}, u32[]{:S(2)}) async-start(bf16[8,2,2,32,1024]{4,3,2,1,0:T(8,128)(2,1)} %get-tuple-element.63), calls=%async_computation | async-start | bytes 4194304 | tf_op jit(solution)/shard_map/all_to_all | solution.py:501
  67.4 2.6 %collective-permute-done.7 = bf16[2,1616,128]{2,1,0:T(8,128)(2,1)S(1)} collective-permute-done((bf16[2,1616,128]{2,1,0:T(8,128)(2,1)}, bf16[2,1616,128]{2,1,0:T(8,128)(2,1)S(1)}, u32[]{:S(2)}, u32[]{:S(2)}) %collective-permute-start.7) | collective-permute-done | bytes 827424 | tf_op jit(solution)/shard_map/ppermute | solution.py:397
  70.0 2.8 %collective-permute-start.9 = (bf16[400,128]{1,0:T(8,128)(2,1)S(1)}, bf16[400,128]{1,0:T(8,128)(2,1)}, u32[]{:S(2)}, u32[]{:S(2)}) collective-permute-start(bf16[400,128]{1,0:T(8,128)(2,1)S(1)} %fusion.6), channel_id=1, source_target_pairs={{0,16},{8,24},{16,0},{24,8},{1,17},{9,25},{17,1},{25,9},{2,18},{10... | collective-permute-start | bytes 307208 | tf_op jit(solution)/shard_map/ppermute | solution.py:397
  72.8 0.9 fusion.2
  73.7 0.2 collective-permute-start.8
  73.9 20.0 %attend_2.1 = (bf16[8,2,2,32,1024]{4,3,2,1,0:T(8,128)(2,1)}, bf16[2,1616,128]{2,1,0:T(8,128)(2,1)}, bf16[2,1616,128]{2,1,0:T(8,128)(2,1)}) custom-call(s32[4,32]{1,0:T(4,128)} %bitcast.27, bf16[4,2,1616,128]{3,2,1,0:T(8,128)(2,1)} %get-tuple-element.43.caches, bf16[4,2,128,1616]{3,2,1,0:T(8,128)(2,1)} %get-tuple-element.44.turned_caches, ...), custom_call_target="tpu_custom_call" | custom-call | flops 7554465792 | bytes 8388608 | tf_op jit(solution)/shard_map/attend_2/pallas_call | solution.py:449
  93.9 1.7 %collective-permute-done.8 = bf16[1616,128]{1,0:T(8,128)(2,1)} collective-permute-done((bf16[1616,128]{1,0:T(8,128)(2,1)}, bf16[1616,128]{1,0:T(8,128)(2,1)}, u32[]{:S(2)}, u32[]{:S(2)}) %collective-permute-start.8) | collective-permute-done | bytes 413728 | tf_op jit(solution)/shard_map/ppermute | solution.py:397
  95.6 4.7 %all-to-all-start.2 = ((bf16[8,2,2,32,1024]{4,3,2,1,0:T(8,128)(2,1)}), bf16[8,2,2,32,1024]{4,3,2,1,0:T(8,128)(2,1)S(1)}, u32[]{:S(2)}, u32[]{:S(2)}) async-start(bf16[8,2,2,32,1024]{4,3,2,1,0:T(8,128)(2,1)} %get-tuple-element.72), calls=%async_computation.2 | async-start | bytes 4194304 | tf_op jit(solution)/shard_map/all_to_all | solution.py:501
  100.3 1.8 %collective-permute-start.10 = (bf16[2,1616,128]{2,1,0:T(8,128)(2,1)}, bf16[2,1616,128]{2,1,0:T(8,128)(2,1)S(1)}, u32[]{:S(2)}, u32[]{:S(2)}) collective-permute-start(bf16[2,1616,128]{2,1,0:T(8,128)(2,1)} %get-tuple-element.79), channel_id=1, source_target_pairs={{0,8},{8,0},{16,24},{24,16},{1,9},{9,1},{17,25},{25,17},{2,10},{10... | collective-permute-start | bytes 2482184 | tf_op jit(solution)/shard_map/ppermute | solution.py:397
  102.1 1.1 fusion.5
  103.1 1.5 %collective-permute-start.11 = (bf16[1216,128]{1,0:T(8,128)(2,1)S(1)}, bf16[1216,128]{1,0:T(8,128)(2,1)S(1)}, u32[]{:S(2)}, u32[]{:S(2)}) collective-permute-start(bf16[1216,128]{1,0:T(8,128)(2,1)S(1)} %fusion.5), channel_id=1, source_target_pairs={{0,16},{8,24},{16,0},{24,8},{1,17},{9,25},{17,1},{25,9},{2,18},{10... | collective-permute-start | bytes 933896 | tf_op jit(solution)/shard_map/ppermute | solution.py:397
  104.6 2.7 %collect_0.1 = (bf16[128,4096]{1,0:T(8,128)(2,1)}, bf16[128,4096]{1,0:T(8,128)(2,1)}) custom-call(s32[4,32]{1,0:T(4,128)S(1)} %bitcast.28, bf16[8,2,2,32,1024]{4,3,2,1,0:T(8,128)(2,1)} %all-to-all-done.returned), custom_call_target="tpu_custom_call" | custom-call | bytes 4194304 | tf_op jit(solution)/shard_map/collect_0/pallas_call | solution.py:484
  107.3 19.9 %collective-permute-done.11 = bf16[1216,128]{1,0:T(8,128)(2,1)S(1)} collective-permute-done((bf16[1216,128]{1,0:T(8,128)(2,1)S(1)}, bf16[1216,128]{1,0:T(8,128)(2,1)S(1)}, u32[]{:S(2)}, u32[]{:S(2)}) %collective-permute-start.11) | collective-permute-done | bytes 311328 | tf_op jit(solution)/shard_map/ppermute | solution.py:397
  127.2 0.7 collective-permute-done.10
  128.0 2.3 %fusion.4 = (bf16[1,1601,128]{2,1,0:T(8,128)(2,1)}, bf16[1,1601,128]{2,1,0:T(8,128)(2,1)}) fusion(bf16[1216,128]{1,0:T(8,128)(2,1)S(1)} %collective-permute-done.11, bf16[400,128]{1,0:T(8,128)(2,1)} %collective-permute-done.9, bf16[2,1616,128]{2,1,0:T(8,128)(2,1)S(1)} %collective-permute-done.10, bf16[2,1616,128]{2,1,0:T(8,128)(2,1)S(1)} %copy-done.5, ...), kind=kLoop, calls=%fused_computation.8 | loop fusion | flops 3073920 | bytes 3282688 | tf_op jit(solution)/shard_map/broadcast_in_dim | solution.py:548
  130.3 3.1 %collect_2.1 = (bf16[128,4096]{1,0:T(8,128)(2,1)}, bf16[128,4096]{1,0:T(8,128)(2,1)}) custom-call(s32[4,32]{1,0:T(4,128)S(1)} %bitcast.29, bf16[8,2,2,32,1024]{4,3,2,1,0:T(8,128)(2,1)S(1)} %all-to-all-done.2.returned, bf16[128,4096]{1,0:T(8,128)(2,1)} %get-tuple-element.74.refs_0_, ...), custom_call_target="tpu_custom_call", output_to_operand_aliasing={{0}: (2, {}), {1}: (3, {})} | custom-call | bytes 4194304 | tf_op jit(solution)/shard_map/collect_2/pallas_call | solution.py:484
  (21 shorter events, 0.1 us)
Async XLA Ops:
  3.5 6.7 %collective-permute-start = (bf16[2,2,32,1024]{3,2,1,0:T(8,128)(2,1)}, bf16[2,2,32,1024]{3,2,1,0:T(8,128)(2,1)S(1)}, u32[]{:S(2)}, u32[]{:S(2)}) collective-permute-start(bf16[2,2,32,1024]{3,2,1,0:T(8,128)(2,1)} %get-tuple-element.46), channel_id=1, source_target_pairs={{0,1},{1,0},{2,3},{3,2},{4,5},{5,4},{6,7},{7,6},{8,9},{9,8},{10,11... | collective-permute-start | bytes 786440 | tf_op jit(solution)/shard_map/ppermute | solution.py:397
  4.0 10.9 %collective-permute-start.1 = (bf16[2,2,32,1024]{3,2,1,0:T(8,128)(2,1)}, bf16[2,2,32,1024]{3,2,1,0:T(8,128)(2,1)S(1)}, u32[]{:S(2)}, u32[]{:S(2)}) collective-permute-start(bf16[2,2,32,1024]{3,2,1,0:T(8,128)(2,1)} %get-tuple-element.47), channel_id=1, source_target_pairs={{0,6},{1,7},{2,4},{3,5},{4,2},{5,3},{6,0},{7,1},{8,14},{9,15},{10,... | collective-permute-start | bytes 786440 | tf_op jit(solution)/shard_map/ppermute | solution.py:397
  7.5 15.1 %collective-permute-start.2 = (bf16[2,2,32,1024]{3,2,1,0:T(8,128)(2,1)}, bf16[2,2,32,1024]{3,2,1,0:T(8,128)(2,1)S(1)}, u32[]{:S(2)}, u32[]{:S(2)}) collective-permute-start(bf16[2,2,32,1024]{3,2,1,0:T(8,128)(2,1)} %get-tuple-element.48), channel_id=1, source_target_pairs={{0,2},{1,3},{2,0},{3,1},{4,6},{5,7},{6,4},{7,5},{8,10},{9,11},{10,... | collective-permute-start | bytes 786440 | tf_op jit(solution)/shard_map/ppermute | solution.py:397
  8.0 14.6 %collective-permute-start.3 = (bf16[2,2,32,1024]{3,2,1,0:T(8,128)(2,1)}, bf16[2,2,32,1024]{3,2,1,0:T(8,128)(2,1)}, u32[]{:S(2)}, u32[]{:S(2)}) collective-permute-start(bf16[2,2,32,1024]{3,2,1,0:T(8,128)(2,1)} %get-tuple-element.49), channel_id=1, source_target_pairs={{0,4},{1,5},{2,6},{3,7},{4,0},{5,1},{6,2},{7,3},{8,12},{9,13},{10,... | collective-permute-start | bytes 786440 | tf_op jit(solution)/shard_map/ppermute | solution.py:397
  8.2 17.7 %collective-permute-start.4 = (bf16[2,2,32,1024]{3,2,1,0:T(8,128)(2,1)}, bf16[2,2,32,1024]{3,2,1,0:T(8,128)(2,1)}, u32[]{:S(2)}, u32[]{:S(2)}) collective-permute-start(bf16[2,2,32,1024]{3,2,1,0:T(8,128)(2,1)} %get-tuple-element.50), channel_id=1, source_target_pairs={{0,7},{1,6},{2,5},{3,4},{4,3},{5,2},{6,1},{7,0},{8,15},{9,14},{10,... | collective-permute-start | bytes 786440 | tf_op jit(solution)/shard_map/ppermute | solution.py:397
  10.2 12.4 %copy-start.1 = (bf16[2,2,32,1024]{3,2,1,0:T(8,128)(2,1)}, bf16[2,2,32,1024]{3,2,1,0:T(8,128)(2,1)S(1)}, u32[]{:S(2)}) copy-start(bf16[2,2,32,1024]{3,2,1,0:T(8,128)(2,1)S(1)} %collective-permute-done.refs_1_) | copy-start | bytes 786436
  10.2 21.3 %collective-permute-start.5 = (bf16[2,2,32,1024]{3,2,1,0:T(8,128)(2,1)}, bf16[2,2,32,1024]{3,2,1,0:T(8,128)(2,1)}, u32[]{:S(2)}, u32[]{:S(2)}) collective-permute-start(bf16[2,2,32,1024]{3,2,1,0:T(8,128)(2,1)} %get-tuple-element.51), channel_id=1, source_target_pairs={{0,3},{1,2},{2,1},{3,0},{4,7},{5,6},{6,5},{7,4},{8,11},{9,10},{10,... | collective-permute-start | bytes 786440 | tf_op jit(solution)/shard_map/ppermute | solution.py:397
  14.9 7.7 %copy-start.2 = (bf16[2,2,32,1024]{3,2,1,0:T(8,128)(2,1)}, bf16[2,2,32,1024]{3,2,1,0:T(8,128)(2,1)S(1)}, u32[]{:S(2)}) copy-start(bf16[2,2,32,1024]{3,2,1,0:T(8,128)(2,1)S(1)} %collective-permute-done.1.refs_2_) | copy-start | bytes 786436
  14.9 16.6 %collective-permute-start.6 = (bf16[2,2,32,1024]{3,2,1,0:T(8,128)(2,1)}, bf16[2,2,32,1024]{3,2,1,0:T(8,128)(2,1)}, u32[]{:S(2)}, u32[]{:S(2)}) collective-permute-start(bf16[2,2,32,1024]{3,2,1,0:T(8,128)(2,1)} %get-tuple-element.52), channel_id=1, source_target_pairs={{0,5},{1,4},{2,7},{3,6},{4,1},{5,0},{6,3},{7,2},{8,13},{9,12},{10,... | collective-permute-start | bytes 786440 | tf_op jit(solution)/shard_map/ppermute | solution.py:397
  22.6 8.9 %copy-start.3 = (bf16[2,2,32,1024]{3,2,1,0:T(8,128)(2,1)}, bf16[2,2,32,1024]{3,2,1,0:T(8,128)(2,1)S(1)}, u32[]{:S(2)}) copy-start(bf16[2,2,32,1024]{3,2,1,0:T(8,128)(2,1)S(1)} %collective-permute-done.2.refs_3_) | copy-start | bytes 786436
  31.5 31.0 %all-to-all-start.1 = ((bf16[8,2,2,32,1024]{4,3,2,1,0:T(8,128)(2,1)}), bf16[8,2,2,32,1024]{4,3,2,1,0:T(8,128)(2,1)}, u32[]{:S(2)}, u32[]{:S(2)}) async-start(bf16[8,2,2,32,1024]{4,3,2,1,0:T(8,128)(2,1)} %get-tuple-element.68), calls=%async_computation.1 | async-start | bytes 4194304 | tf_op jit(solution)/shard_map/all_to_all | solution.py:501
  48.9 21.1 %collective-permute-start.7 = (bf16[2,1616,128]{2,1,0:T(8,128)(2,1)}, bf16[2,1616,128]{2,1,0:T(8,128)(2,1)S(1)}, u32[]{:S(2)}, u32[]{:S(2)}) collective-permute-start(bf16[2,1616,128]{2,1,0:T(8,128)(2,1)} %get-tuple-element.64), channel_id=1, source_target_pairs={{0,8},{8,0},{16,24},{24,16},{1,9},{9,1},{17,25},{25,17},{2,10},{10... | collective-permute-start | bytes 2482184 | tf_op jit(solution)/shard_map/ppermute | solution.py:397
  62.5 7.5 %copy-start.4 = (bf16[2,1616,128]{2,1,0:T(8,128)(2,1)S(1)}, bf16[2,1616,128]{2,1,0:T(8,128)(2,1)}, u32[]{:S(2)}) copy-start(bf16[2,1616,128]{2,1,0:T(8,128)(2,1)} %get-tuple-element.66) | copy-start | bytes 2482180
  62.5 33.1 %all-to-all-start = ((bf16[8,2,2,32,1024]{4,3,2,1,0:T(8,128)(2,1)}), bf16[8,2,2,32,1024]{4,3,2,1,0:T(8,128)(2,1)}, u32[]{:S(2)}, u32[]{:S(2)}) async-start(bf16[8,2,2,32,1024]{4,3,2,1,0:T(8,128)(2,1)} %get-tuple-element.63), calls=%async_computation | async-start | bytes 4194304 | tf_op jit(solution)/shard_map/all_to_all | solution.py:501
  70.0 23.9 %collective-permute-start.9 = (bf16[400,128]{1,0:T(8,128)(2,1)S(1)}, bf16[400,128]{1,0:T(8,128)(2,1)}, u32[]{:S(2)}, u32[]{:S(2)}) collective-permute-start(bf16[400,128]{1,0:T(8,128)(2,1)S(1)} %fusion.6), channel_id=1, source_target_pairs={{0,16},{8,24},{16,0},{24,8},{1,17},{9,25},{17,1},{25,9},{2,18},{10... | collective-permute-start | bytes 307208 | tf_op jit(solution)/shard_map/ppermute | solution.py:397
  73.7 21.9 %collective-permute-start.8 = (bf16[1616,128]{1,0:T(8,128)(2,1)}, bf16[1616,128]{1,0:T(8,128)(2,1)}, u32[]{:S(2)}, u32[]{:S(2)}) collective-permute-start(bf16[1616,128]{1,0:T(8,128)(2,1)} %fusion.2), channel_id=1, source_target_pairs={{0,16},{8,24},{16,0},{24,8},{1,17},{9,25},{17,1},{25,9},{2,18},{10... | collective-permute-start | bytes 1241096 | tf_op jit(solution)/shard_map/ppermute | solution.py:397
  95.6 9.0 %copy-start = (s32[32,4]{0,1:T(4,128)S(1)}, s32[32,4]{0,1:T(4,128)}, u32[]{:S(2)}) copy-start(s32[32,4]{0,1:T(4,128)} %param.8) | copy-start | bytes 1540
  95.6 34.7 %all-to-all-start.2 = ((bf16[8,2,2,32,1024]{4,3,2,1,0:T(8,128)(2,1)}), bf16[8,2,2,32,1024]{4,3,2,1,0:T(8,128)(2,1)S(1)}, u32[]{:S(2)}, u32[]{:S(2)}) async-start(bf16[8,2,2,32,1024]{4,3,2,1,0:T(8,128)(2,1)} %get-tuple-element.72), calls=%async_computation.2 | async-start | bytes 4194304 | tf_op jit(solution)/shard_map/all_to_all | solution.py:501
  100.2 27.7 %copy-start.5 = (bf16[2,1616,128]{2,1,0:T(8,128)(2,1)S(1)}, bf16[2,1616,128]{2,1,0:T(8,128)(2,1)}, u32[]{:S(2)}) copy-start(bf16[2,1616,128]{2,1,0:T(8,128)(2,1)} %get-tuple-element.78) | copy-start | bytes 2482180
  100.3 27.7 %collective-permute-start.10 = (bf16[2,1616,128]{2,1,0:T(8,128)(2,1)}, bf16[2,1616,128]{2,1,0:T(8,128)(2,1)S(1)}, u32[]{:S(2)}, u32[]{:S(2)}) collective-permute-start(bf16[2,1616,128]{2,1,0:T(8,128)(2,1)} %get-tuple-element.79), channel_id=1, source_target_pairs={{0,8},{8,0},{16,24},{24,16},{1,9},{9,1},{17,25},{25,17},{2,10},{10... | collective-permute-start | bytes 2482184 | tf_op jit(solution)/shard_map/ppermute | solution.py:397
  103.1 24.1 %collective-permute-start.11 = (bf16[1216,128]{1,0:T(8,128)(2,1)S(1)}, bf16[1216,128]{1,0:T(8,128)(2,1)S(1)}, u32[]{:S(2)}, u32[]{:S(2)}) collective-permute-start(bf16[1216,128]{1,0:T(8,128)(2,1)S(1)} %fusion.5), channel_id=1, source_target_pairs={{0,16},{8,24},{16,0},{24,8},{1,17},{9,25},{17,1},{25,9},{2,18},{10... | collective-permute-start | bytes 933896 | tf_op jit(solution)/shard_map/ppermute | solution.py:397
